TPU v7x, 32 devices: a whole 2x2x4 slice. The times are simulated.
32 devices in a mesh: ctx: 8 (over y, x, core), tp: 4 (over z).
Axes of the slice: x: 2, y: 2, z: 4, core: 2. Of those that a mesh axis runs over, the one named last changes fastest.
Arguments:
- tokens: bfloat16 [2048, 2304], P('ctx'), may hold values from -6 to 6
- w_query: bfloat16 [2304, 2048], P('ctx', 'tp'), may hold values from -0.375 to 0.375
- w_key: bfloat16 [2304, 1024], P('ctx', 'tp'), may hold values from -0.125 to 0.125
- w_value: bfloat16 [2304, 1024], P('ctx', 'tp'), may hold values from -0.125 to 0.125
- w_out: bfloat16 [2304, 2048], P('ctx', 'tp'), may hold values from -0.125 to 0.125
- w_gate: bfloat16 [2304, 9216], P('ctx', 'tp'), may hold values from -0.125 to 0.125
- w_up: bfloat16 [2304, 9216], P('ctx', 'tp'), may hold values from -0.125 to 0.125
- w_down: bfloat16 [2304, 9216], P('ctx', 'tp'), may hold values from -0.0625 to 0.0625
- norm_attn_in: bfloat16 [2304], P('ctx'), may hold values from 0.099609375 to 1.8984375
- norm_attn_out: bfloat16 [2304], P('ctx'), may hold values from 0.099609375 to 1.8984375
- norm_ffn_in: bfloat16 [2304], P('ctx'), may hold values from 0.099609375 to 1.8984375
- norm_ffn_out: bfloat16 [2304], P('ctx'), may hold values from 0.099609375 to 1.8984375
- cotangent: bfloat16 [2048, 2304], P('ctx'), may hold values from -6 to 6
Outputs:
- output: bfloat16 [2048, 2304], P('ctx')
- grad_tokens: float32 [2048, 2304], P('ctx')
- grad_w_query: float32 [2304, 2048], P('ctx', 'tp')
- grad_w_key: float32 [2304, 1024], P('ctx', 'tp')
- grad_w_value: float32 [2304, 1024], P('ctx', 'tp')
- grad_w_out: float32 [2304, 2048], P('ctx', 'tp')
- grad_w_gate: float32 [2304, 9216], P('ctx', 'tp')
- grad_w_up: float32 [2304, 9216], P('ctx', 'tp')
- grad_w_down: float32 [2304, 9216], P('ctx', 'tp')
- grad_norm_attn_in: float32 [2304], P('ctx')
- grad_norm_attn_out: float32 [2304], P('ctx')
- grad_norm_ffn_in: float32 [2304], P('ctx')
- grad_norm_ffn_out: float32 [2304], P('ctx')
All inputs are finite; a program needn't handle non-finite values.
Results may differ from a plain program's by a relative error of at most 0.028.
Values may be sent and summed in bfloat16 or wider, within the bound.
No kernel may reach another device: no remote copies, remote signals or barrier semaphores. Data moves between devices by JAX's collectives and lax.ppermute only.
A program may use at most 256 MiB of HBM per device.

v0:
```python
import math

import jax
import jax.numpy as jnp
from jax import lax
from jax.sharding import PartitionSpec as P

HD = 256


EPSILON = 1e-06
SOFT_CAP = 50.0
MASKED = -1e30


def rms_scale(values):
    return lax.rsqrt(jnp.mean(values * values, axis=-1, keepdims=True) + EPSILON)


def norm_back(inv_rms, normed, gradient):
    return inv_rms * (gradient - normed * jnp.mean(gradient * normed, axis=-1, keepdims=True))


def rope_tables(offset, row_count, head_width):
    half_width = head_width // 2
    positions = (offset + jnp.arange(row_count, dtype=jnp.int32)).astype(jnp.float32)
    frequency = jnp.exp(
        jnp.arange(half_width, dtype=jnp.float32) * (-2.0 * math.log(10000.0) / head_width)
    )
    angles = positions[:, None] * frequency[None, :]
    return (jnp.cos(angles)[:, None, :], jnp.sin(angles)[:, None, :])


def rotate(values, cos_table, sine_table):
    half_width = values.shape[-1] // 2
    leading = values[..., :half_width]
    trailing = values[..., half_width:]
    return jnp.concatenate(
        [leading * cos_table - trailing * sine_table, trailing * cos_table + leading * sine_table],
        axis=-1,
    )


def gelu_tanh(values):
    return jax.nn.gelu(values, approximate=True)


def product(first_operand, second_operand):
    return jnp.dot(first_operand, second_operand, preferred_element_type=jnp.float32)


def contract(first_operand, second_operand, first_dim, second_dim):
    return lax.dot_general(
        first_operand,
        second_operand,
        (((first_dim,), (second_dim,)), ((), ())),
        preferred_element_type=jnp.float32,
    )


def local(
    tokens,
    w_query,
    w_key,
    w_value,
    w_out,
    w_gate,
    w_up,
    w_down,
    norm_attn_in,
    norm_attn_out,
    norm_ffn_in,
    norm_ffn_out,
    cotangent,
):
    tok_rows = tokens.shape[0]
    heads_local = w_query.shape[1] // HD
    key_heads = w_key.shape[1] // HD
    group_size = heads_local // key_heads
    key_width = key_heads * HD
    ffn_width = w_gate.shape[1]
    cycle_size = lax.axis_size("ctx")
    seq_total = tok_rows * cycle_size
    my_index = lax.axis_index("ctx")
    base_pos = my_index * tok_rows
    query_pos = base_pos + jnp.arange(tok_rows, dtype=jnp.int32)
    last_query = base_pos + tok_rows - 1

    def fetch_attention():
        fetched = (
            lax.all_gather(w_query, "ctx", axis=0, tiled=True),
            lax.all_gather(w_key, "ctx", axis=0, tiled=True),
            lax.all_gather(w_value, "ctx", axis=0, tiled=True),
            lax.all_gather(w_out, "ctx", axis=0, tiled=True),
            lax.all_gather(norm_attn_in, "ctx", axis=0, tiled=True),
            lax.all_gather(norm_attn_out, "ctx", axis=0, tiled=True),
            lax.all_gather(norm_ffn_in, "ctx", axis=0, tiled=True),
            lax.all_gather(norm_ffn_out, "ctx", axis=0, tiled=True),
        )
        return (fetched[:4], tuple((gain.astype(jnp.float32) for gain in fetched[4:])))

    attn_mats, gains = fetch_attention()
    full_query, full_key, full_value, full_out = attn_mats
    gain_one, gain_two, gain_three, gain_four = gains
    tok_float = tokens.astype(jnp.float32)
    inv_one = rms_scale(tok_float)
    normed_one = tok_float * inv_one
    attn_input = (normed_one * gain_one).astype(jnp.bfloat16)
    query_lin = product(attn_input, full_query)
    key_lin = product(attn_input, full_key)
    values_b = product(attn_input, full_value).astype(jnp.bfloat16)
    cos_table, sine_table = rope_tables(base_pos, tok_rows, HD)
    queries = (
        rotate(query_lin.reshape(tok_rows, heads_local, HD), cos_table, sine_table) * HD ** (-0.5)
    ).astype(jnp.bfloat16)
    queries_h = queries.reshape(tok_rows, key_heads, group_size, HD).transpose(1, 2, 0, 3)
    keys_rot = (
        rotate(key_lin.reshape(tok_rows, key_heads, HD), cos_table, sine_table)
        .astype(jnp.bfloat16)
        .reshape(tok_rows, key_width)
    )

    def scores_for(key_piece):
        key_count = key_piece.shape[0]
        key_h = key_piece.reshape(key_count, key_heads, HD)
        raw_scores = jnp.einsum(
            "jgqd,cjd->jgqc", queries_h, key_h, preferred_element_type=jnp.float32
        )
        tanh_part = jnp.tanh(raw_scores / SOFT_CAP)
        key_pos = jnp.arange(key_count, dtype=jnp.int32)
        visible = key_pos[None, :] <= query_pos[:, None]
        return (tanh_part, visible, key_h)

    start_state = (
        jnp.full((key_heads, group_size, tok_rows), MASKED, jnp.float32),
        jnp.zeros((key_heads, group_size, tok_rows), jnp.float32),
        jnp.zeros((key_heads, group_size, tok_rows, HD), jnp.float32),
    )
    pieces = (
        lax.all_gather(keys_rot, "ctx", axis=0, tiled=True),
        lax.all_gather(values_b, "ctx", axis=0, tiled=True),
    )

    def compute(held):
        run_max, run_sum, run_acc = held
        key_piece, value_piece = pieces
        tanh_part, visible, key_h = scores_for(key_piece)
        capped = jnp.where(visible, SOFT_CAP * tanh_part, MASKED)
        new_max = jnp.maximum(run_max, jnp.max(capped, axis=-1))
        weights = jnp.where(visible, jnp.exp(capped - new_max[..., None]), 0.0)
        value_h = value_piece.reshape(key_piece.shape[0], key_heads, HD)
        run_acc = jnp.einsum(
            "jgqc,cjd->jgqd",
            weights.astype(jnp.bfloat16),
            value_h,
            preferred_element_type=jnp.float32,
        )
        run_sum = jnp.sum(weights, axis=-1)
        return (new_max, run_sum, run_acc)

    run_max, run_sum, run_acc = lax.cond(
        jnp.int32(0) > last_query, lambda held: held, compute, start_state
    )
    attn_float = run_acc / run_sum[..., None]
    log_total = run_max + jnp.log(run_sum)
    attn_rows = (
        attn_float.transpose(2, 0, 1, 3).reshape(tok_rows, heads_local * HD).astype(jnp.bfloat16)
    )
    attn_total = lax.psum(contract(attn_rows, full_out, 1, 1).astype(jnp.bfloat16), "tp").astype(
        jnp.float32
    )
    inv_two = rms_scale(attn_total)
    normed_two = attn_total * inv_two
    hidden_res = tok_float + normed_two * gain_two
    inv_three = rms_scale(hidden_res)
    normed_three = hidden_res * inv_three
    ffn_input = (normed_three * gain_three).astype(jnp.bfloat16)
    gate_piece = lax.all_gather(w_gate, "ctx", axis=0, tiled=True)
    up_piece = lax.all_gather(w_up, "ctx", axis=0, tiled=True)
    input_cols = ffn_input
    gate_lin = product(input_cols, gate_piece)
    up_lin = product(input_cols, up_piece)
    activated, gelu_pull = jax.vjp(gelu_tanh, gate_lin)
    hidden_b = (activated * up_lin).astype(jnp.bfloat16)
    ffn_part = contract(hidden_b, lax.all_gather(w_down, "ctx", axis=0, tiled=True), 1, 1)
    ffn_total = lax.psum(ffn_part.astype(jnp.bfloat16), "tp").astype(jnp.float32)
    inv_four = rms_scale(ffn_total)
    normed_four = ffn_total * inv_four
    output = (hidden_res + normed_four * gain_four).astype(jnp.bfloat16)
    grad_output = cotangent.astype(jnp.float32)
    grad_gain_four = jnp.sum(grad_output * normed_four, axis=0)
    grad_ffn = norm_back(inv_four, normed_four, grad_output * gain_four).astype(jnp.bfloat16)
    grad_cols = grad_ffn
    grad_hidden = product(grad_cols, lax.all_gather(w_down, "ctx", axis=0, tiled=True))
    grad_gate = gelu_pull(grad_hidden * up_lin)[0].astype(jnp.bfloat16)
    grad_up = (grad_hidden * activated).astype(jnp.bfloat16)
    gate_up_grad = jnp.concatenate([grad_gate, grad_up], axis=1)
    gate_piece = lax.all_gather(w_gate, "ctx", axis=0, tiled=True)
    up_piece = lax.all_gather(w_up, "ctx", axis=0, tiled=True)
    piece_sum = contract(grad_gate, gate_piece, 1, 1) + contract(grad_up, up_piece, 1, 1)
    grad_ffn_in = lax.psum(piece_sum.astype(jnp.bfloat16), "tp").astype(jnp.float32)
    input_cols = ffn_input
    grad_cols = grad_ffn
    ffn_grads = lax.psum_scatter(
        jnp.concatenate(
            [contract(input_cols, gate_up_grad, 0, 0), contract(grad_cols, hidden_b, 0, 0)], axis=1
        ).astype(jnp.bfloat16),
        "ctx",
        scatter_dimension=0,
        tiled=True,
    ).astype(jnp.float32)
    grad_w_gate = ffn_grads[:, :ffn_width]
    grad_w_up = ffn_grads[:, ffn_width : 2 * ffn_width]
    grad_w_down = ffn_grads[:, 2 * ffn_width :]
    grad_gain_three = jnp.sum(grad_ffn_in * normed_three, axis=0)
    grad_res = grad_output + norm_back(inv_three, normed_three, grad_ffn_in * gain_three)
    grad_gain_two = jnp.sum(grad_res * normed_two, axis=0)
    grad_attn = norm_back(inv_two, normed_two, grad_res * gain_two).astype(jnp.bfloat16)
    attn_mats, gains = fetch_attention()
    full_query, full_key, full_value, full_out = attn_mats
    gain_one = gains[0]
    grad_rows = product(grad_attn, full_out).astype(jnp.bfloat16)
    grad_heads = grad_rows.reshape(tok_rows, key_heads, group_size, HD).transpose(1, 2, 0, 3)
    row_delta = jnp.sum(grad_heads.astype(jnp.float32) * attn_float, axis=-1)

    def block_grads(grad_q, key_piece, value_piece):
        key_count = key_piece.shape[0]
        tanh_part, visible, key_h = scores_for(key_piece)
        weights = jnp.where(visible, jnp.exp(SOFT_CAP * tanh_part - log_total[..., None]), 0.0)
        value_h = value_piece.reshape(key_count, key_heads, HD)
        value_grad = jnp.einsum(
            "jgqc,jgqd->cjd",
            weights.astype(jnp.bfloat16),
            grad_heads,
            preferred_element_type=jnp.float32,
        )
        weight_grad = jnp.einsum(
            "jgqd,cjd->jgqc", grad_heads, value_h, preferred_element_type=jnp.float32
        )
        score_grad = (
            weights * (weight_grad - row_delta[..., None]) * (1.0 - tanh_part * tanh_part)
        ).astype(jnp.bfloat16)
        grad_q = jnp.einsum("jgqc,cjd->jgqd", score_grad, key_h, preferred_element_type=jnp.float32)
        key_grad = jnp.einsum(
            "jgqc,jgqd->cjd", score_grad, queries_h, preferred_element_type=jnp.float32
        )
        return (
            grad_q,
            key_grad.reshape(key_count, key_width),
            value_grad.reshape(key_count, key_width),
        )

    empty_query_grad = jnp.zeros((key_heads, group_size, tok_rows, HD), jnp.float32)
    back_state = (
        empty_query_grad,
        jnp.zeros((seq_total, key_width), jnp.float32),
        jnp.zeros((seq_total, key_width), jnp.float32),
    )
    attend_pieces = (
        lax.all_gather(keys_rot, "ctx", axis=0, tiled=True),
        lax.all_gather(values_b, "ctx", axis=0, tiled=True),
    )

    def compute(held):
        grad_q, grad_keys_all, grad_values_all = held
        key_piece, value_piece = attend_pieces
        key_count = key_piece.shape[0]
        grad_q, key_part, value_part = block_grads(grad_q, key_piece, value_piece)
        grad_keys_all = key_part
        grad_values_all = value_part
        return (grad_q, grad_keys_all, grad_values_all)

    grad_q, grad_keys_all, grad_values_all = lax.cond(
        jnp.int32(0) > last_query, lambda held: held, compute, back_state
    )
    grad_keys_own, grad_values_own = (
        lax.psum_scatter(
            grad_keys_all.astype(jnp.bfloat16), "ctx", scatter_dimension=0, tiled=True
        ).astype(jnp.float32),
        lax.psum_scatter(
            grad_values_all.astype(jnp.bfloat16), "ctx", scatter_dimension=0, tiled=True
        ).astype(jnp.float32),
    )
    grad_query_lin = (
        (
            rotate(
                grad_q.transpose(2, 0, 1, 3).reshape(tok_rows, heads_local, HD),
                cos_table,
                -sine_table,
            )
            * HD ** (-0.5)
        )
        .reshape(tok_rows, heads_local * HD)
        .astype(jnp.bfloat16)
    )
    grad_key_lin = (
        rotate(grad_keys_own.reshape(tok_rows, key_heads, HD), cos_table, -sine_table)
        .reshape(tok_rows, key_width)
        .astype(jnp.bfloat16)
    )
    grad_value_lin = grad_values_own.astype(jnp.bfloat16)
    grad_attn_part = (
        contract(grad_query_lin, full_query, 1, 1)
        + contract(grad_key_lin, full_key, 1, 1)
        + contract(grad_value_lin, full_value, 1, 1)
    )
    grad_attn_in = lax.psum(grad_attn_part.astype(jnp.bfloat16), "tp").astype(jnp.float32)
    grad_gain_one = jnp.sum(grad_attn_in * normed_one, axis=0)
    grad_tokens = grad_res + norm_back(inv_one, normed_one, grad_attn_in * gain_one)
    grad_w_query = contract(attn_input, grad_query_lin, 0, 0)
    grad_w_key = contract(attn_input, grad_key_lin, 0, 0)
    grad_w_value = contract(attn_input, grad_value_lin, 0, 0)
    grad_w_out = contract(grad_attn, attn_rows, 0, 0)
    summed = (
        lax.psum_scatter(
            grad_w_query.astype(jnp.bfloat16), "ctx", scatter_dimension=0, tiled=True
        ).astype(jnp.float32),
        lax.psum_scatter(
            grad_w_key.astype(jnp.bfloat16), "ctx", scatter_dimension=0, tiled=True
        ).astype(jnp.float32),
        lax.psum_scatter(
            grad_w_value.astype(jnp.bfloat16), "ctx", scatter_dimension=0, tiled=True
        ).astype(jnp.float32),
        lax.psum_scatter(
            grad_w_out.astype(jnp.bfloat16), "ctx", scatter_dimension=0, tiled=True
        ).astype(jnp.float32),
        lax.psum_scatter(
            grad_gain_one.astype(jnp.bfloat16), "ctx", scatter_dimension=0, tiled=True
        ).astype(jnp.float32),
        lax.psum_scatter(
            grad_gain_two.astype(jnp.bfloat16), "ctx", scatter_dimension=0, tiled=True
        ).astype(jnp.float32),
        lax.psum_scatter(
            grad_gain_three.astype(jnp.bfloat16), "ctx", scatter_dimension=0, tiled=True
        ).astype(jnp.float32),
        lax.psum_scatter(
            grad_gain_four.astype(jnp.bfloat16), "ctx", scatter_dimension=0, tiled=True
        ).astype(jnp.float32),
    )
    return (
        output,
        grad_tokens,
        summed[0],
        summed[1],
        summed[2],
        summed[3],
        grad_w_gate,
        grad_w_up,
        grad_w_down,
        summed[4],
        summed[5],
        summed[6],
        summed[7],
    )


def solution(mesh):
    return jax.shard_map(
        local,
        mesh=mesh,
        in_specs=(
            P("ctx", None),
            P("ctx", "tp"),
            P("ctx", "tp"),
            P("ctx", "tp"),
            P("ctx", "tp"),
            P("ctx", "tp"),
            P("ctx", "tp"),
            P("ctx", "tp"),
            P("ctx"),
            P("ctx"),
            P("ctx"),
            P("ctx"),
            P("ctx", None),
        ),
        out_specs=(
            P("ctx", None),
            P("ctx", None),
            P("ctx", "tp"),
            P("ctx", "tp"),
            P("ctx", "tp"),
            P("ctx", "tp"),
            P("ctx", "tp"),
            P("ctx", "tp"),
            P("ctx", "tp"),
            P("ctx"),
            P("ctx"),
            P("ctx"),
            P("ctx"),
        ),
        check_vma=False,
    )
```

profile of v0, /device:TPU:0, one launch (start us, length us, event | category | flops | bytes accessed | tf_op | source)
XLA Modules:
  0.0 1135.6 jit_solution(9103914493787538196)
XLA Ops:
  15.0 26.3 %all-reduce.9 = (bf16[2304]{0:T(1024)(128)(2,1)S(1)}, bf16[2304]{0:T(1024)(128)(2,1)S(1)}, bf16[2304]{0:T(1024)(128)(2,1)S(1)}, bf16[2304]{0:T(1024)(128)(2,1)}) all-reduce(bf16[2304]{0:T(1024)(128)(2,1)S(1)} %dynamic-update-slice.2, bf16[2304]{0:T(1024)(128)(2,1)S(1)} %dynamic-update-slice.1, ...), channel_id=1, replica_groups=mesh['ctx'=8,'tp'=4] {'ctx'}, use_global_device_ids=true, to_apply=%add.2 | all-reduce | flops 9216 | bytes 36864
  41.2 1.7 fusion.76
  43.0 2.8 convolution_convert_fusion.9
  45.9 16.9 %all-gather.12.cloned.1.call-done = bf16[2304,256]{1,0:T(8,128)(2,1)} async-done(((bf16[288,256]{1,0:T(8,128)(2,1)}), bf16[2304,256]{1,0:T(8,128)(2,1)}) %all-gather.12.cloned.1.call-update) | async-done | bytes 1179664 | tf_op jit(solution)/shard_map/all_gather | solution.py:92
  62.8 2.0 convolution_bitcast_fusion.3
  68.0 25.8 %all-gather.10.cloned.1.call-done = bf16[2304,512]{1,0:T(8,128)(2,1)} async-done(((bf16[288,512]{1,0:T(8,128)(2,1)}), bf16[2304,512]{1,0:T(8,128)(2,1)}) %all-gather.10.cloned.1.call-update) | async-done | bytes 2359312 | tf_op jit(solution)/shard_map/all_gather | solution.py:91
  93.8 2.8 fusion.117
  97.4 22.2 %all-gather.18.cloned.1.call-done = bf16[2048,256]{1,0:T(8,128)(2,1)} async-done(((bf16[256,256]{1,0:T(8,128)(2,1)}), bf16[2048,256]{1,0:T(8,128)(2,1)}) %all-gather.18.cloned.1.call-update) | async-done | bytes 1048592 | tf_op jit(solution)/shard_map/all_gather | solution.py:141
  119.6 25.9 %all-gather.14.cloned.1.call-done = bf16[2048,256]{0,1:T(8,128)(2,1)} async-done(((bf16[256,256]{0,1:T(8,128)(2,1)}), bf16[2048,256]{0,1:T(8,128)(2,1)}) %all-gather.14.cloned.1.call-update) | async-done | bytes 1048592 | tf_op jit(solution)/shard_map/all_gather | solution.py:140
  145.5 5.4 conditional.2
  145.9 2.8 fusion.122
  152.4 23.9 %all-gather.20.cloned.1.call-done = bf16[2304,512]{1,0:T(8,128)(2,1)} async-done(((bf16[288,512]{1,0:T(8,128)(2,1)}), bf16[2304,512]{1,0:T(8,128)(2,1)}) %all-gather.20.cloned.1.call-update) | async-done | bytes 2359312 | tf_op jit(solution)/shard_map/all_gather | solution.py:94
  176.3 3.5 convolution_convert_fusion.7
  182.5 53.4 %all-reduce.15.cloned.1.call-done = bf16[256,2304]{1,0:T(8,128)(2,1)} async-done(((bf16[256,2304]{1,0:T(8,128)(2,1)}), bf16[256,2304]{1,0:T(8,128)(2,1)}) %all-reduce.15.cloned.1.call-update) | async-done | bytes 1179664 | tf_op jit(solution)/shard_map/psum | solution.py:169
  237.6 2.0 multiply_reduce_fusion.1
  239.5 61.6 %all-gather.22.cloned.1.call-done = bf16[2304,2304]{1,0:T(8,128)(2,1)} async-done(((bf16[288,2304]{1,0:T(8,128)(2,1)}), bf16[2304,2304]{1,0:T(8,128)(2,1)}) %all-gather.22.cloned.1.call-update) | async-done | bytes 10616848 | tf_op jit(solution)/shard_map/all_gather | solution.py:178
  301.2 8.6 fusion.120
  309.8 57.1 %all-gather.24.cloned.1.call-done = bf16[2304,2304]{1,0:T(8,128)(2,1)} async-done(((bf16[288,2304]{1,0:T(8,128)(2,1)}), bf16[2304,2304]{1,0:T(8,128)(2,1)}) %all-gather.24.cloned.1.call-update) | async-done | bytes 10616848 | tf_op jit(solution)/shard_map/all_gather | solution.py:179
  366.9 9.3 multiply_convert_fusion.2
  376.2 56.2 %all-gather.26.cloned.1.call-done = bf16[2304,2304]{1,0:T(8,128)(2,1)} async-done(((bf16[288,2304]{1,0:T(8,128)(2,1)}), bf16[2304,2304]{1,0:T(8,128)(2,1)}) %all-gather.26.cloned.1.call-update) | async-done | bytes 10616848 | tf_op jit(solution)/shard_map/all_gather | solution.py:185
  432.5 8.0 convolution_convert_fusion.6
  442.0 54.5 %all-reduce.17.cloned.1.call-done = bf16[256,2304]{1,0:T(8,128)(2,1)} async-done(((bf16[256,2304]{1,0:T(8,128)(2,1)}), bf16[256,2304]{1,0:T(8,128)(2,1)}) %all-reduce.17.cloned.1.call-update) | async-done | bytes 1179664 | tf_op jit(solution)/shard_map/psum | solution.py:186
  496.5 1.7 fusion.64
  498.3 3.3 fusion.77
  501.6 9.5 multiply_convert_fusion.1
  511.2 2.9 fusion.125
  514.2 8.0 fusion.33
  522.5 55.3 %all-reduce.19.cloned.1.call-done = bf16[256,2304]{1,0:T(8,128)(2,1)} async-done(((bf16[256,2304]{1,0:T(8,128)(2,1)}), bf16[256,2304]{1,0:T(8,128)(2,1)}) %all-reduce.19.cloned.1.call-update) | async-done | bytes 1179664 | tf_op jit(solution)/shard_map/psum | solution.py:201
  577.8 3.2 fusion.65
  581.1 4.9 fusion.59
  590.3 1.7 reshape.398
  592.1 1.9 fusion.108
  593.9 16.7 %conditional.3 = (f32[1,2,256,256]{3,2,1,0:T(8,128)}, bf16[2048,256]{1,0:T(8,128)(2,1)}, bf16[2048,256]{1,0:T(8,128)(2,1)}) conditional(s32[]{:T(128)} %convert_element_type.194, (s32[256]{0:T(256)}, bf16[1,2,256,256]{2,3,1,0:T(8,128)(2,1)}, bf16[2048,256]{0,1:T(8,128)(2,1)}, f32[1,2,256]{2,1,0:T(2,128)}, f32[1,2,256]{2,1,0:T(2,128)}, ...), branch_computations={%region_14.0_spmd, %region_16.17_spmd} | conditional | flops 2700869632 | bytes 38812780 | solution.py:273
  593.9 2.0 copy.59
  599.1 2.1 fusion.22
  601.3 2.4 multiply_convert_fusion
  603.7 2.7 convolution_bitcast_fusion
  608.0 2.7 convolution_bitcast_fusion.1
  610.7 2.3 copy.61
  613.8 2.0 copy.60
  617.8 3.9 fusion.126
  621.7 27.0 %reduce-scatter.8.cloned.1.call-done = bf16[256,256]{0,1:T(8,128)(2,1)} async-done(((bf16[2048,256]{0,1:T(8,128)(2,1)}), bf16[256,256]{0,1:T(8,128)(2,1)}) %reduce-scatter.8.cloned.1.call-update) | async-done | bytes 131088 | tf_op jit(solution)/shard_map/reduce_scatter | solution.py:277
  651.5 4.0 convolution_add_fusion.1
  655.5 32.8 %reduce-scatter.10.cloned.1.call-done = bf16[256,256]{1,0:T(8,128)(2,1)} async-done(((bf16[2048,256]{1,0:T(8,128)(2,1)}), bf16[256,256]{1,0:T(8,128)(2,1)}) %reduce-scatter.10.cloned.1.call-update) | async-done | bytes 131088 | tf_op jit(solution)/shard_map/reduce_scatter | solution.py:280
  688.3 3.6 fusion.32
  692.0 2.6 convolution_convert_fusion.4
  694.6 2.6 convolution_convert_fusion.5
  697.3 3.6 convolution_convert_fusion.2
  700.9 12.1 %convolution_convert_fusion = bf16[2304,4608]{1,0:T(8,128)(2,1)} fusion(bf16[256,2304]{1,0:T(8,128)(2,1)} %copy-done.13, bf16[256,2304]{1,0:T(8,128)(2,1)} %copy-done.14, f32[2304]{0:T(1024)} %copy-done.18, f32[256]{0:T(256)} %copy-done.29, f32[2304]{0:T(1024)S(1)} %convert_element_type.205, f32[256]{0:T(256)S(1)} %add_rsqrt_fusion.2, ...), kind=kOutput, calls=%fused_computation.42 | convolution fusion | flops 5455872000 | bytes 25972736 | tf_op jit(solution)/shard_map/dot_general | solution.py:53
  713.0 2.3 convolution_convert_fusion.3
  715.5 7.3 convolution_convert_fusion.1
  722.8 21.9 %pad_maximum_fusion = bf16[2304,6912]{1,0:T(8,128)(2,1)} fusion(bf16[2304,2304]{1,0:T(8,128)(2,1)} %convolution_convert_fusion.1, bf16[2304,4608]{1,0:T(8,128)(2,1)} %convolution_convert_fusion), kind=kLoop, calls=%fused_computation.41 | loop fusion | flops 63700992 | bytes 63700992 | tf_op jit(solution)/shard_map/concatenate | solution.py:205
  745.5 2.5 all-reduce.21.cloned.1.call-done
  748.0 2.8 fusion.75
  750.7 25.7 %all-reduce.8 = (bf16[2304]{0:T(1024)(128)(2,1)}, bf16[2304]{0:T(1024)(128)(2,1)}, bf16[2304]{0:T(1024)(128)(2,1)}, bf16[2304]{0:T(1024)(128)(2,1)}) all-reduce(bf16[2304]{0:T(1024)(128)(2,1)} %get-tuple-element.116, bf16[2304]{0:T(1024)(128)(2,1)} %get-tuple-element.112, ...), channel_id=9, replica_groups=mesh['ctx'=8,'tp'=4] {'ctx'}, use_global_device_ids=true, to_apply=%region_27.28.clone | all-reduce | flops 9216 | bytes 36864
  779.8 3.4 fusion.52
  783.2 4.2 reduce-scatter.16.cloned.1.call-done
  789.1 38.6 %reduce-scatter.14.cloned.1.call-done = bf16[288,256]{1,0:T(8,128)(2,1)} async-done(((bf16[2304,256]{1,0:T(8,128)(2,1)}), bf16[288,256]{1,0:T(8,128)(2,1)}) %reduce-scatter.14.cloned.1.call-update) | async-done | bytes 147472 | tf_op jit(solution)/shard_map/reduce_scatter | solution.py:318
  829.3 44.7 %reduce-scatter.18.cloned.1.call-done = bf16[288,512]{1,0:T(8,128)(2,1)} async-done(((bf16[2304,512]{1,0:T(8,128)(2,1)}), bf16[288,512]{1,0:T(8,128)(2,1)}) %reduce-scatter.18.cloned.1.call-update) | async-done | bytes 294928 | tf_op jit(solution)/shard_map/reduce_scatter | solution.py:324
  874.0 1.8 convert_element_type.236
  875.8 44.9 %reduce-scatter.12.cloned.1.call-done = bf16[288,512]{1,0:T(8,128)(2,1)} async-done(((bf16[2304,512]{1,0:T(8,128)(2,1)}), bf16[288,512]{1,0:T(8,128)(2,1)}) %reduce-scatter.12.cloned.1.call-update) | async-done | bytes 294928 | tf_op jit(solution)/shard_map/reduce_scatter | solution.py:315
  920.7 1.8 convert_element_type.230
  922.6 200.2 %reduce-scatter.20.cloned.1.call-done = bf16[288,6912]{1,0:T(8,128)(2,1)} async-done(((bf16[2304,6912]{1,0:T(8,128)(2,1)}), bf16[288,6912]{1,0:T(8,128)(2,1)}) %reduce-scatter.20.cloned.1.call-update) | async-done | bytes 3981328 | tf_op jit(solution)/shard_map/reduce_scatter | solution.py:204
  1122.8 5.5 fusion.123
  (185 shorter events, 42.8 us)
Async XLA Ops:
  7.2 35.8 %all-gather.16.cloned.1.call-start = ((), (), s32[]{:S(2)}) async-start(), calls=%async_computation.10 | async-start | bytes 1327104 | tf_op jit(solution)/shard_map/all_gather | solution.py:93
  7.9 54.9 %all-gather.12.cloned.1.call-start = ((), (), s32[]{:S(2)}) async-start(), calls=%async_computation.8 | async-start | bytes 1327104 | tf_op jit(solution)/shard_map/all_gather | solution.py:92
  8.7 85.1 %all-gather.10.cloned.1.call-start = ((), (), s32[]{:S(2)}) async-start(), calls=%async_computation.7 | async-start | bytes 2654208 | tf_op jit(solution)/shard_map/all_gather | solution.py:91
  9.4 110.2 %all-gather.18.cloned.1.call-start = ((), (), s32[]{:S(2)}) async-start(), calls=%async_computation.11 | async-start | bytes 1179648 | tf_op jit(solution)/shard_map/all_gather | solution.py:141
  41.2 52.5 %copy-start.26 = (f32[2304]{0:T(1024)}, f32[2304]{0:T(1024)S(1)}, u32[]{:S(2)}) copy-start(f32[2304]{0:T(1024)S(1)} %convert_element_type.195) | copy-start | bytes 27652
  41.2 21.6 %copy-start = (bf16[256,2304]{1,0:T(8,128)(2,1)S(1)}, bf16[256,2304]{1,0:T(8,128)(2,1)}, u32[]{:S(2)}) copy-start(bf16[256,2304]{1,0:T(8,128)(2,1)} %param.17) | copy-start | bytes 3538948
  42.9 50.8 %copy-start.33 = (f32[256]{0:T(256)}, f32[256]{0:T(256)S(1)}, u32[]{:S(2)}) copy-start(f32[256]{0:T(256)S(1)} %add_rsqrt_fusion.3) | copy-start | bytes 3076
  45.8 99.7 %all-gather.14.cloned.1.call-start = ((), (), s32[]{:S(2)}) async-start(), calls=%async_computation.9 | async-start | bytes 1179648 | tf_op jit(solution)/shard_map/all_gather | solution.py:140
  45.9 22.1 %copy-start.39 = (f32[128]{0:T(128)}, f32[128]{0:T(128)S(1)}, u32[]{:S(2)}) copy-start(f32[128]{0:T(128)S(1)} %multiply_exponential_fusion) | copy-start | bytes 1540
  45.9 22.1 %copy-start.36 = (f32[256]{0:T(256)}, f32[256]{0:T(256)S(1)}, u32[]{:S(2)}) copy-start(f32[256]{0:T(256)S(1)} %fusion.104) | copy-start | bytes 3076
  66.1 110.2 %all-gather.20.cloned.1.call-start = ((), (), s32[]{:S(2)}) async-start(), calls=%async_computation.12 | async-start | bytes 2654208 | tf_op jit(solution)/shard_map/all_gather | solution.py:94
  66.7 169.2 %all-reduce.15.cloned.1.call-start = ((), (), s32[]{:S(2)}) async-start(), calls=%async_computation.13 | async-start | bytes 2359296 | tf_op jit(solution)/shard_map/psum | solution.py:169
  66.7 78.8 %copy-start.40 = (s32[256]{0:T(256)}, s32[256]{0:T(256)S(1)}, u32[]{:S(2)}) copy-start(s32[256]{0:T(256)S(1)} %iota_add_fusion) | copy-start | bytes 3076
  68.0 28.6 %copy-start.15 = (f32[256,128]{0,1:T(8,128)}, f32[256,128]{0,1:T(8,128)S(1)}, u32[]{:S(2)}) copy-start(f32[256,128]{0,1:T(8,128)S(1)} %get-tuple-element.151) | copy-start | bytes 393220
  145.9 2.8 copy-start.41
  150.9 28.9 %copy-start.32 = (f32[1,2,256]{2,1,0:T(2,128)}, f32[1,2,256]{2,1,0:T(2,128)S(1)}, u32[]{:S(2)}) copy-start(f32[1,2,256]{2,1,0:T(2,128)S(1)} %get-tuple-element.65) | copy-start | bytes 6148
  152.4 27.5 %copy-start.12 = (bf16[1,2,256,256]{2,3,1,0:T(8,128)(2,1)}, bf16[1,2,256,256]{2,3,1,0:T(8,128)(2,1)S(1)}, u32[]{:S(2)}) copy-start(bf16[1,2,256,256]{2,3,1,0:T(8,128)(2,1)S(1)} %get-tuple-element.127) | copy-start | bytes 786436
  179.8 121.3 %all-gather.22.cloned.1.call-start = ((), (), s32[]{:S(2)}) async-start(), calls=%async_computation.14 | async-start | bytes 11943936 | tf_op jit(solution)/shard_map/all_gather | solution.py:178
  180.6 186.3 %all-gather.24.cloned.1.call-start = ((), (), s32[]{:S(2)}) async-start(), calls=%async_computation.15 | async-start | bytes 11943936 | tf_op jit(solution)/shard_map/all_gather | solution.py:179
  181.3 251.1 %all-gather.26.cloned.1.call-start = ((), (), s32[]{:S(2)}) async-start(), calls=%async_computation.16 | async-start | bytes 11943936 | tf_op jit(solution)/shard_map/all_gather | solution.py:185
  181.9 314.6 %all-reduce.17.cloned.1.call-start = ((), (), s32[]{:S(2)}) async-start(), calls=%async_computation.17 | async-start | bytes 2359296 | tf_op jit(solution)/shard_map/psum | solution.py:186
  182.4 127.3 %copy-start.18 = (f32[2304]{0:T(1024)}, f32[2304]{0:T(1024)S(1)}, u32[]{:S(2)}) copy-start(f32[2304]{0:T(1024)S(1)} %convert_element_type.206) | copy-start | bytes 27652
  235.9 65.3 %copy-start.1 = (bf16[256,2304]{1,0:T(8,128)(2,1)S(1)}, bf16[256,2304]{1,0:T(8,128)(2,1)}, u32[]{:S(2)}) copy-start(bf16[256,2304]{1,0:T(8,128)(2,1)} %all-reduce.15.cloned.1.call-done) | copy-start | bytes 3538948
  239.5 70.2 %copy-start.29 = (f32[256]{0:T(256)}, f32[256]{0:T(256)S(1)}, u32[]{:S(2)}) copy-start(f32[256]{0:T(256)S(1)} %add_rsqrt_fusion.1) | copy-start | bytes 3076
  376.2 64.2 %copy-start.16 = (bf16[256,2304]{1,0:T(8,128)(2,1)}, bf16[256,2304]{1,0:T(8,128)(2,1)S(1)}, u32[]{:S(2)}) copy-start(bf16[256,2304]{1,0:T(8,128)(2,1)S(1)} %get-tuple-element.154) | copy-start | bytes 3538948
  440.5 137.4 %all-reduce.19.cloned.1.call-start = ((), (), s32[]{:S(2)}) async-start(), calls=%async_computation.18 | async-start | bytes 2359296 | tf_op jit(solution)/shard_map/psum | solution.py:201
  496.5 5.0 copy-start.2
  496.5 5.0 copy-start.20
  496.5 5.0 copy-start.43
  498.3 12.9 %copy-start.30 = (f32[256]{0:T(256)}, f32[256]{0:T(256)S(1)}, u32[]{:S(2)}) copy-start(f32[256]{0:T(256)S(1)} %add_rsqrt_fusion) | copy-start | bytes 3076
  498.3 12.9 %slice-start = ((s8[10616832]{0:T(1024)(128)(4,1)}), s8[4194304]{0:T(1024)(128)(4,1)S(1)}, s32[]{:S(2)}) async-start(s8[10616832]{0:T(1024)(128)(4,1)} %bitcast.118), calls=%async_computation.27 | async-start | bytes 8388608
  501.6 9.6 copy-start.37
  501.6 9.6 slice-start.1
  501.6 9.6 slice-start.2
  511.2 3.0 copy-start.14
  511.2 3.0 copy-start.13
  522.2 126.5 %reduce-scatter.8.cloned.1.call-start = ((), (), s32[]{:S(2)}) async-start(), calls=%async_computation.19 | async-start | bytes 1179648 | tf_op jit(solution)/shard_map/reduce_scatter | solution.py:277
  577.8 3.3 copy-start.5
  577.8 3.3 copy-start.8
  577.8 3.3 copy-start.19
  577.8 3.3 copy-start.21
  586.0 1.4 copy-start.3
  586.0 2.9 copy-start.11
  587.4 1.1 copy-start.7
  599.1 2.2 copy-start.25
  599.1 2.2 copy-start.42
  603.7 2.7 copy-start.17
  613.0 75.4 %reduce-scatter.10.cloned.1.call-start = ((), (), s32[]{:S(2)}) async-start(), calls=%async_computation.20 | async-start | bytes 1179648 | tf_op jit(solution)/shard_map/reduce_scatter | solution.py:280
  613.5 134.4 %all-reduce.21.cloned.1.call-start = ((), (), s32[]{:S(2)}) async-start(), calls=%async_computation.21 | async-start | bytes 2359296 | tf_op jit(solution)/shard_map/psum | solution.py:307
  617.1 0.7 copy-start.9
  692.0 95.5 %reduce-scatter.16.cloned.1.call-start = ((), (), s32[]{:S(2)}) async-start(), calls=%async_computation.24 | async-start | bytes 1327104 | tf_op jit(solution)/shard_map/reduce_scatter | solution.py:321
  694.6 133.1 %reduce-scatter.14.cloned.1.call-start = ((), (), s32[]{:S(2)}) async-start(), calls=%async_computation.23 | async-start | bytes 1327104 | tf_op jit(solution)/shard_map/reduce_scatter | solution.py:318
  697.2 176.7 %reduce-scatter.18.cloned.1.call-start = ((), (), s32[]{:S(2)}) async-start(), calls=%async_computation.25 | async-start | bytes 2654208 | tf_op jit(solution)/shard_map/reduce_scatter | solution.py:324
  700.9 219.9 %reduce-scatter.12.cloned.1.call-start = ((), (), s32[]{:S(2)}) async-start(), calls=%async_computation.22 | async-start | bytes 2654208 | tf_op jit(solution)/shard_map/reduce_scatter | solution.py:315
  700.9 12.1 %copy-start.10 = (bf16[256,2,256]{0,2,1:T(8,128)(2,1)S(1)}, bf16[256,2,256]{0,2,1:T(8,128)(2,1)}, u32[]{:S(2)}) copy-start(bf16[256,2,256]{0,2,1:T(8,128)(2,1)} %copy-done.9) | copy-start | bytes 786436
  700.9 12.1 %copy-start.27 = (f32[2304]{0:T(1024)S(1)}, f32[2304]{0:T(1024)}, u32[]{:S(2)}) copy-start(f32[2304]{0:T(1024)} %copy-done.26) | copy-start | bytes 27652
  700.9 12.1 %copy-start.34 = (f32[256]{0:T(256)S(1)}, f32[256]{0:T(256)}, u32[]{:S(2)}) copy-start(f32[256]{0:T(256)} %copy-done.33) | copy-start | bytes 3076
  713.0 2.5 copy-start.6
  713.0 2.4 copy-start.22
  713.0 2.4 copy-start.31
  715.4 407.4 %reduce-scatter.20.cloned.1.call-start = ((), (), s32[]{:S(2)}) async-start(), calls=%async_computation.26 | async-start | bytes 35831808 | tf_op jit(solution)/shard_map/reduce_scatter | solution.py:204
  744.7 3.3 copy-start.28
  744.7 3.3 copy-start.35
  744.7 35.1 %copy-start.4 = (f32[256,2304]{1,0:T(8,128)S(1)}, f32[256,2304]{1,0:T(8,128)}, u32[]{:S(2)}) copy-start(f32[256,2304]{1,0:T(8,128)} %copy-done.3) | copy-start | bytes 7077892
  (3 other events, 1.9 us)
Sparse Core Ops, SparseCore 0:
  9.9 26.8 all-gather.15
  38.7 24.1 all-gather.11
  64.7 29.0 all-gather.9
  96.1 23.4 all-gather.17
  121.9 23.5 all-gather.13
  147.2 29.0 all-gather.19
  179.9 55.8 all-reduce.14
  237.8 63.3 all-gather.21
  303.0 63.8 all-gather.23
  368.6 63.8 all-gather.25
  440.6 55.8 all-reduce.16
  522.4 55.4 all-reduce.18
  613.1 35.5 reduce-scatter.7
  652.3 35.9 reduce-scatter.9
  692.1 55.8 all-reduce.20
  751.1 36.3 reduce-scatter.15
  790.8 36.7 reduce-scatter.13
  831.4 42.4 reduce-scatter.17
  878.2 42.4 reduce-scatter.11
  924.2 198.5 reduce-scatter.19
where the time goes:
time: 1140 us
  waiting for transfers between devices  853 us (75%)
  matrix products  116 us (10%)
  other arithmetic  72.7 us (6%)
  blocking collectives  52 us (5%)
  local copies, waits for them, and re-layouts  22.8 us (2%)
  between operations  16.7 us (1%)
    reduce_scatter x1, waiting for transfers between devices, local(): lax.psum_scatter(jnp.concatenate([contract(input_cols, gate_up_grad, 0, 0...  200 us
    dot_general x13, matrix products, contract(): lax.dot_general(first_operand, second_operand, (((first_dim,), (second_di...  64.3 us
    all_gather x1, waiting for transfers between devices, local(): gate_piece = lax.all_gather(w_gate, 'ctx', axis=0, tiled=True)  61.6 us
    all_gather x1, waiting for transfers between devices, local(): up_piece = lax.all_gather(w_up, 'ctx', axis=0, tiled=True)  57.1 us
    all_gather x1, waiting for transfers between devices, local(): lax.all_gather(w_down, 'ctx', axis=0, tiled=True)  56.2 us
    psum x1, waiting for transfers between devices, local(): lax.psum(piece_sum.astype(jnp.bfloat16), 'tp').astype(jnp.float32)  55.3 us
    psum x1, waiting for transfers between devices, local(): lax.psum(ffn_part.astype(jnp.bfloat16), 'tp').astype(jnp.float32)  54.5 us
    psum x1, waiting for transfers between devices, local(): lax.psum(contract(attn_rows, full_out, 1, 1).astype(jnp.bfloat16), 'tp')  53.4 us
  transfers between devices with their start and end apart: 20, of which 19 were waited for; matrix products, arithmetic and copies ran while one was open for 11% of the time, Pallas kernels for 0%

commit v1 on v0

v1 whole, which is shorter than its diff:
```python
import math

import jax
import jax.numpy as jnp
from jax import lax
from jax.sharding import PartitionSpec as P

HD = 256


EPSILON = 1e-06
SOFT_CAP = 50.0
MASKED = -1e30


def rms_scale(values):
    return lax.rsqrt(jnp.mean(values * values, axis=-1, keepdims=True) + EPSILON)


def norm_back(inv_rms, normed, gradient):
    return inv_rms * (gradient - normed * jnp.mean(gradient * normed, axis=-1, keepdims=True))


def rotate(values, cos_table, sine_table):
    half_width = values.shape[-1] // 2
    leading = values[..., :half_width]
    trailing = values[..., half_width:]
    return jnp.concatenate(
        [leading * cos_table - trailing * sine_table, trailing * cos_table + leading * sine_table],
        axis=-1,
    )


def gelu_tanh(values):
    return jax.nn.gelu(values, approximate=True)


def product(first_operand, second_operand):
    return jnp.dot(first_operand, second_operand, preferred_element_type=jnp.float32)


def contract(first_operand, second_operand, first_dim, second_dim):
    return lax.dot_general(
        first_operand,
        second_operand,
        (((first_dim,), (second_dim,)), ((), ())),
        preferred_element_type=jnp.float32,
    )


def after(value, *earlier):
    return lax.optimization_barrier((value,) + earlier)[0]


def local(
    tokens,
    w_query,
    w_key,
    w_value,
    w_out,
    w_gate,
    w_up,
    w_down,
    norm_attn_in,
    norm_attn_out,
    norm_ffn_in,
    norm_ffn_out,
    cotangent,
):
    bf16, f32 = jnp.bfloat16, jnp.float32
    tok_rows, width = tokens.shape
    heads_local = w_query.shape[1] // HD
    key_heads = w_key.shape[1] // HD
    group_size = heads_local // key_heads
    query_width = heads_local * HD
    key_width = key_heads * HD
    ring = lax.axis_size("ctx")
    layers = lax.axis_size("tp")
    me = lax.axis_index("ctx")
    my_layer = lax.axis_index("tp")
    shard = width // ring
    own_rows = tok_rows // layers
    far_a, far_b = ring // 4, ring // 2
    near = [1 << bit for bit in range(far_a.bit_length() - 1)]
    order = [0, far_a, far_b, far_a | far_b]
    for bit in near:
        order = order + [block | bit for block in order]

    def swap(value, bit, axis="ctx"):
        count = lax.axis_size(axis)
        return lax.ppermute(value, axis, [(index, index ^ bit) for index in range(count)])

    def spread_far(piece):
        cut = piece.shape[0] // 32 * 16
        from_a, from_b = swap(piece, far_a), swap(piece, far_b)
        top, bottom = swap(from_b[:cut], far_a), swap(from_a[cut:], far_b)
        return jnp.concatenate([piece, from_a, from_b, top, bottom], axis=0), (from_a, from_b)

    def spread_near(block):
        blocks = [block]
        for bit in near:
            blocks = blocks + [swap(held, bit) for held in blocks]
        return blocks

    def collect_near(parts):
        for bit in reversed(near):
            half = len(parts) // 2
            parts = [
                (kept.astype(f32) + swap(sent, bit).astype(f32)).astype(bf16)
                for kept, sent in zip(parts[:half], parts[half:])
            ]
        return parts[0]

    def collect_far(block):
        rows = block.shape[0] // 4
        cut = rows // 32 * 16
        own, for_a, for_b, for_ab = (block[index * rows : (index + 1) * rows] for index in range(4))
        top, bottom = swap(for_ab[:cut], far_a), swap(for_ab[cut:], far_b)
        for_b = jnp.concatenate(
            [(for_b[:cut].astype(f32) + top.astype(f32)).astype(bf16), for_b[cut:]], axis=0
        )
        for_a = jnp.concatenate(
            [for_a[:cut], (for_a[cut:].astype(f32) + bottom.astype(f32)).astype(bf16)], axis=0
        )
        return own.astype(f32) + swap(for_a, far_a).astype(f32) + swap(for_b, far_b).astype(f32)

    def layer_scatter(partial):
        total = partial[:own_rows].astype(f32)
        arrived = [
            swap(partial[step * own_rows : (step + 1) * own_rows], step, "tp")
            for step in range(1, layers)
        ]
        for piece in arrived:
            total = total + piece.astype(f32)
        return total

    def layer_gather(rows):
        return [rows] + [swap(rows, step, "tp") for step in range(1, layers)]

    def rows_in(array):
        return jnp.concatenate(
            [
                lax.dynamic_slice_in_dim(array, (my_layer ^ step) * own_rows, own_rows, 0)
                for step in range(layers)
            ],
            axis=0,
        )

    def columns_in(array):
        return jnp.concatenate(
            [lax.dynamic_slice_in_dim(array, (me ^ block) * shard, shard, 1) for block in order],
            axis=1,
        )

    def columns_out(array):
        result = jnp.zeros_like(array)
        for place, block in enumerate(order):
            result = lax.dynamic_update_slice_in_dim(
                result, array[:, place * shard : (place + 1) * shard], (me ^ block) * shard, 1
            )
        return result

    def rows_out(pieces):
        result = jnp.zeros((tok_rows,) + pieces[0].shape[1:], pieces[0].dtype)
        for step, piece in enumerate(pieces):
            result = lax.dynamic_update_slice_in_dim(
                result, piece, (my_layer ^ step) * own_rows, 0
            )
        return result

    near_count = len(order) // 4
    near_width = 4 * shard

    def by_near(array):
        return [
            array[:, index * near_width : (index + 1) * near_width] for index in range(near_count)
        ]

    def times_rows(activation, blocks):
        total = None
        for part, block in zip(by_near(activation), blocks):
            term = product(part, block)
            total = term if total is None else total + term
        return total

    def times_rows_t(activation, blocks):
        return jnp.concatenate([contract(activation, block, 1, 1) for block in blocks], axis=1)

    def weight_parts(activation, gradient):
        return [
            contract(part, gradient, 0, 0).astype(bf16) for part in by_near(activation)
        ]

    gains = jnp.stack([norm_attn_in, norm_attn_out, norm_ffn_in, norm_ffn_out])
    qkv_width = query_width + 2 * key_width
    qkv = jnp.concatenate([w_query, w_key, w_value], axis=1)
    gain_rows = jnp.zeros((16, qkv_width), bf16).at[:4, :shard].set(gains)
    qkv_far, qkv_done = spread_far(jnp.concatenate([qkv, gain_rows], axis=0))
    out_far, out_done = spread_far(w_out)
    gate_far, gate_done = spread_far(after(w_gate, *out_done))
    up_far, up_done = spread_far(after(w_up, *gate_done))
    down_far, _ = spread_far(after(w_down, *up_done))
    qkv_all = spread_near(qkv_far)
    out_all = spread_near(out_far)
    gate_all = spread_near(gate_far)
    up_all = spread_near(up_far)
    down_all = spread_near(down_far)
    padded = shard + 16
    qkv_all_rows = [block.reshape(4, padded, qkv_width) for block in qkv_all]
    qkv_w = [block[:, :shard].reshape(near_width, qkv_width) for block in qkv_all_rows]
    gain_all = jnp.concatenate(
        [block[index, shard : shard + 4, :shard] for block in qkv_all_rows for index in range(4)],
        axis=1,
    ).astype(f32)
    gain_one, gain_two, gain_three, gain_four = (gain_all[index : index + 1] for index in range(4))

    tok_float = columns_in(rows_in(tokens)).astype(f32)
    own_cot = columns_in(
        lax.dynamic_slice_in_dim(cotangent, my_layer * own_rows, own_rows, 0)
    ).astype(f32)
    attn_input = (tok_float * rms_scale(tok_float) * gain_one).astype(bf16)
    own_tok = tok_float[:own_rows]
    lin = times_rows(attn_input, qkv_w)
    row_place = jnp.concatenate(
        [
            (my_layer ^ step) * own_rows + jnp.arange(own_rows, dtype=jnp.int32)
            for step in range(layers)
        ]
    )
    query_pos = me * tok_rows + row_place
    half_width = HD // 2
    frequency = jnp.exp(
        jnp.arange(half_width, dtype=f32) * (-2.0 * math.log(10000.0) / HD)
    )
    angles = query_pos.astype(f32)[:, None] * frequency[None, :]
    cos_table, sine_table = jnp.cos(angles)[:, None, :], jnp.sin(angles)[:, None, :]
    queries = (
        rotate(lin[:, :query_width].reshape(tok_rows, heads_local, HD), cos_table, sine_table)
        * HD ** (-0.5)
    ).astype(bf16)
    queries_h = queries.reshape(tok_rows, key_heads, group_size, HD).transpose(1, 2, 0, 3)
    keys_rot = (
        rotate(
            lin[:, query_width : query_width + key_width].reshape(tok_rows, key_heads, HD),
            cos_table,
            sine_table,
        )
        .astype(bf16)
        .reshape(tok_rows, key_width)
    )
    values_b = lin[:, query_width + key_width :].astype(bf16)
    pair = jnp.concatenate([keys_rot, values_b], axis=1)
    pair_far = jnp.concatenate(
        [pair, swap(pair, far_a), swap(pair, far_b), swap(pair, far_a | far_b)], axis=0
    )
    pairs = jnp.concatenate(spread_near(pair_far), axis=0)
    key_count = pairs.shape[0]
    key_h = pairs[:, :key_width].reshape(key_count, key_heads, HD)
    value_h = pairs[:, key_width:].reshape(key_count, key_heads, HD)
    key_pos = jnp.concatenate([(me ^ block) * tok_rows + row_place for block in order])
    visible = key_pos[None, :] <= query_pos[:, None]
    tanh_part = jnp.tanh(
        jnp.einsum("jgqd,cjd->jgqc", queries_h, key_h, preferred_element_type=f32) / SOFT_CAP
    )
    capped = jnp.where(visible, SOFT_CAP * tanh_part, MASKED)
    row_max = jnp.max(capped, axis=-1)
    weights = jnp.where(visible, jnp.exp(capped - row_max[..., None]), 0.0)
    row_sum = jnp.sum(weights, axis=-1)
    attn_float = (
        jnp.einsum("jgqc,cjd->jgqd", weights.astype(bf16), value_h, preferred_element_type=f32)
        / row_sum[..., None]
    )
    log_total = row_max + jnp.log(row_sum)
    attn_rows = attn_float.transpose(2, 0, 1, 3).reshape(tok_rows, query_width).astype(bf16)
    attn_total = layer_scatter(times_rows_t(attn_rows, out_all).astype(bf16))
    inv_two = rms_scale(attn_total)
    normed_two = attn_total * inv_two
    hidden_res = own_tok + normed_two * gain_two
    inv_three = rms_scale(hidden_res)
    normed_three = hidden_res * inv_three
    ffn_input = jnp.concatenate(
        layer_gather((normed_three * gain_three).astype(bf16)), axis=0
    )

    gate_lin = times_rows(ffn_input, gate_all)
    up_lin = times_rows(ffn_input, up_all)
    activated, gelu_pull = jax.vjp(gelu_tanh, gate_lin)
    hidden_b = (activated * up_lin).astype(bf16)
    ffn_total = layer_scatter(times_rows_t(hidden_b, down_all).astype(bf16))
    inv_four = rms_scale(ffn_total)
    normed_four = ffn_total * inv_four
    own_output = (hidden_res + normed_four * gain_four).astype(bf16)
    output = rows_out(layer_gather(columns_out(own_output)))

    grad_gain_four = jnp.sum(own_cot * normed_four, axis=0)
    grad_ffn = jnp.concatenate(
        layer_gather(norm_back(inv_four, normed_four, own_cot * gain_four).astype(bf16)), axis=0
    )
    grad_hidden = times_rows(grad_ffn, down_all)
    grad_gate = gelu_pull(grad_hidden * up_lin)[0].astype(bf16)
    grad_up = (grad_hidden * activated).astype(bf16)
    grad_ffn_in = layer_scatter(
        jnp.concatenate(
            [
                contract(grad_gate, gate_block, 1, 1) + contract(grad_up, up_block, 1, 1)
                for gate_block, up_block in zip(gate_all, up_all)
            ],
            axis=1,
        ).astype(bf16)
    )
    grad_w_down = collect_far(collect_near(weight_parts(grad_ffn, hidden_b)))
    grad_w_gate = collect_far(collect_near(weight_parts(ffn_input, grad_gate)))
    grad_w_up = collect_far(collect_near(weight_parts(ffn_input, grad_up)))
    grad_gain_three = jnp.sum(grad_ffn_in * normed_three, axis=0)
    grad_res = own_cot + norm_back(inv_three, normed_three, grad_ffn_in * gain_three)
    grad_gain_two = jnp.sum(grad_res * normed_two, axis=0)

    grad_attn = jnp.concatenate(
        layer_gather(norm_back(inv_two, normed_two, grad_res * gain_two).astype(bf16)), axis=0
    )
    grad_rows = times_rows(grad_attn, out_all).astype(bf16)
    grad_heads = grad_rows.reshape(tok_rows, key_heads, group_size, HD).transpose(1, 2, 0, 3)
    row_delta = jnp.sum(grad_heads.astype(f32) * attn_float, axis=-1)
    probs = jnp.where(visible, jnp.exp(SOFT_CAP * tanh_part - log_total[..., None]), 0.0)
    value_grad = jnp.einsum(
        "jgqc,jgqd->cjd", probs.astype(bf16), grad_heads, preferred_element_type=f32
    )
    weight_grad = jnp.einsum("jgqd,cjd->jgqc", grad_heads, value_h, preferred_element_type=f32)
    score_grad = (
        probs * (weight_grad - row_delta[..., None]) * (1.0 - tanh_part * tanh_part)
    ).astype(bf16)
    grad_q = jnp.einsum("jgqc,cjd->jgqd", score_grad, key_h, preferred_element_type=f32)
    key_grad = jnp.einsum("jgqc,jgqd->cjd", score_grad, queries_h, preferred_element_type=f32)
    pair_grad = jnp.concatenate(
        [key_grad.reshape(key_count, key_width), value_grad.reshape(key_count, key_width)], axis=1
    ).astype(bf16)
    pair_part = collect_near(
        [
            pair_grad[index * 4 * tok_rows : (index + 1) * 4 * tok_rows]
            for index in range(near_count)
        ]
    )
    pair_own = pair_part[:tok_rows].astype(f32)
    for index, step in ((1, far_a), (2, far_b), (3, far_a | far_b)):
        pair_own = pair_own + swap(
            pair_part[index * tok_rows : (index + 1) * tok_rows], step
        ).astype(f32)
    grad_query_lin = (
        rotate(
            grad_q.transpose(2, 0, 1, 3).reshape(tok_rows, heads_local, HD), cos_table, -sine_table
        )
        * HD ** (-0.5)
    ).reshape(tok_rows, query_width)
    grad_key_lin = rotate(
        pair_own[:, :key_width].reshape(tok_rows, key_heads, HD), cos_table, -sine_table
    ).reshape(tok_rows, key_width)
    grad_lin = jnp.concatenate(
        [grad_query_lin, grad_key_lin, pair_own[:, key_width:]], axis=1
    ).astype(bf16)
    grad_attn_in = layer_scatter(times_rows_t(grad_lin, qkv_w).astype(bf16))
    own_inv = rms_scale(own_tok)
    own_normed = own_tok * own_inv
    grad_gain_one = jnp.sum(grad_attn_in * own_normed, axis=0)
    grad_tokens = rows_out(
        layer_gather(
            columns_out(
                grad_res + norm_back(own_inv, own_normed, grad_attn_in * gain_one)
            ).astype(bf16)
        )
    ).astype(f32)

    attn_grads = collect_far(
        collect_near(
            [
                jnp.concatenate([lin_part, out_part], axis=1)
                for lin_part, out_part in zip(
                    weight_parts(attn_input, grad_lin), weight_parts(grad_attn, attn_rows)
                )
            ]
        )
    )
    gain_grads = jnp.stack([grad_gain_one, grad_gain_two, grad_gain_three, grad_gain_four])
    gain_sum = gain_grads
    for bit in [1 << index for index in range(layers.bit_length() - 1)]:
        gain_sum = gain_sum + swap(gain_sum, bit, "tp")
    spread = len(order)
    for bit in reversed([far_a, far_b] + near):
        spread = spread // 2
        gain_sum = gain_sum[:, : spread * shard] + swap(gain_sum[:, spread * shard :], bit)
    return (
        output,
        grad_tokens,
        attn_grads[:, :query_width],
        attn_grads[:, query_width : query_width + key_width],
        attn_grads[:, query_width + key_width : qkv_width],
        attn_grads[:, qkv_width:],
        grad_w_gate,
        grad_w_up,
        grad_w_down,
        gain_sum[0],
        gain_sum[1],
        gain_sum[2],
        gain_sum[3],
    )


def solution(mesh):
    return jax.shard_map(
        local,
        mesh=mesh,
        in_specs=(
            P("ctx", None),
            P("ctx", "tp"),
            P("ctx", "tp"),
            P("ctx", "tp"),
            P("ctx", "tp"),
            P("ctx", "tp"),
            P("ctx", "tp"),
            P("ctx", "tp"),
            P("ctx"),
            P("ctx"),
            P("ctx"),
            P("ctx"),
            P("ctx", None),
        ),
        out_specs=(
            P("ctx", None),
            P("ctx", None),
            P("ctx", "tp"),
            P("ctx", "tp"),
            P("ctx", "tp"),
            P("ctx", "tp"),
            P("ctx", "tp"),
            P("ctx", "tp"),
            P("ctx", "tp"),
            P("ctx"),
            P("ctx"),
            P("ctx"),
            P("ctx"),
        ),
        check_vma=False,
    )
```

time: 1140 us -> 798 us (0.70)
  the two profiles are of different devices: /device:TPU:0 before, /device:TPU:8 now
where the time goes in v1:
time: 798 us; the launch traced here: 782 us
  waiting for transfers between devices  439 us (55%)
  matrix products  109 us (14%)
  local copies, waits for them, and re-layouts  102 us (13%)
  starting transfers between devices  85.3 us (11%)
  other arithmetic  44 us (6%)
    ppermute x85, waiting for transfers between devices, swap(): lax.ppermute(value, axis, [(index, index ^ bit) for index in range(count)])  439 us
    ppermute x85, starting transfers between devices, swap(): lax.ppermute(value, axis, [(index, index ^ bit) for index in range(count)])  85.3 us
    dot_general x20, matrix products, contract(): lax.dot_general(first_operand, second_operand, (((first_dim,), (second_di...  66.6 us
    dot_general x10, matrix products, product(): jnp.dot(first_operand, second_operand, preferred_element_type=jnp.float32)  28.6 us
    dynamic_update_slice x16, local copies, waits for them, and re-layouts, columns_out(): lax.dynamic_update_slice_in_dim(result, array[:, place * shard:(place + 1...  26.8 us
    unnamed x209, local copies, waits for them, and re-layouts  25.8 us
  transfers between devices with their start and end apart: 85, of which 45 were waited for; matrix products, arithmetic and copies ran while one was open for 28% of the time, Pallas kernels for 0%

profile of v1, /device:TPU:8, one launch (start us, length us, event | category | flops | bytes accessed | tf_op | source)
XLA Modules:
  0.0 781.9 jit_solution(9516157427210652647)
XLA Ops:
  18.0 2.6 concatenate.154
  25.7 7.7 collective-permute-done.9
  41.1 26.3 %collective-permute-done.11 = bf16[144,512]{1,0:T(8,128)(2,1)S(1)} collective-permute-done((bf16[144,512]{1,0:T(8,128)(2,1)S(1)}, bf16[144,512]{1,0:T(8,128)(2,1)S(1)}, u32[]{:S(2)}, u32[]{:S(2)}) %collective-permute-start.11) | collective-permute-done | bytes 147488 | tf_op jit(solution)/shard_map/ppermute | solution.py:91
  89.4 41.1 %collective-permute-done.22 = bf16[144,2304]{1,0:T(8,128)(2,1)S(1)} collective-permute-done((bf16[144,2304]{1,0:T(8,128)(2,1)S(1)}, bf16[144,2304]{1,0:T(8,128)(2,1)S(1)}, u32[]{:S(2)}, u32[]{:S(2)}) %collective-permute-start.22) | collective-permute-done | bytes 663584 | tf_op jit(solution)/shard_map/ppermute | solution.py:91
  151.4 26.1 %collective-permute-done.27 = bf16[144,2304]{1,0:T(8,128)(2,1)} collective-permute-done((bf16[144,2304]{1,0:T(8,128)(2,1)}, bf16[144,2304]{1,0:T(8,128)(2,1)}, u32[]{:S(2)}, u32[]{:S(2)}) %collective-permute-start.27) | collective-permute-done | bytes 663584 | tf_op jit(solution)/shard_map/ppermute | solution.py:91
  184.7 4.8 collective-permute-done.6
  194.4 2.5 constant_dynamic-update-slice_fusion.32
  196.9 2.6 constant_dynamic-update-slice_fusion.31
  204.9 2.7 fusion.146
  209.3 2.7 collective-permute-start.15
  212.8 4.1 collective-permute-done.33
  221.8 10.2 %collective-permute-done.15 = bf16[64,2304]{1,0:T(8,128)(2,1)S(1)} collective-permute-done((bf16[64,2304]{1,0:T(8,128)(2,1)S(1)}, bf16[64,2304]{1,0:T(8,128)(2,1)S(1)}, u32[]{:S(2)}, u32[]{:S(2)}) %collective-permute-start.15) | collective-permute-done | bytes 294944 | tf_op jit(solution)/shard_map/ppermute | solution.py:91
  232.0 6.1 collective-permute-done.16
  241.0 3.0 collective-permute-start.18
  244.0 8.8 %collective-permute-done.17 = bf16[64,2304]{1,0:T(8,128)(2,1)S(1)} collective-permute-done((bf16[64,2304]{1,0:T(8,128)(2,1)S(1)}, bf16[64,2304]{1,0:T(8,128)(2,1)S(1)}, u32[]{:S(2)}, u32[]{:S(2)}) %collective-permute-start.17) | collective-permute-done | bytes 294944 | tf_op jit(solution)/shard_map/ppermute | solution.py:91
  257.7 4.4 collective-permute-done.18
  262.9 6.9 collective-permute-done.19
  271.3 4.4 fusion.70
  277.5 5.1 fusion.68
  282.6 3.3 multiply_convert_fusion.2
  285.9 4.7 convolution_convert_fusion.15
  290.6 14.9 %convolution_convert_fusion.14 = bf16[256,1152]{1,0:T(8,128)(2,1)S(1)} fusion(bf16[256,2304]{1,0:T(8,128)(2,1)S(1)} %get-tuple-element.211, bf16[1152,2304]{1,0:T(8,128)(2,1)} %collective-permute-done.34), kind=kOutput, calls=%fused_computation.48 | convolution fusion | flops 1359249408 | bytes 7077888 | tf_op jit(solution)/shard_map/dot_general | solution.py:43
  310.4 6.6 collective-permute-done.35
  317.0 11.3 %collective-permute-done.36 = bf16[64,2304]{1,0:T(8,128)(2,1)S(1)} collective-permute-done((bf16[64,2304]{1,0:T(8,128)(2,1)S(1)}, bf16[64,2304]{1,0:T(8,128)(2,1)S(1)}, u32[]{:S(2)}, u32[]{:S(2)}) %collective-permute-start.36) | collective-permute-done | bytes 294944 | tf_op jit(solution)/shard_map/ppermute | solution.py:91
  328.2 6.0 collective-permute-done.37
  336.4 2.6 collective-permute-start.42
  360.7 19.0 %collective-permute-done.43 = bf16[64,2304]{1,0:T(8,128)(2,1)} collective-permute-done((bf16[64,2304]{1,0:T(8,128)(2,1)}, bf16[64,2304]{1,0:T(8,128)(2,1)}, u32[]{:S(2)}, u32[]{:S(2)}) %collective-permute-start.43) | collective-permute-done | bytes 294944 | tf_op jit(solution)/shard_map/ppermute | solution.py:91
  381.0 4.0 convolution_convert_fusion
  385.0 4.3 fusion.57
  389.4 6.4 fusion.25
  397.5 3.9 convolution_convert_fusion.2
  403.1 4.2 fusion.148
  407.4 4.5 fusion.14
  414.4 4.0 convolution_convert_fusion.4
  419.7 5.8 collective-permute-done.45
  425.4 14.2 %collective-permute-done.46 = bf16[64,2304]{1,0:T(8,128)(2,1)S(1)} collective-permute-done((bf16[64,2304]{1,0:T(8,128)(2,1)S(1)}, bf16[64,2304]{1,0:T(8,128)(2,1)S(1)}, u32[]{:S(2)}, u32[]{:S(2)}) %collective-permute-start.46) | collective-permute-done | bytes 294944 | tf_op jit(solution)/shard_map/ppermute | solution.py:91
  445.3 3.2 collective-permute-done.47
  448.5 6.3 collective-permute-done.48
  454.8 4.7 collective-permute-done.49
  463.5 4.3 fusion.15
  467.9 3.3 multiply_convert_fusion
  479.6 2.6 convolution_convert_fusion.9
  488.9 4.1 collective-permute-done.51
  492.9 6.2 collective-permute-done.52
  503.2 2.8 convolution_convert_fusion.10
  513.9 4.9 collective-permute-done.54
  518.8 11.9 %collective-permute-done.55 = bf16[64,2304]{1,0:T(8,128)(2,1)S(1)} collective-permute-done((bf16[64,2304]{1,0:T(8,128)(2,1)S(1)}, bf16[64,2304]{1,0:T(8,128)(2,1)S(1)}, u32[]{:S(2)}, u32[]{:S(2)}) %collective-permute-start.55) | collective-permute-done | bytes 294944 | tf_op jit(solution)/shard_map/ppermute | solution.py:91
  530.7 5.5 collective-permute-done.56
  537.7 3.0 collective-permute-done.80
  541.6 4.1 collective-permute-done.81
  569.2 7.2 collective-permute-done.57
  577.1 11.1 %collective-permute-done.58 = bf16[64,2304]{1,0:T(8,128)(2,1)S(1)} collective-permute-done((bf16[64,2304]{1,0:T(8,128)(2,1)}, bf16[64,2304]{1,0:T(8,128)(2,1)S(1)}, u32[]{:S(2)}, u32[]{:S(2)}) %collective-permute-start.58) | collective-permute-done | bytes 294944 | tf_op jit(solution)/shard_map/ppermute | solution.py:91
  589.3 13.2 %collective-permute-done.59 = bf16[64,2304]{1,0:T(8,128)(2,1)S(1)} collective-permute-done((bf16[64,2304]{1,0:T(8,128)(2,1)S(1)}, bf16[64,2304]{1,0:T(8,128)(2,1)S(1)}, u32[]{:S(2)}, u32[]{:S(2)}) %collective-permute-start.59) | collective-permute-done | bytes 294944 | tf_op jit(solution)/shard_map/ppermute | solution.py:91
  604.1 4.1 fusion.8
  610.6 4.1 fusion.5
  616.1 4.1 fusion.2
  620.3 2.5 add_convert_fusion
  625.2 22.0 %collective-permute-done.61 = bf16[144,1536]{1,0:T(8,128)(2,1)S(1)} collective-permute-done((bf16[144,1536]{1,0:T(8,128)(2,1)S(1)}, bf16[144,1536]{1,0:T(8,128)(2,1)S(1)}, u32[]{:S(2)}, u32[]{:S(2)}) %collective-permute-start.61) | collective-permute-done | bytes 442400 | tf_op jit(solution)/shard_map/ppermute | solution.py:91
  653.3 11.7 %collective-permute-done.73 = bf16[144,2304]{1,0:T(8,128)(2,1)S(1)} collective-permute-done((bf16[144,2304]{1,0:T(8,128)(2,1)S(1)}, bf16[144,2304]{1,0:T(8,128)(2,1)S(1)}, u32[]{:S(2)}, u32[]{:S(2)}) %collective-permute-start.73) | collective-permute-done | bytes 663584 | tf_op jit(solution)/shard_map/ppermute | solution.py:91
  667.7 11.5 %collective-permute-done.68 = bf16[144,2304]{1,0:T(8,128)(2,1)S(1)} collective-permute-done((bf16[144,2304]{1,0:T(8,128)(2,1)S(1)}, bf16[144,2304]{1,0:T(8,128)(2,1)S(1)}, u32[]{:S(2)}, u32[]{:S(2)}) %collective-permute-start.68) | collective-permute-done | bytes 663584 | tf_op jit(solution)/shard_map/ppermute | solution.py:91
  681.0 17.2 %collective-permute-done.62 = bf16[288,1536]{1,0:T(8,128)(2,1)S(1)} collective-permute-done((bf16[288,1536]{1,0:T(8,128)(2,1)S(1)}, bf16[288,1536]{1,0:T(8,128)(2,1)S(1)}, u32[]{:S(2)}, u32[]{:S(2)}) %collective-permute-start.62) | collective-permute-done | bytes 884768 | tf_op jit(solution)/shard_map/ppermute | solution.py:91
  702.5 24.1 %collective-permute-done.77 = bf16[288,2304]{1,0:T(8,128)(2,1)S(1)} collective-permute-done((bf16[288,2304]{1,0:T(8,128)(2,1)S(1)}, bf16[288,2304]{1,0:T(8,128)(2,1)S(1)}, u32[]{:S(2)}, u32[]{:S(2)}) %collective-permute-start.77) | collective-permute-done | bytes 1327136 | tf_op jit(solution)/shard_map/ppermute | solution.py:91
  729.8 25.2 %collective-permute-done.72 = bf16[288,2304]{1,0:T(8,128)(2,1)S(1)} collective-permute-done((bf16[288,2304]{1,0:T(8,128)(2,1)S(1)}, bf16[288,2304]{1,0:T(8,128)(2,1)S(1)}, u32[]{:S(2)}, u32[]{:S(2)}) %collective-permute-start.72) | collective-permute-done | bytes 1327136 | tf_op jit(solution)/shard_map/ppermute | solution.py:91
  757.1 22.5 %collective-permute-done.67 = bf16[288,2304]{1,0:T(8,128)(2,1)S(1)} collective-permute-done((bf16[288,2304]{1,0:T(8,128)(2,1)S(1)}, bf16[288,2304]{1,0:T(8,128)(2,1)S(1)}, u32[]{:S(2)}, u32[]{:S(2)}) %collective-permute-start.67) | collective-permute-done | bytes 1327136 | tf_op jit(solution)/shard_map/ppermute | solution.py:91
  (530 shorter events, 240.0 us)
Async XLA Ops:
  11.0 62.3 %collective-permute-start = (bf16[304,1024]{1,0:T(8,128)(2,1)}, bf16[304,1024]{1,0:T(8,128)(2,1)S(1)}, u32[]{:S(2)}, u32[]{:S(2)}) collective-permute-start(bf16[304,1024]{1,0:T(8,128)(2,1)} %pad_maximum_fusion.15), channel_id=1, source_target_pairs={{0,8},{4,12},{8,0},{12,4},{16,24},{20,28},{24,16},{28,20},{1,9},{5... | collective-permute-start | bytes 1867784 | tf_op jit(solution)/shard_map/ppermute | solution.py:91
  12.5 57.5 %collective-permute-start.1 = (bf16[304,1024]{1,0:T(8,128)(2,1)}, bf16[304,1024]{1,0:T(8,128)(2,1)}, u32[]{:S(2)}, u32[]{:S(2)}) collective-permute-start(bf16[304,1024]{1,0:T(8,128)(2,1)} %pad_maximum_fusion.15), channel_id=1, source_target_pairs={{0,16},{4,20},{8,24},{12,28},{16,0},{20,4},{24,8},{28,12},{1,17},{... | collective-permute-start | bytes 1867784 | tf_op jit(solution)/shard_map/ppermute | solution.py:91
  14.0 19.4 %collective-permute-start.9 = (bf16[288,512]{1,0:T(8,128)(2,1)}, bf16[288,512]{1,0:T(8,128)(2,1)}, u32[]{:S(2)}, u32[]{:S(2)}) collective-permute-start(bf16[288,512]{1,0:T(8,128)(2,1)} %param.19), channel_id=1, source_target_pairs={{0,8},{4,12},{8,0},{12,4},{16,24},{20,28},{24,16},{28,20},{1,9},{5... | collective-permute-start | bytes 884744 | tf_op jit(solution)/shard_map/ppermute | solution.py:91
  14.5 20.1 %collective-permute-start.10 = (bf16[288,512]{1,0:T(8,128)(2,1)}, bf16[288,512]{1,0:T(8,128)(2,1)}, u32[]{:S(2)}, u32[]{:S(2)}) collective-permute-start(bf16[288,512]{1,0:T(8,128)(2,1)} %param.19), channel_id=1, source_target_pairs={{0,16},{4,20},{8,24},{12,28},{16,0},{20,4},{24,8},{28,12},{1,17},{... | collective-permute-start | bytes 884744 | tf_op jit(solution)/shard_map/ppermute | solution.py:91
  34.6 50.1 %collective-permute-start.20 = (bf16[288,2304]{1,0:T(8,128)(2,1)S(1)}, bf16[288,2304]{1,0:T(8,128)(2,1)S(1)}, u32[]{:S(2)}, u32[]{:S(2)}) collective-permute-start(bf16[288,2304]{1,0:T(8,128)(2,1)S(1)} %copy-done.33), channel_id=1, source_target_pairs={{0,8},{4,12},{8,0},{12,4},{16,24},{20,28},{24,16},{28,20},{1,9},{5... | collective-permute-start | bytes 3981320 | tf_op jit(solution)/shard_map/ppermute | solution.py:91
  35.1 49.6 %collective-permute-start.21 = (bf16[288,2304]{1,0:T(8,128)(2,1)S(1)}, bf16[288,2304]{1,0:T(8,128)(2,1)S(1)}, u32[]{:S(2)}, u32[]{:S(2)}) collective-permute-start(bf16[288,2304]{1,0:T(8,128)(2,1)S(1)} %copy-done.33), channel_id=1, source_target_pairs={{0,16},{4,20},{8,24},{12,28},{16,0},{20,4},{24,8},{28,12},{1,17},{... | collective-permute-start | bytes 3981320 | tf_op jit(solution)/shard_map/ppermute | solution.py:91
  37.6 29.9 %collective-permute-start.11 = (bf16[144,512]{1,0:T(8,128)(2,1)S(1)}, bf16[144,512]{1,0:T(8,128)(2,1)S(1)}, u32[]{:S(2)}, u32[]{:S(2)}) collective-permute-start(bf16[144,512]{1,0:T(8,128)(2,1)S(1)} %slice.607), channel_id=1, source_target_pairs={{0,8},{4,12},{8,0},{12,4},{16,24},{20,28},{24,16},{28,20},{1,9},{5... | collective-permute-start | bytes 442376 | tf_op jit(solution)/shard_map/ppermute | solution.py:91
  81.3 58.7 %collective-permute-start.4 = (bf16[1216,1024]{1,0:T(8,128)(2,1)}, bf16[1216,1024]{1,0:T(8,128)(2,1)S(1)}, u32[]{:S(2)}, u32[]{:S(2)}) collective-permute-start(bf16[1216,1024]{1,0:T(8,128)(2,1)} %constant_dynamic-update-slice_fusion.1), channel_id=1, source_target_pairs={{0,4},{4,0},{8,12},{12,8},{16,20},{20,16},{24,28},{28,24},{1,5},{5... | collective-permute-start | bytes 7471112 | tf_op jit(solution)/shard_map/ppermute | solution.py:91
  84.7 46.1 %collective-permute-start.25 = (bf16[288,2304]{1,0:T(8,128)(2,1)S(1)}, bf16[288,2304]{1,0:T(8,128)(2,1)S(1)}, u32[]{:S(2)}, u32[]{:S(2)}) collective-permute-start(bf16[288,2304]{1,0:T(8,128)(2,1)S(1)} %copy-done.34), channel_id=1, source_target_pairs={{0,8},{4,12},{8,0},{12,4},{16,24},{20,28},{24,16},{28,20},{1,9},{5... | collective-permute-start | bytes 3981320 | tf_op jit(solution)/shard_map/ppermute | solution.py:91
  85.0 45.9 %collective-permute-start.26 = (bf16[288,2304]{1,0:T(8,128)(2,1)S(1)}, bf16[288,2304]{1,0:T(8,128)(2,1)S(1)}, u32[]{:S(2)}, u32[]{:S(2)}) collective-permute-start(bf16[288,2304]{1,0:T(8,128)(2,1)S(1)} %copy-done.34), channel_id=1, source_target_pairs={{0,16},{4,20},{8,24},{12,28},{16,0},{20,4},{24,8},{28,12},{1,17},{... | collective-permute-start | bytes 3981320 | tf_op jit(solution)/shard_map/ppermute | solution.py:91
  87.1 43.5 %collective-permute-start.22 = (bf16[144,2304]{1,0:T(8,128)(2,1)S(1)}, bf16[144,2304]{1,0:T(8,128)(2,1)S(1)}, u32[]{:S(2)}, u32[]{:S(2)}) collective-permute-start(bf16[144,2304]{1,0:T(8,128)(2,1)S(1)} %slice.618), channel_id=1, source_target_pairs={{0,8},{4,12},{8,0},{12,4},{16,24},{20,28},{24,16},{28,20},{1,9},{5... | collective-permute-start | bytes 1990664 | tf_op jit(solution)/shard_map/ppermute | solution.py:91
  88.7 42.1 %collective-permute-start.23 = (bf16[144,2304]{1,0:T(8,128)(2,1)S(1)}, bf16[144,2304]{1,0:T(8,128)(2,1)S(1)}, u32[]{:S(2)}, u32[]{:S(2)}) collective-permute-start(bf16[144,2304]{1,0:T(8,128)(2,1)S(1)} %slice.619), channel_id=1, source_target_pairs={{0,16},{4,20},{8,24},{12,28},{16,0},{20,4},{24,8},{28,12},{1,17},{... | collective-permute-start | bytes 1990664 | tf_op jit(solution)/shard_map/ppermute | solution.py:91
  130.8 60.6 %collective-permute-start.30 = (bf16[288,2304]{1,0:T(8,128)(2,1)}, bf16[288,2304]{1,0:T(8,128)(2,1)}, u32[]{:S(2)}, u32[]{:S(2)}) collective-permute-start(bf16[288,2304]{1,0:T(8,128)(2,1)} %param.22), channel_id=1, source_target_pairs={{0,8},{4,12},{8,0},{12,4},{16,24},{20,28},{24,16},{28,20},{1,9},{5... | collective-permute-start | bytes 3981320 | tf_op jit(solution)/shard_map/ppermute | solution.py:91
  132.6 57.6 %collective-permute-start.31 = (bf16[288,2304]{1,0:T(8,128)(2,1)}, bf16[288,2304]{1,0:T(8,128)(2,1)}, u32[]{:S(2)}, u32[]{:S(2)}) collective-permute-start(bf16[288,2304]{1,0:T(8,128)(2,1)} %param.22), channel_id=1, source_target_pairs={{0,16},{4,20},{8,24},{12,28},{16,0},{20,4},{24,8},{28,12},{1,17},{... | collective-permute-start | bytes 3981320 | tf_op jit(solution)/shard_map/ppermute | solution.py:91
  135.0 42.5 %collective-permute-start.27 = (bf16[144,2304]{1,0:T(8,128)(2,1)}, bf16[144,2304]{1,0:T(8,128)(2,1)}, u32[]{:S(2)}, u32[]{:S(2)}) collective-permute-start(bf16[144,2304]{1,0:T(8,128)(2,1)} %slice.621), channel_id=1, source_target_pairs={{0,8},{4,12},{8,0},{12,4},{16,24},{20,28},{24,16},{28,20},{1,9},{5... | collective-permute-start | bytes 1990664 | tf_op jit(solution)/shard_map/ppermute | solution.py:91
  136.4 44.8 %collective-permute-start.28 = (bf16[144,2304]{1,0:T(8,128)(2,1)}, bf16[144,2304]{1,0:T(8,128)(2,1)}, u32[]{:S(2)}, u32[]{:S(2)}) collective-permute-start(bf16[144,2304]{1,0:T(8,128)(2,1)} %slice.622), channel_id=1, source_target_pairs={{0,16},{4,20},{8,24},{12,28},{16,0},{20,4},{24,8},{28,12},{1,17},{... | collective-permute-start | bytes 1990664 | tf_op jit(solution)/shard_map/ppermute | solution.py:91
  150.0 34.6 %collective-permute-start.5 = (bf16[256,512]{1,0:T(8,128)(2,1)S(1)}, bf16[256,512]{1,0:T(8,128)(2,1)S(1)}, u32[]{:S(2)}, u32[]{:S(2)}) collective-permute-start(bf16[256,512]{1,0:T(8,128)(2,1)S(1)} %get-tuple-element.200), channel_id=1, source_target_pairs={{0,8},{4,12},{8,0},{12,4},{16,24},{20,28},{24,16},{28,20},{1,9},{5... | collective-permute-start | bytes 786440 | tf_op jit(solution)/shard_map/ppermute | solution.py:91
  184.7 23.5 %collective-permute-start.13 = (bf16[1152,512]{1,0:T(8,128)(2,1)S(1)}, bf16[1152,512]{1,0:T(8,128)(2,1)S(1)}, u32[]{:S(2)}, u32[]{:S(2)}) collective-permute-start(bf16[1152,512]{1,0:T(8,128)(2,1)S(1)} %copy-done.7), channel_id=1, source_target_pairs={{0,4},{4,0},{8,12},{12,8},{16,20},{20,16},{24,28},{28,24},{1,5},{5... | collective-permute-start | bytes 3538952 | tf_op jit(solution)/shard_map/ppermute | solution.py:91
  189.5 81.9 %collective-permute-start.24 = (bf16[1152,2304]{1,0:T(8,128)(2,1)}, bf16[1152,2304]{1,0:T(8,128)(2,1)}, u32[]{:S(2)}, u32[]{:S(2)}) collective-permute-start(bf16[1152,2304]{1,0:T(8,128)(2,1)} %copy-done.47), channel_id=1, source_target_pairs={{0,4},{4,0},{8,12},{12,8},{16,20},{20,16},{24,28},{28,24},{1,5},{5... | collective-permute-start | bytes 15925256 | tf_op jit(solution)/shard_map/ppermute | solution.py:91
  190.2 87.3 %collective-permute-start.29 = (bf16[1152,2304]{1,0:T(8,128)(2,1)}, bf16[1152,2304]{1,0:T(8,128)(2,1)}, u32[]{:S(2)}, u32[]{:S(2)}) collective-permute-start(bf16[1152,2304]{1,0:T(8,128)(2,1)} %constant_dynamic-update-slice_fusion.24), channel_id=1, source_target_pairs={{0,4},{4,0},{8,12},{12,8},{16,20},{20,16},{24,28},{28,24},{1,5},{5... | collective-permute-start | bytes 15925256 | tf_op jit(solution)/shard_map/ppermute | solution.py:91
  191.4 17.8 %collective-permute-start.32 = (bf16[144,2304]{1,0:T(8,128)(2,1)S(1)}, bf16[144,2304]{1,0:T(8,128)(2,1)S(1)}, u32[]{:S(2)}, u32[]{:S(2)}) collective-permute-start(bf16[144,2304]{1,0:T(8,128)(2,1)S(1)} %slice.623), channel_id=1, source_target_pairs={{0,8},{4,12},{8,0},{12,4},{16,24},{20,28},{24,16},{28,20},{1,9},{5... | collective-permute-start | bytes 1990664 | tf_op jit(solution)/shard_map/ppermute | solution.py:91
  199.8 17.2 %collective-permute-start.33 = (bf16[144,2304]{1,0:T(8,128)(2,1)S(1)}, bf16[144,2304]{1,0:T(8,128)(2,1)S(1)}, u32[]{:S(2)}, u32[]{:S(2)}) collective-permute-start(bf16[144,2304]{1,0:T(8,128)(2,1)S(1)} %slice.624), channel_id=1, source_target_pairs={{0,16},{4,20},{8,24},{12,28},{16,0},{20,4},{24,8},{28,12},{1,17},{... | collective-permute-start | bytes 1990664 | tf_op jit(solution)/shard_map/ppermute | solution.py:91
  209.3 22.7 %collective-permute-start.15 = (bf16[64,2304]{1,0:T(8,128)(2,1)S(1)}, bf16[64,2304]{1,0:T(8,128)(2,1)S(1)}, u32[]{:S(2)}, u32[]{:S(2)}) collective-permute-start(bf16[64,2304]{1,0:T(8,128)(2,1)S(1)} %get-tuple-element.156), channel_id=1, source_target_pairs={{0,2},{1,3},{2,0},{3,1},{4,6},{5,7},{6,4},{7,5},{8,10},{9,11},{10,... | collective-permute-start | bytes 884744 | tf_op jit(solution)/shard_map/ppermute | solution.py:91
  217.0 21.1 %collective-permute-start.16 = (bf16[64,2304]{1,0:T(8,128)(2,1)S(1)}, bf16[64,2304]{1,0:T(8,128)(2,1)S(1)}, u32[]{:S(2)}, u32[]{:S(2)}) collective-permute-start(bf16[64,2304]{1,0:T(8,128)(2,1)S(1)} %get-tuple-element.155), channel_id=1, source_target_pairs={{0,3},{1,2},{2,1},{3,0},{4,7},{5,6},{6,5},{7,4},{8,11},{9,10},{10,... | collective-permute-start | bytes 884744 | tf_op jit(solution)/shard_map/ppermute | solution.py:91
  221.8 68.8 %collective-permute-start.34 = (bf16[1152,2304]{1,0:T(8,128)(2,1)}, bf16[1152,2304]{1,0:T(8,128)(2,1)}, u32[]{:S(2)}, u32[]{:S(2)}) collective-permute-start(bf16[1152,2304]{1,0:T(8,128)(2,1)} %constant_dynamic-update-slice_fusion.29), channel_id=1, source_target_pairs={{0,4},{4,0},{8,12},{12,8},{16,20},{20,16},{24,28},{28,24},{1,5},{5... | collective-permute-start | bytes 15925256 | tf_op jit(solution)/shard_map/ppermute | solution.py:91
  241.0 21.2 %collective-permute-start.18 = (bf16[64,2304]{1,0:T(8,128)(2,1)S(1)}, bf16[64,2304]{1,0:T(8,128)(2,1)S(1)}, u32[]{:S(2)}, u32[]{:S(2)}) collective-permute-start(bf16[64,2304]{1,0:T(8,128)(2,1)S(1)} %multiply_convert_fusion.5), channel_id=1, source_target_pairs={{0,2},{1,3},{2,0},{3,1},{4,6},{5,7},{6,4},{7,5},{8,10},{9,11},{10,... | collective-permute-start | bytes 884744 | tf_op jit(solution)/shard_map/ppermute | solution.py:91
  252.9 17.0 %collective-permute-start.19 = (bf16[64,2304]{1,0:T(8,128)(2,1)S(1)}, bf16[64,2304]{1,0:T(8,128)(2,1)}, u32[]{:S(2)}, u32[]{:S(2)}) collective-permute-start(bf16[64,2304]{1,0:T(8,128)(2,1)S(1)} %multiply_convert_fusion.5), channel_id=1, source_target_pairs={{0,3},{1,2},{2,1},{3,0},{4,7},{5,6},{6,5},{7,4},{8,11},{9,10},{10,... | collective-permute-start | bytes 884744 | tf_op jit(solution)/shard_map/ppermute | solution.py:91
  305.8 22.5 %collective-permute-start.36 = (bf16[64,2304]{1,0:T(8,128)(2,1)S(1)}, bf16[64,2304]{1,0:T(8,128)(2,1)S(1)}, u32[]{:S(2)}, u32[]{:S(2)}) collective-permute-start(bf16[64,2304]{1,0:T(8,128)(2,1)S(1)} %get-tuple-element.153), channel_id=1, source_target_pairs={{0,2},{1,3},{2,0},{3,1},{4,6},{5,7},{6,4},{7,5},{8,10},{9,11},{10,... | collective-permute-start | bytes 884744 | tf_op jit(solution)/shard_map/ppermute | solution.py:91
  308.1 26.1 %collective-permute-start.37 = (bf16[64,2304]{1,0:T(8,128)(2,1)S(1)}, bf16[64,2304]{1,0:T(8,128)(2,1)S(1)}, u32[]{:S(2)}, u32[]{:S(2)}) collective-permute-start(bf16[64,2304]{1,0:T(8,128)(2,1)S(1)} %get-tuple-element.152), channel_id=1, source_target_pairs={{0,3},{1,2},{2,1},{3,0},{4,7},{5,6},{6,5},{7,4},{8,11},{9,10},{10,... | collective-permute-start | bytes 884744 | tf_op jit(solution)/shard_map/ppermute | solution.py:91
  336.3 23.4 %collective-permute-start.41 = (bf16[64,2304]{1,0:T(8,128)(2,1)}, bf16[64,2304]{1,0:T(8,128)(2,1)}, u32[]{:S(2)}, u32[]{:S(2)}) collective-permute-start(bf16[64,2304]{1,0:T(8,128)(2,1)} %get-tuple-element.176), channel_id=1, source_target_pairs={{0,1},{1,0},{2,3},{3,2},{4,5},{5,4},{6,7},{7,6},{8,9},{9,8},{10,11... | collective-permute-start | bytes 884744 | tf_op jit(solution)/shard_map/ppermute | solution.py:91
  336.4 24.3 %collective-permute-start.42 = (bf16[64,2304]{1,0:T(8,128)(2,1)}, bf16[64,2304]{1,0:T(8,128)(2,1)}, u32[]{:S(2)}, u32[]{:S(2)}) collective-permute-start(bf16[64,2304]{1,0:T(8,128)(2,1)} %get-tuple-element.176), channel_id=1, source_target_pairs={{0,2},{1,3},{2,0},{3,1},{4,6},{5,7},{6,4},{7,5},{8,10},{9,11},{10,... | collective-permute-start | bytes 884744 | tf_op jit(solution)/shard_map/ppermute | solution.py:91
  338.9 40.7 %collective-permute-start.43 = (bf16[64,2304]{1,0:T(8,128)(2,1)}, bf16[64,2304]{1,0:T(8,128)(2,1)}, u32[]{:S(2)}, u32[]{:S(2)}) collective-permute-start(bf16[64,2304]{1,0:T(8,128)(2,1)} %get-tuple-element.176), channel_id=1, source_target_pairs={{0,3},{1,2},{2,1},{3,0},{4,7},{5,6},{6,5},{7,4},{8,11},{9,10},{10,... | collective-permute-start | bytes 884744 | tf_op jit(solution)/shard_map/ppermute | solution.py:91
  354.7 63.7 %collective-permute-start.38 = (bf16[64,2304]{1,0:T(8,128)(2,1)}, bf16[64,2304]{1,0:T(8,128)(2,1)S(1)}, u32[]{:S(2)}, u32[]{:S(2)}) collective-permute-start(bf16[64,2304]{1,0:T(8,128)(2,1)} %dynamic_update_slice.79), channel_id=1, source_target_pairs={{0,1},{1,0},{2,3},{3,2},{4,5},{5,4},{6,7},{7,6},{8,9},{9,8},{10,11... | collective-permute-start | bytes 884744 | tf_op jit(solution)/shard_map/ppermute | solution.py:91
  355.6 88.5 %collective-permute-start.39 = (bf16[64,2304]{1,0:T(8,128)(2,1)}, bf16[64,2304]{1,0:T(8,128)(2,1)S(1)}, u32[]{:S(2)}, u32[]{:S(2)}) collective-permute-start(bf16[64,2304]{1,0:T(8,128)(2,1)} %dynamic_update_slice.79), channel_id=1, source_target_pairs={{0,2},{1,3},{2,0},{3,1},{4,6},{5,7},{6,4},{7,5},{8,10},{9,11},{10,... | collective-permute-start | bytes 884744 | tf_op jit(solution)/shard_map/ppermute | solution.py:91
  359.7 113.5 %collective-permute-start.40 = (bf16[64,2304]{1,0:T(8,128)(2,1)}, bf16[64,2304]{1,0:T(8,128)(2,1)}, u32[]{:S(2)}, u32[]{:S(2)}) collective-permute-start(bf16[64,2304]{1,0:T(8,128)(2,1)} %dynamic_update_slice.79), channel_id=1, source_target_pairs={{0,3},{1,2},{2,1},{3,0},{4,7},{5,6},{6,5},{7,4},{8,11},{9,10},{10,... | collective-permute-start | bytes 884744 | tf_op jit(solution)/shard_map/ppermute | solution.py:91
  412.0 13.4 %collective-permute-start.45 = (bf16[64,2304]{1,0:T(8,128)(2,1)S(1)}, bf16[64,2304]{1,0:T(8,128)(2,1)S(1)}, u32[]{:S(2)}, u32[]{:S(2)}) collective-permute-start(bf16[64,2304]{1,0:T(8,128)(2,1)S(1)} %get-tuple-element.142), channel_id=1, source_target_pairs={{0,2},{1,3},{2,0},{3,1},{4,6},{5,7},{6,4},{7,5},{8,10},{9,11},{10,... | collective-permute-start | bytes 884744 | tf_op jit(solution)/shard_map/ppermute | solution.py:91
  418.4 21.2 %collective-permute-start.46 = (bf16[64,2304]{1,0:T(8,128)(2,1)S(1)}, bf16[64,2304]{1,0:T(8,128)(2,1)S(1)}, u32[]{:S(2)}, u32[]{:S(2)}) collective-permute-start(bf16[64,2304]{1,0:T(8,128)(2,1)S(1)} %get-tuple-element.141), channel_id=1, source_target_pairs={{0,3},{1,2},{2,1},{3,0},{4,7},{5,6},{6,5},{7,4},{8,11},{9,10},{10,... | collective-permute-start | bytes 884744 | tf_op jit(solution)/shard_map/ppermute | solution.py:91
  419.6 184.5 %collective-permute-start.75 = (bf16[1152,2304]{1,0:T(8,128)(2,1)}, bf16[1152,2304]{1,0:T(8,128)(2,1)}, u32[]{:S(2)}, u32[]{:S(2)}) collective-permute-start(bf16[1152,2304]{1,0:T(8,128)(2,1)} %convolution_convert_fusion), channel_id=1, source_target_pairs={{0,4},{4,0},{8,12},{12,8},{16,20},{20,16},{24,28},{28,24},{1,5},{5... | collective-permute-start | bytes 15925256 | tf_op jit(solution)/shard_map/ppermute | solution.py:91
  444.1 15.3 %collective-permute-start.49 = (bf16[64,2304]{1,0:T(8,128)(2,1)S(1)}, bf16[64,2304]{1,0:T(8,128)(2,1)S(1)}, u32[]{:S(2)}, u32[]{:S(2)}) collective-permute-start(bf16[64,2304]{1,0:T(8,128)(2,1)S(1)} %multiply_convert_fusion.4), channel_id=1, source_target_pairs={{0,3},{1,2},{2,1},{3,0},{4,7},{5,6},{6,5},{7,4},{8,11},{9,10},{10,... | collective-permute-start | bytes 884744 | tf_op jit(solution)/shard_map/ppermute | solution.py:91
  448.5 162.2 %collective-permute-start.70 = (bf16[1152,2304]{1,0:T(8,128)(2,1)}, bf16[1152,2304]{1,0:T(8,128)(2,1)}, u32[]{:S(2)}, u32[]{:S(2)}) collective-permute-start(bf16[1152,2304]{1,0:T(8,128)(2,1)} %convolution_convert_fusion.2), channel_id=1, source_target_pairs={{0,4},{4,0},{8,12},{12,8},{16,20},{20,16},{24,28},{28,24},{1,5},{5... | collective-permute-start | bytes 15925256 | tf_op jit(solution)/shard_map/ppermute | solution.py:91
  485.1 14.0 %collective-permute-start.52 = (bf16[256,512]{1,0:T(8,128)(2,1)S(1)}, bf16[256,512]{1,0:T(8,128)(2,1)S(1)}, u32[]{:S(2)}, u32[]{:S(2)}) collective-permute-start(bf16[256,512]{1,0:T(8,128)(2,1)S(1)} %get-tuple-element.171), channel_id=1, source_target_pairs={{0,16},{4,20},{8,24},{12,28},{16,0},{20,4},{24,8},{28,12},{1,17},{... | collective-permute-start | bytes 786440 | tf_op jit(solution)/shard_map/ppermute | solution.py:91
  486.1 13.0 %collective-permute-start.53 = (bf16[256,512]{1,0:T(8,128)(2,1)S(1)}, bf16[256,512]{1,0:T(8,128)(2,1)S(1)}, u32[]{:S(2)}, u32[]{:S(2)}) collective-permute-start(bf16[256,512]{1,0:T(8,128)(2,1)S(1)} %get-tuple-element.170), channel_id=1, source_target_pairs={{0,24},{4,28},{8,16},{12,20},{16,8},{20,12},{24,0},{28,4},{1,25},{... | collective-permute-start | bytes 786440 | tf_op jit(solution)/shard_map/ppermute | solution.py:91
  508.3 22.4 %collective-permute-start.55 = (bf16[64,2304]{1,0:T(8,128)(2,1)S(1)}, bf16[64,2304]{1,0:T(8,128)(2,1)S(1)}, u32[]{:S(2)}, u32[]{:S(2)}) collective-permute-start(bf16[64,2304]{1,0:T(8,128)(2,1)S(1)} %get-tuple-element.139), channel_id=1, source_target_pairs={{0,2},{1,3},{2,0},{3,1},{4,6},{5,7},{6,4},{7,5},{8,10},{9,11},{10,... | collective-permute-start | bytes 884744 | tf_op jit(solution)/shard_map/ppermute | solution.py:91
  510.6 25.7 %collective-permute-start.56 = (bf16[64,2304]{1,0:T(8,128)(2,1)S(1)}, bf16[64,2304]{1,0:T(8,128)(2,1)S(1)}, u32[]{:S(2)}, u32[]{:S(2)}) collective-permute-start(bf16[64,2304]{1,0:T(8,128)(2,1)S(1)} %get-tuple-element.138), channel_id=1, source_target_pairs={{0,3},{1,2},{2,1},{3,0},{4,7},{5,6},{6,5},{7,4},{8,11},{9,10},{10,... | collective-permute-start | bytes 884744 | tf_op jit(solution)/shard_map/ppermute | solution.py:91
  518.8 97.3 %collective-permute-start.65 = (bf16[1152,2304]{1,0:T(8,128)(2,1)}, bf16[1152,2304]{1,0:T(8,128)(2,1)}, u32[]{:S(2)}, u32[]{:S(2)}) collective-permute-start(bf16[1152,2304]{1,0:T(8,128)(2,1)} %convolution_convert_fusion.4), channel_id=1, source_target_pairs={{0,4},{4,0},{8,12},{12,8},{16,20},{20,16},{24,28},{28,24},{1,5},{5... | collective-permute-start | bytes 15925256 | tf_op jit(solution)/shard_map/ppermute | solution.py:91
  537.6 82.6 %collective-permute-start.60 = (bf16[1152,1536]{1,0:T(8,128)(2,1)}, bf16[1152,1536]{1,0:T(8,128)(2,1)}, u32[]{:S(2)}, u32[]{:S(2)}) collective-permute-start(bf16[1152,1536]{1,0:T(8,128)(2,1)} %pad_maximum_fusion), channel_id=1, source_target_pairs={{0,4},{4,0},{8,12},{12,8},{16,20},{20,16},{24,28},{28,24},{1,5},{5... | collective-permute-start | bytes 10616840 | tf_op jit(solution)/shard_map/ppermute | solution.py:91
  547.7 16.4 %collective-permute-start.83 = (f32[4,576]{1,0:T(4,128)S(1)}, f32[4,576]{1,0:T(4,128)}, u32[]{:S(2)}, u32[]{:S(2)}) collective-permute-start(f32[4,576]{1,0:T(4,128)S(1)} %slice.711), channel_id=1, source_target_pairs={{0,16},{4,20},{8,24},{12,28},{16,0},{20,4},{24,8},{28,12},{1,17},{... | collective-permute-start | bytes 27656 | tf_op jit(solution)/shard_map/ppermute | solution.py:91
  588.2 14.3 %collective-permute-start.59 = (bf16[64,2304]{1,0:T(8,128)(2,1)S(1)}, bf16[64,2304]{1,0:T(8,128)(2,1)S(1)}, u32[]{:S(2)}, u32[]{:S(2)}) collective-permute-start(bf16[64,2304]{1,0:T(8,128)(2,1)S(1)} %copy-done.39), channel_id=1, source_target_pairs={{0,3},{1,2},{2,1},{3,0},{4,7},{5,6},{6,5},{7,4},{8,11},{9,10},{10,... | collective-permute-start | bytes 884744 | tf_op jit(solution)/shard_map/ppermute | solution.py:91
  608.4 41.2 %collective-permute-start.76 = (bf16[144,2304]{1,0:T(8,128)(2,1)S(1)}, bf16[144,2304]{1,0:T(8,128)(2,1)S(1)}, u32[]{:S(2)}, u32[]{:S(2)}) collective-permute-start(bf16[144,2304]{1,0:T(8,128)(2,1)S(1)} %get-tuple-element.101), channel_id=1, source_target_pairs={{0,16},{4,20},{8,24},{12,28},{16,0},{20,4},{24,8},{28,12},{1,17},{... | collective-permute-start | bytes 1990664 | tf_op jit(solution)/shard_map/ppermute | solution.py:91
  609.6 41.1 %collective-permute-start.78 = (bf16[144,2304]{1,0:T(8,128)(2,1)S(1)}, bf16[144,2304]{1,0:T(8,128)(2,1)S(1)}, u32[]{:S(2)}, u32[]{:S(2)}) collective-permute-start(bf16[144,2304]{1,0:T(8,128)(2,1)S(1)} %get-tuple-element.100), channel_id=1, source_target_pairs={{0,8},{4,12},{8,0},{12,4},{16,24},{20,28},{24,16},{28,20},{1,9},{5... | collective-permute-start | bytes 1990664 | tf_op jit(solution)/shard_map/ppermute | solution.py:91
  615.0 37.2 %collective-permute-start.71 = (bf16[144,2304]{1,0:T(8,128)(2,1)S(1)}, bf16[144,2304]{1,0:T(8,128)(2,1)S(1)}, u32[]{:S(2)}, u32[]{:S(2)}) collective-permute-start(bf16[144,2304]{1,0:T(8,128)(2,1)S(1)} %get-tuple-element.107), channel_id=1, source_target_pairs={{0,16},{4,20},{8,24},{12,28},{16,0},{20,4},{24,8},{28,12},{1,17},{... | collective-permute-start | bytes 1990664 | tf_op jit(solution)/shard_map/ppermute | solution.py:91
  622.9 24.2 %collective-permute-start.61 = (bf16[144,1536]{1,0:T(8,128)(2,1)S(1)}, bf16[144,1536]{1,0:T(8,128)(2,1)S(1)}, u32[]{:S(2)}, u32[]{:S(2)}) collective-permute-start(bf16[144,1536]{1,0:T(8,128)(2,1)S(1)} %get-tuple-element.121), channel_id=1, source_target_pairs={{0,16},{4,20},{8,24},{12,28},{16,0},{20,4},{24,8},{28,12},{1,17},{... | collective-permute-start | bytes 1327112 | tf_op jit(solution)/shard_map/ppermute | solution.py:91
  624.0 24.3 %collective-permute-start.63 = (bf16[144,1536]{1,0:T(8,128)(2,1)S(1)}, bf16[144,1536]{1,0:T(8,128)(2,1)S(1)}, u32[]{:S(2)}, u32[]{:S(2)}) collective-permute-start(bf16[144,1536]{1,0:T(8,128)(2,1)S(1)} %get-tuple-element.120), channel_id=1, source_target_pairs={{0,8},{4,12},{8,0},{12,4},{16,24},{20,28},{24,16},{28,20},{1,9},{5... | collective-permute-start | bytes 1327112 | tf_op jit(solution)/shard_map/ppermute | solution.py:91
  647.1 17.8 %collective-permute-start.73 = (bf16[144,2304]{1,0:T(8,128)(2,1)S(1)}, bf16[144,2304]{1,0:T(8,128)(2,1)S(1)}, u32[]{:S(2)}, u32[]{:S(2)}) collective-permute-start(bf16[144,2304]{1,0:T(8,128)(2,1)S(1)} %get-tuple-element.106), channel_id=1, source_target_pairs={{0,8},{4,12},{8,0},{12,4},{16,24},{20,28},{24,16},{28,20},{1,9},{5... | collective-permute-start | bytes 1990664 | tf_op jit(solution)/shard_map/ppermute | solution.py:91
  648.3 18.4 %collective-permute-start.66 = (bf16[144,2304]{1,0:T(8,128)(2,1)S(1)}, bf16[144,2304]{1,0:T(8,128)(2,1)S(1)}, u32[]{:S(2)}, u32[]{:S(2)}) collective-permute-start(bf16[144,2304]{1,0:T(8,128)(2,1)S(1)} %get-tuple-element.113), channel_id=1, source_target_pairs={{0,16},{4,20},{8,24},{12,28},{16,0},{20,4},{24,8},{28,12},{1,17},{... | collective-permute-start | bytes 1990664 | tf_op jit(solution)/shard_map/ppermute | solution.py:91
  649.6 29.6 %collective-permute-start.68 = (bf16[144,2304]{1,0:T(8,128)(2,1)S(1)}, bf16[144,2304]{1,0:T(8,128)(2,1)S(1)}, u32[]{:S(2)}, u32[]{:S(2)}) collective-permute-start(bf16[144,2304]{1,0:T(8,128)(2,1)S(1)} %get-tuple-element.112), channel_id=1, source_target_pairs={{0,8},{4,12},{8,0},{12,4},{16,24},{20,28},{24,16},{28,20},{1,9},{5... | collective-permute-start | bytes 1990664 | tf_op jit(solution)/shard_map/ppermute | solution.py:91
  650.8 47.4 %collective-permute-start.62 = (bf16[288,1536]{1,0:T(8,128)(2,1)S(1)}, bf16[288,1536]{1,0:T(8,128)(2,1)S(1)}, u32[]{:S(2)}, u32[]{:S(2)}) collective-permute-start(bf16[288,1536]{1,0:T(8,128)(2,1)S(1)} %pad_maximum_fusion.13), channel_id=1, source_target_pairs={{0,8},{4,12},{8,0},{12,4},{16,24},{20,28},{24,16},{28,20},{1,9},{5... | collective-permute-start | bytes 2654216 | tf_op jit(solution)/shard_map/ppermute | solution.py:91
  652.1 47.2 %collective-permute-start.64 = (bf16[288,1536]{1,0:T(8,128)(2,1)S(1)}, bf16[288,1536]{1,0:T(8,128)(2,1)S(1)}, u32[]{:S(2)}, u32[]{:S(2)}) collective-permute-start(bf16[288,1536]{1,0:T(8,128)(2,1)S(1)} %pad_maximum_fusion.14), channel_id=1, source_target_pairs={{0,16},{4,20},{8,24},{12,28},{16,0},{20,4},{24,8},{28,12},{1,17},{... | collective-permute-start | bytes 2654216 | tf_op jit(solution)/shard_map/ppermute | solution.py:91
  665.0 61.6 %collective-permute-start.77 = (bf16[288,2304]{1,0:T(8,128)(2,1)S(1)}, bf16[288,2304]{1,0:T(8,128)(2,1)S(1)}, u32[]{:S(2)}, u32[]{:S(2)}) collective-permute-start(bf16[288,2304]{1,0:T(8,128)(2,1)S(1)} %pad_maximum_fusion.5), channel_id=1, source_target_pairs={{0,8},{4,12},{8,0},{12,4},{16,24},{20,28},{24,16},{28,20},{1,9},{5... | collective-permute-start | bytes 3981320 | tf_op jit(solution)/shard_map/ppermute | solution.py:91
  666.7 61.0 %collective-permute-start.79 = (bf16[288,2304]{1,0:T(8,128)(2,1)S(1)}, bf16[288,2304]{1,0:T(8,128)(2,1)S(1)}, u32[]{:S(2)}, u32[]{:S(2)}) collective-permute-start(bf16[288,2304]{1,0:T(8,128)(2,1)S(1)} %pad_maximum_fusion.6), channel_id=1, source_target_pairs={{0,16},{4,20},{8,24},{12,28},{16,0},{20,4},{24,8},{28,12},{1,17},{... | collective-permute-start | bytes 3981320 | tf_op jit(solution)/shard_map/ppermute | solution.py:91
  679.2 75.8 %collective-permute-start.72 = (bf16[288,2304]{1,0:T(8,128)(2,1)S(1)}, bf16[288,2304]{1,0:T(8,128)(2,1)S(1)}, u32[]{:S(2)}, u32[]{:S(2)}) collective-permute-start(bf16[288,2304]{1,0:T(8,128)(2,1)S(1)} %pad_maximum_fusion.3), channel_id=1, source_target_pairs={{0,8},{4,12},{8,0},{12,4},{16,24},{20,28},{24,16},{28,20},{1,9},{5... | collective-permute-start | bytes 3981320 | tf_op jit(solution)/shard_map/ppermute | solution.py:91
  698.2 56.9 %collective-permute-start.74 = (bf16[288,2304]{1,0:T(8,128)(2,1)S(1)}, bf16[288,2304]{1,0:T(8,128)(2,1)S(1)}, u32[]{:S(2)}, u32[]{:S(2)}) collective-permute-start(bf16[288,2304]{1,0:T(8,128)(2,1)S(1)} %pad_maximum_fusion.4), channel_id=1, source_target_pairs={{0,16},{4,20},{8,24},{12,28},{16,0},{20,4},{24,8},{28,12},{1,17},{... | collective-permute-start | bytes 3981320 | tf_op jit(solution)/shard_map/ppermute | solution.py:91
  699.3 80.3 %collective-permute-start.67 = (bf16[288,2304]{1,0:T(8,128)(2,1)S(1)}, bf16[288,2304]{1,0:T(8,128)(2,1)S(1)}, u32[]{:S(2)}, u32[]{:S(2)}) collective-permute-start(bf16[288,2304]{1,0:T(8,128)(2,1)S(1)} %pad_maximum_fusion.1), channel_id=1, source_target_pairs={{0,8},{4,12},{8,0},{12,4},{16,24},{20,28},{24,16},{28,20},{1,9},{5... | collective-permute-start | bytes 3981320 | tf_op jit(solution)/shard_map/ppermute | solution.py:91
  726.6 53.1 %collective-permute-start.69 = (bf16[288,2304]{1,0:T(8,128)(2,1)S(1)}, bf16[288,2304]{1,0:T(8,128)(2,1)S(1)}, u32[]{:S(2)}, u32[]{:S(2)}) collective-permute-start(bf16[288,2304]{1,0:T(8,128)(2,1)S(1)} %pad_maximum_fusion.2), channel_id=1, source_target_pairs={{0,16},{4,20},{8,24},{12,28},{16,0},{20,4},{24,8},{28,12},{1,17},{... | collective-permute-start | bytes 3981320 | tf_op jit(solution)/shard_map/ppermute | solution.py:91
  (113 other events, 1319.4 us)

commit v2 on v1

v2 whole, which is shorter than its diff:
```python
import math

import jax
import jax.numpy as jnp
from jax import lax
from jax.sharding import PartitionSpec as P

HD = 256


EPSILON = 1e-06
SOFT_CAP = 50.0
MASKED = -1e30


def rms_scale(values):
    return lax.rsqrt(jnp.mean(values * values, axis=-1, keepdims=True) + EPSILON)


def norm_back(inv_rms, normed, gradient):
    return inv_rms * (gradient - normed * jnp.mean(gradient * normed, axis=-1, keepdims=True))


def rotate(values, cos_table, sine_table):
    half_width = values.shape[-1] // 2
    leading = values[..., :half_width]
    trailing = values[..., half_width:]
    return jnp.concatenate(
        [leading * cos_table - trailing * sine_table, trailing * cos_table + leading * sine_table],
        axis=-1,
    )


def gelu_tanh(values):
    return jax.nn.gelu(values, approximate=True)


def product(first_operand, second_operand):
    return jnp.dot(first_operand, second_operand, preferred_element_type=jnp.float32)


def contract(first_operand, second_operand, first_dim, second_dim):
    return lax.dot_general(
        first_operand,
        second_operand,
        (((first_dim,), (second_dim,)), ((), ())),
        preferred_element_type=jnp.float32,
    )


def after(value, *earlier):
    return lax.optimization_barrier((value,) + earlier)[0]


def local(
    tokens,
    w_query,
    w_key,
    w_value,
    w_out,
    w_gate,
    w_up,
    w_down,
    norm_attn_in,
    norm_attn_out,
    norm_ffn_in,
    norm_ffn_out,
    cotangent,
):
    bf16, f32 = jnp.bfloat16, jnp.float32
    tok_rows, width = tokens.shape
    heads_local = w_query.shape[1] // HD
    key_heads = w_key.shape[1] // HD
    group_size = heads_local // key_heads
    query_width = heads_local * HD
    key_width = key_heads * HD
    ring = lax.axis_size("ctx")
    layers = lax.axis_size("tp")
    me = lax.axis_index("ctx")
    my_layer = lax.axis_index("tp")
    shard = width // ring
    own_rows = tok_rows // layers
    upper = shard // 32 * 16
    far_a, far_b = ring // 4, ring // 2
    near = [1 << bit for bit in range(far_a.bit_length() - 1)]
    order = [0, far_a, far_b, far_a | far_b]
    for bit in near:
        order = order + [block | bit for block in order]
    near_count = ring // 4
    near_width = 4 * shard
    spans = []
    for start in range(0, ring, 4):
        own, for_a, for_b, for_ab = order[start : start + 4]
        spans += [(own, 0), (own, 1), (for_b, 0), (for_a, 1)]
        spans += [(for_a, 0), (for_ab, 0), (for_ab, 1), (for_b, 1)]
    sizes = [shard - upper if half else upper for _, half in spans]
    starts = [sum(sizes[:index]) for index in range(len(sizes))]

    def swap(value, bit, axis="ctx"):
        count = lax.axis_size(axis)
        return lax.ppermute(value, axis, [(index, index ^ bit) for index in range(count)])

    def send_far(piece):
        return swap(piece, far_a), swap(piece, far_b)

    def relay(from_a, from_b):
        return swap(from_b[:upper], far_a), swap(from_a[upper:shard], far_b)

    def far_block(piece, direct, diagonal):
        (a_top, a_bottom), (b_top, b_bottom) = (
            (held[:upper], held[upper:shard]) for held in direct
        )
        return jnp.concatenate(
            [piece[:shard], b_top, a_bottom, a_top, diagonal[0], diagonal[1], b_bottom], axis=0
        )

    def spread_near(block):
        blocks = [block]
        for bit in near:
            blocks = blocks + [swap(held, bit) for held in blocks]
        return blocks

    def reduce_begin(activation, gradient):
        groups = by_near(activation)
        sent = [contract(part, gradient, 0, 0).astype(bf16) for part in groups[near_count // 2 :]]
        return groups[: max(near_count // 2, 1)], gradient, sent if near else []

    def reduce_near(state, *earlier):
        groups, gradient, sent = state
        if earlier:
            gradient = after(gradient, *earlier)
        bounds = (0, 2 * shard, 2 * shard + 2 * upper, 4 * shard)
        arrived = [swap(piece, near[-1]) for piece in sent]
        sums = []
        for index, group in enumerate(groups):
            parts = []
            for low, high in zip(bounds[:-1], bounds[1:]):
                part = contract(group[:, low:high], gradient, 0, 0)
                if arrived:
                    part = part + arrived[index][low:high].astype(f32)
                parts.append(part.astype(bf16))
            sums.append(parts)
        for bit in reversed(near[:-1]):
            half = len(sums) // 2
            sums = [
                [
                    (mine.astype(f32) + swap(piece, bit).astype(f32)).astype(bf16)
                    for mine, piece in zip(kept, sent)
                ]
                for kept, sent in zip(sums[:half], sums[half:])
            ]
        return sums[0]

    def reduce_far(sums, *earlier):
        kept, for_a, for_b = sums
        from_a, from_b = swap(for_a, far_a), swap(for_b, far_b)
        kept_then = after(kept, *earlier) if earlier else kept
        lower = shard - upper
        for_b = kept_then[shard : shard + upper].astype(f32) + from_a[upper:].astype(f32)
        for_a = kept_then[shard + upper :].astype(f32) + from_b[:lower].astype(f32)
        return kept, from_a, from_b, (for_b.astype(bf16), for_a.astype(bf16))

    def reduce_end(state, *columns):
        kept, from_a, from_b, last = state
        last = swap(last[0], far_b), swap(last[1], far_a)
        results = []
        for start, stop in columns:
            own, one, other, top, bottom = (
                piece[:, start:stop].astype(f32) for piece in (kept, from_a, from_b, *last)
            )
            results.append(
                jnp.concatenate(
                    [
                        own[:upper] + one[:upper] + top,
                        own[upper:shard] + other[shard - upper :] + bottom,
                    ],
                    axis=0,
                )
            )
        return results

    def layer_scatter(partial, *earlier):
        pieces = [
            partial[step * own_rows : (step + 1) * own_rows] for step in range(layers)
        ]
        if layers == 4:
            passed_on = swap(pieces[3], 1, "tp")
            arrived = [swap(pieces[1], 1, "tp")]
            pair_sum = (pieces[2].astype(f32) + passed_on.astype(f32)).astype(bf16)
            arrived.append(swap(pair_sum, 2, "tp"))
        else:
            arrived = [swap(pieces[step], step, "tp") for step in range(1, layers)]
        total = after(pieces[0], *earlier) if earlier else pieces[0]
        total = total.astype(f32)
        for piece in arrived:
            total = total + piece.astype(f32)
        return total

    def layer_gather(rows):
        if layers == 4:
            second = swap(rows, 2, "tp")
            first = swap(rows, 1, "tp")
            return [rows, first, second, swap(second, 1, "tp")]
        return [rows] + [swap(rows, step, "tp") for step in range(1, layers)]

    def rows_in(array):
        return jnp.concatenate(
            [
                lax.dynamic_slice_in_dim(array, (my_layer ^ step) * own_rows, own_rows, 0)
                for step in range(layers)
            ],
            axis=0,
        )

    def columns_in(array):
        return jnp.concatenate(
            [
                lax.dynamic_slice_in_dim(array, (me ^ block) * shard + half * upper, size, 1)
                for (block, half), size in zip(spans, sizes)
            ],
            axis=1,
        )

    def columns_out(array):
        def place(block, half):
            in_a, in_b = (block & far_a) // far_a, (block & far_b) // far_b
            values = [
                starts[spans.index((held, half))] for held in (0, far_a, far_b, far_a | far_b)
            ]
            found = (
                values[0]
                + (values[1] - values[0]) * in_a
                + (values[2] - values[0]) * in_b
                + (values[3] + values[0] - values[1] - values[2]) * in_a * in_b
            )
            for index, bit in enumerate(near):
                found = found + (near_width << index) * ((block & bit) // bit)
            return found

        return jnp.concatenate(
            [
                lax.dynamic_slice_in_dim(
                    array, place(me ^ block, half), shard - upper if half else upper, 1
                )
                for block in range(ring)
                for half in (0, 1)
            ],
            axis=1,
        )

    def rows_out(pieces):
        result = jnp.zeros((tok_rows,) + pieces[0].shape[1:], pieces[0].dtype)
        for step, piece in enumerate(pieces):
            result = lax.dynamic_update_slice_in_dim(
                result, piece, (my_layer ^ step) * own_rows, 0
            )
        return result

    def by_near(array):
        return [
            array[:, index * near_width : (index + 1) * near_width] for index in range(near_count)
        ]

    def times_rows(activation, blocks):
        total = None
        for part, block in zip(by_near(activation), blocks):
            term = product(part, block)
            total = term if total is None else total + term
        return total

    def times_rows_t(activation, blocks):
        return jnp.concatenate([contract(activation, block, 1, 1) for block in blocks], axis=1)

    qkv_width = query_width + 2 * key_width
    attn_width = qkv_width + query_width
    first_gain = norm_attn_in.astype(f32)[:, None]
    gain_rows = (
        jnp.zeros((16, attn_width), bf16)
        .at[:3, :shard]
        .set(jnp.stack([norm_attn_out, norm_ffn_in, norm_ffn_out]))
    )
    attn_rows_own = jnp.concatenate(
        [
            (jnp.concatenate([w_query, w_key, w_value], axis=1).astype(f32) * first_gain).astype(
                bf16
            ),
            w_out,
        ],
        axis=1,
    )
    gate_up = lax.all_gather(
        jnp.concatenate([w_gate, w_up], axis=1), "ctx", axis=0, tiled=True
    )
    down_w = lax.all_gather(w_down, "ctx", axis=0, tiled=True)
    attn_direct = send_far(jnp.concatenate([attn_rows_own, gain_rows], axis=0))
    attn_diagonal = relay(*attn_direct)
    attn_w = spread_near(far_block(attn_rows_own, attn_direct, attn_diagonal))
    qkv_w = [block[:, :qkv_width] for block in attn_w]
    out_w = [block[:, qkv_width:] for block in attn_w]
    own_gains = jnp.stack([norm_attn_out, norm_ffn_in, norm_ffn_out])
    gain_a, gain_b = (held[shard : shard + 3, :shard] for held in attn_direct)
    gains_far = jnp.concatenate(
        [
            own_gains,
            gain_b[:, :upper],
            gain_a[:, upper:],
            gain_a[:, :upper],
            swap(gain_b, far_a),
            gain_b[:, upper:],
        ],
        axis=1,
    )
    gain_two, gain_three, gain_four = jnp.split(
        columns_out(jnp.concatenate(spread_near(gains_far), axis=1)).astype(f32), 3
    )

    tok_float = rows_in(tokens).astype(f32)
    own_cot = lax.dynamic_slice_in_dim(cotangent, my_layer * own_rows, own_rows, 0).astype(f32)
    attn_input = columns_in((tok_float * rms_scale(tok_float)).astype(bf16))
    own_tok = tok_float[:own_rows]
    lin = times_rows(attn_input, qkv_w)
    row_place = jnp.concatenate(
        [
            (my_layer ^ step) * own_rows + jnp.arange(own_rows, dtype=jnp.int32)
            for step in range(layers)
        ]
    )
    query_pos = me * tok_rows + row_place
    half_width = HD // 2
    frequency = jnp.exp(
        jnp.arange(half_width, dtype=f32) * (-2.0 * math.log(10000.0) / HD)
    )
    angles = query_pos.astype(f32)[:, None] * frequency[None, :]
    cos_table, sine_table = jnp.cos(angles)[:, None, :], jnp.sin(angles)[:, None, :]
    queries = (
        rotate(lin[:, :query_width].reshape(tok_rows, heads_local, HD), cos_table, sine_table)
        * HD ** (-0.5)
    ).astype(bf16)
    queries_h = queries.reshape(tok_rows, key_heads, group_size, HD).transpose(1, 2, 0, 3)
    keys_rot = (
        rotate(
            lin[:, query_width : query_width + key_width].reshape(tok_rows, key_heads, HD),
            cos_table,
            sine_table,
        )
        .astype(bf16)
        .reshape(tok_rows, key_width)
    )
    values_b = lin[:, query_width + key_width :].astype(bf16)
    pair = jnp.concatenate([keys_rot, values_b], axis=1)
    pair_steps = [swap(pair, step) for step in (far_a, far_b, far_a | far_b)]
    pair_far = jnp.concatenate([pair] + pair_steps, axis=0)
    pairs = jnp.concatenate(spread_near(pair_far), axis=0)
    key_count = pairs.shape[0]
    key_h = pairs[:, :key_width].reshape(key_count, key_heads, HD)
    value_h = pairs[:, key_width:].reshape(key_count, key_heads, HD)
    key_pos = jnp.concatenate([(me ^ block) * tok_rows + row_place for block in order])
    visible = key_pos[None, :] <= query_pos[:, None]
    tanh_part = jnp.tanh(
        jnp.einsum("jgqd,cjd->jgqc", queries_h, key_h, preferred_element_type=f32) / SOFT_CAP
    )
    capped = jnp.where(visible, SOFT_CAP * tanh_part, MASKED)
    row_max = jnp.max(capped, axis=-1)
    weights = jnp.where(visible, jnp.exp(capped - row_max[..., None]), 0.0)
    row_sum = jnp.sum(weights, axis=-1)
    attn_float = (
        jnp.einsum("jgqc,cjd->jgqd", weights.astype(bf16), value_h, preferred_element_type=f32)
        / row_sum[..., None]
    )
    log_total = row_max + jnp.log(row_sum)
    attn_rows = attn_float.transpose(2, 0, 1, 3).reshape(tok_rows, query_width).astype(bf16)
    attn_part = times_rows_t(attn_rows, out_w).astype(bf16)
    attn_total = columns_out(layer_scatter(attn_part))
    inv_two = rms_scale(attn_total)
    normed_two = attn_total * inv_two
    hidden_res = own_tok + normed_two * gain_two
    inv_three = rms_scale(hidden_res)
    normed_three = hidden_res * inv_three
    ffn_input = jnp.concatenate(layer_gather((normed_three * gain_three).astype(bf16)), axis=0)

    ffn_width = w_gate.shape[1]
    both_lin = product(ffn_input, gate_up)
    gate_lin, up_lin = both_lin[:, :ffn_width], both_lin[:, ffn_width:]
    activated, gelu_pull = jax.vjp(gelu_tanh, gate_lin)
    hidden_b = (activated * up_lin).astype(bf16)
    ffn_total = layer_scatter(contract(hidden_b, down_w, 1, 1).astype(bf16))
    inv_four = rms_scale(ffn_total)
    normed_four = ffn_total * inv_four
    own_output = (hidden_res + normed_four * gain_four).astype(bf16)
    grad_gain_four = jnp.sum(own_cot * normed_four, axis=0)
    grad_ffn = jnp.concatenate(
        layer_gather(norm_back(inv_four, normed_four, own_cot * gain_four).astype(bf16)), axis=0
    )
    down_sum = lax.psum_scatter(
        contract(grad_ffn, hidden_b, 0, 0).astype(bf16), "ctx", scatter_dimension=0, tiled=True
    )
    grad_hidden = product(grad_ffn, down_w)
    grad_gate = gelu_pull(grad_hidden * up_lin)[0].astype(bf16)
    grad_up = (grad_hidden * activated).astype(bf16)
    grad_both = jnp.concatenate([grad_gate, grad_up], axis=1)
    grad_in_part = contract(grad_both, gate_up, 1, 1).astype(bf16)
    grad_ffn_in = layer_scatter(grad_in_part)
    both_sum = lax.psum_scatter(
        contract(ffn_input, after(grad_both, grad_in_part), 0, 0).astype(bf16),
        "ctx",
        scatter_dimension=0,
        tiled=True,
    )
    grad_gain_three = jnp.sum(grad_ffn_in * normed_three, axis=0)
    grad_res = own_cot + norm_back(inv_three, normed_three, grad_ffn_in * gain_three)
    grad_gain_two = jnp.sum(grad_res * normed_two, axis=0)

    grad_attn = jnp.concatenate(
        layer_gather(columns_in(norm_back(inv_two, normed_two, grad_res * gain_two).astype(bf16))),
        axis=0,
    )
    grad_rows = times_rows(grad_attn, out_w).astype(bf16)
    grad_heads = grad_rows.reshape(tok_rows, key_heads, group_size, HD).transpose(1, 2, 0, 3)
    row_delta = jnp.sum(grad_heads.astype(f32) * attn_float, axis=-1)
    probs = jnp.where(visible, jnp.exp(SOFT_CAP * tanh_part - log_total[..., None]), 0.0)
    value_grad = jnp.einsum(
        "jgqc,jgqd->cjd", probs.astype(bf16), grad_heads, preferred_element_type=f32
    )
    weight_grad = jnp.einsum("jgqd,cjd->jgqc", grad_heads, value_h, preferred_element_type=f32)
    score_grad = (
        probs * (weight_grad - row_delta[..., None]) * (1.0 - tanh_part * tanh_part)
    ).astype(bf16)
    grad_q = jnp.einsum("jgqc,cjd->jgqd", score_grad, key_h, preferred_element_type=f32)
    key_grad = jnp.einsum("jgqc,jgqd->cjd", score_grad, queries_h, preferred_element_type=f32)
    pair_grad = jnp.concatenate(
        [key_grad.reshape(key_count, key_width), value_grad.reshape(key_count, key_width)], axis=1
    ).astype(bf16)
    pair_part = [
        pair_grad[index * 4 * tok_rows : (index + 1) * 4 * tok_rows] for index in range(near_count)
    ]
    for bit in reversed(near):
        half = len(pair_part) // 2
        pair_part = [
            (kept.astype(f32) + swap(sent, bit).astype(f32)).astype(bf16)
            for kept, sent in zip(pair_part[:half], pair_part[half:])
        ]
    pair_part = pair_part[0]
    output = rows_out(layer_gather(after(own_output, pair_part)))
    out_sums = reduce_near(reduce_begin(after(grad_attn, pair_part), attn_rows))
    pair_own = pair_part[:tok_rows].astype(f32)
    for index, step in ((1, far_a), (2, far_b), (3, far_a | far_b)):
        pair_own = pair_own + swap(
            pair_part[index * tok_rows : (index + 1) * tok_rows], step
        ).astype(f32)
    pair_own = after(pair_own, *out_sums)
    grad_query_lin = (
        rotate(
            grad_q.transpose(2, 0, 1, 3).reshape(tok_rows, heads_local, HD), cos_table, -sine_table
        )
        * HD ** (-0.5)
    ).reshape(tok_rows, query_width)
    grad_key_lin = rotate(
        pair_own[:, :key_width].reshape(tok_rows, key_heads, HD), cos_table, -sine_table
    ).reshape(tok_rows, key_width)
    grad_lin = jnp.concatenate(
        [grad_query_lin, grad_key_lin, pair_own[:, key_width:]], axis=1
    ).astype(bf16)
    grad_in_part = times_rows_t(grad_lin, qkv_w).astype(bf16)
    lin_sums = reduce_near(reduce_begin(after(attn_input, grad_in_part), grad_lin))
    grad_attn_in = columns_out(layer_scatter(grad_in_part, *lin_sums, *out_sums))
    lin_far = reduce_far(lin_sums)
    out_far = reduce_far(out_sums)
    own_inv = rms_scale(own_tok)
    own_normed = own_tok * own_inv
    grad_gain_one = jnp.sum(grad_attn_in * own_normed, axis=0)
    token_pieces = layer_gather(
        (grad_res + norm_back(own_inv, own_normed, grad_attn_in)).astype(bf16)
    )
    grad_tokens = rows_out(token_pieces).astype(f32)

    grad_w_query, grad_w_key, grad_w_value = reduce_end(
        lin_far,
        (0, query_width),
        (query_width, query_width + key_width),
        (query_width + key_width, qkv_width),
    )
    (grad_w_out,) = reduce_end(out_far, (0, query_width))
    gain_grads = columns_in(
        jnp.stack([grad_gain_one, grad_gain_two, grad_gain_three, grad_gain_four])
    )
    gain_sum = after(gain_grads, token_pieces[2])
    for bit in [1 << index for index in range(layers.bit_length() - 1)]:
        gain_sum = gain_sum + swap(gain_sum, bit, "tp")
    for bit in reversed(near):
        half = gain_sum.shape[1] // 2
        gain_sum = gain_sum[:, :half] + swap(gain_sum[:, half:], bit)
    lower = shard - upper
    from_a = swap(gain_sum[:, 2 * shard : 2 * shard + 2 * upper], far_a)
    from_b = swap(gain_sum[:, 2 * shard + 2 * upper :], far_b)
    last_b = swap(gain_sum[:, shard : shard + upper] + from_a[:, upper:], far_b)
    last_a = swap(gain_sum[:, shard + upper : 2 * shard] + from_b[:, :lower], far_a)
    gain_sum = jnp.concatenate(
        [
            gain_sum[:, :upper] + from_a[:, :upper] + last_b,
            gain_sum[:, upper:shard] + from_b[:, lower:] + last_a,
        ],
        axis=1,
    )
    return (
        output,
        grad_tokens,
        grad_w_query * first_gain,
        grad_w_key * first_gain,
        grad_w_value * first_gain,
        grad_w_out,
        both_sum[:, :ffn_width].astype(f32),
        both_sum[:, ffn_width:].astype(f32),
        down_sum.astype(f32),
        gain_sum[0] / first_gain[:, 0],
        gain_sum[1],
        gain_sum[2],
        gain_sum[3],
    )


def solution(mesh):
    return jax.shard_map(
        local,
        mesh=mesh,
        in_specs=(
            P("ctx", None),
            P("ctx", "tp"),
            P("ctx", "tp"),
            P("ctx", "tp"),
            P("ctx", "tp"),
            P("ctx", "tp"),
            P("ctx", "tp"),
            P("ctx", "tp"),
            P("ctx"),
            P("ctx"),
            P("ctx"),
            P("ctx"),
            P("ctx", None),
        ),
        out_specs=(
            P("ctx", None),
            P("ctx", None),
            P("ctx", "tp"),
            P("ctx", "tp"),
            P("ctx", "tp"),
            P("ctx", "tp"),
            P("ctx", "tp"),
            P("ctx", "tp"),
            P("ctx", "tp"),
            P("ctx"),
            P("ctx"),
            P("ctx"),
            P("ctx"),
        ),
        check_vma=False,
    )
```

time: 798 us -> 574 us (0.72)
  the two profiles are of different devices: /device:TPU:8 before, /device:TPU:0 now
where the time goes in v2:
time: 574 us; the launch traced here: 568 us
  waiting for transfers between devices  256 us (45%)
  matrix products  110 us (19%)
  starting transfers between devices  68.9 us (12%)
  local copies, waits for them, and re-layouts  63.6 us (11%)
  other arithmetic  53.8 us (9%)
  between operations  15.9 us (3%)
    ppermute x59, waiting for transfers between devices, swap(): lax.ppermute(value, axis, [(index, index ^ bit) for index in range(count)])  242 us
    ppermute x59, starting transfers between devices, swap(): lax.ppermute(value, axis, [(index, index ^ bit) for index in range(count)])  68.5 us
    dot_general x16, matrix products, contract(): lax.dot_general(first_operand, second_operand, (((first_dim,), (second_di...  63.1 us
    dot_general x6, matrix products, product(): jnp.dot(first_operand, second_operand, preferred_element_type=jnp.float32)  30.1 us
    unnamed x226, local copies, waits for them, and re-layouts  19.6 us
    all_gather x1, waiting for transfers between devices, local(): down_w = lax.all_gather(w_down, 'ctx', axis=0, tiled=True)  14.7 us
  transfers between devices with their start and end apart: 63, of which 39 were waited for; matrix products, arithmetic and copies ran while one was open for 33% of the time, Pallas kernels for 0%

profile of v2, /device:TPU:0, one launch (start us, length us, event | category | flops | bytes accessed | tf_op | source)
XLA Modules:
  0.0 568.3 jit_solution(11424335916729444669)
XLA Ops:
  7.2 3.4 pad_maximum_fusion
  12.0 3.0 collective-permute-start
  17.6 29.2 %collective-permute-done = bf16[304,1536]{1,0:T(8,128)(2,1)S(1)} collective-permute-done((bf16[304,1536]{1,0:T(8,128)(2,1)S(1)}, bf16[304,1536]{1,0:T(8,128)(2,1)S(1)}, u32[]{:S(2)}, u32[]{:S(2)}) %collective-permute-start) | collective-permute-done | bytes 933920 | tf_op jit(solution)/shard_map/ppermute | solution.py:101
  48.9 2.5 collective-permute-done.1
  55.2 13.9 %collective-permute-done.2 = bf16[144,1536]{1,0:T(8,128)(2,1)S(1)} collective-permute-done((bf16[144,1536]{1,0:T(8,128)(2,1)S(1)}, bf16[144,1536]{1,0:T(8,128)(2,1)S(1)}, u32[]{:S(2)}, u32[]{:S(2)}) %collective-permute-start.2) | collective-permute-done | bytes 442400 | tf_op jit(solution)/shard_map/ppermute | solution.py:101
  69.8 3.8 collective-permute-done.3
  83.2 3.2 fusion.24
  86.6 2.5 fusion.30
  95.1 10.2 %collective-permute-done.5 = bf16[256,512]{1,0:T(8,128)(2,1)S(1)} collective-permute-done((bf16[256,512]{1,0:T(8,128)(2,1)S(1)}, bf16[256,512]{1,0:T(8,128)(2,1)S(1)}, u32[]{:S(2)}, u32[]{:S(2)}) %collective-permute-start.5) | collective-permute-done | bytes 262176 | tf_op jit(solution)/shard_map/ppermute | solution.py:101
  105.3 3.0 collective-permute-done.6
  108.3 8.1 %collective-permute-done.7 = bf16[256,512]{1,0:T(8,128)(2,1)S(1)} collective-permute-done((bf16[256,512]{1,0:T(8,128)(2,1)S(1)}, bf16[256,512]{1,0:T(8,128)(2,1)S(1)}, u32[]{:S(2)}, u32[]{:S(2)}) %collective-permute-start.7) | collective-permute-done | bytes 262176 | tf_op jit(solution)/shard_map/ppermute | solution.py:101
  121.3 2.3 constant_dynamic-update-slice_fusion.5
  123.6 2.8 select_reduce_fusion
  129.6 2.4 fusion.159
  142.4 4.5 collective-permute-done.10
  148.6 2.5 collective-permute-start.11
  161.4 2.8 collective-permute-done.11
  170.0 3.7 collective-permute-start.14
  173.7 10.1 %collective-permute-done.15 = bf16[64,2304]{1,0:T(8,128)(2,1)S(1)} collective-permute-done((bf16[64,2304]{1,0:T(8,128)(2,1)S(1)}, bf16[64,2304]{1,0:T(8,128)(2,1)S(1)}, u32[]{:S(2)}, u32[]{:S(2)}) %collective-permute-start.15) | collective-permute-done | bytes 294944 | tf_op jit(solution)/shard_map/ppermute | solution.py:101
  185.3 5.4 collective-permute-done.16
  190.7 10.5 %fusion.81 = f32[256,4608]{1,0:T(8,128)S(1)} fusion(bf16[2304,4608]{1,0:T(8,128)(2,1)} %all-gather.3.cloned.1.call-done, bf16[64,2304]{1,0:T(8,128)(2,1)} %collective-permute-done.16, bf16[64,2304]{1,0:T(8,128)(2,1)} %copy-done.66, bf16[64,2304]{1,0:T(8,128)(2,1)} %copy-done.68, bf16[64,2304]{1,0:T(8,128)(2,1)} %copy-done.30), kind=kOutput, calls=%fused_computation.192 | convolution fusion | flops 5440536576 | bytes 27131904 | tf_op jit(solution)/shard_map/dot_general | solution.py:39
  201.2 2.1 copy-done.7
  205.2 14.7 %all-gather.5.cloned.1.call-done = bf16[2304,2304]{1,0:T(8,128)(2,1)} async-done(((bf16[288,2304]{1,0:T(8,128)(2,1)}), bf16[2304,2304]{1,0:T(8,128)(2,1)}) %all-gather.5.cloned.1.call-update) | async-done | bytes 10616848 | tf_op jit(solution)/shard_map/all_gather | solution.py:294
  219.8 7.3 %convolution_convert_fusion.3 = bf16[256,2304]{1,0:T(8,128)(2,1)S(1)} fusion(bf16[256,2304]{1,0:T(8,128)(2,1)} %multiply_convert_fusion.2, bf16[2304,2304]{1,0:T(8,128)(2,1)} %all-gather.5.cloned.1.call-done), kind=kOutput, calls=%fused_computation.8 | convolution fusion | flops 2718498816 | bytes 12976128 | tf_op jit(solution)/shard_map/dot_general | solution.py:43
  229.3 7.8 %collective-permute-done.18 = bf16[64,2304]{1,0:T(8,128)(2,1)S(1)} collective-permute-done((bf16[64,2304]{1,0:T(8,128)(2,1)S(1)}, bf16[64,2304]{1,0:T(8,128)(2,1)S(1)}, u32[]{:S(2)}, u32[]{:S(2)}) %collective-permute-start.18) | collective-permute-done | bytes 294944 | tf_op jit(solution)/shard_map/ppermute | solution.py:101
  237.2 2.5 collective-permute-start.19
  239.7 8.2 %collective-permute-done.17 = bf16[64,2304]{1,0:T(8,128)(2,1)S(1)} collective-permute-done((bf16[64,2304]{1,0:T(8,128)(2,1)S(1)}, bf16[64,2304]{1,0:T(8,128)(2,1)S(1)}, u32[]{:S(2)}, u32[]{:S(2)}) %collective-permute-start.17) | collective-permute-done | bytes 294944 | tf_op jit(solution)/shard_map/ppermute | solution.py:101
  247.9 4.3 collective-permute-done.19
  254.4 3.9 collective-permute-start.20
  258.3 8.4 %collective-permute-done.21 = bf16[64,2304]{1,0:T(8,128)(2,1)S(1)} collective-permute-done((bf16[64,2304]{1,0:T(8,128)(2,1)S(1)}, bf16[64,2304]{1,0:T(8,128)(2,1)S(1)}, u32[]{:S(2)}, u32[]{:S(2)}) %collective-permute-start.21) | collective-permute-done | bytes 294944 | tf_op jit(solution)/shard_map/ppermute | solution.py:101
  267.4 6.9 %collective-permute-done.22 = bf16[64,2304]{1,0:T(8,128)(2,1)S(1)} collective-permute-done((bf16[64,2304]{1,0:T(8,128)(2,1)S(1)}, bf16[64,2304]{1,0:T(8,128)(2,1)S(1)}, u32[]{:S(2)}, u32[]{:S(2)}) %collective-permute-start.22) | collective-permute-done | bytes 294944 | tf_op jit(solution)/shard_map/ppermute | solution.py:101
  275.0 5.5 convolution_convert_fusion.1
  280.8 9.8 %fusion.14 = (bf16[256,2304]{1,0:T(8,128)(2,1)S(1)}, bf16[256,2304]{1,0:T(8,128)(2,1)S(1)}) fusion(f32[256,4608]{1,0:T(8,128)} %copy-done.7, bf16[2304,2304]{1,0:T(8,128)(2,1)} %all-gather.5.cloned.1.call-done, bf16[64,2304]{1,0:T(8,128)(2,1)} %copy-done.109, bf16[64,2304]{1,0:T(8,128)(2,1)} %copy-done.107, bf16[64,2304]{1,0:T(8,128)(2,1)} %copy-done.108, ...), kind=kOutput, calls=%fused_computation.34 | convolution fusion | flops 2736783360 | bytes 18874368 | tf_op jit(solution)/shard_map/dot_general | solution.py:39
  292.3 14.9 %convolution_convert_fusion.2 = bf16[256,2304]{1,0:T(8,128)(2,1)} fusion(bf16[2304,4608]{1,0:T(8,128)(2,1)} %all-gather.3.cloned.1.call-done, bf16[256,2304]{1,0:T(8,128)(2,1)} %copy-done.50, bf16[256,2304]{1,0:T(8,128)(2,1)} %copy-done.49), kind=kOutput, calls=%fused_computation.7 | convolution fusion | flops 5441126400 | bytes 24772608 | tf_op jit(solution)/shard_map/dot_general | solution.py:43
  307.2 11.5 %convolution_convert_fusion = bf16[2304,4608]{1,0:T(8,128)(2,1)} fusion(bf16[256,4608]{1,0:T(8,128)(2,1)S(1)} %pad_maximum_fusion.1, bf16[64,2304]{1,0:T(8,128)(2,1)} %collective-permute-done.16, bf16[64,2304]{1,0:T(8,128)(2,1)S(1)} %copy-done.67, bf16[64,2304]{1,0:T(8,128)(2,1)} %copy-done.68, bf16[64,2304]{1,0:T(8,128)(2,1)S(1)} %copy-done.31), kind=kOutput, calls=%fused_computation | convolution fusion | flops 5451153408 | bytes 24772608 | tf_op jit(solution)/shard_map/dot_general | solution.py:43
  321.9 7.9 %collective-permute-done.24 = bf16[64,2304]{1,0:T(8,128)(2,1)S(1)} collective-permute-done((bf16[64,2304]{1,0:T(8,128)(2,1)S(1)}, bf16[64,2304]{1,0:T(8,128)(2,1)S(1)}, u32[]{:S(2)}, u32[]{:S(2)}) %collective-permute-start.24) | collective-permute-done | bytes 294944 | tf_op jit(solution)/shard_map/ppermute | solution.py:101
  330.9 3.1 collective-permute-start.25
  334.1 5.5 collective-permute-done.23
  339.6 5.5 collective-permute-done.25
  346.9 2.1 multiply_reduce_fusion.2
  350.5 3.8 collective-permute-start.26
  354.3 7.5 %collective-permute-done.27 = bf16[64,2304]{1,0:T(8,128)(2,1)S(1)} collective-permute-done((bf16[64,2304]{1,0:T(8,128)(2,1)S(1)}, bf16[64,2304]{1,0:T(8,128)(2,1)S(1)}, u32[]{:S(2)}, u32[]{:S(2)}) %collective-permute-start.27) | collective-permute-done | bytes 294944 | tf_op jit(solution)/shard_map/ppermute | solution.py:101
  362.7 5.9 %collective-permute-done.28 = bf16[64,2304]{1,0:T(8,128)(2,1)S(1)} collective-permute-done((bf16[64,2304]{1,0:T(8,128)(2,1)S(1)}, bf16[64,2304]{1,0:T(8,128)(2,1)S(1)}, u32[]{:S(2)}, u32[]{:S(2)}) %collective-permute-start.28) | collective-permute-done | bytes 294944 | tf_op jit(solution)/shard_map/ppermute | solution.py:101
  368.6 2.2 fusion.35
  374.2 5.3 multiply_convert_fusion
  385.5 4.4 concatenate.181
  393.8 3.3 convolution_bitcast_fusion.2
  407.3 4.0 collective-permute-start.31
  414.7 16.7 %collective-permute-done.34 = bf16[256,512]{1,0:T(8,128)(2,1)S(1)} collective-permute-done((bf16[256,512]{1,0:T(8,128)(2,1)}, bf16[256,512]{1,0:T(8,128)(2,1)S(1)}, u32[]{:S(2)}, u32[]{:S(2)}) %collective-permute-start.34) | collective-permute-done | bytes 262176 | tf_op jit(solution)/shard_map/ppermute | solution.py:101
  432.9 2.3 add_convert_fusion.9
  437.3 2.6 fusion.160
  444.6 2.6 convolution_convert_fusion.7
  447.2 2.8 convolution_convert_fusion.6
  456.3 3.6 collective-permute-done.39
  460.1 2.1 collective-permute-start.40
  462.2 7.2 %collective-permute-done.50 = bf16[288,512]{1,0:T(8,128)(2,1)S(1)} collective-permute-done((bf16[288,512]{1,0:T(8,128)(2,1)S(1)}, bf16[288,512]{1,0:T(8,128)(2,1)S(1)}, u32[]{:S(2)}, u32[]{:S(2)}) %collective-permute-start.50) | collective-permute-done | bytes 294944 | tf_op jit(solution)/shard_map/ppermute | solution.py:101
  484.0 2.2 collective-permute-start.42
  486.6 12.1 %collective-permute-done.42 = bf16[64,2304]{1,0:T(8,128)(2,1)S(1)} collective-permute-done((bf16[64,2304]{1,0:T(8,128)(2,1)}, bf16[64,2304]{1,0:T(8,128)(2,1)S(1)}, u32[]{:S(2)}, u32[]{:S(2)}) %collective-permute-start.42) | collective-permute-done | bytes 294944 | tf_op jit(solution)/shard_map/ppermute | solution.py:101
  500.4 2.3 collective-permute-done.52
  511.4 22.8 %collective-permute-done.55 = f32[4,288]{1,0:T(4,128)S(1)} collective-permute-done((f32[4,288]{1,0:T(4,128)S(1)}, f32[4,288]{1,0:T(4,128)S(1)}, u32[]{:S(2)}, u32[]{:S(2)}) %collective-permute-start.55) | collective-permute-done | bytes 4640 | tf_op jit(solution)/shard_map/ppermute | solution.py:101
  539.8 3.2 collective-permute-done.58
  547.6 3.8 collective-permute-done.45
  554.1 3.0 convert_element_type.438
  557.1 4.5 slice_convert_fusion
  (469 shorter events, 160.5 us)
Async XLA Ops:
  7.2 183.5 %all-gather.3.cloned.1.call-start = ((), (), s32[]{:S(2)}) async-start(), calls=%async_computation.2 | async-start | bytes 23887872 | tf_op jit(solution)/shard_map/all_gather | solution.py:291
  10.7 209.1 %all-gather.5.cloned.1.call-start = ((), (), s32[]{:S(2)}) async-start(), calls=%async_computation.3 | async-start | bytes 11943936 | tf_op jit(solution)/shard_map/all_gather | solution.py:294
  12.0 34.7 %collective-permute-start = (bf16[304,1536]{1,0:T(8,128)(2,1)S(1)}, bf16[304,1536]{1,0:T(8,128)(2,1)S(1)}, u32[]{:S(2)}, u32[]{:S(2)}) collective-permute-start(bf16[304,1536]{1,0:T(8,128)(2,1)S(1)} %fusion.46), channel_id=1, source_target_pairs={{0,16},{4,20},{8,24},{12,28},{16,0},{20,4},{24,8},{28,12},{1,17},{... | collective-permute-start | bytes 2801672 | tf_op jit(solution)/shard_map/ppermute | solution.py:101
  15.0 36.3 %collective-permute-start.1 = (bf16[304,1536]{1,0:T(8,128)(2,1)S(1)}, bf16[304,1536]{1,0:T(8,128)(2,1)}, u32[]{:S(2)}, u32[]{:S(2)}) collective-permute-start(bf16[304,1536]{1,0:T(8,128)(2,1)S(1)} %fusion.46), channel_id=1, source_target_pairs={{0,8},{4,12},{8,0},{12,4},{16,24},{20,28},{24,16},{28,20},{1,9},{5... | collective-permute-start | bytes 2801672 | tf_op jit(solution)/shard_map/ppermute | solution.py:101
  16.6 537.5 %reduce-scatter.5.cloned.1.call-start = ((), (), s32[]{:S(2)}) async-start(), calls=%async_computation.5 | async-start | bytes 11943936 | tf_op jit(solution)/shard_map/reduce_scatter | solution.py:394
  47.6 21.4 %collective-permute-start.2 = (bf16[144,1536]{1,0:T(8,128)(2,1)S(1)}, bf16[144,1536]{1,0:T(8,128)(2,1)S(1)}, u32[]{:S(2)}, u32[]{:S(2)}) collective-permute-start(bf16[144,1536]{1,0:T(8,128)(2,1)S(1)} %get-tuple-element.111), channel_id=1, source_target_pairs={{0,8},{4,12},{8,0},{12,4},{16,24},{20,28},{24,16},{28,20},{1,9},{5... | collective-permute-start | bytes 1327112 | tf_op jit(solution)/shard_map/ppermute | solution.py:101
  53.3 20.3 %collective-permute-start.3 = (bf16[144,1536]{1,0:T(8,128)(2,1)S(1)}, bf16[144,1536]{1,0:T(8,128)(2,1)S(1)}, u32[]{:S(2)}, u32[]{:S(2)}) collective-permute-start(bf16[144,1536]{1,0:T(8,128)(2,1)S(1)} %get-tuple-element.109), channel_id=1, source_target_pairs={{0,16},{4,20},{8,24},{12,28},{16,0},{20,4},{24,8},{28,12},{1,17},{... | collective-permute-start | bytes 1327112 | tf_op jit(solution)/shard_map/ppermute | solution.py:101
  75.3 7.9 %collective-permute-start.4 = (bf16[1152,1536]{1,0:T(8,128)(2,1)}, bf16[1152,1536]{1,0:T(8,128)(2,1)}, u32[]{:S(2)}, u32[]{:S(2)}) collective-permute-start(bf16[1152,1536]{1,0:T(8,128)(2,1)} %slice_dynamic-update-slice_fusion), channel_id=1, source_target_pairs={{0,4},{4,0},{8,12},{12,8},{16,20},{20,16},{24,28},{28,24},{1,5},{5... | collective-permute-start | bytes 10616840 | tf_op jit(solution)/shard_map/ppermute | solution.py:101
  76.7 39.9 %copy-start.85 = (f32[256]{0:T(256)}, f32[256]{0:T(256)S(1)}, u32[]{:S(2)}) copy-start(f32[256]{0:T(256)S(1)} %convert_element_type.342) | copy-start | bytes 3076
  90.5 14.8 %collective-permute-start.5 = (bf16[256,512]{1,0:T(8,128)(2,1)S(1)}, bf16[256,512]{1,0:T(8,128)(2,1)S(1)}, u32[]{:S(2)}, u32[]{:S(2)}) collective-permute-start(bf16[256,512]{1,0:T(8,128)(2,1)S(1)} %get-tuple-element.183), channel_id=1, source_target_pairs={{0,8},{4,12},{8,0},{12,4},{16,24},{20,28},{24,16},{28,20},{1,9},{5... | collective-permute-start | bytes 786440 | tf_op jit(solution)/shard_map/ppermute | solution.py:101
  92.2 16.1 %collective-permute-start.6 = (bf16[256,512]{1,0:T(8,128)(2,1)S(1)}, bf16[256,512]{1,0:T(8,128)(2,1)S(1)}, u32[]{:S(2)}, u32[]{:S(2)}) collective-permute-start(bf16[256,512]{1,0:T(8,128)(2,1)S(1)} %get-tuple-element.183), channel_id=1, source_target_pairs={{0,16},{4,20},{8,24},{12,28},{16,0},{20,4},{24,8},{28,12},{1,17},{... | collective-permute-start | bytes 786440 | tf_op jit(solution)/shard_map/ppermute | solution.py:101
  93.0 23.4 %collective-permute-start.7 = (bf16[256,512]{1,0:T(8,128)(2,1)S(1)}, bf16[256,512]{1,0:T(8,128)(2,1)S(1)}, u32[]{:S(2)}, u32[]{:S(2)}) collective-permute-start(bf16[256,512]{1,0:T(8,128)(2,1)S(1)} %get-tuple-element.183), channel_id=1, source_target_pairs={{0,24},{4,28},{8,16},{12,20},{16,8},{20,12},{24,0},{28,4},{1,25},{... | collective-permute-start | bytes 786440 | tf_op jit(solution)/shard_map/ppermute | solution.py:101
  116.5 4.8 collective-permute-start.8
  136.7 10.2 %collective-permute-start.10 = (bf16[64,2304]{1,0:T(8,128)(2,1)}, bf16[64,2304]{1,0:T(8,128)(2,1)}, u32[]{:S(2)}, u32[]{:S(2)}) collective-permute-start(bf16[64,2304]{1,0:T(8,128)(2,1)} %get-tuple-element.85), channel_id=1, source_target_pairs={{0,1},{1,0},{2,3},{3,2},{4,5},{5,4},{6,7},{7,6},{8,9},{9,8},{10,11... | collective-permute-start | bytes 884744 | tf_op jit(solution)/shard_map/ppermute | solution.py:101
  139.4 13.2 %collective-permute-start.12 = (bf16[3,288]{1,0:T(4,128)(2,1)S(1)}, bf16[3,288]{1,0:T(4,128)(2,1)}, u32[]{:S(2)}, u32[]{:S(2)}) collective-permute-start(bf16[3,288]{1,0:T(4,128)(2,1)S(1)} %slice.592), channel_id=1, source_target_pairs={{0,8},{4,12},{8,0},{12,4},{16,24},{20,28},{24,16},{28,20},{1,9},{5... | collective-permute-start | bytes 5192 | tf_op jit(solution)/shard_map/ppermute | solution.py:101
  141.7 19.6 %collective-permute-start.9 = (bf16[64,2304]{1,0:T(8,128)(2,1)}, bf16[64,2304]{1,0:T(8,128)(2,1)}, u32[]{:S(2)}, u32[]{:S(2)}) collective-permute-start(bf16[64,2304]{1,0:T(8,128)(2,1)} %get-tuple-element.84), channel_id=1, source_target_pairs={{0,1},{1,0},{2,3},{3,2},{4,5},{5,4},{6,7},{7,6},{8,9},{9,8},{10,11... | collective-permute-start | bytes 884744 | tf_op jit(solution)/shard_map/ppermute | solution.py:101
  148.6 15.5 %collective-permute-start.11 = (bf16[64,2304]{1,0:T(8,128)(2,1)}, bf16[64,2304]{1,0:T(8,128)(2,1)}, u32[]{:S(2)}, u32[]{:S(2)}) collective-permute-start(bf16[64,2304]{1,0:T(8,128)(2,1)} %add_convert_fusion.14), channel_id=1, source_target_pairs={{0,2},{1,3},{2,0},{3,1},{4,6},{5,7},{6,4},{7,5},{8,10},{9,11},{10,... | collective-permute-start | bytes 884744 | tf_op jit(solution)/shard_map/ppermute | solution.py:101
  153.9 1.5 collective-permute-start.13
  169.3 14.5 %collective-permute-start.15 = (bf16[64,2304]{1,0:T(8,128)(2,1)S(1)}, bf16[64,2304]{1,0:T(8,128)(2,1)S(1)}, u32[]{:S(2)}, u32[]{:S(2)}) collective-permute-start(bf16[64,2304]{1,0:T(8,128)(2,1)S(1)} %multiply_convert_fusion.6), channel_id=1, source_target_pairs={{0,2},{1,3},{2,0},{3,1},{4,6},{5,7},{6,4},{7,5},{8,10},{9,11},{10,... | collective-permute-start | bytes 884744 | tf_op jit(solution)/shard_map/ppermute | solution.py:101
  170.0 13.9 %collective-permute-start.14 = (bf16[64,2304]{1,0:T(8,128)(2,1)S(1)}, bf16[64,2304]{1,0:T(8,128)(2,1)S(1)}, u32[]{:S(2)}, u32[]{:S(2)}) collective-permute-start(bf16[64,2304]{1,0:T(8,128)(2,1)S(1)} %multiply_convert_fusion.6), channel_id=1, source_target_pairs={{0,1},{1,0},{2,3},{3,2},{4,5},{5,4},{6,7},{7,6},{8,9},{9,8},{10,11... | collective-permute-start | bytes 884744 | tf_op jit(solution)/shard_map/ppermute | solution.py:101
  183.8 6.8 %collective-permute-start.16 = (bf16[64,2304]{1,0:T(8,128)(2,1)S(1)}, bf16[64,2304]{1,0:T(8,128)(2,1)}, u32[]{:S(2)}, u32[]{:S(2)}) collective-permute-start(bf16[64,2304]{1,0:T(8,128)(2,1)S(1)} %collective-permute-done.15), channel_id=1, source_target_pairs={{0,1},{1,0},{2,3},{3,2},{4,5},{5,4},{6,7},{7,6},{8,9},{9,8},{10,11... | collective-permute-start | bytes 884744 | tf_op jit(solution)/shard_map/ppermute | solution.py:101
  227.2 9.9 %collective-permute-start.18 = (bf16[64,2304]{1,0:T(8,128)(2,1)S(1)}, bf16[64,2304]{1,0:T(8,128)(2,1)S(1)}, u32[]{:S(2)}, u32[]{:S(2)}) collective-permute-start(bf16[64,2304]{1,0:T(8,128)(2,1)S(1)} %get-tuple-element.83), channel_id=1, source_target_pairs={{0,1},{1,0},{2,3},{3,2},{4,5},{5,4},{6,7},{7,6},{8,9},{9,8},{10,11... | collective-permute-start | bytes 884744 | tf_op jit(solution)/shard_map/ppermute | solution.py:101
  228.8 19.1 %collective-permute-start.17 = (bf16[64,2304]{1,0:T(8,128)(2,1)S(1)}, bf16[64,2304]{1,0:T(8,128)(2,1)S(1)}, u32[]{:S(2)}, u32[]{:S(2)}) collective-permute-start(bf16[64,2304]{1,0:T(8,128)(2,1)S(1)} %get-tuple-element.82), channel_id=1, source_target_pairs={{0,1},{1,0},{2,3},{3,2},{4,5},{5,4},{6,7},{7,6},{8,9},{9,8},{10,11... | collective-permute-start | bytes 884744 | tf_op jit(solution)/shard_map/ppermute | solution.py:101
  237.2 15.0 %collective-permute-start.19 = (bf16[64,2304]{1,0:T(8,128)(2,1)S(1)}, bf16[64,2304]{1,0:T(8,128)(2,1)S(1)}, u32[]{:S(2)}, u32[]{:S(2)}) collective-permute-start(bf16[64,2304]{1,0:T(8,128)(2,1)S(1)} %add_convert_fusion.13), channel_id=1, source_target_pairs={{0,2},{1,3},{2,0},{3,1},{4,6},{5,7},{6,4},{7,5},{8,10},{9,11},{10,... | collective-permute-start | bytes 884744 | tf_op jit(solution)/shard_map/ppermute | solution.py:101
  254.4 12.3 %collective-permute-start.21 = (bf16[64,2304]{1,0:T(8,128)(2,1)S(1)}, bf16[64,2304]{1,0:T(8,128)(2,1)S(1)}, u32[]{:S(2)}, u32[]{:S(2)}) collective-permute-start(bf16[64,2304]{1,0:T(8,128)(2,1)S(1)} %get-tuple-element.67), channel_id=1, source_target_pairs={{0,2},{1,3},{2,0},{3,1},{4,6},{5,7},{6,4},{7,5},{8,10},{9,11},{10,... | collective-permute-start | bytes 884744 | tf_op jit(solution)/shard_map/ppermute | solution.py:101
  254.4 13.0 %collective-permute-start.20 = (bf16[64,2304]{1,0:T(8,128)(2,1)S(1)}, bf16[64,2304]{1,0:T(8,128)(2,1)S(1)}, u32[]{:S(2)}, u32[]{:S(2)}) collective-permute-start(bf16[64,2304]{1,0:T(8,128)(2,1)S(1)} %get-tuple-element.67), channel_id=1, source_target_pairs={{0,1},{1,0},{2,3},{3,2},{4,5},{5,4},{6,7},{7,6},{8,9},{9,8},{10,11... | collective-permute-start | bytes 884744 | tf_op jit(solution)/shard_map/ppermute | solution.py:101
  266.7 7.5 %collective-permute-start.22 = (bf16[64,2304]{1,0:T(8,128)(2,1)S(1)}, bf16[64,2304]{1,0:T(8,128)(2,1)S(1)}, u32[]{:S(2)}, u32[]{:S(2)}) collective-permute-start(bf16[64,2304]{1,0:T(8,128)(2,1)S(1)} %collective-permute-done.21), channel_id=1, source_target_pairs={{0,1},{1,0},{2,3},{3,2},{4,5},{5,4},{6,7},{7,6},{8,9},{9,8},{10,11... | collective-permute-start | bytes 884744 | tf_op jit(solution)/shard_map/ppermute | solution.py:101
  280.6 276.5 %reduce-scatter.3.cloned.1.call-start = ((), (), s32[]{:S(2)}) async-start(), calls=%async_computation.4 | async-start | bytes 23887872 | tf_op jit(solution)/shard_map/reduce_scatter | solution.py:403
  319.9 10.0 %collective-permute-start.24 = (bf16[64,2304]{1,0:T(8,128)(2,1)S(1)}, bf16[64,2304]{1,0:T(8,128)(2,1)S(1)}, u32[]{:S(2)}, u32[]{:S(2)}) collective-permute-start(bf16[64,2304]{1,0:T(8,128)(2,1)S(1)} %get-tuple-element.81), channel_id=1, source_target_pairs={{0,1},{1,0},{2,3},{3,2},{4,5},{5,4},{6,7},{7,6},{8,9},{9,8},{10,11... | collective-permute-start | bytes 884744 | tf_op jit(solution)/shard_map/ppermute | solution.py:101
  321.7 17.9 %collective-permute-start.23 = (bf16[64,2304]{1,0:T(8,128)(2,1)S(1)}, bf16[64,2304]{1,0:T(8,128)(2,1)S(1)}, u32[]{:S(2)}, u32[]{:S(2)}) collective-permute-start(bf16[64,2304]{1,0:T(8,128)(2,1)S(1)} %get-tuple-element.80), channel_id=1, source_target_pairs={{0,1},{1,0},{2,3},{3,2},{4,5},{5,4},{6,7},{7,6},{8,9},{9,8},{10,11... | collective-permute-start | bytes 884744 | tf_op jit(solution)/shard_map/ppermute | solution.py:101
  330.9 14.2 %collective-permute-start.25 = (bf16[64,2304]{1,0:T(8,128)(2,1)S(1)}, bf16[64,2304]{1,0:T(8,128)(2,1)S(1)}, u32[]{:S(2)}, u32[]{:S(2)}) collective-permute-start(bf16[64,2304]{1,0:T(8,128)(2,1)S(1)} %add_convert_fusion.11), channel_id=1, source_target_pairs={{0,2},{1,3},{2,0},{3,1},{4,6},{5,7},{6,4},{7,5},{8,10},{9,11},{10,... | collective-permute-start | bytes 884744 | tf_op jit(solution)/shard_map/ppermute | solution.py:101
  350.4 11.4 %collective-permute-start.27 = (bf16[64,2304]{1,0:T(8,128)(2,1)S(1)}, bf16[64,2304]{1,0:T(8,128)(2,1)S(1)}, u32[]{:S(2)}, u32[]{:S(2)}) collective-permute-start(bf16[64,2304]{1,0:T(8,128)(2,1)S(1)} %concatenate.174), channel_id=1, source_target_pairs={{0,2},{1,3},{2,0},{3,1},{4,6},{5,7},{6,4},{7,5},{8,10},{9,11},{10,... | collective-permute-start | bytes 884744 | tf_op jit(solution)/shard_map/ppermute | solution.py:101
  350.5 12.2 %collective-permute-start.26 = (bf16[64,2304]{1,0:T(8,128)(2,1)S(1)}, bf16[64,2304]{1,0:T(8,128)(2,1)S(1)}, u32[]{:S(2)}, u32[]{:S(2)}) collective-permute-start(bf16[64,2304]{1,0:T(8,128)(2,1)S(1)} %concatenate.174), channel_id=1, source_target_pairs={{0,1},{1,0},{2,3},{3,2},{4,5},{5,4},{6,7},{7,6},{8,9},{9,8},{10,11... | collective-permute-start | bytes 884744 | tf_op jit(solution)/shard_map/ppermute | solution.py:101
  361.8 6.7 %collective-permute-start.28 = (bf16[64,2304]{1,0:T(8,128)(2,1)S(1)}, bf16[64,2304]{1,0:T(8,128)(2,1)S(1)}, u32[]{:S(2)}, u32[]{:S(2)}) collective-permute-start(bf16[64,2304]{1,0:T(8,128)(2,1)S(1)} %collective-permute-done.27), channel_id=1, source_target_pairs={{0,1},{1,0},{2,3},{3,2},{4,5},{5,4},{6,7},{7,6},{8,9},{9,8},{10,11... | collective-permute-start | bytes 884744 | tf_op jit(solution)/shard_map/ppermute | solution.py:101
  385.5 11.6 %collective-permute-start.29 = (bf16[1024,512]{1,0:T(8,128)(2,1)}, bf16[1024,512]{1,0:T(8,128)(2,1)}, u32[]{:S(2)}, u32[]{:S(2)}) collective-permute-start(bf16[1024,512]{1,0:T(8,128)(2,1)} %pad_maximum_fusion.6), channel_id=1, source_target_pairs={{0,4},{4,0},{8,12},{12,8},{16,20},{20,16},{24,28},{28,24},{1,5},{5... | collective-permute-start | bytes 3145736 | tf_op jit(solution)/shard_map/ppermute | solution.py:101
  400.4 32.6 %collective-permute-start.36 = (bf16[1152,512]{1,0:T(8,128)(2,1)}, bf16[1152,512]{1,0:T(8,128)(2,1)}, u32[]{:S(2)}, u32[]{:S(2)}) collective-permute-start(bf16[1152,512]{1,0:T(8,128)(2,1)} %convolution_convert_fusion.5), channel_id=1, source_target_pairs={{0,4},{4,0},{8,12},{12,8},{16,20},{20,16},{24,28},{28,24},{1,5},{5... | collective-permute-start | bytes 3538952 | tf_op jit(solution)/shard_map/ppermute | solution.py:101
  401.8 10.7 %collective-permute-start.33 = (bf16[256,512]{1,0:T(8,128)(2,1)}, bf16[256,512]{1,0:T(8,128)(2,1)}, u32[]{:S(2)}, u32[]{:S(2)}) collective-permute-start(bf16[256,512]{1,0:T(8,128)(2,1)} %get-tuple-element.106), channel_id=1, source_target_pairs={{0,8},{4,12},{8,0},{12,4},{16,24},{20,28},{24,16},{28,20},{1,9},{5... | collective-permute-start | bytes 786440 | tf_op jit(solution)/shard_map/ppermute | solution.py:101
  405.8 27.1 %collective-permute-start.30 = (bf16[64,2304]{1,0:T(8,128)(2,1)}, bf16[64,2304]{1,0:T(8,128)(2,1)S(1)}, u32[]{:S(2)}, u32[]{:S(2)}) collective-permute-start(bf16[64,2304]{1,0:T(8,128)(2,1)} %get-tuple-element.32), channel_id=1, source_target_pairs={{0,1},{1,0},{2,3},{3,2},{4,5},{5,4},{6,7},{7,6},{8,9},{9,8},{10,11... | collective-permute-start | bytes 884744 | tf_op jit(solution)/shard_map/ppermute | solution.py:101
  407.3 25.2 %collective-permute-start.31 = (bf16[64,2304]{1,0:T(8,128)(2,1)}, bf16[64,2304]{1,0:T(8,128)(2,1)}, u32[]{:S(2)}, u32[]{:S(2)}) collective-permute-start(bf16[64,2304]{1,0:T(8,128)(2,1)} %get-tuple-element.32), channel_id=1, source_target_pairs={{0,2},{1,3},{2,0},{3,1},{4,6},{5,7},{6,4},{7,5},{8,10},{9,11},{10,... | collective-permute-start | bytes 884744 | tf_op jit(solution)/shard_map/ppermute | solution.py:101
  411.3 20.1 %collective-permute-start.34 = (bf16[256,512]{1,0:T(8,128)(2,1)}, bf16[256,512]{1,0:T(8,128)(2,1)S(1)}, u32[]{:S(2)}, u32[]{:S(2)}) collective-permute-start(bf16[256,512]{1,0:T(8,128)(2,1)} %get-tuple-element.108), channel_id=1, source_target_pairs={{0,16},{4,20},{8,24},{12,28},{16,0},{20,4},{24,8},{28,12},{1,17},{... | collective-permute-start | bytes 786440 | tf_op jit(solution)/shard_map/ppermute | solution.py:101
  412.5 18.9 %collective-permute-start.35 = (bf16[256,512]{1,0:T(8,128)(2,1)}, bf16[256,512]{1,0:T(8,128)(2,1)S(1)}, u32[]{:S(2)}, u32[]{:S(2)}) collective-permute-start(bf16[256,512]{1,0:T(8,128)(2,1)} %get-tuple-element.107), channel_id=1, source_target_pairs={{0,24},{4,28},{8,16},{12,20},{16,8},{20,12},{24,0},{28,4},{1,25},{... | collective-permute-start | bytes 786440 | tf_op jit(solution)/shard_map/ppermute | solution.py:101
  432.5 19.3 %collective-permute-start.32 = (bf16[64,2304]{1,0:T(8,128)(2,1)}, bf16[64,2304]{1,0:T(8,128)(2,1)}, u32[]{:S(2)}, u32[]{:S(2)}) collective-permute-start(bf16[64,2304]{1,0:T(8,128)(2,1)} %collective-permute-done.31), channel_id=1, source_target_pairs={{0,1},{1,0},{2,3},{3,2},{4,5},{5,4},{6,7},{7,6},{8,9},{9,8},{10,11... | collective-permute-start | bytes 884744 | tf_op jit(solution)/shard_map/ppermute | solution.py:101
  442.8 30.2 %collective-permute-start.37 = (bf16[1152,1024]{1,0:T(8,128)(2,1)S(1)}, bf16[1152,1024]{1,0:T(8,128)(2,1)S(1)}, u32[]{:S(2)}, u32[]{:S(2)}) collective-permute-start(bf16[1152,1024]{1,0:T(8,128)(2,1)S(1)} %convolution_convert_fusion.4), channel_id=1, source_target_pairs={{0,4},{4,0},{8,12},{12,8},{16,20},{20,16},{24,28},{28,24},{1,5},{5... | collective-permute-start | bytes 7077896 | tf_op jit(solution)/shard_map/ppermute | solution.py:101
  450.1 9.9 %collective-permute-start.39 = (bf16[64,2304]{1,0:T(8,128)(2,1)S(1)}, bf16[64,2304]{1,0:T(8,128)(2,1)S(1)}, u32[]{:S(2)}, u32[]{:S(2)}) collective-permute-start(bf16[64,2304]{1,0:T(8,128)(2,1)S(1)} %get-tuple-element.79), channel_id=1, source_target_pairs={{0,1},{1,0},{2,3},{3,2},{4,5},{5,4},{6,7},{7,6},{8,9},{9,8},{10,11... | collective-permute-start | bytes 884744 | tf_op jit(solution)/shard_map/ppermute | solution.py:101
  453.5 15.9 %collective-permute-start.50 = (bf16[288,512]{1,0:T(8,128)(2,1)S(1)}, bf16[288,512]{1,0:T(8,128)(2,1)S(1)}, u32[]{:S(2)}, u32[]{:S(2)}) collective-permute-start(bf16[288,512]{1,0:T(8,128)(2,1)S(1)} %copy-done.74), channel_id=1, source_target_pairs={{0,16},{4,20},{8,24},{12,28},{16,0},{20,4},{24,8},{28,12},{1,17},{... | collective-permute-start | bytes 884744 | tf_op jit(solution)/shard_map/ppermute | solution.py:101
  454.6 15.9 %collective-permute-start.48 = (bf16[288,512]{1,0:T(8,128)(2,1)S(1)}, bf16[288,512]{1,0:T(8,128)(2,1)S(1)}, u32[]{:S(2)}, u32[]{:S(2)}) collective-permute-start(bf16[288,512]{1,0:T(8,128)(2,1)S(1)} %copy-done.73), channel_id=1, source_target_pairs={{0,8},{4,12},{8,0},{12,4},{16,24},{20,28},{24,16},{28,20},{1,9},{5... | collective-permute-start | bytes 884744 | tf_op jit(solution)/shard_map/ppermute | solution.py:101
  455.5 21.7 %collective-permute-start.38 = (bf16[64,2304]{1,0:T(8,128)(2,1)S(1)}, bf16[64,2304]{1,0:T(8,128)(2,1)S(1)}, u32[]{:S(2)}, u32[]{:S(2)}) collective-permute-start(bf16[64,2304]{1,0:T(8,128)(2,1)S(1)} %get-tuple-element.78), channel_id=1, source_target_pairs={{0,1},{1,0},{2,3},{3,2},{4,5},{5,4},{6,7},{7,6},{8,9},{9,8},{10,11... | collective-permute-start | bytes 884744 | tf_op jit(solution)/shard_map/ppermute | solution.py:101
  460.1 17.2 %collective-permute-start.40 = (bf16[64,2304]{1,0:T(8,128)(2,1)S(1)}, bf16[64,2304]{1,0:T(8,128)(2,1)S(1)}, u32[]{:S(2)}, u32[]{:S(2)}) collective-permute-start(bf16[64,2304]{1,0:T(8,128)(2,1)S(1)} %add_convert_fusion.8), channel_id=1, source_target_pairs={{0,2},{1,3},{2,0},{3,1},{4,6},{5,7},{6,4},{7,5},{8,10},{9,11},{10,... | collective-permute-start | bytes 884744 | tf_op jit(solution)/shard_map/ppermute | solution.py:101
  471.2 27.8 %collective-permute-start.49 = (bf16[144,512]{1,0:T(8,128)(2,1)}, bf16[144,512]{1,0:T(8,128)(2,1)}, u32[]{:S(2)}, u32[]{:S(2)}) collective-permute-start(bf16[144,512]{1,0:T(8,128)(2,1)} %get-tuple-element.127), channel_id=1, source_target_pairs={{0,16},{4,20},{8,24},{12,28},{16,0},{20,4},{24,8},{28,12},{1,17},{... | collective-permute-start | bytes 442376 | tf_op jit(solution)/shard_map/ppermute | solution.py:101
  472.1 26.9 %collective-permute-start.51 = (bf16[144,512]{1,0:T(8,128)(2,1)}, bf16[144,512]{1,0:T(8,128)(2,1)}, u32[]{:S(2)}, u32[]{:S(2)}) collective-permute-start(bf16[144,512]{1,0:T(8,128)(2,1)} %get-tuple-element.128), channel_id=1, source_target_pairs={{0,8},{4,12},{8,0},{12,4},{16,24},{20,28},{24,16},{28,20},{1,9},{5... | collective-permute-start | bytes 442376 | tf_op jit(solution)/shard_map/ppermute | solution.py:101
  484.0 14.7 %collective-permute-start.42 = (bf16[64,2304]{1,0:T(8,128)(2,1)}, bf16[64,2304]{1,0:T(8,128)(2,1)S(1)}, u32[]{:S(2)}, u32[]{:S(2)}) collective-permute-start(bf16[64,2304]{1,0:T(8,128)(2,1)} %get-tuple-element.55), channel_id=1, source_target_pairs={{0,2},{1,3},{2,0},{3,1},{4,6},{5,7},{6,4},{7,5},{8,10},{9,11},{10,... | collective-permute-start | bytes 884744 | tf_op jit(solution)/shard_map/ppermute | solution.py:101
  498.7 4.0 collective-permute-start.52
  502.7 5.3 collective-permute-start.53
  505.2 39.2 %collective-permute-start.46 = (bf16[288,1024]{1,0:T(8,128)(2,1)}, bf16[288,1024]{1,0:T(8,128)(2,1)S(1)}, u32[]{:S(2)}, u32[]{:S(2)}) collective-permute-start(bf16[288,1024]{1,0:T(8,128)(2,1)} %add_convert_fusion.2), channel_id=1, source_target_pairs={{0,16},{4,20},{8,24},{12,28},{16,0},{20,4},{24,8},{28,12},{1,17},{... | collective-permute-start | bytes 1769480 | tf_op jit(solution)/shard_map/ppermute | solution.py:101
  505.8 38.5 %collective-permute-start.44 = (bf16[288,1024]{1,0:T(8,128)(2,1)S(1)}, bf16[288,1024]{1,0:T(8,128)(2,1)S(1)}, u32[]{:S(2)}, u32[]{:S(2)}) collective-permute-start(bf16[288,1024]{1,0:T(8,128)(2,1)S(1)} %copy-done.106), channel_id=1, source_target_pairs={{0,8},{4,12},{8,0},{12,4},{16,24},{20,28},{24,16},{28,20},{1,9},{5... | collective-permute-start | bytes 1769480 | tf_op jit(solution)/shard_map/ppermute | solution.py:101
  508.0 1.3 collective-permute-start.54
  508.2 27.4 %collective-permute-start.41 = (bf16[64,2304]{1,0:T(8,128)(2,1)}, bf16[64,2304]{1,0:T(8,128)(2,1)S(1)}, u32[]{:S(2)}, u32[]{:S(2)}) collective-permute-start(bf16[64,2304]{1,0:T(8,128)(2,1)} %get-tuple-element.55), channel_id=1, source_target_pairs={{0,1},{1,0},{2,3},{3,2},{4,5},{5,4},{6,7},{7,6},{8,9},{9,8},{10,11... | collective-permute-start | bytes 884744 | tf_op jit(solution)/shard_map/ppermute | solution.py:101
  509.4 24.8 %collective-permute-start.55 = (f32[4,288]{1,0:T(4,128)S(1)}, f32[4,288]{1,0:T(4,128)S(1)}, u32[]{:S(2)}, u32[]{:S(2)}) collective-permute-start(f32[4,288]{1,0:T(4,128)S(1)} %get-tuple-element.203), channel_id=1, source_target_pairs={{0,8},{4,12},{8,0},{12,4},{16,24},{20,28},{24,16},{28,20},{1,9},{5... | collective-permute-start | bytes 13832 | tf_op jit(solution)/shard_map/ppermute | solution.py:101
  510.4 35.6 %collective-permute-start.43 = (bf16[64,2304]{1,0:T(8,128)(2,1)S(1)}, bf16[64,2304]{1,0:T(8,128)(2,1)S(1)}, u32[]{:S(2)}, u32[]{:S(2)}) collective-permute-start(bf16[64,2304]{1,0:T(8,128)(2,1)S(1)} %collective-permute-done.42), channel_id=1, source_target_pairs={{0,1},{1,0},{2,3},{3,2},{4,5},{5,4},{6,7},{7,6},{8,9},{9,8},{10,11... | collective-permute-start | bytes 884744 | tf_op jit(solution)/shard_map/ppermute | solution.py:101
  534.2 3.6 collective-permute-start.57
  535.7 3.6 collective-permute-start.56
  539.4 3.6 collective-permute-start.58
  544.5 6.8 %collective-permute-start.45 = (bf16[144,1024]{1,0:T(8,128)(2,1)S(1)}, bf16[144,1024]{1,0:T(8,128)(2,1)S(1)}, u32[]{:S(2)}, u32[]{:S(2)}) collective-permute-start(bf16[144,1024]{1,0:T(8,128)(2,1)S(1)} %get-tuple-element.75), channel_id=1, source_target_pairs={{0,16},{4,20},{8,24},{12,28},{16,0},{20,4},{24,8},{28,12},{1,17},{... | collective-permute-start | bytes 884744 | tf_op jit(solution)/shard_map/ppermute | solution.py:101
  545.3 6.7 %collective-permute-start.47 = (bf16[144,1024]{1,0:T(8,128)(2,1)S(1)}, bf16[144,1024]{1,0:T(8,128)(2,1)S(1)}, u32[]{:S(2)}, u32[]{:S(2)}) collective-permute-start(bf16[144,1024]{1,0:T(8,128)(2,1)S(1)} %get-tuple-element.76), channel_id=1, source_target_pairs={{0,8},{4,12},{8,0},{12,4},{16,24},{20,28},{24,16},{28,20},{1,9},{5... | collective-permute-start | bytes 884744 | tf_op jit(solution)/shard_map/ppermute | solution.py:101
  (109 other events, 914.1 us)
Sparse Core Ops, SparseCore 0:
  10.8 143.2 all-gather.2
  156.0 63.8 all-gather.4
  280.7 83.4 reduce-scatter.4
  367.7 171.4 reduce-scatter.2

commit v3 on v1

v3 whole, which is shorter than its diff:
```python
import functools
import math

import jax
import jax.numpy as jnp
from jax import lax
from jax.experimental import pallas as pl
from jax.experimental.pallas import tpu as pltpu
from jax.sharding import PartitionSpec as P

HD = 256


EPSILON = 1e-06
SOFT_CAP = 50.0
MASKED = -1e30

bf16, f32 = jnp.bfloat16, jnp.float32


def rms_scale(values):
    return lax.rsqrt(jnp.mean(values * values, axis=-1, keepdims=True) + EPSILON)


def norm_back(inv_rms, normed, gradient):
    return inv_rms * (gradient - normed * jnp.mean(gradient * normed, axis=-1, keepdims=True))


def rotate(values, cos_table, sine_table):
    half_width = values.shape[-1] // 2
    leading = values[..., :half_width]
    trailing = values[..., half_width:]
    return jnp.concatenate(
        [leading * cos_table - trailing * sine_table, trailing * cos_table + leading * sine_table],
        axis=-1,
    )


def gelu_tanh(values):
    return jax.nn.gelu(values, approximate=True)


def product(first_operand, second_operand):
    return jnp.dot(first_operand, second_operand, preferred_element_type=f32)


def contract(first_operand, second_operand, first_dim, second_dim):
    return lax.dot_general(
        first_operand,
        second_operand,
        (((first_dim,), (second_dim,)), ((), ())),
        preferred_element_type=f32,
    )


def after(value, *earlier):
    return lax.optimization_barrier((value,) + earlier)[0]


def swap(value, bit, axis="ctx"):
    count = lax.axis_size(axis)
    return lax.ppermute(value, axis, [(index, index ^ bit) for index in range(count)])


WHOLE = pl.BlockSpec(memory_space=pltpu.VMEM)
SCALARS = pl.BlockSpec(memory_space=pltpu.SMEM)
VMEM_BYTES = 24 * 2**20


def shape_of(dims, kind):
    return jax.ShapeDtypeStruct(dims, kind)


def key_block(key_count):
    return math.gcd(key_count, 512)


def attend_kernel(steps, group, query_ref, pair_ref, place_ref, key_place_ref, out_ref, rows_ref, log_ref):
    step = pl.program_id(0)
    rows = place_ref.shape[0]

    @pl.when(step == 0)
    def _():
        out_ref[...] = jnp.zeros_like(out_ref)
        log_ref[...] = jnp.zeros_like(log_ref)

    keys, values = pair_ref[:, :HD], pair_ref[:, HD:]
    scores = contract(query_ref[...], keys, 1, 1)
    capped = SOFT_CAP * jnp.tanh(scores * (1.0 / SOFT_CAP))
    visible = key_place_ref[...] <= place_ref[...]
    weights = jnp.where(visible, jnp.exp(capped), 0.0)
    log_ref[...] += jnp.sum(weights, axis=-1, keepdims=True)
    out_ref[...] += product(weights.astype(bf16), values)

    @pl.when(step == steps - 1)
    def _():
        total = log_ref[...]
        result = out_ref[...] / total
        out_ref[...] = result
        log_ref[...] = jnp.log(total)
        each = rows // group
        for head in range(group):
            rows_ref[:, head * HD : (head + 1) * HD] = result[head * each : (head + 1) * each].astype(bf16)


def attend(queries, pairs, places, key_places, group):
    rows, key_count = queries.shape[0], pairs.shape[0]
    block = key_block(key_count)
    steps = key_count // block
    fixed = lambda step: (0, 0)
    return pl.pallas_call(
        functools.partial(attend_kernel, steps, group),
        grid=(steps,),
        in_specs=[
            pl.BlockSpec((rows, HD), fixed),
            pl.BlockSpec((block, 2 * HD), lambda step: (step, 0)),
            pl.BlockSpec((rows, 1), fixed),
            pl.BlockSpec((1, block), lambda step: (0, step)),
        ],
        out_specs=[
            pl.BlockSpec((rows, HD), fixed),
            pl.BlockSpec((rows // group, group * HD), fixed),
            pl.BlockSpec((rows, 1), fixed),
        ],
        out_shape=[
            shape_of((rows, HD), f32),
            shape_of((rows // group, group * HD), bf16),
            shape_of((rows, 1), f32),
        ],
        compiler_params=pltpu.CompilerParams(vmem_limit_bytes=VMEM_BYTES),
        name="attend",
    )(queries, pairs, places, key_places)


def attend_back_kernel(
    query_ref, grad_ref, out_ref, log_ref, pair_ref, place_ref, key_place_ref, query_grad_ref, pair_grad_ref, delta_ref
):
    @pl.when(pl.program_id(0) == 0)
    def _():
        query_grad_ref[...] = jnp.zeros_like(query_grad_ref)
        delta_ref[...] = jnp.sum(grad_ref[...].astype(f32) * out_ref[...], axis=-1, keepdims=True)

    queries, grads = query_ref[...], grad_ref[...]
    keys, values = pair_ref[:, :HD], pair_ref[:, HD:]
    part = jnp.tanh(contract(queries, keys, 1, 1) * (1.0 / SOFT_CAP))
    visible = key_place_ref[...] <= place_ref[...]
    probs = jnp.where(visible, jnp.exp(SOFT_CAP * part - log_ref[...]), 0.0)
    pair_grad_ref[:, HD:] = contract(probs.astype(bf16), grads, 0, 0).astype(bf16)
    slope = contract(grads, values, 1, 1) - delta_ref[...]
    score_grad = (probs * slope * (1.0 - part * part)).astype(bf16)
    query_grad_ref[...] += product(score_grad, keys)
    pair_grad_ref[:, :HD] = contract(score_grad, queries, 0, 0).astype(bf16)


def attend_back(queries, grads, outs, logs, pairs, places, key_places):
    rows, key_count = queries.shape[0], pairs.shape[0]
    block = key_block(key_count)
    fixed = lambda step: (0, 0)
    tall = pl.BlockSpec((rows, HD), fixed)
    column = pl.BlockSpec((rows, 1), fixed)
    moving = pl.BlockSpec((block, 2 * HD), lambda step: (step, 0))
    return pl.pallas_call(
        attend_back_kernel,
        grid=(key_count // block,),
        in_specs=[tall, tall, tall, column, moving, column, pl.BlockSpec((1, block), lambda step: (0, step))],
        out_specs=[tall, moving],
        out_shape=[shape_of((rows, HD), f32), shape_of((key_count, 2 * HD), bf16)],
        scratch_shapes=[pltpu.VMEM((rows, 1), f32)],
        compiler_params=pltpu.CompilerParams(vmem_limit_bytes=VMEM_BYTES),
        name="attend_back",
    )(queries, grads, outs, logs, pairs, places, key_places)


def local(
    tokens,
    w_query,
    w_key,
    w_value,
    w_out,
    w_gate,
    w_up,
    w_down,
    norm_attn_in,
    norm_attn_out,
    norm_ffn_in,
    norm_ffn_out,
    cotangent,
):
    tok_rows, width = tokens.shape
    heads_local = w_query.shape[1] // HD
    key_heads = w_key.shape[1] // HD
    query_width = heads_local * HD
    key_width = key_heads * HD
    qkv_width = query_width + 2 * key_width
    ffn_width = w_gate.shape[1]
    ring = lax.axis_size("ctx")
    layers = lax.axis_size("tp")
    me = lax.axis_index("ctx")
    my_layer = lax.axis_index("tp")
    shard = width // ring
    own_rows = tok_rows // layers
    upper = shard // 32 * 16
    far_a, far_b = ring // 4, ring // 2
    near = [1 << bit for bit in range(far_a.bit_length() - 1)]
    order = [0, far_a, far_b, far_a | far_b]
    for bit in near:
        order = order + [block | bit for block in order]
    near_width = 4 * shard
    gather_factors = tok_rows * ring <= width

    def spread_far(piece):
        from_a, from_b = swap(piece, far_a), swap(piece, far_b)
        return from_a, from_b, swap(from_b[:upper], far_a), swap(from_a[upper:shard], far_b)

    def spread_near(block):
        blocks = [block]
        for bit in near:
            blocks = blocks + [swap(held, bit) for held in blocks]
        return blocks

    def by_near(array):
        return [array[:, start : start + near_width] for start in range(0, width, near_width)]

    def times_rows(activation, blocks):
        total = None
        for part, block in zip(by_near(activation), blocks):
            term = product(part, block)
            total = term if total is None else total + term
        return total

    def times_rows_t(activation, blocks):
        return jnp.concatenate([contract(activation, block, 1, 1) for block in blocks], axis=1)

    def layer_scatter(partial, first=None, second=None):
        pieces = [partial[step * own_rows : (step + 1) * own_rows] for step in range(layers)]
        done_first = first(partial) if first else ()
        if layers == 4:
            passed_on = swap(pieces[3], 1, "tp")
            arrived = [swap(pieces[1], 1, "tp")]
            held = after(pieces[2], *done_first) if first else pieces[2]
            pair_sum = (held.astype(f32) + passed_on.astype(f32)).astype(bf16)
            arrived.append(swap(pair_sum, 2, "tp"))
        else:
            pair_sum = partial
            arrived = [swap(pieces[step], step, "tp") for step in range(1, layers)]
        done_second = second(pair_sum) if second else ()
        total = after(pieces[0], *done_first, *done_second).astype(f32)
        for piece in arrived:
            total = total + piece.astype(f32)
        return total, done_first, done_second

    def layer_gather(rows, first=None, second=None):
        done_first = first(rows) if first else ()
        if layers == 4:
            across = swap(rows, 2, "tp")
            beside = swap(rows, 1, "tp")
            across_then = after(across, *done_first) if first else across
            pieces = [rows, beside, across, swap(across_then, 1, "tp")]
        else:
            across_then = rows
            pieces = [rows] + [swap(rows, step, "tp") for step in range(1, layers)]
        done_second = second(across_then) if second else ()
        if first or second:
            pieces[0] = after(pieces[0], *done_first, *done_second)
        return pieces, done_first, done_second

    def rows_in(array):
        return jnp.concatenate(
            [
                lax.dynamic_slice_in_dim(array, (my_layer ^ step) * own_rows, own_rows, 0)
                for step in range(layers)
            ],
            axis=0,
        )

    def rows_out(pieces):
        result = jnp.zeros((tok_rows,) + pieces[0].shape[1:], pieces[0].dtype)
        for step, piece in enumerate(pieces):
            result = lax.dynamic_update_slice_in_dim(
                result, piece, (my_layer ^ step) * own_rows, 0
            )
        return result

    def columns_in(array):
        return jnp.concatenate(
            [lax.dynamic_slice_in_dim(array, (me ^ block) * shard, shard, 1) for block in order],
            axis=1,
        )

    def columns_out(array):
        def place(block):
            found = (block & far_a) // far_a + 2 * ((block & far_b) // far_b)
            for index, bit in enumerate(near):
                found = found + (4 << index) * ((block & bit) // bit)
            return found

        return jnp.concatenate(
            [
                lax.dynamic_slice_in_dim(array, place(me ^ block) * shard, shard, 1)
                for block in range(ring)
            ],
            axis=1,
        )

    def rows_of_all(array):
        return lax.all_gather(array, "ctx", axis=0, tiled=True)

    def columns_by_owner(*arrays):
        stacked = jnp.stack([array.reshape(tok_rows, ring, shard) for array in arrays])
        return stacked.transpose(2, 0, 1, 3)

    def columns_of_owner(stacked):
        found = lax.all_to_all(stacked, "ctx", split_axis=0, concat_axis=0, tiled=True)
        return [
            found[:, index].reshape(ring * tok_rows, shard) for index in range(found.shape[1])
        ]

    def sum_scatter(partial):
        return lax.psum_scatter(
            partial.astype(bf16), "ctx", scatter_dimension=0, tiled=True
        ).astype(f32)

    def products_kernel(me_ref, input_ref, lin_ref, grad_ref, rows_ref, out_ref):
        for place, block in enumerate(order):
            rows = pl.ds(pl.multiple_of((me_ref[0] ^ block) * shard, 16), shard)
            here = slice(place * shard, (place + 1) * shard)
            out_ref[rows, :qkv_width] = contract(input_ref[:, here], lin_ref[...], 0, 0).astype(bf16)
            out_ref[rows, qkv_width:] = contract(grad_ref[:, here], rows_ref[...], 0, 0).astype(bf16)

    def attn_products(inputs, lin, grads, rows):
        if shard % 16:
            return jnp.concatenate(
                [
                    contract(columns_out(inputs), lin, 0, 0),
                    contract(columns_out(grads), rows, 0, 0),
                ],
                axis=1,
            ).astype(bf16)
        return pl.pallas_call(
            products_kernel,
            in_specs=[SCALARS] + [WHOLE] * 4,
            out_specs=WHOLE,
            out_shape=shape_of((width, qkv_width + query_width), bf16),
            compiler_params=pltpu.CompilerParams(vmem_limit_bytes=VMEM_BYTES),
            name="attn_products",
        )(me[None], inputs, lin, grads, rows)

    first_gain = norm_attn_in.astype(f32)[:, None]
    gate_up = rows_of_all(jnp.concatenate([w_gate, w_up], axis=1))
    down_w = rows_of_all(w_down)
    qkv_own = (
        jnp.concatenate([w_query, w_key, w_value], axis=1).astype(f32) * first_gain
    ).astype(bf16)
    attn_own = jnp.concatenate([qkv_own, w_out], axis=1)
    own_gains = jnp.stack([norm_attn_out, norm_ffn_in, norm_ffn_out])
    gain_rows = jnp.zeros((16, attn_own.shape[1]), bf16).at[:3, :shard].set(own_gains)
    from_a, from_b, top, bottom = spread_far(jnp.concatenate([attn_own, gain_rows], axis=0))
    attn_w = spread_near(
        jnp.concatenate([attn_own, from_a[:shard], from_b[:shard], top, bottom], axis=0)
    )
    qkv_w = [block[:, :qkv_width] for block in attn_w]
    out_w = [block[:, qkv_width:] for block in attn_w]
    gain_a, gain_b = (held[shard : shard + 3, :shard] for held in (from_a, from_b))
    gains = jnp.concatenate(
        spread_near(
            jnp.concatenate([own_gains, gain_a, gain_b, swap(gain_b, far_a)], axis=1)
        ),
        axis=1,
    )
    gain_two, gain_three, gain_four = jnp.split(columns_out(gains).astype(f32), 3)

    tok_float = rows_in(tokens).astype(f32)
    own_cot = lax.dynamic_slice_in_dim(cotangent, my_layer * own_rows, own_rows, 0).astype(f32)
    norm_input = (tok_float * rms_scale(tok_float)).astype(bf16)
    own_tok = tok_float[:own_rows]
    attn_input = columns_in(norm_input)
    lin = times_rows(attn_input, qkv_w)
    row_place = jnp.concatenate(
        [
            (my_layer ^ step) * own_rows + jnp.arange(own_rows, dtype=jnp.int32)
            for step in range(layers)
        ]
    )
    query_pos = me * tok_rows + row_place
    half_width = HD // 2
    frequency = jnp.exp(jnp.arange(half_width, dtype=f32) * (-2.0 * math.log(10000.0) / HD))
    angles = query_pos.astype(f32)[:, None] * frequency[None, :]
    cos_table, sine_table = jnp.cos(angles)[:, None, :], jnp.sin(angles)[:, None, :]
    queries = (
        rotate(lin[:, :query_width].reshape(tok_rows, heads_local, HD), cos_table, sine_table)
        * HD ** (-0.5)
    ).astype(bf16)
    assert key_heads == 1
    query_rows = queries.reshape(tok_rows, heads_local, HD).transpose(1, 0, 2).reshape(-1, HD)
    keys_rot = (
        rotate(
            lin[:, query_width : query_width + key_width].reshape(tok_rows, key_heads, HD),
            cos_table,
            sine_table,
        )
        .astype(bf16)
        .reshape(tok_rows, key_width)
    )
    values_b = lin[:, query_width + key_width :].astype(bf16)
    pair = jnp.concatenate([keys_rot, values_b], axis=1)
    pair_far = jnp.concatenate(
        [pair] + [swap(pair, step) for step in (far_a, far_b, far_a | far_b)], axis=0
    )
    pairs = jnp.concatenate(spread_near(pair_far), axis=0)
    key_count = pairs.shape[0]
    key_places = jnp.concatenate([(me ^ block) * tok_rows + row_place for block in order])[None, :]
    places = jnp.tile(query_pos, heads_local)[:, None]
    attn_float, attn_rows, attn_log = attend(query_rows, pairs, places, key_places, heads_local)
    attn_total, _, _ = layer_scatter(times_rows_t(attn_rows, out_w).astype(bf16))
    attn_total = columns_out(attn_total)
    inv_two = rms_scale(attn_total)
    normed_two = attn_total * inv_two
    hidden_res = own_tok + normed_two * gain_two
    inv_three = rms_scale(hidden_res)
    normed_three = hidden_res * inv_three
    pieces, _, _ = layer_gather((normed_three * gain_three).astype(bf16))
    ffn_input = jnp.concatenate(pieces, axis=0)

    both_lin = product(ffn_input, gate_up)
    gate_lin, up_lin = both_lin[:, :ffn_width], both_lin[:, ffn_width:]
    activated, gelu_pull = jax.vjp(gelu_tanh, gate_lin)
    hidden_b = (activated * up_lin).astype(bf16)
    if gather_factors:
        all_hidden = rows_of_all(hidden_b)
    ffn_total, _, _ = layer_scatter(contract(hidden_b, down_w, 1, 1).astype(bf16))
    inv_four = rms_scale(ffn_total)
    normed_four = ffn_total * inv_four
    own_output = (hidden_res + normed_four * gain_four).astype(bf16)

    grad_gain_four = jnp.sum(own_cot * normed_four, axis=0)
    pieces, _, _ = layer_gather(norm_back(inv_four, normed_four, own_cot * gain_four).astype(bf16))
    grad_ffn = jnp.concatenate(pieces, axis=0)
    sent_output = after(own_output, grad_ffn)
    if layers == 4:
        output_pieces = [own_output, swap(sent_output, 1, "tp"), swap(sent_output, 2, "tp")]
    else:
        output_pieces, _, _ = layer_gather(sent_output)
    grad_hidden = product(grad_ffn, down_w)
    grad_gate = gelu_pull(grad_hidden * up_lin)[0].astype(bf16)
    grad_up = (grad_hidden * activated).astype(bf16)
    grad_both = jnp.concatenate([grad_gate, grad_up], axis=1)
    if gather_factors:
        all_both = rows_of_all(after(grad_both, all_hidden))
    else:
        grad_w_down = sum_scatter(contract(grad_ffn, hidden_b, 0, 0))
        grad_w_both = sum_scatter(contract(ffn_input, grad_both, 0, 0))
        grad_w_gate, grad_w_up = grad_w_both[:, :ffn_width], grad_w_both[:, ffn_width:]
    grad_in_part = contract(grad_both, gate_up, 1, 1).astype(bf16)
    grad_in_part = after(grad_in_part, *output_pieces[1:])
    if gather_factors:
        grad_ffn_in, (by_owner,), _ = layer_scatter(
            grad_in_part, lambda then: (columns_by_owner(ffn_input, after(grad_ffn, then)),)
        )
    else:
        grad_ffn_in, _, _ = layer_scatter(grad_in_part)
    grad_res = own_cot + norm_back(inv_three, normed_three, grad_ffn_in * gain_three)
    grad_gain_two = jnp.sum(grad_res * normed_two, axis=0)

    own_grad_attn = norm_back(inv_two, normed_two, grad_res * gain_two)
    pieces, _, _ = layer_gather(columns_in(own_grad_attn.astype(bf16)))
    grad_attn = jnp.concatenate(pieces, axis=0)
    grad_rows = times_rows(grad_attn, out_w).astype(bf16)
    grad_heads = grad_rows.reshape(tok_rows, heads_local, HD).transpose(1, 0, 2).reshape(-1, HD)
    grad_q, pair_grad = attend_back(
        query_rows, grad_heads, attn_float, attn_log, pairs, places, key_places
    )
    near_rows = 4 * tok_rows
    pair_part = [
        pair_grad[start : start + near_rows] for start in range(0, key_count, near_rows)
    ]
    for bit in reversed(near):
        half = len(pair_part) // 2
        pair_part = [
            (kept.astype(f32) + swap(sent, bit).astype(f32)).astype(bf16)
            for kept, sent in zip(pair_part[:half], pair_part[half:])
        ]
    pair_part = pair_part[0]
    if layers == 4:
        output_pieces.append(swap(after(output_pieces[2], grad_rows), 1, "tp"))
    output = rows_out(output_pieces)
    arrived = [
        swap(pair_part[index * tok_rows : (index + 1) * tok_rows], step)
        for index, step in ((1, far_a), (2, far_b), (3, far_a | far_b))
    ]
    if gather_factors:
        ffn_cols, down_cols = columns_of_owner(after(by_owner, arrived[0]))
    pair_own = pair_part[:tok_rows].astype(f32)
    for piece in arrived:
        pair_own = pair_own + piece.astype(f32)
    grad_query_lin = (
        rotate(
            grad_q.reshape(heads_local, tok_rows, HD).transpose(1, 0, 2), cos_table, -sine_table
        )
        * HD ** (-0.5)
    ).reshape(tok_rows, query_width)
    grad_key_lin = rotate(
        pair_own[:, :key_width].reshape(tok_rows, key_heads, HD), cos_table, -sine_table
    ).reshape(tok_rows, key_width)
    grad_lin = jnp.concatenate(
        [grad_query_lin, grad_key_lin, pair_own[:, key_width:]], axis=1
    ).astype(bf16)
    grad_in_part = times_rows_t(grad_lin, qkv_w).astype(bf16)

    def products(then):
        lin = after(grad_lin, then, all_both) if gather_factors else after(grad_lin, then)
        return (attn_products(attn_input, lin, grad_attn, attn_rows),)

    def gate_gradient(then):
        return (contract(after(ffn_cols, then), all_both[:, :ffn_width], 0, 0),)

    def up_gradient(then):
        return (contract(after(ffn_cols, then), all_both[:, ffn_width:], 0, 0),)

    def down_gradient(then):
        return (contract(after(down_cols, then), all_hidden, 0, 0),)

    grad_attn_total, (partial,), _ = layer_scatter(grad_in_part, products)
    if gather_factors:
        grad_attn_total = after(grad_attn_total, ffn_cols, down_cols)
    attn_sums = sum_scatter(partial)
    grad_w_lin, grad_w_out = attn_sums[:, :qkv_width], attn_sums[:, qkv_width:]
    grad_attn_in = columns_out(grad_attn_total)
    own_inv = rms_scale(own_tok)
    own_normed = own_tok * own_inv
    own_grad = (grad_res + norm_back(own_inv, own_normed, grad_attn_in)).astype(bf16)
    if gather_factors:
        token_pieces, (grad_w_gate,), _ = layer_gather(own_grad, gate_gradient)
        (grad_w_up,) = up_gradient(token_pieces[3])
        (grad_w_down,) = down_gradient(grad_w_up)
    else:
        token_pieces, _, _ = layer_gather(own_grad)
    grad_tokens = rows_out(token_pieces).astype(f32)

    third_gain = norm_ffn_in.astype(f32)
    gain_third = (
        jnp.sum(w_gate.astype(f32) * grad_w_gate + w_up.astype(f32) * grad_w_up, axis=1)
        / third_gain
    )[None, :]
    gain_sum = columns_in(
        jnp.stack([jnp.sum(grad_attn_in * own_normed, axis=0), grad_gain_two, grad_gain_four])
    )
    gain_sum = after(gain_sum, token_pieces[2])
    for bit in [1 << index for index in range(layers.bit_length() - 1)]:
        gain_third = gain_third + swap(gain_third, bit, "tp")
        gain_sum = gain_sum + swap(gain_sum, bit, "tp")
    for bit in reversed(near):
        half = gain_sum.shape[1] // 2
        gain_sum = gain_sum[:, :half] + swap(gain_sum[:, half:], bit)
    own_gain = gain_sum[:, :shard]
    for index, step in ((1, far_a), (2, far_b), (3, far_a | far_b)):
        own_gain = own_gain + swap(gain_sum[:, index * shard : (index + 1) * shard], step)
    return (
        output,
        grad_tokens,
        grad_w_lin[:, :query_width] * first_gain,
        grad_w_lin[:, query_width : query_width + key_width] * first_gain,
        grad_w_lin[:, query_width + key_width :] * first_gain,
        grad_w_out,
        grad_w_gate,
        grad_w_up,
        grad_w_down,
        own_gain[0] / first_gain[:, 0],
        own_gain[1],
        gain_third[0],
        own_gain[2],
    )


def solution(mesh):
    rows, block = P("ctx", None), P("ctx", "tp")
    gain = P("ctx")
    return jax.shard_map(
        local,
        mesh=mesh,
        in_specs=(rows,) + (block,) * 7 + (gain,) * 4 + (rows,),
        out_specs=(rows, rows) + (block,) * 7 + (gain,) * 4,
        check_vma=False,
    )
```

time: 798 us -> 507 us (0.64)
  the two profiles are of different devices: /device:TPU:8 before, /device:TPU:0 now
where the time goes in v3:
time: 507 us; the launch traced here: 503 us
  waiting for transfers between devices  223 us (44%)
  matrix products  76.9 us (15%)
  local copies, waits for them, and re-layouts  65.8 us (13%)
  starting transfers between devices  59.1 us (12%)
  other arithmetic  52.1 us (10%)
  between operations  15.7 us (3%)
  Pallas kernels  10.6 us (2%)
    ppermute x50, waiting for transfers between devices, swap(): lax.ppermute(value, axis, [(index, index ^ bit) for index in range(count)])  199 us
    ppermute x50, starting transfers between devices, swap(): lax.ppermute(value, axis, [(index, index ^ bit) for index in range(count)])  54.2 us
    dot_general x9, matrix products, contract(): lax.dot_general(first_operand, second_operand, (((first_dim,), (second_di...  49.3 us
    dot_general x6, matrix products, product(): return jnp.dot(first_operand, second_operand, preferred_element_type=f32)  27.5 us
    unnamed x196, local copies, waits for them, and re-layouts  21.1 us
    all_gather x4, waiting for transfers between devices, rows_of_all(): return lax.all_gather(array, 'ctx', axis=0, tiled=True)  13.1 us
    all_to_all x1, waiting for transfers between devices, columns_of_owner(): lax.all_to_all(stacked, 'ctx', split_axis=0, concat_axis=0, tiled=True)  10.2 us
  transfers between devices with their start and end apart: 56, of which 36 were waited for; matrix products, arithmetic and copies ran while one was open for 35% of the time, Pallas kernels for 2%

profile of v3, /device:TPU:0, one launch (start us, length us, event | category | flops | bytes accessed | tf_op | source)
XLA Modules:
  0.0 502.7 jit_solution(3824483202833115112)
XLA Ops:
  7.2 3.4 pad_maximum_fusion
  12.0 3.0 collective-permute-start.1
  17.5 29.2 %collective-permute-done.1 = bf16[304,1536]{1,0:T(8,128)(2,1)S(1)} collective-permute-done((bf16[304,1536]{1,0:T(8,128)(2,1)S(1)}, bf16[304,1536]{1,0:T(8,128)(2,1)S(1)}, u32[]{:S(2)}, u32[]{:S(2)}) %collective-permute-start.1) | collective-permute-done | bytes 933920 | tf_op jit(solution)/shard_map/ppermute | solution.py:62
  48.1 3.3 collective-permute-done
  53.7 15.3 %collective-permute-done.2 = bf16[144,1536]{1,0:T(8,128)(2,1)S(1)} collective-permute-done((bf16[144,1536]{1,0:T(8,128)(2,1)S(1)}, bf16[144,1536]{1,0:T(8,128)(2,1)S(1)}, u32[]{:S(2)}, u32[]{:S(2)}) %collective-permute-start.2) | collective-permute-done | bytes 442400 | tf_op jit(solution)/shard_map/ppermute | solution.py:62
  69.7 2.0 collective-permute-done.3
  80.0 3.0 fusion.12
  83.1 3.3 fusion.18
  88.1 2.5 collective-permute-start.5
  92.7 10.9 %collective-permute-done.5 = bf16[256,512]{1,0:T(8,128)(2,1)} collective-permute-done((bf16[256,512]{1,0:T(8,128)(2,1)}, bf16[256,512]{1,0:T(8,128)(2,1)}, u32[]{:S(2)}, u32[]{:S(2)}) %collective-permute-start.5) | collective-permute-done | bytes 262176 | tf_op jit(solution)/shard_map/ppermute | solution.py:62
  103.6 4.3 collective-permute-done.6
  107.9 6.2 %collective-permute-done.7 = bf16[256,512]{1,0:T(8,128)(2,1)} collective-permute-done((bf16[256,512]{1,0:T(8,128)(2,1)}, bf16[256,512]{1,0:T(8,128)(2,1)}, u32[]{:S(2)}, u32[]{:S(2)}) %collective-permute-start.7) | collective-permute-done | bytes 262176 | tf_op jit(solution)/shard_map/ppermute | solution.py:62
  114.1 2.2 pad_maximum_fusion.6
  116.5 2.0 fusion.67
  120.3 2.2 reshape.353
  128.5 2.7 attend.1
  131.3 2.2 convolution_convert_fusion.5
  138.2 7.9 %collective-permute-done.10 = bf16[64,2304]{1,0:T(8,128)(2,1)S(1)} collective-permute-done((bf16[64,2304]{1,0:T(8,128)(2,1)S(1)}, bf16[64,2304]{1,0:T(8,128)(2,1)S(1)}, u32[]{:S(2)}, u32[]{:S(2)}) %collective-permute-start.10) | collective-permute-done | bytes 294944 | tf_op jit(solution)/shard_map/ppermute | solution.py:62
  146.9 2.4 collective-permute-start.11
  157.5 5.5 %collective-permute-done.11 = bf16[64,2304]{1,0:T(8,128)(2,1)} collective-permute-done((bf16[64,2304]{1,0:T(8,128)(2,1)}, bf16[64,2304]{1,0:T(8,128)(2,1)}, u32[]{:S(2)}, u32[]{:S(2)}) %collective-permute-start.11) | collective-permute-done | bytes 294944 | tf_op jit(solution)/shard_map/ppermute | solution.py:62
  169.5 3.5 collective-permute-start.14
  173.1 10.9 %collective-permute-done.15 = bf16[64,2304]{1,0:T(8,128)(2,1)S(1)} collective-permute-done((bf16[64,2304]{1,0:T(8,128)(2,1)S(1)}, bf16[64,2304]{1,0:T(8,128)(2,1)S(1)}, u32[]{:S(2)}, u32[]{:S(2)}) %collective-permute-start.15) | collective-permute-done | bytes 294944 | tf_op jit(solution)/shard_map/ppermute | solution.py:62
  185.4 6.5 %collective-permute-done.16 = bf16[64,2304]{1,0:T(8,128)(2,1)} collective-permute-done((bf16[64,2304]{1,0:T(8,128)(2,1)S(1)}, bf16[64,2304]{1,0:T(8,128)(2,1)}, u32[]{:S(2)}, u32[]{:S(2)}) %collective-permute-start.16) | collective-permute-done | bytes 294944 | tf_op jit(solution)/shard_map/ppermute | solution.py:62
  191.9 10.5 %fusion.71 = f32[256,4608]{1,0:T(8,128)S(1)} fusion(bf16[2304,4608]{1,0:T(8,128)(2,1)} %all-gather.5.cloned.1.call-done, bf16[64,2304]{1,0:T(8,128)(2,1)} %collective-permute-done.16, bf16[64,2304]{1,0:T(8,128)(2,1)} %copy-done.48, bf16[64,2304]{1,0:T(8,128)(2,1)} %copy-done.50, bf16[64,2304]{1,0:T(8,128)(2,1)} %copy-done.31), kind=kOutput, calls=%fused_computation.266 | convolution fusion | flops 5440536576 | bytes 27131904 | tf_op jit(solution)/shard_map/dot_general | solution.py:44
  202.4 2.2 copy-done.20
  206.8 13.1 %all-gather.7.cloned.1.call-done = bf16[2304,2304]{1,0:T(8,128)(2,1)} async-done(((bf16[288,2304]{1,0:T(8,128)(2,1)}), bf16[2304,2304]{1,0:T(8,128)(2,1)}) %all-gather.7.cloned.1.call-update) | async-done | bytes 10616848 | tf_op jit(solution)/shard_map/all_gather | solution.py:306
  219.8 7.5 %convolution_convert_fusion.1 = bf16[256,2304]{1,0:T(8,128)(2,1)S(1)} fusion(bf16[256,2304]{1,0:T(8,128)(2,1)} %multiply_convert_fusion.1, bf16[2304,2304]{1,0:T(8,128)(2,1)} %all-gather.7.cloned.1.call-done), kind=kOutput, calls=%fused_computation.5 | convolution fusion | flops 2718498816 | bytes 12976128 | tf_op jit(solution)/shard_map/dot_general | solution.py:48
  229.5 7.8 %collective-permute-done.18 = bf16[64,2304]{1,0:T(8,128)(2,1)S(1)} collective-permute-done((bf16[64,2304]{1,0:T(8,128)(2,1)S(1)}, bf16[64,2304]{1,0:T(8,128)(2,1)S(1)}, u32[]{:S(2)}, u32[]{:S(2)}) %collective-permute-start.18) | collective-permute-done | bytes 294944 | tf_op jit(solution)/shard_map/ppermute | solution.py:62
  237.4 2.5 collective-permute-start.19
  239.8 8.2 %collective-permute-done.17 = bf16[64,2304]{1,0:T(8,128)(2,1)S(1)} collective-permute-done((bf16[64,2304]{1,0:T(8,128)(2,1)S(1)}, bf16[64,2304]{1,0:T(8,128)(2,1)S(1)}, u32[]{:S(2)}, u32[]{:S(2)}) %collective-permute-start.17) | collective-permute-done | bytes 294944 | tf_op jit(solution)/shard_map/ppermute | solution.py:62
  248.0 4.5 collective-permute-done.19
  254.0 3.9 collective-permute-start.20
  257.9 8.3 %collective-permute-done.21 = bf16[64,2304]{1,0:T(8,128)(2,1)S(1)} collective-permute-done((bf16[64,2304]{1,0:T(8,128)(2,1)S(1)}, bf16[64,2304]{1,0:T(8,128)(2,1)S(1)}, u32[]{:S(2)}, u32[]{:S(2)}) %collective-permute-start.21) | collective-permute-done | bytes 294944 | tf_op jit(solution)/shard_map/ppermute | solution.py:62
  266.9 6.8 %collective-permute-done.22 = bf16[64,2304]{1,0:T(8,128)(2,1)S(1)} collective-permute-done((bf16[64,2304]{1,0:T(8,128)(2,1)S(1)}, bf16[64,2304]{1,0:T(8,128)(2,1)S(1)}, u32[]{:S(2)}, u32[]{:S(2)}) %collective-permute-start.22) | collective-permute-done | bytes 294944 | tf_op jit(solution)/shard_map/ppermute | solution.py:62
  273.7 7.1 %fusion.10 = (bf16[256,2304]{1,0:T(8,128)(2,1)S(1)}, bf16[256,2304]{1,0:T(8,128)(2,1)S(1)}) fusion(f32[256,4608]{1,0:T(8,128)} %copy-done.20, bf16[2304,2304]{1,0:T(8,128)(2,1)S(1)} %copy-done.87, bf16[64,2304]{1,0:T(8,128)(2,1)S(1)} %collective-permute-done.22, bf16[64,2304]{1,0:T(8,128)(2,1)S(1)} %collective-permute-done.21, ...), kind=kOutput, calls=%fused_computation.20 | convolution fusion | flops 2736783360 | bytes 18874368 | tf_op jit(solution)/shard_map/dot_general | solution.py:44
  284.9 2.2 constant_dynamic-update-slice_fusion.15
  290.1 3.4 collective-permute-start.24
  293.4 12.1 %convolution_convert_fusion = bf16[256,2304]{1,0:T(8,128)(2,1)S(1)} fusion(bf16[2304,4608]{1,0:T(8,128)(2,1)} %all-gather.5.cloned.1.call-done, bf16[256,2304]{1,0:T(8,128)(2,1)} %copy-done.44, bf16[256,2304]{1,0:T(8,128)(2,1)S(1)} %copy-done.43), kind=kOutput, calls=%fused_computation.4 | convolution fusion | flops 5441126400 | bytes 24772608 | tf_op jit(solution)/shard_map/dot_general | solution.py:48
  307.6 2.1 pad_maximum_fusion.3
  309.6 2.4 copy.40
  312.0 2.4 copy.41
  314.4 3.3 maximum_bitcast_fusion
  321.3 7.4 %collective-permute-done.25 = bf16[64,2304]{1,0:T(8,128)(2,1)S(1)} collective-permute-done((bf16[64,2304]{1,0:T(8,128)(2,1)S(1)}, bf16[64,2304]{1,0:T(8,128)(2,1)S(1)}, u32[]{:S(2)}, u32[]{:S(2)}) %collective-permute-start.25) | collective-permute-done | bytes 294944 | tf_op jit(solution)/shard_map/ppermute | solution.py:62
  328.8 8.8 %collective-permute-done.27 = bf16[64,2304]{1,0:T(8,128)(2,1)S(1)} collective-permute-done((bf16[64,2304]{1,0:T(8,128)(2,1)S(1)}, bf16[64,2304]{1,0:T(8,128)(2,1)S(1)}, u32[]{:S(2)}, u32[]{:S(2)}) %collective-permute-start.27) | collective-permute-done | bytes 294944 | tf_op jit(solution)/shard_map/ppermute | solution.py:62
  337.9 2.0 multiply_reduce_fusion.1
  341.5 9.0 %collective-permute-done.29 = bf16[64,2304]{1,0:T(8,128)(2,1)S(1)} collective-permute-done((bf16[64,2304]{1,0:T(8,128)(2,1)S(1)}, bf16[64,2304]{1,0:T(8,128)(2,1)S(1)}, u32[]{:S(2)}, u32[]{:S(2)}) %collective-permute-start.29) | collective-permute-done | bytes 294944 | tf_op jit(solution)/shard_map/ppermute | solution.py:62
  350.5 4.3 collective-permute-done.28
  354.8 4.1 collective-permute-done.30
  363.6 5.2 %attend_back.1 = (f32[512,256]{1,0:T(8,128)S(1)}, bf16[2048,512]{1,0:T(8,128)(2,1)S(1)}) custom-call(bf16[512,256]{1,0:T(8,128)(2,1)S(1)} %bitcast.65, bf16[512,256]{1,0:T(8,128)(2,1)S(1)} %bitcast.66, f32[512,256]{1,0:T(8,128)S(1)} %copy-done.6, f32[512,1]{1,0:T(8,128)S(1)} %copy-done.10, ...), custom_call_target="tpu_custom_call" | custom-call | tf_op jit(solution)/shard_map/attend_back/pallas_call | solution.py:162
  371.3 3.2 concatenate.149.input_ref
  386.0 4.2 collective-permute-done.33
  391.9 4.5 all-to-all-start
  398.9 2.5 convolution_convert_fusion.3
  401.4 2.5 convolution_convert_fusion.2
  405.2 2.8 attn_products.1
  408.0 2.9 copy-done
  415.6 10.2 %all-to-all-done = bf16[8,2,256,288]{2,3,1,0:T(8,128)(2,1)} async-done(((bf16[8,2,256,288]{2,3,1,0:T(8,128)(2,1)}), bf16[8,2,256,288]{2,3,1,0:T(8,128)(2,1)}, u32[]{:S(2)}, u32[]{:S(2)}) %all-to-all-start) | async-done | bytes 2359328 | tf_op jit(solution)/shard_map/all_to_all | solution.py:313
  436.1 11.2 %collective-permute-done.40 = bf16[64,2304]{1,0:T(8,128)(2,1)S(1)} collective-permute-done((bf16[64,2304]{1,0:T(8,128)(2,1)}, bf16[64,2304]{1,0:T(8,128)(2,1)S(1)}, u32[]{:S(2)}, u32[]{:S(2)}) %collective-permute-start.40) | collective-permute-done | bytes 294944 | tf_op jit(solution)/shard_map/ppermute | solution.py:62
  447.3 7.5 %fusion.2 = f32[288,2304]{1,0:T(8,128)S(1)} fusion(bf16[2048,288]{0,1:T(8,128)(2,1)} %bitcast.76, bf16[2048,4608]{1,0:T(8,128)(2,1)} %all-gather.11.cloned.1.call-done), kind=kOutput, calls=%fused_computation.2 | convolution fusion | flops 2717908992 | bytes 13271040 | tf_op jit(solution)/shard_map/dot_general | solution.py:48
  461.3 4.1 collective-permute-start.45
  467.0 2.1 collective-permute-done.46
  471.6 8.8 %add_reduce_fusion = (f32[288]{0:T(512)S(1)}, f32[288,2304]{1,0:T(8,128)}) fusion(bf16[288,2304]{1,0:T(8,128)(2,1)S(1)} %copy-done.29, f32[288,2304]{1,0:T(8,128)S(1)} %fusion.2, bf16[288,2304]{1,0:T(8,128)(2,1)S(1)} %copy-done.30, bf16[2048,288]{0,1:T(8,128)(2,1)S(1)} %bitcast.77, bf16[2048,4608]{1,0:T(8,128)(2,1)} %all-gather.11.cloned.1.call-done), kind=kOutput, calls=%fused_computation.9 | convolution fusion | flops 2721890048 | bytes 18580608 | tf_op jit(solution)/shard_map/dot_general | solution.py:48
  482.3 4.4 fusion.77
  488.4 2.9 collective-permute-done.49
  (413 shorter events, 127.9 us)
Async XLA Ops:
  7.2 184.7 %all-gather.5.cloned.1.call-start = ((), (), s32[]{:S(2)}) async-start(), calls=%async_computation.2 | async-start | bytes 23887872 | tf_op jit(solution)/shard_map/all_gather | solution.py:306
  10.7 209.1 %all-gather.7.cloned.1.call-start = ((), (), s32[]{:S(2)}) async-start(), calls=%async_computation.3 | async-start | bytes 11943936 | tf_op jit(solution)/shard_map/all_gather | solution.py:306
  11.5 272.3 %all-gather.9.cloned.1.call-start = ((), (), s32[]{:S(2)}) async-start(), calls=%async_computation.4 | async-start | bytes 10616832 | tf_op jit(solution)/shard_map/all_gather | solution.py:306
  12.0 34.7 %collective-permute-start.1 = (bf16[304,1536]{1,0:T(8,128)(2,1)S(1)}, bf16[304,1536]{1,0:T(8,128)(2,1)S(1)}, u32[]{:S(2)}, u32[]{:S(2)}) collective-permute-start(bf16[304,1536]{1,0:T(8,128)(2,1)S(1)} %fusion.27), channel_id=1, source_target_pairs={{0,16},{4,20},{8,24},{12,28},{16,0},{20,4},{24,8},{28,12},{1,17},{... | collective-permute-start | bytes 2801672 | tf_op jit(solution)/shard_map/ppermute | solution.py:62
  15.0 36.4 %collective-permute-start = (bf16[304,1536]{1,0:T(8,128)(2,1)S(1)}, bf16[304,1536]{1,0:T(8,128)(2,1)S(1)}, u32[]{:S(2)}, u32[]{:S(2)}) collective-permute-start(bf16[304,1536]{1,0:T(8,128)(2,1)S(1)} %fusion.27), channel_id=1, source_target_pairs={{0,8},{4,12},{8,0},{12,4},{16,24},{20,28},{24,16},{28,20},{1,9},{5... | collective-permute-start | bytes 2801672 | tf_op jit(solution)/shard_map/ppermute | solution.py:62
  46.8 22.2 %collective-permute-start.2 = (bf16[144,1536]{1,0:T(8,128)(2,1)S(1)}, bf16[144,1536]{1,0:T(8,128)(2,1)S(1)}, u32[]{:S(2)}, u32[]{:S(2)}) collective-permute-start(bf16[144,1536]{1,0:T(8,128)(2,1)S(1)} %slice.301), channel_id=1, source_target_pairs={{0,8},{4,12},{8,0},{12,4},{16,24},{20,28},{24,16},{28,20},{1,9},{5... | collective-permute-start | bytes 1327112 | tf_op jit(solution)/shard_map/ppermute | solution.py:62
  51.5 20.3 %collective-permute-start.3 = (bf16[144,1536]{1,0:T(8,128)(2,1)S(1)}, bf16[144,1536]{1,0:T(8,128)(2,1)S(1)}, u32[]{:S(2)}, u32[]{:S(2)}) collective-permute-start(bf16[144,1536]{1,0:T(8,128)(2,1)S(1)} %slice.302), channel_id=1, source_target_pairs={{0,16},{4,20},{8,24},{12,28},{16,0},{20,4},{24,8},{28,12},{1,17},{... | collective-permute-start | bytes 1327112 | tf_op jit(solution)/shard_map/ppermute | solution.py:62
  72.6 7.4 %collective-permute-start.4 = (bf16[1152,1536]{1,0:T(8,128)(2,1)}, bf16[1152,1536]{1,0:T(8,128)(2,1)}, u32[]{:S(2)}, u32[]{:S(2)}) collective-permute-start(bf16[1152,1536]{1,0:T(8,128)(2,1)} %constant_dynamic-update-slice_fusion), channel_id=1, source_target_pairs={{0,4},{4,0},{8,12},{12,8},{16,20},{20,16},{24,28},{28,24},{1,5},{5... | collective-permute-start | bytes 10616840 | tf_op jit(solution)/shard_map/ppermute | solution.py:62
  88.1 15.5 %collective-permute-start.5 = (bf16[256,512]{1,0:T(8,128)(2,1)}, bf16[256,512]{1,0:T(8,128)(2,1)}, u32[]{:S(2)}, u32[]{:S(2)}) collective-permute-start(bf16[256,512]{1,0:T(8,128)(2,1)} %get-tuple-element.159), channel_id=1, source_target_pairs={{0,8},{4,12},{8,0},{12,4},{16,24},{20,28},{24,16},{28,20},{1,9},{5... | collective-permute-start | bytes 786440 | tf_op jit(solution)/shard_map/ppermute | solution.py:62
  90.6 17.4 %collective-permute-start.6 = (bf16[256,512]{1,0:T(8,128)(2,1)}, bf16[256,512]{1,0:T(8,128)(2,1)}, u32[]{:S(2)}, u32[]{:S(2)}) collective-permute-start(bf16[256,512]{1,0:T(8,128)(2,1)} %get-tuple-element.159), channel_id=1, source_target_pairs={{0,16},{4,20},{8,24},{12,28},{16,0},{20,4},{24,8},{28,12},{1,17},{... | collective-permute-start | bytes 786440 | tf_op jit(solution)/shard_map/ppermute | solution.py:62
  90.6 23.6 %collective-permute-start.7 = (bf16[256,512]{1,0:T(8,128)(2,1)}, bf16[256,512]{1,0:T(8,128)(2,1)}, u32[]{:S(2)}, u32[]{:S(2)}) collective-permute-start(bf16[256,512]{1,0:T(8,128)(2,1)} %get-tuple-element.159), channel_id=1, source_target_pairs={{0,24},{4,28},{8,16},{12,20},{16,8},{20,12},{24,0},{28,4},{1,25},{... | collective-permute-start | bytes 786440 | tf_op jit(solution)/shard_map/ppermute | solution.py:62
  116.3 10.9 %collective-permute-start.8 = (bf16[1024,512]{1,0:T(8,128)(2,1)}, bf16[1024,512]{1,0:T(8,128)(2,1)}, u32[]{:S(2)}, u32[]{:S(2)}) collective-permute-start(bf16[1024,512]{1,0:T(8,128)(2,1)} %pad_maximum_fusion.6), channel_id=1, source_target_pairs={{0,4},{4,0},{8,12},{12,8},{16,20},{20,16},{24,28},{28,24},{1,5},{5... | collective-permute-start | bytes 3145736 | tf_op jit(solution)/shard_map/ppermute | solution.py:62
  136.1 9.9 %collective-permute-start.10 = (bf16[64,2304]{1,0:T(8,128)(2,1)S(1)}, bf16[64,2304]{1,0:T(8,128)(2,1)S(1)}, u32[]{:S(2)}, u32[]{:S(2)}) collective-permute-start(bf16[64,2304]{1,0:T(8,128)(2,1)S(1)} %get-tuple-element.111), channel_id=1, source_target_pairs={{0,1},{1,0},{2,3},{3,2},{4,5},{5,4},{6,7},{7,6},{8,9},{9,8},{10,11... | collective-permute-start | bytes 884744 | tf_op jit(solution)/shard_map/ppermute | solution.py:62
  137.7 19.8 %collective-permute-start.9 = (bf16[64,2304]{1,0:T(8,128)(2,1)}, bf16[64,2304]{1,0:T(8,128)(2,1)}, u32[]{:S(2)}, u32[]{:S(2)}) collective-permute-start(bf16[64,2304]{1,0:T(8,128)(2,1)} %get-tuple-element.110), channel_id=1, source_target_pairs={{0,1},{1,0},{2,3},{3,2},{4,5},{5,4},{6,7},{7,6},{8,9},{9,8},{10,11... | collective-permute-start | bytes 884744 | tf_op jit(solution)/shard_map/ppermute | solution.py:62
  146.9 16.1 %collective-permute-start.11 = (bf16[64,2304]{1,0:T(8,128)(2,1)}, bf16[64,2304]{1,0:T(8,128)(2,1)}, u32[]{:S(2)}, u32[]{:S(2)}) collective-permute-start(bf16[64,2304]{1,0:T(8,128)(2,1)} %add_convert_fusion.6), channel_id=1, source_target_pairs={{0,2},{1,3},{2,0},{3,1},{4,6},{5,7},{6,4},{7,5},{8,10},{9,11},{10,... | collective-permute-start | bytes 884744 | tf_op jit(solution)/shard_map/ppermute | solution.py:62
  151.6 3.6 collective-permute-start.12
  155.3 1.2 collective-permute-start.13
  168.7 33.7 %copy-start.78 = (f32[64]{0:T(128)}, f32[64]{0:T(128)S(1)}, u32[]{:S(2)}) copy-start(f32[64]{0:T(128)S(1)} %add_rsqrt_fusion.3) | copy-start | bytes 772
  168.8 15.1 %collective-permute-start.15 = (bf16[64,2304]{1,0:T(8,128)(2,1)S(1)}, bf16[64,2304]{1,0:T(8,128)(2,1)S(1)}, u32[]{:S(2)}, u32[]{:S(2)}) collective-permute-start(bf16[64,2304]{1,0:T(8,128)(2,1)S(1)} %multiply_convert_fusion.5), channel_id=1, source_target_pairs={{0,2},{1,3},{2,0},{3,1},{4,6},{5,7},{6,4},{7,5},{8,10},{9,11},{10,... | collective-permute-start | bytes 884744 | tf_op jit(solution)/shard_map/ppermute | solution.py:62
  169.5 14.5 %collective-permute-start.14 = (bf16[64,2304]{1,0:T(8,128)(2,1)S(1)}, bf16[64,2304]{1,0:T(8,128)(2,1)S(1)}, u32[]{:S(2)}, u32[]{:S(2)}) collective-permute-start(bf16[64,2304]{1,0:T(8,128)(2,1)S(1)} %multiply_convert_fusion.5), channel_id=1, source_target_pairs={{0,1},{1,0},{2,3},{3,2},{4,5},{5,4},{6,7},{7,6},{8,9},{9,8},{10,11... | collective-permute-start | bytes 884744 | tf_op jit(solution)/shard_map/ppermute | solution.py:62
  184.0 7.9 %collective-permute-start.16 = (bf16[64,2304]{1,0:T(8,128)(2,1)S(1)}, bf16[64,2304]{1,0:T(8,128)(2,1)}, u32[]{:S(2)}, u32[]{:S(2)}) collective-permute-start(bf16[64,2304]{1,0:T(8,128)(2,1)S(1)} %collective-permute-done.15), channel_id=1, source_target_pairs={{0,1},{1,0},{2,3},{3,2},{4,5},{5,4},{6,7},{7,6},{8,9},{9,8},{10,11... | collective-permute-start | bytes 884744 | tf_op jit(solution)/shard_map/ppermute | solution.py:62
  206.5 198.7 %all-gather.11.cloned.1.call-start = ((), (), s32[]{:S(2)}) async-start(), calls=%async_computation.5 | async-start | bytes 21233664 | tf_op jit(solution)/shard_map/all_gather | solution.py:306
  219.8 53.9 %copy-start.87 = (bf16[2304,2304]{1,0:T(8,128)(2,1)S(1)}, bf16[2304,2304]{1,0:T(8,128)(2,1)}, u32[]{:S(2)}) copy-start(bf16[2304,2304]{1,0:T(8,128)(2,1)} %all-gather.7.cloned.1.call-done) | copy-start | bytes 31850500
  227.3 25.4 %copy-start.46 = (bf16[256,2304]{1,0:T(8,128)(2,1)S(1)}, bf16[256,2304]{1,0:T(8,128)(2,1)}, u32[]{:S(2)}) copy-start(bf16[256,2304]{1,0:T(8,128)(2,1)} %param.27) | copy-start | bytes 3538948
  227.3 25.4 %copy-start.66 = (f32[2304]{0:T(1024)S(1)}, f32[2304]{0:T(1024)}, u32[]{:S(2)}) copy-start(f32[2304]{0:T(1024)} %get-tuple-element.78) | copy-start | bytes 27652
  227.4 26.3 %copy-start.14 = (bf16[64,2304]{1,0:T(8,128)(2,1)}, bf16[64,2304]{1,0:T(8,128)(2,1)S(1)}, u32[]{:S(2)}) copy-start(bf16[64,2304]{1,0:T(8,128)(2,1)S(1)} %get-tuple-element.106) | copy-start | bytes 884740
  227.4 9.9 %collective-permute-start.18 = (bf16[64,2304]{1,0:T(8,128)(2,1)S(1)}, bf16[64,2304]{1,0:T(8,128)(2,1)S(1)}, u32[]{:S(2)}, u32[]{:S(2)}) collective-permute-start(bf16[64,2304]{1,0:T(8,128)(2,1)S(1)} %get-tuple-element.107), channel_id=1, source_target_pairs={{0,1},{1,0},{2,3},{3,2},{4,5},{5,4},{6,7},{7,6},{8,9},{9,8},{10,11... | collective-permute-start | bytes 884744 | tf_op jit(solution)/shard_map/ppermute | solution.py:62
  228.9 19.0 %collective-permute-start.17 = (bf16[64,2304]{1,0:T(8,128)(2,1)S(1)}, bf16[64,2304]{1,0:T(8,128)(2,1)S(1)}, u32[]{:S(2)}, u32[]{:S(2)}) collective-permute-start(bf16[64,2304]{1,0:T(8,128)(2,1)S(1)} %get-tuple-element.108), channel_id=1, source_target_pairs={{0,1},{1,0},{2,3},{3,2},{4,5},{5,4},{6,7},{7,6},{8,9},{9,8},{10,11... | collective-permute-start | bytes 884744 | tf_op jit(solution)/shard_map/ppermute | solution.py:62
  237.4 15.1 %collective-permute-start.19 = (bf16[64,2304]{1,0:T(8,128)(2,1)S(1)}, bf16[64,2304]{1,0:T(8,128)(2,1)S(1)}, u32[]{:S(2)}, u32[]{:S(2)}) collective-permute-start(bf16[64,2304]{1,0:T(8,128)(2,1)S(1)} %add_convert_fusion.5), channel_id=1, source_target_pairs={{0,2},{1,3},{2,0},{3,1},{4,6},{5,7},{6,4},{7,5},{8,10},{9,11},{10,... | collective-permute-start | bytes 884744 | tf_op jit(solution)/shard_map/ppermute | solution.py:62
  253.9 26.9 %copy-start.35 = (bf16[64,2304]{1,0:T(8,128)(2,1)}, bf16[64,2304]{1,0:T(8,128)(2,1)S(1)}, u32[]{:S(2)}) copy-start(bf16[64,2304]{1,0:T(8,128)(2,1)S(1)} %fusion.32) | copy-start | bytes 884740
  253.9 12.3 %collective-permute-start.21 = (bf16[64,2304]{1,0:T(8,128)(2,1)S(1)}, bf16[64,2304]{1,0:T(8,128)(2,1)S(1)}, u32[]{:S(2)}, u32[]{:S(2)}) collective-permute-start(bf16[64,2304]{1,0:T(8,128)(2,1)S(1)} %fusion.32), channel_id=1, source_target_pairs={{0,2},{1,3},{2,0},{3,1},{4,6},{5,7},{6,4},{7,5},{8,10},{9,11},{10,... | collective-permute-start | bytes 884744 | tf_op jit(solution)/shard_map/ppermute | solution.py:62
  254.0 12.9 %collective-permute-start.20 = (bf16[64,2304]{1,0:T(8,128)(2,1)S(1)}, bf16[64,2304]{1,0:T(8,128)(2,1)S(1)}, u32[]{:S(2)}, u32[]{:S(2)}) collective-permute-start(bf16[64,2304]{1,0:T(8,128)(2,1)S(1)} %fusion.32), channel_id=1, source_target_pairs={{0,1},{1,0},{2,3},{3,2},{4,5},{5,4},{6,7},{7,6},{8,9},{9,8},{10,11... | collective-permute-start | bytes 884744 | tf_op jit(solution)/shard_map/ppermute | solution.py:62
  266.2 7.4 %collective-permute-start.22 = (bf16[64,2304]{1,0:T(8,128)(2,1)S(1)}, bf16[64,2304]{1,0:T(8,128)(2,1)S(1)}, u32[]{:S(2)}, u32[]{:S(2)}) collective-permute-start(bf16[64,2304]{1,0:T(8,128)(2,1)S(1)} %collective-permute-done.21), channel_id=1, source_target_pairs={{0,1},{1,0},{2,3},{3,2},{4,5},{5,4},{6,7},{7,6},{8,9},{9,8},{10,11... | collective-permute-start | bytes 884744 | tf_op jit(solution)/shard_map/ppermute | solution.py:62
  288.3 17.3 %collective-permute-start.23 = (bf16[64,2304]{1,0:T(8,128)(2,1)}, bf16[64,2304]{1,0:T(8,128)(2,1)S(1)}, u32[]{:S(2)}, u32[]{:S(2)}) collective-permute-start(bf16[64,2304]{1,0:T(8,128)(2,1)} %get-tuple-element.49), channel_id=1, source_target_pairs={{0,1},{1,0},{2,3},{3,2},{4,5},{5,4},{6,7},{7,6},{8,9},{9,8},{10,11... | collective-permute-start | bytes 884744 | tf_op jit(solution)/shard_map/ppermute | solution.py:62
  290.1 15.5 %collective-permute-start.24 = (bf16[64,2304]{1,0:T(8,128)(2,1)}, bf16[64,2304]{1,0:T(8,128)(2,1)}, u32[]{:S(2)}, u32[]{:S(2)}) collective-permute-start(bf16[64,2304]{1,0:T(8,128)(2,1)} %get-tuple-element.49), channel_id=1, source_target_pairs={{0,2},{1,3},{2,0},{3,1},{4,6},{5,7},{6,4},{7,5},{8,10},{9,11},{10,... | collective-permute-start | bytes 884744 | tf_op jit(solution)/shard_map/ppermute | solution.py:62
  306.7 12.2 %collective-permute-start.26 = (bf16[64,2304]{1,0:T(8,128)(2,1)}, bf16[64,2304]{1,0:T(8,128)(2,1)}, u32[]{:S(2)}, u32[]{:S(2)}) collective-permute-start(bf16[64,2304]{1,0:T(8,128)(2,1)} %get-tuple-element.103), channel_id=1, source_target_pairs={{0,1},{1,0},{2,3},{3,2},{4,5},{5,4},{6,7},{7,6},{8,9},{9,8},{10,11... | collective-permute-start | bytes 884744 | tf_op jit(solution)/shard_map/ppermute | solution.py:62
  317.7 11.1 %collective-permute-start.25 = (bf16[64,2304]{1,0:T(8,128)(2,1)S(1)}, bf16[64,2304]{1,0:T(8,128)(2,1)S(1)}, u32[]{:S(2)}, u32[]{:S(2)}) collective-permute-start(bf16[64,2304]{1,0:T(8,128)(2,1)S(1)} %copy-done.59), channel_id=1, source_target_pairs={{0,1},{1,0},{2,3},{3,2},{4,5},{5,4},{6,7},{7,6},{8,9},{9,8},{10,11... | collective-permute-start | bytes 884744 | tf_op jit(solution)/shard_map/ppermute | solution.py:62
  319.9 17.7 %collective-permute-start.27 = (bf16[64,2304]{1,0:T(8,128)(2,1)S(1)}, bf16[64,2304]{1,0:T(8,128)(2,1)S(1)}, u32[]{:S(2)}, u32[]{:S(2)}) collective-permute-start(bf16[64,2304]{1,0:T(8,128)(2,1)S(1)} %add_convert_fusion.3), channel_id=1, source_target_pairs={{0,2},{1,3},{2,0},{3,1},{4,6},{5,7},{6,4},{7,5},{8,10},{9,11},{10,... | collective-permute-start | bytes 884744 | tf_op jit(solution)/shard_map/ppermute | solution.py:62
  341.2 9.2 %collective-permute-start.29 = (bf16[64,2304]{1,0:T(8,128)(2,1)S(1)}, bf16[64,2304]{1,0:T(8,128)(2,1)S(1)}, u32[]{:S(2)}, u32[]{:S(2)}) collective-permute-start(bf16[64,2304]{1,0:T(8,128)(2,1)S(1)} %concatenate.143), channel_id=1, source_target_pairs={{0,2},{1,3},{2,0},{3,1},{4,6},{5,7},{6,4},{7,5},{8,10},{9,11},{10,... | collective-permute-start | bytes 884744 | tf_op jit(solution)/shard_map/ppermute | solution.py:62
  341.3 13.4 %collective-permute-start.28 = (bf16[64,2304]{1,0:T(8,128)(2,1)S(1)}, bf16[64,2304]{1,0:T(8,128)(2,1)S(1)}, u32[]{:S(2)}, u32[]{:S(2)}) collective-permute-start(bf16[64,2304]{1,0:T(8,128)(2,1)S(1)} %concatenate.143), channel_id=1, source_target_pairs={{0,1},{1,0},{2,3},{3,2},{4,5},{5,4},{6,7},{7,6},{8,9},{9,8},{10,11... | collective-permute-start | bytes 884744 | tf_op jit(solution)/shard_map/ppermute | solution.py:62
  350.5 8.4 %collective-permute-start.30 = (bf16[64,2304]{1,0:T(8,128)(2,1)S(1)}, bf16[64,2304]{1,0:T(8,128)(2,1)S(1)}, u32[]{:S(2)}, u32[]{:S(2)}) collective-permute-start(bf16[64,2304]{1,0:T(8,128)(2,1)S(1)} %collective-permute-done.29), channel_id=1, source_target_pairs={{0,1},{1,0},{2,3},{3,2},{4,5},{5,4},{6,7},{7,6},{8,9},{9,8},{10,11... | collective-permute-start | bytes 884744 | tf_op jit(solution)/shard_map/ppermute | solution.py:62
  371.3 7.3 %collective-permute-start.32 = (bf16[1024,512]{1,0:T(8,128)(2,1)}, bf16[1024,512]{1,0:T(8,128)(2,1)}, u32[]{:S(2)}, u32[]{:S(2)}) collective-permute-start(bf16[1024,512]{1,0:T(8,128)(2,1)} %slice.268), channel_id=1, source_target_pairs={{0,4},{4,0},{8,12},{12,8},{16,20},{20,16},{24,28},{28,24},{1,5},{5... | collective-permute-start | bytes 3145736 | tf_op jit(solution)/shard_map/ppermute | solution.py:62
  381.1 9.2 %collective-permute-start.33 = (bf16[256,512]{1,0:T(8,128)(2,1)S(1)}, bf16[256,512]{1,0:T(8,128)(2,1)}, u32[]{:S(2)}, u32[]{:S(2)}) collective-permute-start(bf16[256,512]{1,0:T(8,128)(2,1)S(1)} %get-tuple-element.124), channel_id=1, source_target_pairs={{0,8},{4,12},{8,0},{12,4},{16,24},{20,28},{24,16},{28,20},{1,9},{5... | collective-permute-start | bytes 786440 | tf_op jit(solution)/shard_map/ppermute | solution.py:62
  382.6 14.3 %collective-permute-start.34 = (bf16[256,512]{1,0:T(8,128)(2,1)}, bf16[256,512]{1,0:T(8,128)(2,1)}, u32[]{:S(2)}, u32[]{:S(2)}) collective-permute-start(bf16[256,512]{1,0:T(8,128)(2,1)} %get-tuple-element.126), channel_id=1, source_target_pairs={{0,16},{4,20},{8,24},{12,28},{16,0},{20,4},{24,8},{28,12},{1,17},{... | collective-permute-start | bytes 786440 | tf_op jit(solution)/shard_map/ppermute | solution.py:62
  383.1 13.8 %collective-permute-start.35 = (bf16[256,512]{1,0:T(8,128)(2,1)}, bf16[256,512]{1,0:T(8,128)(2,1)}, u32[]{:S(2)}, u32[]{:S(2)}) collective-permute-start(bf16[256,512]{1,0:T(8,128)(2,1)} %get-tuple-element.125), channel_id=1, source_target_pairs={{0,24},{4,28},{8,16},{12,20},{16,8},{20,12},{24,0},{28,4},{1,25},{... | collective-permute-start | bytes 786440 | tf_op jit(solution)/shard_map/ppermute | solution.py:62
  385.9 25.1 %collective-permute-start.31 = (bf16[64,2304]{1,0:T(8,128)(2,1)}, bf16[64,2304]{1,0:T(8,128)(2,1)}, u32[]{:S(2)}, u32[]{:S(2)}) collective-permute-start(bf16[64,2304]{1,0:T(8,128)(2,1)} %collective-permute-done.24), channel_id=1, source_target_pairs={{0,1},{1,0},{2,3},{3,2},{4,5},{5,4},{6,7},{7,6},{8,9},{9,8},{10,11... | collective-permute-start | bytes 884744 | tf_op jit(solution)/shard_map/ppermute | solution.py:62
  391.9 34.0 %all-to-all-start = ((bf16[8,2,256,288]{2,3,1,0:T(8,128)(2,1)}), bf16[8,2,256,288]{2,3,1,0:T(8,128)(2,1)}, u32[]{:S(2)}, u32[]{:S(2)}) async-start(bf16[8,2,256,288]{2,3,1,0:T(8,128)(2,1)} %copy.45), calls=%async_computation | async-start | bytes 4718592 | tf_op jit(solution)/shard_map/all_to_all | solution.py:313
  396.4 95.4 %reduce-scatter.2.cloned.1.call-start = ((), (), s32[]{:S(2)}) async-start(), calls=%async_computation.6 | async-start | bytes 7962624 | tf_op jit(solution)/shard_map/reduce_scatter | solution.py:319
  404.9 9.6 %collective-permute-start.37 = (bf16[64,2304]{1,0:T(8,128)(2,1)}, bf16[64,2304]{1,0:T(8,128)(2,1)}, u32[]{:S(2)}, u32[]{:S(2)}) collective-permute-start(bf16[64,2304]{1,0:T(8,128)(2,1)} %get-tuple-element.101), channel_id=1, source_target_pairs={{0,1},{1,0},{2,3},{3,2},{4,5},{5,4},{6,7},{7,6},{8,9},{9,8},{10,11... | collective-permute-start | bytes 884744 | tf_op jit(solution)/shard_map/ppermute | solution.py:62
  412.7 17.4 %collective-permute-start.36 = (bf16[64,2304]{1,0:T(8,128)(2,1)S(1)}, bf16[64,2304]{1,0:T(8,128)(2,1)S(1)}, u32[]{:S(2)}, u32[]{:S(2)}) collective-permute-start(bf16[64,2304]{1,0:T(8,128)(2,1)S(1)} %copy-done.52), channel_id=1, source_target_pairs={{0,1},{1,0},{2,3},{3,2},{4,5},{5,4},{6,7},{7,6},{8,9},{9,8},{10,11... | collective-permute-start | bytes 884744 | tf_op jit(solution)/shard_map/ppermute | solution.py:62
  415.5 15.6 %collective-permute-start.38 = (bf16[64,2304]{1,0:T(8,128)(2,1)S(1)}, bf16[64,2304]{1,0:T(8,128)(2,1)S(1)}, u32[]{:S(2)}, u32[]{:S(2)}) collective-permute-start(bf16[64,2304]{1,0:T(8,128)(2,1)S(1)} %add_convert_fusion.2), channel_id=1, source_target_pairs={{0,2},{1,3},{2,0},{3,1},{4,6},{5,7},{6,4},{7,5},{8,10},{9,11},{10,... | collective-permute-start | bytes 884744 | tf_op jit(solution)/shard_map/ppermute | solution.py:62
  435.1 12.2 %collective-permute-start.40 = (bf16[64,2304]{1,0:T(8,128)(2,1)}, bf16[64,2304]{1,0:T(8,128)(2,1)S(1)}, u32[]{:S(2)}, u32[]{:S(2)}) collective-permute-start(bf16[64,2304]{1,0:T(8,128)(2,1)} %add_convert_fusion.1), channel_id=1, source_target_pairs={{0,2},{1,3},{2,0},{3,1},{4,6},{5,7},{6,4},{7,5},{8,10},{9,11},{10,... | collective-permute-start | bytes 884744 | tf_op jit(solution)/shard_map/ppermute | solution.py:62
  435.1 24.9 %collective-permute-start.39 = (bf16[64,2304]{1,0:T(8,128)(2,1)}, bf16[64,2304]{1,0:T(8,128)(2,1)S(1)}, u32[]{:S(2)}, u32[]{:S(2)}) collective-permute-start(bf16[64,2304]{1,0:T(8,128)(2,1)} %add_convert_fusion.1), channel_id=1, source_target_pairs={{0,1},{1,0},{2,3},{3,2},{4,5},{5,4},{6,7},{7,6},{8,9},{9,8},{10,11... | collective-permute-start | bytes 884744 | tf_op jit(solution)/shard_map/ppermute | solution.py:62
  447.3 7.6 %collective-permute-start.42 = (f32[3,2304]{1,0:T(4,128)S(1)}, f32[3,2304]{1,0:T(4,128)S(1)}, u32[]{:S(2)}, u32[]{:S(2)}) collective-permute-start(f32[3,2304]{1,0:T(4,128)S(1)} %concatenate.151), channel_id=1, source_target_pairs={{0,1},{1,0},{2,3},{3,2},{4,5},{5,4},{6,7},{7,6},{8,9},{9,8},{10,11... | collective-permute-start | bytes 82952 | tf_op jit(solution)/shard_map/ppermute | solution.py:62
  447.3 24.3 %copy-start.40 = (bf16[36,8,8,256]{3,1,2,0:T(8,128)(2,1)S(1)}, bf16[36,8,8,256]{3,1,2,0:T(8,128)(2,1)}, u32[]{:S(2)}) copy-start(bf16[36,8,8,256]{3,1,2,0:T(8,128)(2,1)} %copy.52) | copy-start | bytes 3538948
  454.8 25.6 %copy-start.88 = (f32[288,2304]{1,0:T(8,128)}, f32[288,2304]{1,0:T(8,128)S(1)}, u32[]{:S(2)}) copy-start(f32[288,2304]{1,0:T(8,128)S(1)} %fusion.2) | copy-start | bytes 7962628
  454.9 5.0 %collective-permute-start.43 = (f32[3,2304]{1,0:T(4,128)S(1)}, f32[3,2304]{1,0:T(4,128)S(1)}, u32[]{:S(2)}, u32[]{:S(2)}) collective-permute-start(f32[3,2304]{1,0:T(4,128)S(1)} %add.558), channel_id=1, source_target_pairs={{0,2},{1,3},{2,0},{3,1},{4,6},{5,7},{6,4},{7,5},{8,10},{9,11},{10,... | collective-permute-start | bytes 82952 | tf_op jit(solution)/shard_map/ppermute | solution.py:62
  457.6 13.9 %collective-permute-start.41 = (bf16[64,2304]{1,0:T(8,128)(2,1)S(1)}, bf16[64,2304]{1,0:T(8,128)(2,1)S(1)}, u32[]{:S(2)}, u32[]{:S(2)}) collective-permute-start(bf16[64,2304]{1,0:T(8,128)(2,1)S(1)} %collective-permute-done.40), channel_id=1, source_target_pairs={{0,1},{1,0},{2,3},{3,2},{4,5},{5,4},{6,7},{7,6},{8,9},{9,8},{10,11... | collective-permute-start | bytes 884744 | tf_op jit(solution)/shard_map/ppermute | solution.py:62
  459.9 1.3 collective-permute-start.44
  461.3 5.7 %collective-permute-start.45 = (f32[3,288]{1,0:T(4,128)S(1)}, f32[3,288]{1,0:T(4,128)S(1)}, u32[]{:S(2)}, u32[]{:S(2)}) collective-permute-start(f32[3,288]{1,0:T(4,128)S(1)} %get-tuple-element.169), channel_id=1, source_target_pairs={{0,8},{4,12},{8,0},{12,4},{16,24},{20,28},{24,16},{28,20},{1,9},{5... | collective-permute-start | bytes 10376 | tf_op jit(solution)/shard_map/ppermute | solution.py:62
  465.3 3.8 collective-permute-start.46
  465.7 4.6 collective-permute-start.47
  480.4 6.4 %collective-permute-start.48 = (f32[1,288]{1,0:T(1,128)S(1)}, f32[1,288]{1,0:T(1,128)S(1)}, u32[]{:S(2)}, u32[]{:S(2)}) collective-permute-start(f32[1,288]{1,0:T(1,128)S(1)} %broadcast_in_dim.8), channel_id=1, source_target_pairs={{0,1},{1,0},{2,3},{3,2},{4,5},{5,4},{6,7},{7,6},{8,9},{9,8},{10,11... | collective-permute-start | bytes 3464 | tf_op jit(solution)/shard_map/ppermute | solution.py:62
  486.8 4.5 collective-permute-start.49
  (84 other events, 492.1 us)
Sparse Core Ops, SparseCore 0:
  10.8 143.2 all-gather.4
  156.0 63.8 all-gather.6
  222.3 58.8 all-gather.8
  283.9 99.9 all-gather.10
  411.1 65.0 reduce-scatter.1

commit v4 on v3

--- a/solution.py
+++ b/solution.py
@@ -244,10 +244,16 @@
             pair_sum = partial
             arrived = [swap(pieces[step], step, "tp") for step in range(1, layers)]
         done_second = second(pair_sum) if second else ()
-        total = after(pieces[0], *done_first, *done_second).astype(f32)
+        if done_first or done_second:
+            arrived[0] = after(arrived[0], *done_first, *done_second)
+        return (partial, arrived), done_first, done_second
+
+    def sum_of(parts):
+        partial, arrived = parts
+        total = partial[:own_rows].astype(f32)
         for piece in arrived:
             total = total + piece.astype(f32)
-        return total, done_first, done_second
+        return total
 
     def layer_gather(rows, first=None, second=None):
         done_first = first(rows) if first else ()
@@ -305,15 +311,98 @@
     def rows_of_all(array):
         return lax.all_gather(array, "ctx", axis=0, tiled=True)
 
-    def columns_by_owner(*arrays):
-        stacked = jnp.stack([array.reshape(tok_rows, ring, shard) for array in arrays])
-        return stacked.transpose(2, 0, 1, 3)
-
-    def columns_of_owner(stacked):
-        found = lax.all_to_all(stacked, "ctx", split_axis=0, concat_axis=0, tiled=True)
-        return [
-            found[:, index].reshape(ring * tok_rows, shard) for index in range(found.shape[1])
-        ]
+    def in_order(me_ref, source_ref, target_ref, inverse):
+        for index in range(ring):
+
+            @pl.when(me_ref[0] == index)
+            def _():
+                for place, block in enumerate(order):
+                    here = slice(place * shard, (place + 1) * shard)
+                    there = slice((index ^ block) * shard, ((index ^ block) + 1) * shard)
+                    if inverse:
+                        target_ref[:, there] = source_ref[:, here]
+                    else:
+                        target_ref[:, here] = source_ref[:, there]
+
+    in_kernels = ring <= 8 and own_rows % 16 == 0 and layers == 4
+
+    def on_own_rows(body, partial, arrived, others, outs, name, scratch=1):
+        def kernel(me_ref, part_ref, one_ref, two_ref, *refs):
+            total = part_ref[...].astype(f32) + one_ref[...].astype(f32) + two_ref[...].astype(f32)
+            body(me_ref, total, *refs)
+
+        wide = pl.BlockSpec((own_rows, width), lambda step: (0, 0))
+        return pl.pallas_call(
+            kernel,
+            grid=(1,),
+            in_specs=[SCALARS, wide] + [WHOLE] * (2 + len(others)),
+            out_specs=[WHOLE] * len(outs),
+            out_shape=[shape_of((rows, width), kind) for rows, kind in outs],
+            scratch_shapes=[pltpu.VMEM((own_rows, width), f32)] * scratch,
+            compiler_params=pltpu.CompilerParams(vmem_limit_bytes=VMEM_BYTES),
+            name=name,
+        )(me[None], partial, *arrived, *others)
+
+    def residual_body(me_ref, total, tok_ref, gain_ref, attn_ref, hidden_ref, input_ref, held_ref):
+        held_ref[...] = total
+        in_order(me_ref, held_ref, attn_ref, True)
+        attn = attn_ref[...]
+        hidden = tok_ref[...] + attn * rms_scale(attn) * gain_ref[0:1, :]
+        hidden_ref[...] = hidden
+        input_ref[...] = (hidden * rms_scale(hidden) * gain_ref[1:2, :]).astype(bf16)
+
+    def output_body(me_ref, total, hidden_ref, cot_ref, gain_ref, out_ref, grad_ref, gain_grad_ref):
+        inverse = rms_scale(total)
+        normed = total * inverse
+        gain, cot = gain_ref[2:3, :], cot_ref[...]
+        out_ref[...] = (hidden_ref[...] + normed * gain).astype(bf16)
+        gain_grad_ref[...] = jnp.sum(cot * normed, axis=0, keepdims=True)
+        grad_ref[...] = norm_back(inverse, normed, cot * gain).astype(bf16)
+
+    def residual_back_body(
+        me_ref, total, hidden_ref, attn_ref, cot_ref, gain_ref, res_ref, grad_ref, gain_grad_ref, held_ref, moved_ref
+    ):
+        hidden, attn = hidden_ref[...], attn_ref[...]
+        inverse = rms_scale(hidden)
+        res = cot_ref[...] + norm_back(inverse, hidden * inverse, total * gain_ref[1:2, :])
+        res_ref[...] = res
+        inverse = rms_scale(attn)
+        normed = attn * inverse
+        gain_grad_ref[...] = jnp.sum(res * normed, axis=0, keepdims=True)
+        held_ref[...] = norm_back(inverse, normed, res * gain_ref[0:1, :])
+        in_order(me_ref, held_ref, moved_ref, False)
+        grad_ref[...] = moved_ref[...].astype(bf16)
+
+    def token_back_body(me_ref, total, tok_ref, res_ref, gain_ref, grad_ref, gain_grad_ref, held_ref, moved_ref):
+        held_ref[...] = total
+        in_order(me_ref, held_ref, moved_ref, True)
+        tok, grad = tok_ref[...], moved_ref[...]
+        inverse = rms_scale(tok)
+        normed = tok * inverse
+        gain_grad_ref[...] = jnp.sum(grad * normed, axis=0, keepdims=True)
+        grad_ref[...] = (
+            res_ref[...] + norm_back(inverse, normed, grad * gain_ref[3:4, :])
+        ).astype(bf16)
+
+    def by_owner_kernel(first_ref, second_ref, out_ref):
+        for block in range(ring):
+            here = slice(block * shard, (block + 1) * shard)
+            out_ref[block, :, :shard] = first_ref[:, here]
+            out_ref[block, :, shard:] = second_ref[:, here]
+
+    def columns_by_owner(first, second):
+        rows = first.shape[0]
+        if not in_kernels:
+            stacked = jnp.stack([array.reshape(rows, ring, shard) for array in (first, second)])
+            return stacked.transpose(2, 1, 0, 3).reshape(ring, rows, 2 * shard)
+        return pl.pallas_call(
+            by_owner_kernel,
+            in_specs=[WHOLE] * 2,
+            out_specs=WHOLE,
+            out_shape=shape_of((ring, rows, 2 * shard), bf16),
+            compiler_params=pltpu.CompilerParams(vmem_limit_bytes=VMEM_BYTES),
+            name="by_owner",
+        )(first, second)
 
     def sum_scatter(partial):
         return lax.psum_scatter(
@@ -345,35 +434,35 @@
             name="attn_products",
         )(me[None], inputs, lin, grads, rows)
 
-    first_gain = norm_attn_in.astype(f32)[:, None]
     gate_up = rows_of_all(jnp.concatenate([w_gate, w_up], axis=1))
     down_w = rows_of_all(w_down)
-    qkv_own = (
-        jnp.concatenate([w_query, w_key, w_value], axis=1).astype(f32) * first_gain
-    ).astype(bf16)
-    attn_own = jnp.concatenate([qkv_own, w_out], axis=1)
-    own_gains = jnp.stack([norm_attn_out, norm_ffn_in, norm_ffn_out])
-    gain_rows = jnp.zeros((16, attn_own.shape[1]), bf16).at[:3, :shard].set(own_gains)
+    attn_own = jnp.concatenate([w_query, w_key, w_value, w_out], axis=1)
+    own_gains = jnp.stack([norm_attn_out, norm_ffn_in, norm_ffn_out, norm_attn_in])
+    gain_rows = jnp.zeros((16, attn_own.shape[1]), bf16).at[:4, :shard].set(own_gains)
     from_a, from_b, top, bottom = spread_far(jnp.concatenate([attn_own, gain_rows], axis=0))
     attn_w = spread_near(
         jnp.concatenate([attn_own, from_a[:shard], from_b[:shard], top, bottom], axis=0)
     )
     qkv_w = [block[:, :qkv_width] for block in attn_w]
     out_w = [block[:, qkv_width:] for block in attn_w]
-    gain_a, gain_b = (held[shard : shard + 3, :shard] for held in (from_a, from_b))
+    gain_a, gain_b = (held[shard : shard + 4, :shard] for held in (from_a, from_b))
     gains = jnp.concatenate(
         spread_near(
             jnp.concatenate([own_gains, gain_a, gain_b, swap(gain_b, far_a)], axis=1)
         ),
         axis=1,
     )
-    gain_two, gain_three, gain_four = jnp.split(columns_out(gains).astype(f32), 3)
+    all_gains = columns_out(gains).astype(f32)
+    gain_two, gain_three, gain_four, gain_one = jnp.split(all_gains, 4)
 
     tok_float = rows_in(tokens).astype(f32)
     own_cot = lax.dynamic_slice_in_dim(cotangent, my_layer * own_rows, own_rows, 0).astype(f32)
-    norm_input = (tok_float * rms_scale(tok_float)).astype(bf16)
     own_tok = tok_float[:own_rows]
-    attn_input = columns_in(norm_input)
+    attn_input = lax.optimization_barrier(
+        (
+            columns_in(rows_in(tokens)).astype(f32) * rms_scale(tok_float) * gains[3:].astype(f32)
+        ).astype(bf16)
+    )
     lin = times_rows(attn_input, qkv_w)
     row_place = jnp.concatenate(
         [
@@ -411,14 +500,20 @@
     key_places = jnp.concatenate([(me ^ block) * tok_rows + row_place for block in order])[None, :]
     places = jnp.tile(query_pos, heads_local)[:, None]
     attn_float, attn_rows, attn_log = attend(query_rows, pairs, places, key_places, heads_local)
-    attn_total, _, _ = layer_scatter(times_rows_t(attn_rows, out_w).astype(bf16))
-    attn_total = columns_out(attn_total)
-    inv_two = rms_scale(attn_total)
-    normed_two = attn_total * inv_two
-    hidden_res = own_tok + normed_two * gain_two
-    inv_three = rms_scale(hidden_res)
-    normed_three = hidden_res * inv_three
-    pieces, _, _ = layer_gather((normed_three * gain_three).astype(bf16))
+    parts, _, _ = layer_scatter(times_rows_t(attn_rows, out_w).astype(bf16))
+    if in_kernels:
+        attn_total, hidden_res, own_input = on_own_rows(
+            residual_body,
+            *parts,
+            (own_tok, all_gains),
+            [(own_rows, f32), (own_rows, f32), (own_rows, bf16)],
+            "residual",
+        )
+    else:
+        attn_total = columns_out(sum_of(parts))
+        hidden_res = own_tok + attn_total * rms_scale(attn_total) * gain_two
+        own_input = (hidden_res * rms_scale(hidden_res) * gain_three).astype(bf16)
+    pieces, _, _ = layer_gather(own_input)
     ffn_input = jnp.concatenate(pieces, axis=0)
 
     both_lin = product(ffn_input, gate_up)
@@ -427,14 +522,34 @@
     hidden_b = (activated * up_lin).astype(bf16)
     if gather_factors:
         all_hidden = rows_of_all(hidden_b)
-    ffn_total, _, _ = layer_scatter(contract(hidden_b, down_w, 1, 1).astype(bf16))
-    inv_four = rms_scale(ffn_total)
-    normed_four = ffn_total * inv_four
-    own_output = (hidden_res + normed_four * gain_four).astype(bf16)
-
-    grad_gain_four = jnp.sum(own_cot * normed_four, axis=0)
-    pieces, _, _ = layer_gather(norm_back(inv_four, normed_four, own_cot * gain_four).astype(bf16))
+    parts, _, _ = layer_scatter(contract(hidden_b, down_w, 1, 1).astype(bf16))
+    if in_kernels:
+        own_output, own_grad_ffn, grad_gain_four = on_own_rows(
+            output_body,
+            *parts,
+            (hidden_res, own_cot, all_gains),
+            [(own_rows, bf16), (own_rows, bf16), (1, f32)],
+            "output",
+            scratch=0,
+        )
+    else:
+        ffn_total = sum_of(parts)
+        inv_four = rms_scale(ffn_total)
+        normed_four = ffn_total * inv_four
+        own_output = (hidden_res + normed_four * gain_four).astype(bf16)
+        grad_gain_four = jnp.sum(own_cot * normed_four, axis=0, keepdims=True)
+        own_grad_ffn = norm_back(inv_four, normed_four, own_cot * gain_four).astype(bf16)
+
+    pieces, _, _ = layer_gather(own_grad_ffn)
     grad_ffn = jnp.concatenate(pieces, axis=0)
+    if gather_factors:
+        own_columns = lax.all_to_all(
+            columns_by_owner(own_input, own_grad_ffn),
+            "ctx",
+            split_axis=0,
+            concat_axis=0,
+            tiled=True,
+        )
     sent_output = after(own_output, grad_ffn)
     if layers == 4:
         output_pieces = [own_output, swap(sent_output, 1, "tp"), swap(sent_output, 2, "tp")]
@@ -452,23 +567,41 @@
         grad_w_gate, grad_w_up = grad_w_both[:, :ffn_width], grad_w_both[:, ffn_width:]
     grad_in_part = contract(grad_both, gate_up, 1, 1).astype(bf16)
     grad_in_part = after(grad_in_part, *output_pieces[1:])
-    if gather_factors:
-        grad_ffn_in, (by_owner,), _ = layer_scatter(
-            grad_in_part, lambda then: (columns_by_owner(ffn_input, after(grad_ffn, then)),)
+    parts, _, _ = layer_scatter(grad_in_part)
+    if in_kernels:
+        grad_res, own_grad_attn, grad_gain_two = on_own_rows(
+            residual_back_body,
+            *parts,
+            (hidden_res, attn_total, own_cot, all_gains),
+            [(own_rows, f32), (own_rows, bf16), (1, f32)],
+            "residual_back",
+            scratch=2,
         )
     else:
-        grad_ffn_in, _, _ = layer_scatter(grad_in_part)
-    grad_res = own_cot + norm_back(inv_three, normed_three, grad_ffn_in * gain_three)
-    grad_gain_two = jnp.sum(grad_res * normed_two, axis=0)
-
-    own_grad_attn = norm_back(inv_two, normed_two, grad_res * gain_two)
-    pieces, _, _ = layer_gather(columns_in(own_grad_attn.astype(bf16)))
+        inv_three = rms_scale(hidden_res)
+        grad_res = own_cot + norm_back(
+            inv_three, hidden_res * inv_three, sum_of(parts) * gain_three
+        )
+        inv_two = rms_scale(attn_total)
+        normed_two = attn_total * inv_two
+        grad_gain_two = jnp.sum(grad_res * normed_two, axis=0, keepdims=True)
+        own_grad_attn = norm_back(inv_two, normed_two, grad_res * gain_two)
+        own_grad_attn = columns_in(own_grad_attn.astype(bf16))
+
+    pieces, _, _ = layer_gather(own_grad_attn)
     grad_attn = jnp.concatenate(pieces, axis=0)
     grad_rows = times_rows(grad_attn, out_w).astype(bf16)
     grad_heads = grad_rows.reshape(tok_rows, heads_local, HD).transpose(1, 0, 2).reshape(-1, HD)
     grad_q, pair_grad = attend_back(
         query_rows, grad_heads, attn_float, attn_log, pairs, places, key_places
     )
+    if gather_factors:
+        pair_grad = after(pair_grad, own_columns)
+        columns_then = after(own_columns, grad_attn)
+        if layers == 4:
+            column_pieces = [columns_then] + [swap(columns_then, bit, "tp") for bit in (1, 2)]
+        else:
+            column_pieces, _, _ = layer_gather(columns_then)
     near_rows = 4 * tok_rows
     pair_part = [
         pair_grad[start : start + near_rows] for start in range(0, key_count, near_rows)
@@ -482,16 +615,16 @@
     pair_part = pair_part[0]
     if layers == 4:
         output_pieces.append(swap(after(output_pieces[2], grad_rows), 1, "tp"))
-    output = rows_out(output_pieces)
     arrived = [
         swap(pair_part[index * tok_rows : (index + 1) * tok_rows], step)
         for index, step in ((1, far_a), (2, far_b), (3, far_a | far_b))
     ]
-    if gather_factors:
-        ffn_cols, down_cols = columns_of_owner(after(by_owner, arrived[0]))
-    pair_own = pair_part[:tok_rows].astype(f32)
+    pair_own = after(pair_part[:tok_rows], output_pieces[3]).astype(f32)
     for piece in arrived:
         pair_own = pair_own + piece.astype(f32)
+    if gather_factors:
+        if layers == 4:
+            column_pieces.append(swap(after(column_pieces[2], arrived[0]), 1, "tp"))
     grad_query_lin = (
         rotate(
             grad_q.reshape(heads_local, tok_rows, HD).transpose(1, 0, 2), cos_table, -sine_table
@@ -504,37 +637,50 @@
     grad_lin = jnp.concatenate(
         [grad_query_lin, grad_key_lin, pair_own[:, key_width:]], axis=1
     ).astype(bf16)
-    grad_in_part = times_rows_t(grad_lin, qkv_w).astype(bf16)
-
-    def products(then):
-        lin = after(grad_lin, then, all_both) if gather_factors else after(grad_lin, then)
-        return (attn_products(attn_input, lin, grad_attn, attn_rows),)
+    partial = attn_products(
+        attn_input,
+        after(grad_lin, all_both) if gather_factors else grad_lin,
+        grad_attn,
+        attn_rows,
+    )
+    attn_sums = sum_scatter(partial)
+    grad_w_lin, grad_w_out = attn_sums[:, :qkv_width], attn_sums[:, qkv_width:]
+    grad_in_part = times_rows_t(after(grad_lin, partial), qkv_w).astype(bf16)
+
+    if gather_factors:
+        columns = jnp.stack([after(piece, grad_in_part) for piece in column_pieces], axis=1)
+        columns = columns.reshape(tok_rows * ring, 2 * shard)
+        ffn_cols, down_cols = columns[:, :shard], columns[:, shard:]
 
     def gate_gradient(then):
         return (contract(after(ffn_cols, then), all_both[:, :ffn_width], 0, 0),)
 
-    def up_gradient(then):
-        return (contract(after(ffn_cols, then), all_both[:, ffn_width:], 0, 0),)
-
-    def down_gradient(then):
-        return (contract(after(down_cols, then), all_hidden, 0, 0),)
-
-    grad_attn_total, (partial,), _ = layer_scatter(grad_in_part, products)
     if gather_factors:
-        grad_attn_total = after(grad_attn_total, ffn_cols, down_cols)
-    attn_sums = sum_scatter(partial)
-    grad_w_lin, grad_w_out = attn_sums[:, :qkv_width], attn_sums[:, qkv_width:]
-    grad_attn_in = columns_out(grad_attn_total)
-    own_inv = rms_scale(own_tok)
-    own_normed = own_tok * own_inv
-    own_grad = (grad_res + norm_back(own_inv, own_normed, grad_attn_in)).astype(bf16)
+        parts, _, (grad_w_gate,) = layer_scatter(grad_in_part, None, gate_gradient)
+    else:
+        parts, _, _ = layer_scatter(grad_in_part)
+    if in_kernels:
+        own_grad, grad_gain_one = on_own_rows(
+            token_back_body,
+            *parts,
+            (own_tok, grad_res, all_gains),
+            [(own_rows, bf16), (1, f32)],
+            "token_back",
+            scratch=2,
+        )
+    else:
+        grad_attn_in = columns_out(sum_of(parts))
+        own_inv = rms_scale(own_tok)
+        own_normed = own_tok * own_inv
+        own_grad = grad_res + norm_back(own_inv, own_normed, grad_attn_in * gain_one)
+        own_grad = own_grad.astype(bf16)
+        grad_gain_one = jnp.sum(grad_attn_in * own_normed, axis=0, keepdims=True)
+    token_pieces, _, _ = layer_gather(own_grad)
     if gather_factors:
-        token_pieces, (grad_w_gate,), _ = layer_gather(own_grad, gate_gradient)
-        (grad_w_up,) = up_gradient(token_pieces[3])
-        (grad_w_down,) = down_gradient(grad_w_up)
-    else:
-        token_pieces, _, _ = layer_gather(own_grad)
+        grad_w_up = contract(after(ffn_cols, own_grad), all_both[:, ffn_width:], 0, 0)
+        grad_w_down = contract(after(down_cols, token_pieces[2], grad_w_up), all_hidden, 0, 0)
     grad_tokens = rows_out(token_pieces).astype(f32)
+    output = rows_out([after(output_pieces[0], token_pieces[3])] + output_pieces[1:])
 
     third_gain = norm_ffn_in.astype(f32)
     gain_third = (
@@ -542,31 +688,31 @@
         / third_gain
     )[None, :]
     gain_sum = columns_in(
-        jnp.stack([jnp.sum(grad_attn_in * own_normed, axis=0), grad_gain_two, grad_gain_four])
-    )
-    gain_sum = after(gain_sum, token_pieces[2])
-    for bit in [1 << index for index in range(layers.bit_length() - 1)]:
-        gain_third = gain_third + swap(gain_third, bit, "tp")
-        gain_sum = gain_sum + swap(gain_sum, bit, "tp")
+        jnp.concatenate([grad_gain_one, grad_gain_two, grad_gain_four], axis=0)
+    )
+    gain_sum = after(gain_sum, token_pieces[1])
     for bit in reversed(near):
         half = gain_sum.shape[1] // 2
         gain_sum = gain_sum[:, :half] + swap(gain_sum[:, half:], bit)
     own_gain = gain_sum[:, :shard]
     for index, step in ((1, far_a), (2, far_b), (3, far_a | far_b)):
         own_gain = own_gain + swap(gain_sum[:, index * shard : (index + 1) * shard], step)
+    own_gain = jnp.concatenate([own_gain, gain_third], axis=0)
+    for bit in [1 << index for index in range(layers.bit_length() - 1)]:
+        own_gain = own_gain + swap(own_gain, bit, "tp")
     return (
         output,
         grad_tokens,
-        grad_w_lin[:, :query_width] * first_gain,
-        grad_w_lin[:, query_width : query_width + key_width] * first_gain,
-        grad_w_lin[:, query_width + key_width :] * first_gain,
+        grad_w_lin[:, :query_width],
+        grad_w_lin[:, query_width : query_width + key_width],
+        grad_w_lin[:, query_width + key_width :],
         grad_w_out,
         grad_w_gate,
         grad_w_up,
         grad_w_down,
-        own_gain[0] / first_gain[:, 0],
+        own_gain[0],
         own_gain[1],
-        gain_third[0],
+        own_gain[3],
         own_gain[2],
     )
 

time: 507 us -> 507 us (level)
  other arithmetic: 52.1 us -> 29.7 us
  local copies, waits for them, and re-layouts: 65.8 us -> 46.9 us
  Pallas kernels: 10.6 us -> 28.3 us
  waiting for transfers between devices: 223 us -> 235 us
  starting transfers between devices: 59.1 us -> 64.6 us
    ppermute x50 -> x51, waiting for transfers between devices: 199 us -> 226 us  [swap(): lax.ppermute(value, axis, [(index, index ^ bit) for index in range(count)])]
    pallas_call x0 -> x5, Pallas kernels: none -> 17.3 us  [the longest x4 17.1 us: on_own_rows(): pl.pallas_call(kernel, grid=(1,), in_specs=[SCALARS, wide] + [WHOLE] * (2...]
    all_to_all x1, waiting for transfers between devices: 10.2 us -> 0.01 us  [local(): lax.all_to_all(columns_by_owner(own_input, own_grad_ffn), 'ctx', split_ax...]
    ppermute x50 -> x51, starting transfers between devices: 54.2 us -> 60.2 us  [swap(): lax.ppermute(value, axis, [(index, index ^ bit) for index in range(count)])]
    dynamic_update_slice x7, local copies, waits for them, and re-layouts: 5.5 us -> 0.2 us  [rows_out(): lax.dynamic_update_slice_in_dim(result, piece, (my_layer ^ step) * own_ro...]
    unnamed x196 -> x200, local copies, waits for them, and re-layouts: 21.1 us -> 25.4 us
  transfers between devices with their start and end apart: 56 -> 57, of which waited for: 36 -> 38; matrix products, arithmetic and copies ran while one was open for 35% -> 26% of each run, Pallas kernels for 2% -> 6%
where the time goes in v4:
time: 507 us; the launch traced here: 498 us
  waiting for transfers between devices  235 us (46%)
  matrix products  77.2 us (15%)
  starting transfers between devices  64.6 us (13%)
  local copies, waits for them, and re-layouts  46.9 us (9%)
  other arithmetic  29.7 us (6%)
  Pallas kernels  28.3 us (6%)
  between operations  15.8 us (3%)
    ppermute x51, waiting for transfers between devices, swap(): lax.ppermute(value, axis, [(index, index ^ bit) for index in range(count)])  226 us
    ppermute x51, starting transfers between devices, swap(): lax.ppermute(value, axis, [(index, index ^ bit) for index in range(count)])  60.2 us
    dot_general x9, matrix products, contract(): lax.dot_general(first_operand, second_operand, (((first_dim,), (second_di...  53.2 us
    unnamed x200, local copies, waits for them, and re-layouts  25.4 us
    dot_general x6, matrix products, product(): return jnp.dot(first_operand, second_operand, preferred_element_type=f32)  24 us
    pallas_call x4, Pallas kernels, on_own_rows(): pl.pallas_call(kernel, grid=(1,), in_specs=[SCALARS, wide] + [WHOLE] * (2...  17.1 us
  transfers between devices with their start and end apart: 57, of which 38 were waited for; matrix products, arithmetic and copies ran while one was open for 26% of the time, Pallas kernels for 6%

profile of v4, /device:TPU:0, one launch (start us, length us, event | category | flops | bytes accessed | tf_op | source)
XLA Modules:
  0.0 497.8 jit_solution(3353623285373466614)
XLA Ops:
  7.2 3.4 pad_maximum_fusion
  12.8 3.0 collective-permute-start.1
  20.1 28.6 %collective-permute-done.1 = bf16[304,1536]{1,0:T(8,128)(2,1)S(1)} collective-permute-done((bf16[304,1536]{1,0:T(8,128)(2,1)}, bf16[304,1536]{1,0:T(8,128)(2,1)S(1)}, u32[]{:S(2)}, u32[]{:S(2)}) %collective-permute-start.1) | collective-permute-done | bytes 933920 | tf_op jit(solution)/shard_map/ppermute | solution.py:62
  50.1 3.3 collective-permute-done
  55.6 15.3 %collective-permute-done.4 = bf16[144,1536]{1,0:T(8,128)(2,1)S(1)} collective-permute-done((bf16[144,1536]{1,0:T(8,128)(2,1)S(1)}, bf16[144,1536]{1,0:T(8,128)(2,1)S(1)}, u32[]{:S(2)}, u32[]{:S(2)}) %collective-permute-start.4) | collective-permute-done | bytes 442400 | tf_op jit(solution)/shard_map/ppermute | solution.py:62
  77.0 2.4 collective-permute-start.2
  82.9 2.6 concatenate.109
  87.5 3.0 fusion.12
  90.5 2.6 fusion.18
  98.3 11.5 %collective-permute-done.7 = bf16[256,512]{1,0:T(8,128)(2,1)S(1)} collective-permute-done((bf16[256,512]{1,0:T(8,128)(2,1)}, bf16[256,512]{1,0:T(8,128)(2,1)S(1)}, u32[]{:S(2)}, u32[]{:S(2)}) %collective-permute-start.7) | collective-permute-done | bytes 262176 | tf_op jit(solution)/shard_map/ppermute | solution.py:62
  109.8 3.9 collective-permute-done.8
  113.7 7.0 %collective-permute-done.9 = bf16[256,512]{1,0:T(8,128)(2,1)} collective-permute-done((bf16[256,512]{1,0:T(8,128)(2,1)}, bf16[256,512]{1,0:T(8,128)(2,1)}, u32[]{:S(2)}, u32[]{:S(2)}) %collective-permute-start.9) | collective-permute-done | bytes 262176 | tf_op jit(solution)/shard_map/ppermute | solution.py:62
  128.7 2.7 attend.1
  131.4 2.2 convolution_convert_fusion.5
  142.7 4.0 collective-permute-done.12
  147.8 2.6 collective-permute-start.13
  151.5 4.9 collective-permute-done.11.one_ref
  156.4 6.6 %collective-permute-done.13.two_ref = bf16[64,2304]{1,0:T(8,128)(2,1)S(1)} collective-permute-done((bf16[64,2304]{1,0:T(8,128)(2,1)S(1)}, bf16[64,2304]{1,0:T(8,128)(2,1)S(1)}, u32[]{:S(2)}, u32[]{:S(2)}) %collective-permute-start.13) | collective-permute-done | bytes 294944 | tf_op jit(solution)/shard_map/ppermute | solution.py:62
  163.0 13.4 %residual.1 = (f32[64,2304]{1,0:T(8,128)S(1)}, f32[64,2304]{1,0:T(8,128)S(1)}, bf16[64,2304]{1,0:T(8,128)(2,1)S(1)}) custom-call(s32[1]{0:T(128)} %bitcast.me_ref, bf16[256,2304]{1,0:T(8,128)(2,1)S(1)} %pad_maximum_fusion.3.part_ref, bf16[64,2304]{1,0:T(8,128)(2,1)S(1)} %collective-permute-done.11.one_ref, ...), custom_call_target="tpu_custom_call" | custom-call | tf_op jit(solution)/shard_map/residual/pallas_call | solution.py:335
  178.1 4.3 collective-permute-start.14
  182.4 10.0 %collective-permute-done.15 = bf16[64,2304]{1,0:T(8,128)(2,1)S(1)} collective-permute-done((bf16[64,2304]{1,0:T(8,128)(2,1)S(1)}, bf16[64,2304]{1,0:T(8,128)(2,1)S(1)}, u32[]{:S(2)}, u32[]{:S(2)}) %collective-permute-start.15) | collective-permute-done | bytes 294944 | tf_op jit(solution)/shard_map/ppermute | solution.py:62
  193.2 6.2 %collective-permute-done.16 = bf16[64,2304]{1,0:T(8,128)(2,1)} collective-permute-done((bf16[64,2304]{1,0:T(8,128)(2,1)S(1)}, bf16[64,2304]{1,0:T(8,128)(2,1)}, u32[]{:S(2)}, u32[]{:S(2)}) %collective-permute-start.16) | collective-permute-done | bytes 294944 | tf_op jit(solution)/shard_map/ppermute | solution.py:62
  199.3 10.4 %fusion.22 = f32[256,4608]{1,0:T(8,128)S(1)} fusion(bf16[2304,4608]{1,0:T(8,128)(2,1)} %all-gather.5.cloned.1.call-done, bf16[64,2304]{1,0:T(8,128)(2,1)} %collective-permute-done.16, bf16[64,2304]{1,0:T(8,128)(2,1)S(1)} %collective-permute-done.15, bf16[64,2304]{1,0:T(8,128)(2,1)} %copy-done.84, bf16[64,2304]{1,0:T(8,128)(2,1)S(1)} %get-tuple-element.62.first_ref), kind=kOutput, calls=%fused_computation.55 | convolution fusion | flops 5440536576 | bytes 27131904 | tf_op jit(solution)/shard_map/dot_general | solution.py:44
  209.7 2.2 copy-done.42
  213.8 7.0 %all-gather.7.cloned.1.call-done = bf16[2304,2304]{1,0:T(8,128)(2,1)} async-done(((bf16[288,2304]{1,0:T(8,128)(2,1)}), bf16[2304,2304]{1,0:T(8,128)(2,1)}) %all-gather.7.cloned.1.call-update) | async-done | bytes 10616848 | tf_op jit(solution)/shard_map/all_gather | solution.py:312
  220.8 7.5 %convolution_convert_fusion.1.part_ref = bf16[256,2304]{1,0:T(8,128)(2,1)S(1)} fusion(bf16[256,2304]{1,0:T(8,128)(2,1)} %multiply_convert_fusion.1, bf16[2304,2304]{1,0:T(8,128)(2,1)} %all-gather.7.cloned.1.call-done), kind=kOutput, calls=%fused_computation.5 | convolution fusion | flops 2718498816 | bytes 12976128 | tf_op jit(solution)/shard_map/dot_general | solution.py:48
  230.4 7.8 %collective-permute-done.18 = bf16[64,2304]{1,0:T(8,128)(2,1)S(1)} collective-permute-done((bf16[64,2304]{1,0:T(8,128)(2,1)S(1)}, bf16[64,2304]{1,0:T(8,128)(2,1)S(1)}, u32[]{:S(2)}, u32[]{:S(2)}) %collective-permute-start.18) | collective-permute-done | bytes 294944 | tf_op jit(solution)/shard_map/ppermute | solution.py:62
  238.3 2.5 collective-permute-start.19
  241.8 7.1 %collective-permute-done.17.one_ref = bf16[64,2304]{1,0:T(8,128)(2,1)S(1)} collective-permute-done((bf16[64,2304]{1,0:T(8,128)(2,1)S(1)}, bf16[64,2304]{1,0:T(8,128)(2,1)S(1)}, u32[]{:S(2)}, u32[]{:S(2)}) %collective-permute-start.17) | collective-permute-done | bytes 294944 | tf_op jit(solution)/shard_map/ppermute | solution.py:62
  248.9 4.5 collective-permute-done.19.two_ref
  254.7 3.4 collective-permute-start.21
  258.1 10.8 %collective-permute-done.21 = bf16[64,2304]{1,0:T(8,128)(2,1)S(1)} collective-permute-done((bf16[64,2304]{1,0:T(8,128)(2,1)S(1)}, bf16[64,2304]{1,0:T(8,128)(2,1)S(1)}, u32[]{:S(2)}, u32[]{:S(2)}) %collective-permute-start.21) | collective-permute-done | bytes 294944 | tf_op jit(solution)/shard_map/ppermute | solution.py:62
  270.4 5.2 %collective-permute-done.22 = bf16[64,2304]{1,0:T(8,128)(2,1)S(1)} collective-permute-done((bf16[64,2304]{1,0:T(8,128)(2,1)S(1)}, bf16[64,2304]{1,0:T(8,128)(2,1)S(1)}, u32[]{:S(2)}, u32[]{:S(2)}) %collective-permute-start.22) | collective-permute-done | bytes 294944 | tf_op jit(solution)/shard_map/ppermute | solution.py:62
  275.6 4.1 fusion.10
  286.3 12.7 %convolution_convert_fusion.part_ref = bf16[256,2304]{1,0:T(8,128)(2,1)S(1)} fusion(bf16[2304,4608]{1,0:T(8,128)(2,1)} %all-gather.5.cloned.1.call-done, bf16[256,2304]{1,0:T(8,128)(2,1)} %copy-done.55, bf16[256,2304]{1,0:T(8,128)(2,1)} %copy-done.54), kind=kOutput, calls=%fused_computation.4 | convolution fusion | flops 5441126400 | bytes 24772608 | tf_op jit(solution)/shard_map/dot_general | solution.py:48
  302.9 11.1 %collective-permute-done.26 = bf16[64,2304]{1,0:T(8,128)(2,1)S(1)} collective-permute-done((bf16[64,2304]{1,0:T(8,128)(2,1)S(1)}, bf16[64,2304]{1,0:T(8,128)(2,1)S(1)}, u32[]{:S(2)}, u32[]{:S(2)}) %collective-permute-start.26) | collective-permute-done | bytes 294944 | tf_op jit(solution)/shard_map/ppermute | solution.py:62
  315.9 4.2 all-to-all-start
  320.2 5.3 %collective-permute-done.27.two_ref = bf16[64,2304]{1,0:T(8,128)(2,1)} collective-permute-done((bf16[64,2304]{1,0:T(8,128)(2,1)}, bf16[64,2304]{1,0:T(8,128)(2,1)}, u32[]{:S(2)}, u32[]{:S(2)}) %collective-permute-start.27) | collective-permute-done | bytes 294944 | tf_op jit(solution)/shard_map/ppermute | solution.py:62
  333.8 11.4 %collective-permute-done.29 = bf16[64,2304]{1,0:T(8,128)(2,1)S(1)} collective-permute-done((bf16[64,2304]{1,0:T(8,128)(2,1)S(1)}, bf16[64,2304]{1,0:T(8,128)(2,1)S(1)}, u32[]{:S(2)}, u32[]{:S(2)}) %collective-permute-start.29) | collective-permute-done | bytes 294944 | tf_op jit(solution)/shard_map/ppermute | solution.py:62
  345.3 6.7 %collective-permute-done.30 = bf16[64,2304]{1,0:T(8,128)(2,1)S(1)} collective-permute-done((bf16[64,2304]{1,0:T(8,128)(2,1)S(1)}, bf16[64,2304]{1,0:T(8,128)(2,1)S(1)}, u32[]{:S(2)}, u32[]{:S(2)}) %collective-permute-start.30) | collective-permute-done | bytes 294944 | tf_op jit(solution)/shard_map/ppermute | solution.py:62
  352.0 2.2 fusion.30
  356.2 5.6 %attend_back.1 = (f32[512,256]{1,0:T(8,128)S(1)}, bf16[2048,512]{1,0:T(8,128)(2,1)S(1)}) custom-call(bf16[512,256]{1,0:T(8,128)(2,1)S(1)} %bitcast.55, bf16[512,256]{1,0:T(8,128)(2,1)S(1)} %bitcast.56, f32[512,256]{1,0:T(8,128)S(1)} %copy-done.26, f32[512,1]{1,0:T(8,128)S(1)} %copy-done.32, ...), custom_call_target="tpu_custom_call" | custom-call | tf_op jit(solution)/shard_map/attend_back/pallas_call | solution.py:162
  365.2 3.5 collective-permute-start.38
  369.1 3.2 collective-permute-start.35
  373.6 6.4 %collective-permute-done.32 = bf16[64,2304]{1,0:T(8,128)(2,1)S(1)} collective-permute-done((bf16[64,2304]{1,0:T(8,128)(2,1)}, bf16[64,2304]{1,0:T(8,128)(2,1)S(1)}, u32[]{:S(2)}, u32[]{:S(2)}) %collective-permute-start.32) | collective-permute-done | bytes 294944 | tf_op jit(solution)/shard_map/ppermute | solution.py:62
  380.0 5.0 %collective-permute-done.35 = bf16[256,512]{1,0:T(8,128)(2,1)S(1)} collective-permute-done((bf16[256,512]{1,0:T(8,128)(2,1)S(1)}, bf16[256,512]{1,0:T(8,128)(2,1)S(1)}, u32[]{:S(2)}, u32[]{:S(2)}) %collective-permute-start.35) | collective-permute-done | bytes 262176 | tf_op jit(solution)/shard_map/ppermute | solution.py:62
  385.0 6.1 %collective-permute-done.34 = bf16[256,512]{1,0:T(8,128)(2,1)S(1)} collective-permute-done((bf16[256,512]{1,0:T(8,128)(2,1)S(1)}, bf16[256,512]{1,0:T(8,128)(2,1)S(1)}, u32[]{:S(2)}, u32[]{:S(2)}) %collective-permute-start.34) | collective-permute-done | bytes 262176 | tf_op jit(solution)/shard_map/ppermute | solution.py:62
  391.2 5.3 %collective-permute-done.33 = bf16[256,512]{1,0:T(8,128)(2,1)S(1)} collective-permute-done((bf16[256,512]{1,0:T(8,128)(2,1)S(1)}, bf16[256,512]{1,0:T(8,128)(2,1)S(1)}, u32[]{:S(2)}, u32[]{:S(2)}) %collective-permute-start.33) | collective-permute-done | bytes 262176 | tf_op jit(solution)/shard_map/ppermute | solution.py:62
  402.3 2.7 attn_products.1
  405.0 3.0 copy-done
  408.0 2.5 convolution_convert_fusion.3
  410.5 2.5 convolution_convert_fusion.2
  414.8 5.5 %collective-permute-done.39 = bf16[8,64,576]{2,1,0:T(8,128)(2,1)} collective-permute-done((bf16[8,64,576]{2,1,0:T(8,128)(2,1)}, bf16[8,64,576]{2,1,0:T(8,128)(2,1)}, u32[]{:S(2)}, u32[]{:S(2)}) %collective-permute-start.39) | collective-permute-done | bytes 589856 | tf_op jit(solution)/shard_map/ppermute | solution.py:62
  420.3 2.6 pad_maximum_fusion.1
  425.3 6.3 %collective-permute-done.40 = bf16[64,2304]{1,0:T(8,128)(2,1)S(1)} collective-permute-done((bf16[64,2304]{1,0:T(8,128)(2,1)S(1)}, bf16[64,2304]{1,0:T(8,128)(2,1)S(1)}, u32[]{:S(2)}, u32[]{:S(2)}) %collective-permute-start.40) | collective-permute-done | bytes 294944 | tf_op jit(solution)/shard_map/ppermute | solution.py:62
  432.8 8.4 %fusion.2 = f32[288,2304]{1,0:T(8,128)} fusion(bf16[2048,288]{1,0:T(8,128)(2,1)S(1)} %get-tuple-element.91, bf16[2048,4608]{1,0:T(8,128)(2,1)} %all-gather.11.cloned.1.call-done), kind=kOutput, calls=%fused_computation.2 | convolution fusion | flops 2717908992 | bytes 13271040 | tf_op jit(solution)/shard_map/dot_general | solution.py:48
  441.2 5.1 %collective-permute-done.41.two_ref = bf16[64,2304]{1,0:T(8,128)(2,1)S(1)} collective-permute-done((bf16[64,2304]{1,0:T(8,128)(2,1)S(1)}, bf16[64,2304]{1,0:T(8,128)(2,1)S(1)}, u32[]{:S(2)}, u32[]{:S(2)}) %collective-permute-start.41) | collective-permute-done | bytes 294944 | tf_op jit(solution)/shard_map/ppermute | solution.py:62
  447.4 2.5 collective-permute-start.42
  450.2 6.7 %add_reduce_fusion = (f32[288]{0:T(512)S(1)}, f32[288,2304]{1,0:T(8,128)}) fusion(bf16[288,2304]{1,0:T(8,128)(2,1)S(1)} %copy-done.47, f32[288,2304]{1,0:T(8,128)} %fusion.2, bf16[288,2304]{1,0:T(8,128)(2,1)S(1)} %copy-done.48, bf16[2048,288]{1,0:T(8,128)(2,1)S(1)} %get-tuple-element.91, bf16[2048,4608]{1,0:T(8,128)(2,1)S(1)} %bitcast.67), kind=kOutput, calls=%fused_computation.9 | convolution fusion | flops 2721890048 | bytes 18973824 | tf_op jit(solution)/shard_map/dot_general | solution.py:48
  457.1 4.8 collective-permute-done.44
  463.6 3.1 collective-permute-start.48
  467.4 8.7 %fusion.80 = f32[288,2304]{1,0:T(8,128)} fusion(bf16[2048,288]{1,0:T(8,128)(2,1)} %get-tuple-element.92, bf16[2048,2304]{1,0:T(8,128)(2,1)} %all-gather.9.cloned.1.call-done), kind=kOutput, calls=%fused_computation.224 | convolution fusion | flops 2717908992 | bytes 13271040 | tf_op jit(solution)/shard_map/dot_general | solution.py:48
  479.9 2.7 collective-permute-start.50
  488.0 2.3 fusion.77
  (388 shorter events, 108.1 us)
Async XLA Ops:
  7.2 192.2 %all-gather.5.cloned.1.call-start = ((), (), s32[]{:S(2)}) async-start(), calls=%async_computation.2 | async-start | bytes 23887872 | tf_op jit(solution)/shard_map/all_gather | solution.py:312
  10.7 210.1 %all-gather.7.cloned.1.call-start = ((), (), s32[]{:S(2)}) async-start(), calls=%async_computation.3 | async-start | bytes 11943936 | tf_op jit(solution)/shard_map/all_gather | solution.py:312
  11.5 271.2 %all-gather.9.cloned.1.call-start = ((), (), s32[]{:S(2)}) async-start(), calls=%async_computation.4 | async-start | bytes 10616832 | tf_op jit(solution)/shard_map/all_gather | solution.py:312
  12.8 35.9 %collective-permute-start.1 = (bf16[304,1536]{1,0:T(8,128)(2,1)}, bf16[304,1536]{1,0:T(8,128)(2,1)S(1)}, u32[]{:S(2)}, u32[]{:S(2)}) collective-permute-start(bf16[304,1536]{1,0:T(8,128)(2,1)} %fusion.35), channel_id=1, source_target_pairs={{0,16},{4,20},{8,24},{12,28},{16,0},{20,4},{24,8},{28,12},{1,17},{... | collective-permute-start | bytes 2801672 | tf_op jit(solution)/shard_map/ppermute | solution.py:62
  15.8 37.7 %collective-permute-start = (bf16[304,1536]{1,0:T(8,128)(2,1)}, bf16[304,1536]{1,0:T(8,128)(2,1)S(1)}, u32[]{:S(2)}, u32[]{:S(2)}) collective-permute-start(bf16[304,1536]{1,0:T(8,128)(2,1)} %fusion.35), channel_id=1, source_target_pairs={{0,8},{4,12},{8,0},{12,4},{16,24},{20,28},{24,16},{28,20},{1,9},{5... | collective-permute-start | bytes 2801672 | tf_op jit(solution)/shard_map/ppermute | solution.py:62
  48.8 22.0 %collective-permute-start.4 = (bf16[144,1536]{1,0:T(8,128)(2,1)S(1)}, bf16[144,1536]{1,0:T(8,128)(2,1)S(1)}, u32[]{:S(2)}, u32[]{:S(2)}) collective-permute-start(bf16[144,1536]{1,0:T(8,128)(2,1)S(1)} %slice.300), channel_id=1, source_target_pairs={{0,8},{4,12},{8,0},{12,4},{16,24},{20,28},{24,16},{28,20},{1,9},{5... | collective-permute-start | bytes 1327112 | tf_op jit(solution)/shard_map/ppermute | solution.py:62
  53.5 20.3 %collective-permute-start.5 = (bf16[144,1536]{1,0:T(8,128)(2,1)S(1)}, bf16[144,1536]{1,0:T(8,128)(2,1)S(1)}, u32[]{:S(2)}, u32[]{:S(2)}) collective-permute-start(bf16[144,1536]{1,0:T(8,128)(2,1)S(1)} %slice.301), channel_id=1, source_target_pairs={{0,16},{4,20},{8,24},{12,28},{16,0},{20,4},{24,8},{28,12},{1,17},{... | collective-permute-start | bytes 1327112 | tf_op jit(solution)/shard_map/ppermute | solution.py:62
  74.6 12.9 %collective-permute-start.6 = (bf16[1152,1536]{1,0:T(8,128)(2,1)}, bf16[1152,1536]{1,0:T(8,128)(2,1)}, u32[]{:S(2)}, u32[]{:S(2)}) collective-permute-start(bf16[1152,1536]{1,0:T(8,128)(2,1)} %constant_dynamic-update-slice_fusion), channel_id=1, source_target_pairs={{0,4},{4,0},{8,12},{12,8},{16,20},{20,16},{24,28},{28,24},{1,5},{5... | collective-permute-start | bytes 10616840 | tf_op jit(solution)/shard_map/ppermute | solution.py:62
  77.0 4.0 collective-permute-start.2
  81.7 3.8 collective-permute-start.3
  94.1 30.1 %slice-start = ((f32[256,1024]{1,0:T(8,128)}), f32[256,512]{1,0:T(8,128)S(1)}, s32[]{:S(2)}) async-start(f32[256,1024]{1,0:T(8,128)} %copy-done.45), calls=%async_computation.7 | async-start | bytes 1048576 | tf_op jit(solution)/shard_map/slice | solution.py:479
  94.8 15.0 %collective-permute-start.7 = (bf16[256,512]{1,0:T(8,128)(2,1)}, bf16[256,512]{1,0:T(8,128)(2,1)S(1)}, u32[]{:S(2)}, u32[]{:S(2)}) collective-permute-start(bf16[256,512]{1,0:T(8,128)(2,1)} %get-tuple-element.146), channel_id=1, source_target_pairs={{0,8},{4,12},{8,0},{12,4},{16,24},{20,28},{24,16},{28,20},{1,9},{5... | collective-permute-start | bytes 786440 | tf_op jit(solution)/shard_map/ppermute | solution.py:62
  96.7 17.0 %collective-permute-start.8 = (bf16[256,512]{1,0:T(8,128)(2,1)}, bf16[256,512]{1,0:T(8,128)(2,1)S(1)}, u32[]{:S(2)}, u32[]{:S(2)}) collective-permute-start(bf16[256,512]{1,0:T(8,128)(2,1)} %get-tuple-element.146), channel_id=1, source_target_pairs={{0,16},{4,20},{8,24},{12,28},{16,0},{20,4},{24,8},{28,12},{1,17},{... | collective-permute-start | bytes 786440 | tf_op jit(solution)/shard_map/ppermute | solution.py:62
  96.9 23.8 %collective-permute-start.9 = (bf16[256,512]{1,0:T(8,128)(2,1)}, bf16[256,512]{1,0:T(8,128)(2,1)}, u32[]{:S(2)}, u32[]{:S(2)}) collective-permute-start(bf16[256,512]{1,0:T(8,128)(2,1)} %get-tuple-element.146), channel_id=1, source_target_pairs={{0,24},{4,28},{8,16},{12,20},{16,8},{20,12},{24,0},{28,4},{1,25},{... | collective-permute-start | bytes 786440 | tf_op jit(solution)/shard_map/ppermute | solution.py:62
  122.7 4.7 collective-permute-start.10
  136.6 10.2 %collective-permute-start.12 = (bf16[64,2304]{1,0:T(8,128)(2,1)}, bf16[64,2304]{1,0:T(8,128)(2,1)}, u32[]{:S(2)}, u32[]{:S(2)}) collective-permute-start(bf16[64,2304]{1,0:T(8,128)(2,1)} %get-tuple-element.116), channel_id=1, source_target_pairs={{0,1},{1,0},{2,3},{3,2},{4,5},{5,4},{6,7},{7,6},{8,9},{9,8},{10,11... | collective-permute-start | bytes 884744 | tf_op jit(solution)/shard_map/ppermute | solution.py:62
  142.0 34.4 %copy-start.17 = (f32[4,2304]{1,0:T(4,128)}, f32[4,2304]{1,0:T(4,128)S(1)}, u32[]{:S(2)}) copy-start(f32[4,2304]{1,0:T(4,128)S(1)} %convert_element_type.132.refs_1_.refs_2_.refs_3_) | copy-start | bytes 110596
  142.0 14.4 %collective-permute-start.11 = (bf16[64,2304]{1,0:T(8,128)(2,1)}, bf16[64,2304]{1,0:T(8,128)(2,1)S(1)}, u32[]{:S(2)}, u32[]{:S(2)}) collective-permute-start(bf16[64,2304]{1,0:T(8,128)(2,1)} %get-tuple-element.117), channel_id=1, source_target_pairs={{0,1},{1,0},{2,3},{3,2},{4,5},{5,4},{6,7},{7,6},{8,9},{9,8},{10,11... | collective-permute-start | bytes 884744 | tf_op jit(solution)/shard_map/ppermute | solution.py:62
  147.8 15.2 %collective-permute-start.13 = (bf16[64,2304]{1,0:T(8,128)(2,1)S(1)}, bf16[64,2304]{1,0:T(8,128)(2,1)S(1)}, u32[]{:S(2)}, u32[]{:S(2)}) collective-permute-start(bf16[64,2304]{1,0:T(8,128)(2,1)S(1)} %add_convert_fusion.4), channel_id=1, source_target_pairs={{0,2},{1,3},{2,0},{3,1},{4,6},{5,7},{6,4},{7,5},{8,10},{9,11},{10,... | collective-permute-start | bytes 884744 | tf_op jit(solution)/shard_map/ppermute | solution.py:62
  178.1 31.7 %copy-start.27 = (bf16[64,2304]{1,0:T(8,128)(2,1)}, bf16[64,2304]{1,0:T(8,128)(2,1)S(1)}, u32[]{:S(2)}) copy-start(bf16[64,2304]{1,0:T(8,128)(2,1)S(1)} %get-tuple-element.62.first_ref) | copy-start | bytes 884740
  178.1 14.3 %collective-permute-start.15 = (bf16[64,2304]{1,0:T(8,128)(2,1)S(1)}, bf16[64,2304]{1,0:T(8,128)(2,1)S(1)}, u32[]{:S(2)}, u32[]{:S(2)}) collective-permute-start(bf16[64,2304]{1,0:T(8,128)(2,1)S(1)} %get-tuple-element.62.first_ref), channel_id=1, source_target_pairs={{0,2},{1,3},{2,0},{3,1},{4,6},{5,7},{6,4},{7,5},{8,10},{9,11},{10,... | collective-permute-start | bytes 884744 | tf_op jit(solution)/shard_map/ppermute | solution.py:62
  178.1 14.4 %collective-permute-start.14 = (bf16[64,2304]{1,0:T(8,128)(2,1)S(1)}, bf16[64,2304]{1,0:T(8,128)(2,1)S(1)}, u32[]{:S(2)}, u32[]{:S(2)}) collective-permute-start(bf16[64,2304]{1,0:T(8,128)(2,1)S(1)} %get-tuple-element.62.first_ref), channel_id=1, source_target_pairs={{0,1},{1,0},{2,3},{3,2},{4,5},{5,4},{6,7},{7,6},{8,9},{9,8},{10,11... | collective-permute-start | bytes 884744 | tf_op jit(solution)/shard_map/ppermute | solution.py:62
  192.4 7.0 %collective-permute-start.16 = (bf16[64,2304]{1,0:T(8,128)(2,1)S(1)}, bf16[64,2304]{1,0:T(8,128)(2,1)}, u32[]{:S(2)}, u32[]{:S(2)}) collective-permute-start(bf16[64,2304]{1,0:T(8,128)(2,1)S(1)} %collective-permute-done.15), channel_id=1, source_target_pairs={{0,1},{1,0},{2,3},{3,2},{4,5},{5,4},{6,7},{7,6},{8,9},{9,8},{10,11... | collective-permute-start | bytes 884744 | tf_op jit(solution)/shard_map/ppermute | solution.py:62
  213.8 187.3 %all-gather.11.cloned.1.call-start = ((), (), s32[]{:S(2)}) async-start(), calls=%async_computation.5 | async-start | bytes 21233664 | tf_op jit(solution)/shard_map/all_gather | solution.py:312
  220.8 54.8 %copy-start.83 = (bf16[2304,2304]{1,0:T(8,128)(2,1)S(1)}, bf16[2304,2304]{1,0:T(8,128)(2,1)}, u32[]{:S(2)}) copy-start(bf16[2304,2304]{1,0:T(8,128)(2,1)} %all-gather.7.cloned.1.call-done) | copy-start | bytes 31850500
  228.3 9.9 %collective-permute-start.18 = (bf16[64,2304]{1,0:T(8,128)(2,1)S(1)}, bf16[64,2304]{1,0:T(8,128)(2,1)S(1)}, u32[]{:S(2)}, u32[]{:S(2)}) collective-permute-start(bf16[64,2304]{1,0:T(8,128)(2,1)S(1)} %get-tuple-element.114), channel_id=1, source_target_pairs={{0,1},{1,0},{2,3},{3,2},{4,5},{5,4},{6,7},{7,6},{8,9},{9,8},{10,11... | collective-permute-start | bytes 884744 | tf_op jit(solution)/shard_map/ppermute | solution.py:62
  229.9 19.0 %collective-permute-start.17 = (bf16[64,2304]{1,0:T(8,128)(2,1)S(1)}, bf16[64,2304]{1,0:T(8,128)(2,1)S(1)}, u32[]{:S(2)}, u32[]{:S(2)}) collective-permute-start(bf16[64,2304]{1,0:T(8,128)(2,1)S(1)} %get-tuple-element.115), channel_id=1, source_target_pairs={{0,1},{1,0},{2,3},{3,2},{4,5},{5,4},{6,7},{7,6},{8,9},{9,8},{10,11... | collective-permute-start | bytes 884744 | tf_op jit(solution)/shard_map/ppermute | solution.py:62
  238.3 15.1 %collective-permute-start.19 = (bf16[64,2304]{1,0:T(8,128)(2,1)S(1)}, bf16[64,2304]{1,0:T(8,128)(2,1)S(1)}, u32[]{:S(2)}, u32[]{:S(2)}) collective-permute-start(bf16[64,2304]{1,0:T(8,128)(2,1)S(1)} %add_convert_fusion.3), channel_id=1, source_target_pairs={{0,2},{1,3},{2,0},{3,1},{4,6},{5,7},{6,4},{7,5},{8,10},{9,11},{10,... | collective-permute-start | bytes 884744 | tf_op jit(solution)/shard_map/ppermute | solution.py:62
  254.1 16.3 %collective-permute-start.20 = (bf16[64,2304]{1,0:T(8,128)(2,1)S(1)}, bf16[64,2304]{1,0:T(8,128)(2,1)S(1)}, u32[]{:S(2)}, u32[]{:S(2)}) collective-permute-start(bf16[64,2304]{1,0:T(8,128)(2,1)S(1)} %get-tuple-element.65.second_ref), channel_id=1, source_target_pairs={{0,1},{1,0},{2,3},{3,2},{4,5},{5,4},{6,7},{7,6},{8,9},{9,8},{10,11... | collective-permute-start | bytes 884744 | tf_op jit(solution)/shard_map/ppermute | solution.py:62
  254.7 14.2 %collective-permute-start.21 = (bf16[64,2304]{1,0:T(8,128)(2,1)S(1)}, bf16[64,2304]{1,0:T(8,128)(2,1)S(1)}, u32[]{:S(2)}, u32[]{:S(2)}) collective-permute-start(bf16[64,2304]{1,0:T(8,128)(2,1)S(1)} %get-tuple-element.65.second_ref), channel_id=1, source_target_pairs={{0,2},{1,3},{2,0},{3,1},{4,6},{5,7},{6,4},{7,5},{8,10},{9,11},{10,... | collective-permute-start | bytes 884744 | tf_op jit(solution)/shard_map/ppermute | solution.py:62
  268.8 6.7 %collective-permute-start.22 = (bf16[64,2304]{1,0:T(8,128)(2,1)S(1)}, bf16[64,2304]{1,0:T(8,128)(2,1)S(1)}, u32[]{:S(2)}, u32[]{:S(2)}) collective-permute-start(bf16[64,2304]{1,0:T(8,128)(2,1)S(1)} %collective-permute-done.21), channel_id=1, source_target_pairs={{0,1},{1,0},{2,3},{3,2},{4,5},{5,4},{6,7},{7,6},{8,9},{9,8},{10,11... | collective-permute-start | bytes 884744 | tf_op jit(solution)/shard_map/ppermute | solution.py:62
  282.7 32.1 %copy-start.16 = (bf16[64,2304]{1,0:T(8,128)(2,1)S(1)}, bf16[64,2304]{1,0:T(8,128)(2,1)}, u32[]{:S(2)}) copy-start(bf16[64,2304]{1,0:T(8,128)(2,1)} %copy-done.15) | copy-start | bytes 884740
  282.7 32.1 %copy-start.28 = (bf16[64,2304]{1,0:T(8,128)(2,1)S(1)}, bf16[64,2304]{1,0:T(8,128)(2,1)}, u32[]{:S(2)}) copy-start(bf16[64,2304]{1,0:T(8,128)(2,1)} %copy-done.27) | copy-start | bytes 884740
  282.7 16.3 %collective-permute-start.23 = (bf16[64,2304]{1,0:T(8,128)(2,1)}, bf16[64,2304]{1,0:T(8,128)(2,1)S(1)}, u32[]{:S(2)}, u32[]{:S(2)}) collective-permute-start(bf16[64,2304]{1,0:T(8,128)(2,1)} %copy-done.29), channel_id=1, source_target_pairs={{0,1},{1,0},{2,3},{3,2},{4,5},{5,4},{6,7},{7,6},{8,9},{9,8},{10,11... | collective-permute-start | bytes 884744 | tf_op jit(solution)/shard_map/ppermute | solution.py:62
  284.3 15.8 %collective-permute-start.24 = (bf16[64,2304]{1,0:T(8,128)(2,1)}, bf16[64,2304]{1,0:T(8,128)(2,1)S(1)}, u32[]{:S(2)}, u32[]{:S(2)}) collective-permute-start(bf16[64,2304]{1,0:T(8,128)(2,1)} %copy-done.29), channel_id=1, source_target_pairs={{0,2},{1,3},{2,0},{3,1},{4,6},{5,7},{6,4},{7,5},{8,10},{9,11},{10,... | collective-permute-start | bytes 884744 | tf_op jit(solution)/shard_map/ppermute | solution.py:62
  300.9 13.1 %collective-permute-start.26 = (bf16[64,2304]{1,0:T(8,128)(2,1)S(1)}, bf16[64,2304]{1,0:T(8,128)(2,1)S(1)}, u32[]{:S(2)}, u32[]{:S(2)}) collective-permute-start(bf16[64,2304]{1,0:T(8,128)(2,1)S(1)} %get-tuple-element.112), channel_id=1, source_target_pairs={{0,1},{1,0},{2,3},{3,2},{4,5},{5,4},{6,7},{7,6},{8,9},{9,8},{10,11... | collective-permute-start | bytes 884744 | tf_op jit(solution)/shard_map/ppermute | solution.py:62
  301.2 18.9 %collective-permute-start.25 = (bf16[64,2304]{1,0:T(8,128)(2,1)}, bf16[64,2304]{1,0:T(8,128)(2,1)}, u32[]{:S(2)}, u32[]{:S(2)}) collective-permute-start(bf16[64,2304]{1,0:T(8,128)(2,1)} %get-tuple-element.113), channel_id=1, source_target_pairs={{0,1},{1,0},{2,3},{3,2},{4,5},{5,4},{6,7},{7,6},{8,9},{9,8},{10,11... | collective-permute-start | bytes 884744 | tf_op jit(solution)/shard_map/ppermute | solution.py:62
  314.8 10.7 %collective-permute-start.27 = (bf16[64,2304]{1,0:T(8,128)(2,1)}, bf16[64,2304]{1,0:T(8,128)(2,1)}, u32[]{:S(2)}, u32[]{:S(2)}) collective-permute-start(bf16[64,2304]{1,0:T(8,128)(2,1)} %add_convert_fusion.2), channel_id=1, source_target_pairs={{0,2},{1,3},{2,0},{3,1},{4,6},{5,7},{6,4},{7,5},{8,10},{9,11},{10,... | collective-permute-start | bytes 884744 | tf_op jit(solution)/shard_map/ppermute | solution.py:62
  315.9 47.2 %all-to-all-start = ((bf16[8,64,576]{2,1,0:T(8,128)(2,1)}), bf16[8,64,576]{2,1,0:T(8,128)(2,1)}, u32[]{:S(2)}, u32[]{:S(2)}) async-start(bf16[8,64,576]{2,1,0:T(8,128)(2,1)} %copy-done.5), calls=%async_computation | async-start | bytes 1310720 | tf_op jit(solution)/shard_map/all_to_all | solution.py:546
  320.1 167.9 %reduce-scatter.2.cloned.1.call-start = ((), (), s32[]{:S(2)}) async-start(), calls=%async_computation.6 | async-start | bytes 7962624 | tf_op jit(solution)/shard_map/reduce_scatter | solution.py:408
  331.7 13.5 %collective-permute-start.28 = (bf16[64,2304]{1,0:T(8,128)(2,1)S(1)}, bf16[64,2304]{1,0:T(8,128)(2,1)S(1)}, u32[]{:S(2)}, u32[]{:S(2)}) collective-permute-start(bf16[64,2304]{1,0:T(8,128)(2,1)S(1)} %get-tuple-element.69), channel_id=1, source_target_pairs={{0,1},{1,0},{2,3},{3,2},{4,5},{5,4},{6,7},{7,6},{8,9},{9,8},{10,11... | collective-permute-start | bytes 884744 | tf_op jit(solution)/shard_map/ppermute | solution.py:62
  331.8 13.4 %collective-permute-start.29 = (bf16[64,2304]{1,0:T(8,128)(2,1)S(1)}, bf16[64,2304]{1,0:T(8,128)(2,1)S(1)}, u32[]{:S(2)}, u32[]{:S(2)}) collective-permute-start(bf16[64,2304]{1,0:T(8,128)(2,1)S(1)} %get-tuple-element.69), channel_id=1, source_target_pairs={{0,2},{1,3},{2,0},{3,1},{4,6},{5,7},{6,4},{7,5},{8,10},{9,11},{10,... | collective-permute-start | bytes 884744 | tf_op jit(solution)/shard_map/ppermute | solution.py:62
  345.2 6.7 %collective-permute-start.30 = (bf16[64,2304]{1,0:T(8,128)(2,1)S(1)}, bf16[64,2304]{1,0:T(8,128)(2,1)S(1)}, u32[]{:S(2)}, u32[]{:S(2)}) collective-permute-start(bf16[64,2304]{1,0:T(8,128)(2,1)S(1)} %collective-permute-done.29), channel_id=1, source_target_pairs={{0,1},{1,0},{2,3},{3,2},{4,5},{5,4},{6,7},{7,6},{8,9},{9,8},{10,11... | collective-permute-start | bytes 884744 | tf_op jit(solution)/shard_map/ppermute | solution.py:62
  364.5 4.2 collective-permute-start.31
  364.6 15.4 %collective-permute-start.32 = (bf16[64,2304]{1,0:T(8,128)(2,1)}, bf16[64,2304]{1,0:T(8,128)(2,1)S(1)}, u32[]{:S(2)}, u32[]{:S(2)}) collective-permute-start(bf16[64,2304]{1,0:T(8,128)(2,1)} %copy-done.65), channel_id=1, source_target_pairs={{0,1},{1,0},{2,3},{3,2},{4,5},{5,4},{6,7},{7,6},{8,9},{9,8},{10,11... | collective-permute-start | bytes 884744 | tf_op jit(solution)/shard_map/ppermute | solution.py:62
  365.2 33.1 %collective-permute-start.38 = (bf16[8,64,576]{2,1,0:T(8,128)(2,1)}, bf16[8,64,576]{2,1,0:T(8,128)(2,1)}, u32[]{:S(2)}, u32[]{:S(2)}) collective-permute-start(bf16[8,64,576]{2,1,0:T(8,128)(2,1)} %all-to-all-done), channel_id=1, source_target_pairs={{0,2},{1,3},{2,0},{3,1},{4,6},{5,7},{6,4},{7,5},{8,10},{9,11},{10,... | collective-permute-start | bytes 1769480 | tf_op jit(solution)/shard_map/ppermute | solution.py:62
  369.1 15.9 %collective-permute-start.35 = (bf16[256,512]{1,0:T(8,128)(2,1)S(1)}, bf16[256,512]{1,0:T(8,128)(2,1)S(1)}, u32[]{:S(2)}, u32[]{:S(2)}) collective-permute-start(bf16[256,512]{1,0:T(8,128)(2,1)S(1)} %get-tuple-element.131), channel_id=1, source_target_pairs={{0,24},{4,28},{8,16},{12,20},{16,8},{20,12},{24,0},{28,4},{1,25},{... | collective-permute-start | bytes 786440 | tf_op jit(solution)/shard_map/ppermute | solution.py:62
  372.3 18.9 %collective-permute-start.34 = (bf16[256,512]{1,0:T(8,128)(2,1)S(1)}, bf16[256,512]{1,0:T(8,128)(2,1)S(1)}, u32[]{:S(2)}, u32[]{:S(2)}) collective-permute-start(bf16[256,512]{1,0:T(8,128)(2,1)S(1)} %get-tuple-element.132), channel_id=1, source_target_pairs={{0,16},{4,20},{8,24},{12,28},{16,0},{20,4},{24,8},{28,12},{1,17},{... | collective-permute-start | bytes 786440 | tf_op jit(solution)/shard_map/ppermute | solution.py:62
  372.4 24.0 %collective-permute-start.33 = (bf16[256,512]{1,0:T(8,128)(2,1)S(1)}, bf16[256,512]{1,0:T(8,128)(2,1)S(1)}, u32[]{:S(2)}, u32[]{:S(2)}) collective-permute-start(bf16[256,512]{1,0:T(8,128)(2,1)S(1)} %get-tuple-element.133), channel_id=1, source_target_pairs={{0,8},{4,12},{8,0},{12,4},{16,24},{20,28},{24,16},{28,20},{1,9},{5... | collective-permute-start | bytes 786440 | tf_op jit(solution)/shard_map/ppermute | solution.py:62
  373.5 27.5 %copy-start.2 = (bf16[256,2304]{1,0:T(8,128)(2,1)S(1)}, bf16[256,2304]{1,0:T(8,128)(2,1)}, u32[]{:S(2)}) copy-start(bf16[256,2304]{1,0:T(8,128)(2,1)} %copy-done.1) | copy-start | bytes 3538948
  380.0 40.3 %collective-permute-start.37 = (bf16[8,64,576]{2,1,0:T(8,128)(2,1)}, bf16[8,64,576]{2,1,0:T(8,128)(2,1)}, u32[]{:S(2)}, u32[]{:S(2)}) collective-permute-start(bf16[8,64,576]{2,1,0:T(8,128)(2,1)} %all-to-all-done), channel_id=1, source_target_pairs={{0,1},{1,0},{2,3},{3,2},{4,5},{5,4},{6,7},{7,6},{8,9},{9,8},{10,11... | collective-permute-start | bytes 1769480 | tf_op jit(solution)/shard_map/ppermute | solution.py:62
  398.3 22.0 %collective-permute-start.39 = (bf16[8,64,576]{2,1,0:T(8,128)(2,1)}, bf16[8,64,576]{2,1,0:T(8,128)(2,1)}, u32[]{:S(2)}, u32[]{:S(2)}) collective-permute-start(bf16[8,64,576]{2,1,0:T(8,128)(2,1)} %collective-permute-done.38), channel_id=1, source_target_pairs={{0,1},{1,0},{2,3},{3,2},{4,5},{5,4},{6,7},{7,6},{8,9},{9,8},{10,11... | collective-permute-start | bytes 1769480 | tf_op jit(solution)/shard_map/ppermute | solution.py:62
  413.1 28.1 %collective-permute-start.36 = (bf16[64,2304]{1,0:T(8,128)(2,1)S(1)}, bf16[64,2304]{1,0:T(8,128)(2,1)S(1)}, u32[]{:S(2)}, u32[]{:S(2)}) collective-permute-start(bf16[64,2304]{1,0:T(8,128)(2,1)S(1)} %get-tuple-element.111), channel_id=1, source_target_pairs={{0,1},{1,0},{2,3},{3,2},{4,5},{5,4},{6,7},{7,6},{8,9},{9,8},{10,11... | collective-permute-start | bytes 884744 | tf_op jit(solution)/shard_map/ppermute | solution.py:62
  423.2 8.4 %collective-permute-start.40 = (bf16[64,2304]{1,0:T(8,128)(2,1)S(1)}, bf16[64,2304]{1,0:T(8,128)(2,1)S(1)}, u32[]{:S(2)}, u32[]{:S(2)}) collective-permute-start(bf16[64,2304]{1,0:T(8,128)(2,1)S(1)} %get-tuple-element.110), channel_id=1, source_target_pairs={{0,1},{1,0},{2,3},{3,2},{4,5},{5,4},{6,7},{7,6},{8,9},{9,8},{10,11... | collective-permute-start | bytes 884744 | tf_op jit(solution)/shard_map/ppermute | solution.py:62
  431.7 14.7 %collective-permute-start.41 = (bf16[64,2304]{1,0:T(8,128)(2,1)S(1)}, bf16[64,2304]{1,0:T(8,128)(2,1)S(1)}, u32[]{:S(2)}, u32[]{:S(2)}) collective-permute-start(bf16[64,2304]{1,0:T(8,128)(2,1)S(1)} %add_convert_fusion.1), channel_id=1, source_target_pairs={{0,2},{1,3},{2,0},{3,1},{4,6},{5,7},{6,4},{7,5},{8,10},{9,11},{10,... | collective-permute-start | bytes 884744 | tf_op jit(solution)/shard_map/ppermute | solution.py:62
  447.3 14.6 %collective-permute-start.44 = (bf16[64,2304]{1,0:T(8,128)(2,1)S(1)}, bf16[64,2304]{1,0:T(8,128)(2,1)S(1)}, u32[]{:S(2)}, u32[]{:S(2)}) collective-permute-start(bf16[64,2304]{1,0:T(8,128)(2,1)S(1)} %get-tuple-element.89), channel_id=1, source_target_pairs={{0,1},{1,0},{2,3},{3,2},{4,5},{5,4},{6,7},{7,6},{8,9},{9,8},{10,11... | collective-permute-start | bytes 884744 | tf_op jit(solution)/shard_map/ppermute | solution.py:62
  447.4 15.8 %collective-permute-start.42 = (bf16[64,2304]{1,0:T(8,128)(2,1)S(1)}, bf16[64,2304]{1,0:T(8,128)(2,1)S(1)}, u32[]{:S(2)}, u32[]{:S(2)}) collective-permute-start(bf16[64,2304]{1,0:T(8,128)(2,1)S(1)} %get-tuple-element.89), channel_id=1, source_target_pairs={{0,2},{1,3},{2,0},{3,1},{4,6},{5,7},{6,4},{7,5},{8,10},{9,11},{10,... | collective-permute-start | bytes 884744 | tf_op jit(solution)/shard_map/ppermute | solution.py:62
  462.0 1.6 collective-permute-start.45
  463.3 21.9 %collective-permute-start.43 = (bf16[64,2304]{1,0:T(8,128)(2,1)S(1)}, bf16[64,2304]{1,0:T(8,128)(2,1)S(1)}, u32[]{:S(2)}, u32[]{:S(2)}) collective-permute-start(bf16[64,2304]{1,0:T(8,128)(2,1)S(1)} %collective-permute-done.42), channel_id=1, source_target_pairs={{0,1},{1,0},{2,3},{3,2},{4,5},{5,4},{6,7},{7,6},{8,9},{9,8},{10,11... | collective-permute-start | bytes 884744 | tf_op jit(solution)/shard_map/ppermute | solution.py:62
  463.6 12.5 %collective-permute-start.48 = (f32[3,288]{1,0:T(4,128)S(1)}, f32[3,288]{1,0:T(4,128)S(1)}, u32[]{:S(2)}, u32[]{:S(2)}) collective-permute-start(f32[3,288]{1,0:T(4,128)S(1)} %get-tuple-element.157), channel_id=1, source_target_pairs={{0,24},{4,28},{8,16},{12,20},{16,8},{20,12},{24,0},{28,4},{1,25},{... | collective-permute-start | bytes 10376 | tf_op jit(solution)/shard_map/ppermute | solution.py:62
  466.8 9.4 %collective-permute-start.47 = (f32[3,288]{1,0:T(4,128)S(1)}, f32[3,288]{1,0:T(4,128)S(1)}, u32[]{:S(2)}, u32[]{:S(2)}) collective-permute-start(f32[3,288]{1,0:T(4,128)S(1)} %get-tuple-element.158), channel_id=1, source_target_pairs={{0,16},{4,20},{8,24},{12,28},{16,0},{20,4},{24,8},{28,12},{1,17},{... | collective-permute-start | bytes 10376 | tf_op jit(solution)/shard_map/ppermute | solution.py:62
  466.9 9.3 %collective-permute-start.46 = (f32[3,288]{1,0:T(4,128)S(1)}, f32[3,288]{1,0:T(4,128)S(1)}, u32[]{:S(2)}, u32[]{:S(2)}) collective-permute-start(f32[3,288]{1,0:T(4,128)S(1)} %get-tuple-element.156), channel_id=1, source_target_pairs={{0,8},{4,12},{8,0},{12,4},{16,24},{20,28},{24,16},{28,20},{1,9},{5... | collective-permute-start | bytes 10376 | tf_op jit(solution)/shard_map/ppermute | solution.py:62
  476.2 3.7 collective-permute-start.49
  479.9 4.6 collective-permute-start.50
  (84 other events, 671.5 us)
Sparse Core Ops, SparseCore 0:
  10.8 144.1 all-gather.4
  156.9 63.8 all-gather.6
  223.2 58.8 all-gather.8
  284.4 116.5 all-gather.10
  408.1 65.7 reduce-scatter.1

commit v5 on v4

--- a/solution.py
+++ b/solution.py
@@ -678,9 +678,8 @@
     token_pieces, _, _ = layer_gather(own_grad)
     if gather_factors:
         grad_w_up = contract(after(ffn_cols, own_grad), all_both[:, ffn_width:], 0, 0)
-        grad_w_down = contract(after(down_cols, token_pieces[2], grad_w_up), all_hidden, 0, 0)
     grad_tokens = rows_out(token_pieces).astype(f32)
-    output = rows_out([after(output_pieces[0], token_pieces[3])] + output_pieces[1:])
+    output = rows_out([after(output_pieces[0], own_grad)] + output_pieces[1:])
 
     third_gain = norm_ffn_in.astype(f32)
     gain_third = (
@@ -698,8 +697,10 @@
     for index, step in ((1, far_a), (2, far_b), (3, far_a | far_b)):
         own_gain = own_gain + swap(gain_sum[:, index * shard : (index + 1) * shard], step)
     own_gain = jnp.concatenate([own_gain, gain_third], axis=0)
-    for bit in [1 << index for index in range(layers.bit_length() - 1)]:
-        own_gain = own_gain + swap(own_gain, bit, "tp")
+    for piece in [swap(own_gain, step, "tp") for step in range(1, layers)]:
+        own_gain = own_gain + piece
+    if gather_factors:
+        grad_w_down = contract(after(down_cols, own_gain), all_hidden, 0, 0)
     return (
         output,
         grad_tokens,

time: 507 us -> 503 us (level)
    ppermute x51 -> x52, waiting for transfers between devices: 226 us -> 222 us  [swap(): lax.ppermute(value, axis, [(index, index ^ bit) for index in range(count)])]
    ppermute x51 -> x52, starting transfers between devices: 60.2 us -> 59.9 us  [swap(): lax.ppermute(value, axis, [(index, index ^ bit) for index in range(count)])]
  transfers between devices with their start and end apart: 57 -> 58, of which waited for: 38 -> 40; matrix products, arithmetic and copies ran while one was open for 26% -> 26% of each run, Pallas kernels for 6% -> 6%
where the time goes in v5:
time: 503 us; the launch traced here: 493 us
  waiting for transfers between devices  231 us (46%)
  matrix products  76.1 us (15%)
  starting transfers between devices  64.3 us (13%)
  local copies, waits for them, and re-layouts  49 us (10%)
  other arithmetic  28.7 us (6%)
  Pallas kernels  28.4 us (6%)
  between operations  15.8 us (3%)
    ppermute x52, waiting for transfers between devices, swap(): lax.ppermute(value, axis, [(index, index ^ bit) for index in range(count)])  222 us
    ppermute x52, starting transfers between devices, swap(): lax.ppermute(value, axis, [(index, index ^ bit) for index in range(count)])  59.9 us
    dot_general x9, matrix products, contract(): lax.dot_general(first_operand, second_operand, (((first_dim,), (second_di...  52 us
    unnamed x200, local copies, waits for them, and re-layouts  26.2 us
    dot_general x6, matrix products, product(): return jnp.dot(first_operand, second_operand, preferred_element_type=f32)  24 us
    pallas_call x4, Pallas kernels, on_own_rows(): pl.pallas_call(kernel, grid=(1,), in_specs=[SCALARS, wide] + [WHOLE] * (2...  17.1 us
  transfers between devices with their start and end apart: 58, of which 40 were waited for; matrix products, arithmetic and copies ran while one was open for 26% of the time, Pallas kernels for 6%

profile of v5, /device:TPU:0, one launch (start us, length us, event | category | flops | bytes accessed | tf_op | source)
XLA Modules:
  0.0 492.9 jit_solution(1831996548058850029)
XLA Ops:
  7.2 3.4 pad_maximum_fusion
  11.9 3.0 collective-permute-start.1
  19.3 27.2 %collective-permute-done.1 = bf16[304,1536]{1,0:T(8,128)(2,1)S(1)} collective-permute-done((bf16[304,1536]{1,0:T(8,128)(2,1)S(1)}, bf16[304,1536]{1,0:T(8,128)(2,1)S(1)}, u32[]{:S(2)}, u32[]{:S(2)}) %collective-permute-start.1) | collective-permute-done | bytes 933920 | tf_op jit(solution)/shard_map/ppermute | solution.py:62
  47.9 3.3 collective-permute-done
  53.3 15.4 %collective-permute-done.4 = bf16[144,1536]{1,0:T(8,128)(2,1)S(1)} collective-permute-done((bf16[144,1536]{1,0:T(8,128)(2,1)S(1)}, bf16[144,1536]{1,0:T(8,128)(2,1)S(1)}, u32[]{:S(2)}, u32[]{:S(2)}) %collective-permute-start.4) | collective-permute-done | bytes 442400 | tf_op jit(solution)/shard_map/ppermute | solution.py:62
  76.0 2.5 collective-permute-start.2
  82.0 2.6 concatenate.109
  86.6 3.0 fusion.12
  89.6 2.6 fusion.18
  97.4 11.5 %collective-permute-done.7 = bf16[256,512]{1,0:T(8,128)(2,1)S(1)} collective-permute-done((bf16[256,512]{1,0:T(8,128)(2,1)}, bf16[256,512]{1,0:T(8,128)(2,1)S(1)}, u32[]{:S(2)}, u32[]{:S(2)}) %collective-permute-start.7) | collective-permute-done | bytes 262176 | tf_op jit(solution)/shard_map/ppermute | solution.py:62
  108.9 4.0 collective-permute-done.8
  112.9 6.9 %collective-permute-done.9 = bf16[256,512]{1,0:T(8,128)(2,1)} collective-permute-done((bf16[256,512]{1,0:T(8,128)(2,1)}, bf16[256,512]{1,0:T(8,128)(2,1)}, u32[]{:S(2)}, u32[]{:S(2)}) %collective-permute-start.9) | collective-permute-done | bytes 262176 | tf_op jit(solution)/shard_map/ppermute | solution.py:62
  127.7 2.7 attend.1
  130.5 2.2 convolution_convert_fusion.5
  141.7 4.0 collective-permute-done.12
  146.8 2.5 collective-permute-start.13
  150.5 4.9 %collective-permute-done.11.one_ref = bf16[64,2304]{1,0:T(8,128)(2,1)S(1)} collective-permute-done((bf16[64,2304]{1,0:T(8,128)(2,1)}, bf16[64,2304]{1,0:T(8,128)(2,1)S(1)}, u32[]{:S(2)}, u32[]{:S(2)}) %collective-permute-start.11) | collective-permute-done | bytes 294944 | tf_op jit(solution)/shard_map/ppermute | solution.py:62
  155.4 6.8 %collective-permute-done.13.two_ref = bf16[64,2304]{1,0:T(8,128)(2,1)S(1)} collective-permute-done((bf16[64,2304]{1,0:T(8,128)(2,1)S(1)}, bf16[64,2304]{1,0:T(8,128)(2,1)S(1)}, u32[]{:S(2)}, u32[]{:S(2)}) %collective-permute-start.13) | collective-permute-done | bytes 294944 | tf_op jit(solution)/shard_map/ppermute | solution.py:62
  162.2 13.4 %residual.1 = (f32[64,2304]{1,0:T(8,128)S(1)}, f32[64,2304]{1,0:T(8,128)S(1)}, bf16[64,2304]{1,0:T(8,128)(2,1)S(1)}) custom-call(s32[1]{0:T(128)} %bitcast.me_ref, bf16[256,2304]{1,0:T(8,128)(2,1)S(1)} %pad_maximum_fusion.3.part_ref, bf16[64,2304]{1,0:T(8,128)(2,1)S(1)} %collective-permute-done.11.one_ref, ...), custom_call_target="tpu_custom_call" | custom-call | tf_op jit(solution)/shard_map/residual/pallas_call | solution.py:335
  177.3 4.2 collective-permute-start.14
  181.5 10.3 %collective-permute-done.15 = bf16[64,2304]{1,0:T(8,128)(2,1)S(1)} collective-permute-done((bf16[64,2304]{1,0:T(8,128)(2,1)S(1)}, bf16[64,2304]{1,0:T(8,128)(2,1)S(1)}, u32[]{:S(2)}, u32[]{:S(2)}) %collective-permute-start.15) | collective-permute-done | bytes 294944 | tf_op jit(solution)/shard_map/ppermute | solution.py:62
  192.6 6.5 %collective-permute-done.16 = bf16[64,2304]{1,0:T(8,128)(2,1)} collective-permute-done((bf16[64,2304]{1,0:T(8,128)(2,1)S(1)}, bf16[64,2304]{1,0:T(8,128)(2,1)}, u32[]{:S(2)}, u32[]{:S(2)}) %collective-permute-start.16) | collective-permute-done | bytes 294944 | tf_op jit(solution)/shard_map/ppermute | solution.py:62
  199.1 10.4 %fusion.22 = f32[256,4608]{1,0:T(8,128)S(1)} fusion(bf16[2304,4608]{1,0:T(8,128)(2,1)} %all-gather.5.cloned.1.call-done, bf16[64,2304]{1,0:T(8,128)(2,1)} %collective-permute-done.16, bf16[64,2304]{1,0:T(8,128)(2,1)S(1)} %collective-permute-done.15, bf16[64,2304]{1,0:T(8,128)(2,1)} %copy-done.86, bf16[64,2304]{1,0:T(8,128)(2,1)S(1)} %get-tuple-element.62.first_ref), kind=kOutput, calls=%fused_computation.55 | convolution fusion | flops 5440536576 | bytes 27131904 | tf_op jit(solution)/shard_map/dot_general | solution.py:44
  209.6 2.2 copy-done.42
  213.6 6.1 %all-gather.7.cloned.1.call-done = bf16[2304,2304]{1,0:T(8,128)(2,1)} async-done(((bf16[288,2304]{1,0:T(8,128)(2,1)}), bf16[2304,2304]{1,0:T(8,128)(2,1)}) %all-gather.7.cloned.1.call-update) | async-done | bytes 10616848 | tf_op jit(solution)/shard_map/all_gather | solution.py:312
  219.7 7.5 %convolution_convert_fusion.1.part_ref = bf16[256,2304]{1,0:T(8,128)(2,1)S(1)} fusion(bf16[256,2304]{1,0:T(8,128)(2,1)} %multiply_convert_fusion.1, bf16[2304,2304]{1,0:T(8,128)(2,1)} %all-gather.7.cloned.1.call-done), kind=kOutput, calls=%fused_computation.5 | convolution fusion | flops 2718498816 | bytes 12976128 | tf_op jit(solution)/shard_map/dot_general | solution.py:48
  229.3 7.8 %collective-permute-done.18 = bf16[64,2304]{1,0:T(8,128)(2,1)S(1)} collective-permute-done((bf16[64,2304]{1,0:T(8,128)(2,1)S(1)}, bf16[64,2304]{1,0:T(8,128)(2,1)S(1)}, u32[]{:S(2)}, u32[]{:S(2)}) %collective-permute-start.18) | collective-permute-done | bytes 294944 | tf_op jit(solution)/shard_map/ppermute | solution.py:62
  237.2 2.5 collective-permute-start.19
  240.7 7.1 %collective-permute-done.17.one_ref = bf16[64,2304]{1,0:T(8,128)(2,1)S(1)} collective-permute-done((bf16[64,2304]{1,0:T(8,128)(2,1)S(1)}, bf16[64,2304]{1,0:T(8,128)(2,1)S(1)}, u32[]{:S(2)}, u32[]{:S(2)}) %collective-permute-start.17) | collective-permute-done | bytes 294944 | tf_op jit(solution)/shard_map/ppermute | solution.py:62
  247.8 4.5 collective-permute-done.19.two_ref
  253.6 3.4 collective-permute-start.21
  257.0 10.8 %collective-permute-done.21 = bf16[64,2304]{1,0:T(8,128)(2,1)S(1)} collective-permute-done((bf16[64,2304]{1,0:T(8,128)(2,1)S(1)}, bf16[64,2304]{1,0:T(8,128)(2,1)S(1)}, u32[]{:S(2)}, u32[]{:S(2)}) %collective-permute-start.21) | collective-permute-done | bytes 294944 | tf_op jit(solution)/shard_map/ppermute | solution.py:62
  269.3 5.2 %collective-permute-done.22 = bf16[64,2304]{1,0:T(8,128)(2,1)S(1)} collective-permute-done((bf16[64,2304]{1,0:T(8,128)(2,1)S(1)}, bf16[64,2304]{1,0:T(8,128)(2,1)S(1)}, u32[]{:S(2)}, u32[]{:S(2)}) %collective-permute-start.22) | collective-permute-done | bytes 294944 | tf_op jit(solution)/shard_map/ppermute | solution.py:62
  274.5 4.1 fusion.10
  283.2 2.1 collective-permute-start.24
  285.3 12.7 %convolution_convert_fusion.part_ref = bf16[256,2304]{1,0:T(8,128)(2,1)S(1)} fusion(bf16[2304,4608]{1,0:T(8,128)(2,1)} %all-gather.5.cloned.1.call-done, bf16[256,2304]{1,0:T(8,128)(2,1)} %copy-done.57, bf16[256,2304]{1,0:T(8,128)(2,1)} %copy-done.56), kind=kOutput, calls=%fused_computation.4 | convolution fusion | flops 5441126400 | bytes 24772608 | tf_op jit(solution)/shard_map/dot_general | solution.py:48
  301.8 11.1 %collective-permute-done.26 = bf16[64,2304]{1,0:T(8,128)(2,1)S(1)} collective-permute-done((bf16[64,2304]{1,0:T(8,128)(2,1)S(1)}, bf16[64,2304]{1,0:T(8,128)(2,1)S(1)}, u32[]{:S(2)}, u32[]{:S(2)}) %collective-permute-start.26) | collective-permute-done | bytes 294944 | tf_op jit(solution)/shard_map/ppermute | solution.py:62
  314.8 4.2 all-to-all-start
  319.1 5.3 %collective-permute-done.27.two_ref = bf16[64,2304]{1,0:T(8,128)(2,1)} collective-permute-done((bf16[64,2304]{1,0:T(8,128)(2,1)}, bf16[64,2304]{1,0:T(8,128)(2,1)}, u32[]{:S(2)}, u32[]{:S(2)}) %collective-permute-start.27) | collective-permute-done | bytes 294944 | tf_op jit(solution)/shard_map/ppermute | solution.py:62
  332.8 11.4 %collective-permute-done.29 = bf16[64,2304]{1,0:T(8,128)(2,1)S(1)} collective-permute-done((bf16[64,2304]{1,0:T(8,128)(2,1)S(1)}, bf16[64,2304]{1,0:T(8,128)(2,1)S(1)}, u32[]{:S(2)}, u32[]{:S(2)}) %collective-permute-start.29) | collective-permute-done | bytes 294944 | tf_op jit(solution)/shard_map/ppermute | solution.py:62
  344.2 6.7 %collective-permute-done.30 = bf16[64,2304]{1,0:T(8,128)(2,1)S(1)} collective-permute-done((bf16[64,2304]{1,0:T(8,128)(2,1)S(1)}, bf16[64,2304]{1,0:T(8,128)(2,1)S(1)}, u32[]{:S(2)}, u32[]{:S(2)}) %collective-permute-start.30) | collective-permute-done | bytes 294944 | tf_op jit(solution)/shard_map/ppermute | solution.py:62
  350.9 2.2 fusion.30
  355.1 5.6 %attend_back.1 = (f32[512,256]{1,0:T(8,128)S(1)}, bf16[2048,512]{1,0:T(8,128)(2,1)S(1)}) custom-call(bf16[512,256]{1,0:T(8,128)(2,1)S(1)} %bitcast.55, bf16[512,256]{1,0:T(8,128)(2,1)S(1)} %bitcast.56, f32[512,256]{1,0:T(8,128)S(1)} %copy-done.26, f32[512,1]{1,0:T(8,128)S(1)} %copy-done.32, ...), custom_call_target="tpu_custom_call" | custom-call | tf_op jit(solution)/shard_map/attend_back/pallas_call | solution.py:162
  364.1 3.5 collective-permute-start.38
  368.0 3.3 collective-permute-start.35
  372.5 6.4 %collective-permute-done.32 = bf16[64,2304]{1,0:T(8,128)(2,1)S(1)} collective-permute-done((bf16[64,2304]{1,0:T(8,128)(2,1)}, bf16[64,2304]{1,0:T(8,128)(2,1)S(1)}, u32[]{:S(2)}, u32[]{:S(2)}) %collective-permute-start.32) | collective-permute-done | bytes 294944 | tf_op jit(solution)/shard_map/ppermute | solution.py:62
  379.0 5.0 %collective-permute-done.35 = bf16[256,512]{1,0:T(8,128)(2,1)S(1)} collective-permute-done((bf16[256,512]{1,0:T(8,128)(2,1)S(1)}, bf16[256,512]{1,0:T(8,128)(2,1)S(1)}, u32[]{:S(2)}, u32[]{:S(2)}) %collective-permute-start.35) | collective-permute-done | bytes 262176 | tf_op jit(solution)/shard_map/ppermute | solution.py:62
  384.0 6.1 %collective-permute-done.34 = bf16[256,512]{1,0:T(8,128)(2,1)S(1)} collective-permute-done((bf16[256,512]{1,0:T(8,128)(2,1)S(1)}, bf16[256,512]{1,0:T(8,128)(2,1)S(1)}, u32[]{:S(2)}, u32[]{:S(2)}) %collective-permute-start.34) | collective-permute-done | bytes 262176 | tf_op jit(solution)/shard_map/ppermute | solution.py:62
  390.1 5.3 %collective-permute-done.33 = bf16[256,512]{1,0:T(8,128)(2,1)S(1)} collective-permute-done((bf16[256,512]{1,0:T(8,128)(2,1)S(1)}, bf16[256,512]{1,0:T(8,128)(2,1)S(1)}, u32[]{:S(2)}, u32[]{:S(2)}) %collective-permute-start.33) | collective-permute-done | bytes 262176 | tf_op jit(solution)/shard_map/ppermute | solution.py:62
  401.2 2.7 attn_products.1
  403.9 3.0 copy-done
  406.9 2.5 convolution_convert_fusion.3
  409.4 2.5 convolution_convert_fusion.2
  413.6 5.6 %collective-permute-done.39 = bf16[8,64,576]{2,1,0:T(8,128)(2,1)} collective-permute-done((bf16[8,64,576]{2,1,0:T(8,128)(2,1)}, bf16[8,64,576]{2,1,0:T(8,128)(2,1)}, u32[]{:S(2)}, u32[]{:S(2)}) %collective-permute-start.39) | collective-permute-done | bytes 589856 | tf_op jit(solution)/shard_map/ppermute | solution.py:62
  419.2 2.6 pad_maximum_fusion.1
  424.2 6.3 %collective-permute-done.40 = bf16[64,2304]{1,0:T(8,128)(2,1)S(1)} collective-permute-done((bf16[64,2304]{1,0:T(8,128)(2,1)S(1)}, bf16[64,2304]{1,0:T(8,128)(2,1)S(1)}, u32[]{:S(2)}, u32[]{:S(2)}) %collective-permute-start.40) | collective-permute-done | bytes 294944 | tf_op jit(solution)/shard_map/ppermute | solution.py:62
  431.7 8.3 %fusion.2 = f32[288,2304]{1,0:T(8,128)} fusion(bf16[2048,288]{1,0:T(8,128)(2,1)S(1)} %get-tuple-element.91, bf16[2048,4608]{1,0:T(8,128)(2,1)} %all-gather.11.cloned.1.call-done), kind=kOutput, calls=%fused_computation.2 | convolution fusion | flops 2717908992 | bytes 13271040 | tf_op jit(solution)/shard_map/dot_general | solution.py:48
  440.0 5.3 %collective-permute-done.41.two_ref = bf16[64,2304]{1,0:T(8,128)(2,1)S(1)} collective-permute-done((bf16[64,2304]{1,0:T(8,128)(2,1)S(1)}, bf16[64,2304]{1,0:T(8,128)(2,1)S(1)}, u32[]{:S(2)}, u32[]{:S(2)}) %collective-permute-start.41) | collective-permute-done | bytes 294944 | tf_op jit(solution)/shard_map/ppermute | solution.py:62
  446.4 2.4 collective-permute-start.43
  451.4 9.8 %add_reduce_fusion = (f32[288]{0:T(512)S(1)}, f32[288,2304]{1,0:T(8,128)}) fusion(bf16[288,2304]{1,0:T(8,128)(2,1)S(1)} %copy-done.50, f32[288,2304]{1,0:T(8,128)} %fusion.2, bf16[288,2304]{1,0:T(8,128)(2,1)S(1)} %copy-done.51, bf16[2048,288]{1,0:T(8,128)(2,1)S(1)} %copy-done.49, bf16[2048,4608]{1,0:T(8,128)(2,1)} %all-gather.11.cloned.1.call-done), kind=kOutput, calls=%fused_computation.9 | convolution fusion | flops 2721890048 | bytes 18580608 | tf_op jit(solution)/shard_map/dot_general | solution.py:48
  462.6 3.1 collective-permute-start.48
  471.6 2.6 collective-permute-start.49
  476.2 4.6 fusion.80
  483.0 2.3 fusion.77
  (388 shorter events, 108.2 us)
Async XLA Ops:
  7.2 192.0 %all-gather.5.cloned.1.call-start = ((), (), s32[]{:S(2)}) async-start(), calls=%async_computation.2 | async-start | bytes 23887872 | tf_op jit(solution)/shard_map/all_gather | solution.py:312
  10.7 209.0 %all-gather.7.cloned.1.call-start = ((), (), s32[]{:S(2)}) async-start(), calls=%async_computation.3 | async-start | bytes 11943936 | tf_op jit(solution)/shard_map/all_gather | solution.py:312
  11.5 270.1 %all-gather.9.cloned.1.call-start = ((), (), s32[]{:S(2)}) async-start(), calls=%async_computation.4 | async-start | bytes 10616832 | tf_op jit(solution)/shard_map/all_gather | solution.py:312
  11.9 34.6 %collective-permute-start.1 = (bf16[304,1536]{1,0:T(8,128)(2,1)S(1)}, bf16[304,1536]{1,0:T(8,128)(2,1)S(1)}, u32[]{:S(2)}, u32[]{:S(2)}) collective-permute-start(bf16[304,1536]{1,0:T(8,128)(2,1)S(1)} %fusion.35), channel_id=1, source_target_pairs={{0,16},{4,20},{8,24},{12,28},{16,0},{20,4},{24,8},{28,12},{1,17},{... | collective-permute-start | bytes 2801672 | tf_op jit(solution)/shard_map/ppermute | solution.py:62
  14.9 36.3 %collective-permute-start = (bf16[304,1536]{1,0:T(8,128)(2,1)S(1)}, bf16[304,1536]{1,0:T(8,128)(2,1)S(1)}, u32[]{:S(2)}, u32[]{:S(2)}) collective-permute-start(bf16[304,1536]{1,0:T(8,128)(2,1)S(1)} %fusion.35), channel_id=1, source_target_pairs={{0,8},{4,12},{8,0},{12,4},{16,24},{20,28},{24,16},{28,20},{1,9},{5... | collective-permute-start | bytes 2801672 | tf_op jit(solution)/shard_map/ppermute | solution.py:62
  46.5 22.2 %collective-permute-start.4 = (bf16[144,1536]{1,0:T(8,128)(2,1)S(1)}, bf16[144,1536]{1,0:T(8,128)(2,1)S(1)}, u32[]{:S(2)}, u32[]{:S(2)}) collective-permute-start(bf16[144,1536]{1,0:T(8,128)(2,1)S(1)} %slice.300), channel_id=1, source_target_pairs={{0,8},{4,12},{8,0},{12,4},{16,24},{20,28},{24,16},{28,20},{1,9},{5... | collective-permute-start | bytes 1327112 | tf_op jit(solution)/shard_map/ppermute | solution.py:62
  51.2 20.3 %collective-permute-start.5 = (bf16[144,1536]{1,0:T(8,128)(2,1)S(1)}, bf16[144,1536]{1,0:T(8,128)(2,1)S(1)}, u32[]{:S(2)}, u32[]{:S(2)}) collective-permute-start(bf16[144,1536]{1,0:T(8,128)(2,1)S(1)} %slice.301), channel_id=1, source_target_pairs={{0,16},{4,20},{8,24},{12,28},{16,0},{20,4},{24,8},{28,12},{1,17},{... | collective-permute-start | bytes 1327112 | tf_op jit(solution)/shard_map/ppermute | solution.py:62
  72.3 14.3 %collective-permute-start.6 = (bf16[1152,1536]{1,0:T(8,128)(2,1)}, bf16[1152,1536]{1,0:T(8,128)(2,1)}, u32[]{:S(2)}, u32[]{:S(2)}) collective-permute-start(bf16[1152,1536]{1,0:T(8,128)(2,1)} %constant_dynamic-update-slice_fusion), channel_id=1, source_target_pairs={{0,4},{4,0},{8,12},{12,8},{16,20},{20,16},{24,28},{28,24},{1,5},{5... | collective-permute-start | bytes 10616840 | tf_op jit(solution)/shard_map/ppermute | solution.py:62
  76.0 4.1 collective-permute-start.2
  80.8 3.9 collective-permute-start.3
  93.2 30.1 %slice-start = ((f32[256,1024]{1,0:T(8,128)}), f32[256,512]{1,0:T(8,128)S(1)}, s32[]{:S(2)}) async-start(f32[256,1024]{1,0:T(8,128)} %copy-done.45), calls=%async_computation.7 | async-start | bytes 1048576 | tf_op jit(solution)/shard_map/slice | solution.py:479
  93.9 15.0 %collective-permute-start.7 = (bf16[256,512]{1,0:T(8,128)(2,1)}, bf16[256,512]{1,0:T(8,128)(2,1)S(1)}, u32[]{:S(2)}, u32[]{:S(2)}) collective-permute-start(bf16[256,512]{1,0:T(8,128)(2,1)} %get-tuple-element.146), channel_id=1, source_target_pairs={{0,8},{4,12},{8,0},{12,4},{16,24},{20,28},{24,16},{28,20},{1,9},{5... | collective-permute-start | bytes 786440 | tf_op jit(solution)/shard_map/ppermute | solution.py:62
  95.9 16.9 %collective-permute-start.8 = (bf16[256,512]{1,0:T(8,128)(2,1)}, bf16[256,512]{1,0:T(8,128)(2,1)S(1)}, u32[]{:S(2)}, u32[]{:S(2)}) collective-permute-start(bf16[256,512]{1,0:T(8,128)(2,1)} %get-tuple-element.146), channel_id=1, source_target_pairs={{0,16},{4,20},{8,24},{12,28},{16,0},{20,4},{24,8},{28,12},{1,17},{... | collective-permute-start | bytes 786440 | tf_op jit(solution)/shard_map/ppermute | solution.py:62
  96.0 23.8 %collective-permute-start.9 = (bf16[256,512]{1,0:T(8,128)(2,1)}, bf16[256,512]{1,0:T(8,128)(2,1)}, u32[]{:S(2)}, u32[]{:S(2)}) collective-permute-start(bf16[256,512]{1,0:T(8,128)(2,1)} %get-tuple-element.146), channel_id=1, source_target_pairs={{0,24},{4,28},{8,16},{12,20},{16,8},{20,12},{24,0},{28,4},{1,25},{... | collective-permute-start | bytes 786440 | tf_op jit(solution)/shard_map/ppermute | solution.py:62
  121.8 4.6 collective-permute-start.10
  135.6 10.1 %collective-permute-start.12 = (bf16[64,2304]{1,0:T(8,128)(2,1)}, bf16[64,2304]{1,0:T(8,128)(2,1)}, u32[]{:S(2)}, u32[]{:S(2)}) collective-permute-start(bf16[64,2304]{1,0:T(8,128)(2,1)} %get-tuple-element.116), channel_id=1, source_target_pairs={{0,1},{1,0},{2,3},{3,2},{4,5},{5,4},{6,7},{7,6},{8,9},{9,8},{10,11... | collective-permute-start | bytes 884744 | tf_op jit(solution)/shard_map/ppermute | solution.py:62
  141.1 34.6 %copy-start.17 = (f32[4,2304]{1,0:T(4,128)}, f32[4,2304]{1,0:T(4,128)S(1)}, u32[]{:S(2)}) copy-start(f32[4,2304]{1,0:T(4,128)S(1)} %convert_element_type.132.refs_1_.refs_2_.refs_3_) | copy-start | bytes 110596
  141.1 14.3 %collective-permute-start.11 = (bf16[64,2304]{1,0:T(8,128)(2,1)}, bf16[64,2304]{1,0:T(8,128)(2,1)S(1)}, u32[]{:S(2)}, u32[]{:S(2)}) collective-permute-start(bf16[64,2304]{1,0:T(8,128)(2,1)} %get-tuple-element.117), channel_id=1, source_target_pairs={{0,1},{1,0},{2,3},{3,2},{4,5},{5,4},{6,7},{7,6},{8,9},{9,8},{10,11... | collective-permute-start | bytes 884744 | tf_op jit(solution)/shard_map/ppermute | solution.py:62
  146.8 15.4 %collective-permute-start.13 = (bf16[64,2304]{1,0:T(8,128)(2,1)S(1)}, bf16[64,2304]{1,0:T(8,128)(2,1)S(1)}, u32[]{:S(2)}, u32[]{:S(2)}) collective-permute-start(bf16[64,2304]{1,0:T(8,128)(2,1)S(1)} %add_convert_fusion.4), channel_id=1, source_target_pairs={{0,2},{1,3},{2,0},{3,1},{4,6},{5,7},{6,4},{7,5},{8,10},{9,11},{10,... | collective-permute-start | bytes 884744 | tf_op jit(solution)/shard_map/ppermute | solution.py:62
  177.3 32.3 %copy-start.27 = (bf16[64,2304]{1,0:T(8,128)(2,1)}, bf16[64,2304]{1,0:T(8,128)(2,1)S(1)}, u32[]{:S(2)}) copy-start(bf16[64,2304]{1,0:T(8,128)(2,1)S(1)} %get-tuple-element.62.first_ref) | copy-start | bytes 884740
  177.3 14.5 %collective-permute-start.15 = (bf16[64,2304]{1,0:T(8,128)(2,1)S(1)}, bf16[64,2304]{1,0:T(8,128)(2,1)S(1)}, u32[]{:S(2)}, u32[]{:S(2)}) collective-permute-start(bf16[64,2304]{1,0:T(8,128)(2,1)S(1)} %get-tuple-element.62.first_ref), channel_id=1, source_target_pairs={{0,2},{1,3},{2,0},{3,1},{4,6},{5,7},{6,4},{7,5},{8,10},{9,11},{10,... | collective-permute-start | bytes 884744 | tf_op jit(solution)/shard_map/ppermute | solution.py:62
  177.3 14.6 %collective-permute-start.14 = (bf16[64,2304]{1,0:T(8,128)(2,1)S(1)}, bf16[64,2304]{1,0:T(8,128)(2,1)S(1)}, u32[]{:S(2)}, u32[]{:S(2)}) collective-permute-start(bf16[64,2304]{1,0:T(8,128)(2,1)S(1)} %get-tuple-element.62.first_ref), channel_id=1, source_target_pairs={{0,1},{1,0},{2,3},{3,2},{4,5},{5,4},{6,7},{7,6},{8,9},{9,8},{10,11... | collective-permute-start | bytes 884744 | tf_op jit(solution)/shard_map/ppermute | solution.py:62
  191.8 7.3 %collective-permute-start.16 = (bf16[64,2304]{1,0:T(8,128)(2,1)S(1)}, bf16[64,2304]{1,0:T(8,128)(2,1)}, u32[]{:S(2)}, u32[]{:S(2)}) collective-permute-start(bf16[64,2304]{1,0:T(8,128)(2,1)S(1)} %collective-permute-done.15), channel_id=1, source_target_pairs={{0,1},{1,0},{2,3},{3,2},{4,5},{5,4},{6,7},{7,6},{8,9},{9,8},{10,11... | collective-permute-start | bytes 884744 | tf_op jit(solution)/shard_map/ppermute | solution.py:62
  213.6 186.3 %all-gather.11.cloned.1.call-start = ((), (), s32[]{:S(2)}) async-start(), calls=%async_computation.5 | async-start | bytes 21233664 | tf_op jit(solution)/shard_map/all_gather | solution.py:312
  219.7 54.8 %copy-start.85 = (bf16[2304,2304]{1,0:T(8,128)(2,1)S(1)}, bf16[2304,2304]{1,0:T(8,128)(2,1)}, u32[]{:S(2)}) copy-start(bf16[2304,2304]{1,0:T(8,128)(2,1)} %all-gather.7.cloned.1.call-done) | copy-start | bytes 31850500
  227.2 9.9 %collective-permute-start.18 = (bf16[64,2304]{1,0:T(8,128)(2,1)S(1)}, bf16[64,2304]{1,0:T(8,128)(2,1)S(1)}, u32[]{:S(2)}, u32[]{:S(2)}) collective-permute-start(bf16[64,2304]{1,0:T(8,128)(2,1)S(1)} %get-tuple-element.114), channel_id=1, source_target_pairs={{0,1},{1,0},{2,3},{3,2},{4,5},{5,4},{6,7},{7,6},{8,9},{9,8},{10,11... | collective-permute-start | bytes 884744 | tf_op jit(solution)/shard_map/ppermute | solution.py:62
  228.8 19.0 %collective-permute-start.17 = (bf16[64,2304]{1,0:T(8,128)(2,1)S(1)}, bf16[64,2304]{1,0:T(8,128)(2,1)S(1)}, u32[]{:S(2)}, u32[]{:S(2)}) collective-permute-start(bf16[64,2304]{1,0:T(8,128)(2,1)S(1)} %get-tuple-element.115), channel_id=1, source_target_pairs={{0,1},{1,0},{2,3},{3,2},{4,5},{5,4},{6,7},{7,6},{8,9},{9,8},{10,11... | collective-permute-start | bytes 884744 | tf_op jit(solution)/shard_map/ppermute | solution.py:62
  237.2 15.1 %collective-permute-start.19 = (bf16[64,2304]{1,0:T(8,128)(2,1)S(1)}, bf16[64,2304]{1,0:T(8,128)(2,1)S(1)}, u32[]{:S(2)}, u32[]{:S(2)}) collective-permute-start(bf16[64,2304]{1,0:T(8,128)(2,1)S(1)} %add_convert_fusion.3), channel_id=1, source_target_pairs={{0,2},{1,3},{2,0},{3,1},{4,6},{5,7},{6,4},{7,5},{8,10},{9,11},{10,... | collective-permute-start | bytes 884744 | tf_op jit(solution)/shard_map/ppermute | solution.py:62
  253.0 16.3 %collective-permute-start.20 = (bf16[64,2304]{1,0:T(8,128)(2,1)S(1)}, bf16[64,2304]{1,0:T(8,128)(2,1)S(1)}, u32[]{:S(2)}, u32[]{:S(2)}) collective-permute-start(bf16[64,2304]{1,0:T(8,128)(2,1)S(1)} %get-tuple-element.65.second_ref), channel_id=1, source_target_pairs={{0,1},{1,0},{2,3},{3,2},{4,5},{5,4},{6,7},{7,6},{8,9},{9,8},{10,11... | collective-permute-start | bytes 884744 | tf_op jit(solution)/shard_map/ppermute | solution.py:62
  253.6 14.2 %collective-permute-start.21 = (bf16[64,2304]{1,0:T(8,128)(2,1)S(1)}, bf16[64,2304]{1,0:T(8,128)(2,1)S(1)}, u32[]{:S(2)}, u32[]{:S(2)}) collective-permute-start(bf16[64,2304]{1,0:T(8,128)(2,1)S(1)} %get-tuple-element.65.second_ref), channel_id=1, source_target_pairs={{0,2},{1,3},{2,0},{3,1},{4,6},{5,7},{6,4},{7,5},{8,10},{9,11},{10,... | collective-permute-start | bytes 884744 | tf_op jit(solution)/shard_map/ppermute | solution.py:62
  267.8 6.7 %collective-permute-start.22 = (bf16[64,2304]{1,0:T(8,128)(2,1)S(1)}, bf16[64,2304]{1,0:T(8,128)(2,1)S(1)}, u32[]{:S(2)}, u32[]{:S(2)}) collective-permute-start(bf16[64,2304]{1,0:T(8,128)(2,1)S(1)} %collective-permute-done.21), channel_id=1, source_target_pairs={{0,1},{1,0},{2,3},{3,2},{4,5},{5,4},{6,7},{7,6},{8,9},{9,8},{10,11... | collective-permute-start | bytes 884744 | tf_op jit(solution)/shard_map/ppermute | solution.py:62
  281.6 32.1 %copy-start.16 = (bf16[64,2304]{1,0:T(8,128)(2,1)S(1)}, bf16[64,2304]{1,0:T(8,128)(2,1)}, u32[]{:S(2)}) copy-start(bf16[64,2304]{1,0:T(8,128)(2,1)} %copy-done.15) | copy-start | bytes 884740
  281.6 32.1 %copy-start.28 = (bf16[64,2304]{1,0:T(8,128)(2,1)S(1)}, bf16[64,2304]{1,0:T(8,128)(2,1)}, u32[]{:S(2)}) copy-start(bf16[64,2304]{1,0:T(8,128)(2,1)} %copy-done.27) | copy-start | bytes 884740
  281.6 16.3 %collective-permute-start.23 = (bf16[64,2304]{1,0:T(8,128)(2,1)}, bf16[64,2304]{1,0:T(8,128)(2,1)S(1)}, u32[]{:S(2)}, u32[]{:S(2)}) collective-permute-start(bf16[64,2304]{1,0:T(8,128)(2,1)} %copy-done.29), channel_id=1, source_target_pairs={{0,1},{1,0},{2,3},{3,2},{4,5},{5,4},{6,7},{7,6},{8,9},{9,8},{10,11... | collective-permute-start | bytes 884744 | tf_op jit(solution)/shard_map/ppermute | solution.py:62
  283.2 15.8 %collective-permute-start.24 = (bf16[64,2304]{1,0:T(8,128)(2,1)}, bf16[64,2304]{1,0:T(8,128)(2,1)S(1)}, u32[]{:S(2)}, u32[]{:S(2)}) collective-permute-start(bf16[64,2304]{1,0:T(8,128)(2,1)} %copy-done.29), channel_id=1, source_target_pairs={{0,2},{1,3},{2,0},{3,1},{4,6},{5,7},{6,4},{7,5},{8,10},{9,11},{10,... | collective-permute-start | bytes 884744 | tf_op jit(solution)/shard_map/ppermute | solution.py:62
  299.8 13.1 %collective-permute-start.26 = (bf16[64,2304]{1,0:T(8,128)(2,1)S(1)}, bf16[64,2304]{1,0:T(8,128)(2,1)S(1)}, u32[]{:S(2)}, u32[]{:S(2)}) collective-permute-start(bf16[64,2304]{1,0:T(8,128)(2,1)S(1)} %get-tuple-element.112), channel_id=1, source_target_pairs={{0,1},{1,0},{2,3},{3,2},{4,5},{5,4},{6,7},{7,6},{8,9},{9,8},{10,11... | collective-permute-start | bytes 884744 | tf_op jit(solution)/shard_map/ppermute | solution.py:62
  300.2 18.9 %collective-permute-start.25 = (bf16[64,2304]{1,0:T(8,128)(2,1)}, bf16[64,2304]{1,0:T(8,128)(2,1)}, u32[]{:S(2)}, u32[]{:S(2)}) collective-permute-start(bf16[64,2304]{1,0:T(8,128)(2,1)} %get-tuple-element.113), channel_id=1, source_target_pairs={{0,1},{1,0},{2,3},{3,2},{4,5},{5,4},{6,7},{7,6},{8,9},{9,8},{10,11... | collective-permute-start | bytes 884744 | tf_op jit(solution)/shard_map/ppermute | solution.py:62
  313.7 10.7 %collective-permute-start.27 = (bf16[64,2304]{1,0:T(8,128)(2,1)}, bf16[64,2304]{1,0:T(8,128)(2,1)}, u32[]{:S(2)}, u32[]{:S(2)}) collective-permute-start(bf16[64,2304]{1,0:T(8,128)(2,1)} %add_convert_fusion.2), channel_id=1, source_target_pairs={{0,2},{1,3},{2,0},{3,1},{4,6},{5,7},{6,4},{7,5},{8,10},{9,11},{10,... | collective-permute-start | bytes 884744 | tf_op jit(solution)/shard_map/ppermute | solution.py:62
  314.8 47.2 %all-to-all-start = ((bf16[8,64,576]{2,1,0:T(8,128)(2,1)}), bf16[8,64,576]{2,1,0:T(8,128)(2,1)}, u32[]{:S(2)}, u32[]{:S(2)}) async-start(bf16[8,64,576]{2,1,0:T(8,128)(2,1)} %copy-done.5), calls=%async_computation | async-start | bytes 1310720 | tf_op jit(solution)/shard_map/all_to_all | solution.py:546
  319.0 164.0 %reduce-scatter.2.cloned.1.call-start = ((), (), s32[]{:S(2)}) async-start(), calls=%async_computation.6 | async-start | bytes 7962624 | tf_op jit(solution)/shard_map/reduce_scatter | solution.py:408
  330.7 13.5 %collective-permute-start.28 = (bf16[64,2304]{1,0:T(8,128)(2,1)S(1)}, bf16[64,2304]{1,0:T(8,128)(2,1)S(1)}, u32[]{:S(2)}, u32[]{:S(2)}) collective-permute-start(bf16[64,2304]{1,0:T(8,128)(2,1)S(1)} %get-tuple-element.69), channel_id=1, source_target_pairs={{0,1},{1,0},{2,3},{3,2},{4,5},{5,4},{6,7},{7,6},{8,9},{9,8},{10,11... | collective-permute-start | bytes 884744 | tf_op jit(solution)/shard_map/ppermute | solution.py:62
  330.7 13.4 %collective-permute-start.29 = (bf16[64,2304]{1,0:T(8,128)(2,1)S(1)}, bf16[64,2304]{1,0:T(8,128)(2,1)S(1)}, u32[]{:S(2)}, u32[]{:S(2)}) collective-permute-start(bf16[64,2304]{1,0:T(8,128)(2,1)S(1)} %get-tuple-element.69), channel_id=1, source_target_pairs={{0,2},{1,3},{2,0},{3,1},{4,6},{5,7},{6,4},{7,5},{8,10},{9,11},{10,... | collective-permute-start | bytes 884744 | tf_op jit(solution)/shard_map/ppermute | solution.py:62
  344.2 6.7 %collective-permute-start.30 = (bf16[64,2304]{1,0:T(8,128)(2,1)S(1)}, bf16[64,2304]{1,0:T(8,128)(2,1)S(1)}, u32[]{:S(2)}, u32[]{:S(2)}) collective-permute-start(bf16[64,2304]{1,0:T(8,128)(2,1)S(1)} %collective-permute-done.29), channel_id=1, source_target_pairs={{0,1},{1,0},{2,3},{3,2},{4,5},{5,4},{6,7},{7,6},{8,9},{9,8},{10,11... | collective-permute-start | bytes 884744 | tf_op jit(solution)/shard_map/ppermute | solution.py:62
  363.5 4.1 collective-permute-start.31
  363.6 15.4 %collective-permute-start.32 = (bf16[64,2304]{1,0:T(8,128)(2,1)}, bf16[64,2304]{1,0:T(8,128)(2,1)S(1)}, u32[]{:S(2)}, u32[]{:S(2)}) collective-permute-start(bf16[64,2304]{1,0:T(8,128)(2,1)} %copy-done.67), channel_id=1, source_target_pairs={{0,1},{1,0},{2,3},{3,2},{4,5},{5,4},{6,7},{7,6},{8,9},{9,8},{10,11... | collective-permute-start | bytes 884744 | tf_op jit(solution)/shard_map/ppermute | solution.py:62
  364.1 33.0 %collective-permute-start.38 = (bf16[8,64,576]{2,1,0:T(8,128)(2,1)}, bf16[8,64,576]{2,1,0:T(8,128)(2,1)}, u32[]{:S(2)}, u32[]{:S(2)}) collective-permute-start(bf16[8,64,576]{2,1,0:T(8,128)(2,1)} %all-to-all-done), channel_id=1, source_target_pairs={{0,2},{1,3},{2,0},{3,1},{4,6},{5,7},{6,4},{7,5},{8,10},{9,11},{10,... | collective-permute-start | bytes 1769480 | tf_op jit(solution)/shard_map/ppermute | solution.py:62
  368.0 16.0 %collective-permute-start.35 = (bf16[256,512]{1,0:T(8,128)(2,1)S(1)}, bf16[256,512]{1,0:T(8,128)(2,1)S(1)}, u32[]{:S(2)}, u32[]{:S(2)}) collective-permute-start(bf16[256,512]{1,0:T(8,128)(2,1)S(1)} %get-tuple-element.131), channel_id=1, source_target_pairs={{0,24},{4,28},{8,16},{12,20},{16,8},{20,12},{24,0},{28,4},{1,25},{... | collective-permute-start | bytes 786440 | tf_op jit(solution)/shard_map/ppermute | solution.py:62
  371.2 18.9 %collective-permute-start.34 = (bf16[256,512]{1,0:T(8,128)(2,1)S(1)}, bf16[256,512]{1,0:T(8,128)(2,1)S(1)}, u32[]{:S(2)}, u32[]{:S(2)}) collective-permute-start(bf16[256,512]{1,0:T(8,128)(2,1)S(1)} %get-tuple-element.132), channel_id=1, source_target_pairs={{0,16},{4,20},{8,24},{12,28},{16,0},{20,4},{24,8},{28,12},{1,17},{... | collective-permute-start | bytes 786440 | tf_op jit(solution)/shard_map/ppermute | solution.py:62
  371.4 24.0 %collective-permute-start.33 = (bf16[256,512]{1,0:T(8,128)(2,1)S(1)}, bf16[256,512]{1,0:T(8,128)(2,1)S(1)}, u32[]{:S(2)}, u32[]{:S(2)}) collective-permute-start(bf16[256,512]{1,0:T(8,128)(2,1)S(1)} %get-tuple-element.133), channel_id=1, source_target_pairs={{0,8},{4,12},{8,0},{12,4},{16,24},{20,28},{24,16},{28,20},{1,9},{5... | collective-permute-start | bytes 786440 | tf_op jit(solution)/shard_map/ppermute | solution.py:62
  378.9 40.3 %collective-permute-start.37 = (bf16[8,64,576]{2,1,0:T(8,128)(2,1)}, bf16[8,64,576]{2,1,0:T(8,128)(2,1)}, u32[]{:S(2)}, u32[]{:S(2)}) collective-permute-start(bf16[8,64,576]{2,1,0:T(8,128)(2,1)} %all-to-all-done), channel_id=1, source_target_pairs={{0,1},{1,0},{2,3},{3,2},{4,5},{5,4},{6,7},{7,6},{8,9},{9,8},{10,11... | collective-permute-start | bytes 1769480 | tf_op jit(solution)/shard_map/ppermute | solution.py:62
  397.2 22.1 %collective-permute-start.39 = (bf16[8,64,576]{2,1,0:T(8,128)(2,1)}, bf16[8,64,576]{2,1,0:T(8,128)(2,1)}, u32[]{:S(2)}, u32[]{:S(2)}) collective-permute-start(bf16[8,64,576]{2,1,0:T(8,128)(2,1)} %collective-permute-done.38), channel_id=1, source_target_pairs={{0,1},{1,0},{2,3},{3,2},{4,5},{5,4},{6,7},{7,6},{8,9},{9,8},{10,11... | collective-permute-start | bytes 1769480 | tf_op jit(solution)/shard_map/ppermute | solution.py:62
  412.0 28.0 %collective-permute-start.36 = (bf16[64,2304]{1,0:T(8,128)(2,1)S(1)}, bf16[64,2304]{1,0:T(8,128)(2,1)S(1)}, u32[]{:S(2)}, u32[]{:S(2)}) collective-permute-start(bf16[64,2304]{1,0:T(8,128)(2,1)S(1)} %get-tuple-element.111), channel_id=1, source_target_pairs={{0,1},{1,0},{2,3},{3,2},{4,5},{5,4},{6,7},{7,6},{8,9},{9,8},{10,11... | collective-permute-start | bytes 884744 | tf_op jit(solution)/shard_map/ppermute | solution.py:62
  422.1 8.4 %collective-permute-start.40 = (bf16[64,2304]{1,0:T(8,128)(2,1)S(1)}, bf16[64,2304]{1,0:T(8,128)(2,1)S(1)}, u32[]{:S(2)}, u32[]{:S(2)}) collective-permute-start(bf16[64,2304]{1,0:T(8,128)(2,1)S(1)} %get-tuple-element.110), channel_id=1, source_target_pairs={{0,1},{1,0},{2,3},{3,2},{4,5},{5,4},{6,7},{7,6},{8,9},{9,8},{10,11... | collective-permute-start | bytes 884744 | tf_op jit(solution)/shard_map/ppermute | solution.py:62
  430.6 14.7 %collective-permute-start.41 = (bf16[64,2304]{1,0:T(8,128)(2,1)S(1)}, bf16[64,2304]{1,0:T(8,128)(2,1)S(1)}, u32[]{:S(2)}, u32[]{:S(2)}) collective-permute-start(bf16[64,2304]{1,0:T(8,128)(2,1)S(1)} %add_convert_fusion.1), channel_id=1, source_target_pairs={{0,2},{1,3},{2,0},{3,1},{4,6},{5,7},{6,4},{7,5},{8,10},{9,11},{10,... | collective-permute-start | bytes 884744 | tf_op jit(solution)/shard_map/ppermute | solution.py:62
  446.3 14.9 %collective-permute-start.42 = (bf16[64,2304]{1,0:T(8,128)(2,1)S(1)}, bf16[64,2304]{1,0:T(8,128)(2,1)S(1)}, u32[]{:S(2)}, u32[]{:S(2)}) collective-permute-start(bf16[64,2304]{1,0:T(8,128)(2,1)S(1)} %get-tuple-element.89), channel_id=1, source_target_pairs={{0,1},{1,0},{2,3},{3,2},{4,5},{5,4},{6,7},{7,6},{8,9},{9,8},{10,11... | collective-permute-start | bytes 884744 | tf_op jit(solution)/shard_map/ppermute | solution.py:62
  446.4 20.0 %collective-permute-start.43 = (bf16[64,2304]{1,0:T(8,128)(2,1)S(1)}, bf16[64,2304]{1,0:T(8,128)(2,1)S(1)}, u32[]{:S(2)}, u32[]{:S(2)}) collective-permute-start(bf16[64,2304]{1,0:T(8,128)(2,1)S(1)} %get-tuple-element.89), channel_id=1, source_target_pairs={{0,2},{1,3},{2,0},{3,1},{4,6},{5,7},{6,4},{7,5},{8,10},{9,11},{10,... | collective-permute-start | bytes 884744 | tf_op jit(solution)/shard_map/ppermute | solution.py:62
  461.3 1.3 collective-permute-start.45
  462.6 4.9 collective-permute-start.48
  465.8 3.7 collective-permute-start.47
  466.0 3.7 collective-permute-start.46
  466.5 15.0 %collective-permute-start.44 = (bf16[64,2304]{1,0:T(8,128)(2,1)S(1)}, bf16[64,2304]{1,0:T(8,128)(2,1)S(1)}, u32[]{:S(2)}, u32[]{:S(2)}) collective-permute-start(bf16[64,2304]{1,0:T(8,128)(2,1)S(1)} %collective-permute-done.43), channel_id=1, source_target_pairs={{0,1},{1,0},{2,3},{3,2},{4,5},{5,4},{6,7},{7,6},{8,9},{9,8},{10,11... | collective-permute-start | bytes 884744 | tf_op jit(solution)/shard_map/ppermute | solution.py:62
  469.7 5.6 %collective-permute-start.51 = (f32[4,288]{1,0:T(4,128)S(1)}, f32[4,288]{1,0:T(4,128)S(1)}, u32[]{:S(2)}, u32[]{:S(2)}) collective-permute-start(f32[4,288]{1,0:T(4,128)S(1)} %pad_maximum_fusion.10), channel_id=1, source_target_pairs={{0,3},{1,2},{2,1},{3,0},{4,7},{5,6},{6,5},{7,4},{8,11},{9,10},{10,... | collective-permute-start | bytes 13832 | tf_op jit(solution)/shard_map/ppermute | solution.py:62
  471.6 4.5 collective-permute-start.50
  471.6 4.5 collective-permute-start.49
  (85 other events, 691.3 us)
Sparse Core Ops, SparseCore 0:
  10.8 143.0 all-gather.4
  155.8 63.8 all-gather.6
  222.2 58.8 all-gather.8
  283.3 116.5 all-gather.10
  407.0 65.7 reduce-scatter.1

commit v6 on v5

--- a/solution.py
+++ b/solution.py
@@ -133,7 +133,7 @@
 
 
 def attend_back_kernel(
-    query_ref, grad_ref, out_ref, log_ref, pair_ref, place_ref, key_place_ref, query_grad_ref, pair_grad_ref, delta_ref
+    steps, query_ref, grad_ref, out_ref, log_ref, pair_ref, place_ref, key_place_ref, query_grad_ref, own_ref, near_ref, delta_ref
 ):
     @pl.when(pl.program_id(0) == 0)
     def _():
@@ -145,11 +145,21 @@
     part = jnp.tanh(contract(queries, keys, 1, 1) * (1.0 / SOFT_CAP))
     visible = key_place_ref[...] <= place_ref[...]
     probs = jnp.where(visible, jnp.exp(SOFT_CAP * part - log_ref[...]), 0.0)
-    pair_grad_ref[:, HD:] = contract(probs.astype(bf16), grads, 0, 0).astype(bf16)
+    value_grad = contract(probs.astype(bf16), grads, 0, 0).astype(bf16)
     slope = contract(grads, values, 1, 1) - delta_ref[...]
     score_grad = (probs * slope * (1.0 - part * part)).astype(bf16)
     query_grad_ref[...] += product(score_grad, keys)
-    pair_grad_ref[:, :HD] = contract(score_grad, queries, 0, 0).astype(bf16)
+    key_grad = contract(score_grad, queries, 0, 0).astype(bf16)
+
+    @pl.when(pl.program_id(0) < steps // 2)
+    def _():
+        own_ref[:, :HD] = key_grad
+        own_ref[:, HD:] = value_grad
+
+    @pl.when(pl.program_id(0) >= steps // 2)
+    def _():
+        near_ref[:, :HD] = key_grad
+        near_ref[:, HD:] = value_grad
 
 
 def attend_back(queries, grads, outs, logs, pairs, places, key_places):
@@ -159,12 +169,16 @@
     tall = pl.BlockSpec((rows, HD), fixed)
     column = pl.BlockSpec((rows, 1), fixed)
     moving = pl.BlockSpec((block, 2 * HD), lambda step: (step, 0))
+    steps = key_count // block
+    first = pl.BlockSpec((block, 2 * HD), lambda step: (jnp.minimum(step, steps // 2 - 1), 0))
+    second = pl.BlockSpec((block, 2 * HD), lambda step: (jnp.maximum(step - steps // 2, 0), 0))
+    half = shape_of((key_count // 2, 2 * HD), bf16)
     return pl.pallas_call(
-        attend_back_kernel,
-        grid=(key_count // block,),
+        functools.partial(attend_back_kernel, steps),
+        grid=(steps,),
         in_specs=[tall, tall, tall, column, moving, column, pl.BlockSpec((1, block), lambda step: (0, step))],
-        out_specs=[tall, moving],
-        out_shape=[shape_of((rows, HD), f32), shape_of((key_count, 2 * HD), bf16)],
+        out_specs=[tall, first, second],
+        out_shape=[shape_of((rows, HD), f32), half, half],
         scratch_shapes=[pltpu.VMEM((rows, 1), f32)],
         compiler_params=pltpu.CompilerParams(vmem_limit_bytes=VMEM_BYTES),
         name="attend_back",
@@ -430,7 +444,7 @@
             in_specs=[SCALARS] + [WHOLE] * 4,
             out_specs=WHOLE,
             out_shape=shape_of((width, qkv_width + query_width), bf16),
-            compiler_params=pltpu.CompilerParams(vmem_limit_bytes=VMEM_BYTES),
+            compiler_params=pltpu.CompilerParams(vmem_limit_bytes=56 * 2**20),
             name="attn_products",
         )(me[None], inputs, lin, grads, rows)
 
@@ -592,11 +606,11 @@
     grad_attn = jnp.concatenate(pieces, axis=0)
     grad_rows = times_rows(grad_attn, out_w).astype(bf16)
     grad_heads = grad_rows.reshape(tok_rows, heads_local, HD).transpose(1, 0, 2).reshape(-1, HD)
-    grad_q, pair_grad = attend_back(
+    grad_q, *pair_halves = attend_back(
         query_rows, grad_heads, attn_float, attn_log, pairs, places, key_places
     )
     if gather_factors:
-        pair_grad = after(pair_grad, own_columns)
+        pair_halves = [after(half, own_columns) for half in pair_halves]
         columns_then = after(own_columns, grad_attn)
         if layers == 4:
             column_pieces = [columns_then] + [swap(columns_then, bit, "tp") for bit in (1, 2)]
@@ -604,7 +618,9 @@
             column_pieces, _, _ = layer_gather(columns_then)
     near_rows = 4 * tok_rows
     pair_part = [
-        pair_grad[start : start + near_rows] for start in range(0, key_count, near_rows)
+        half[start : start + near_rows]
+        for half in pair_halves
+        for start in range(0, half.shape[0], near_rows)
     ]
     for bit in reversed(near):
         half = len(pair_part) // 2

time: 503 us -> 504 us (level)
  waiting for transfers between devices: 231 us -> 225 us
    ppermute x52, waiting for transfers between devices: 222 us -> 217 us  [swap(): lax.ppermute(value, axis, [(index, index ^ bit) for index in range(count)])]
    unnamed x200 -> x196, local copies, waits for them, and re-layouts: 26.2 us -> 23.6 us
  transfers between devices with their start and end apart: 58 -> 58, of which waited for: 40 -> 39; matrix products, arithmetic and copies ran while one was open for 26% -> 27% of each run, Pallas kernels for 6% -> 7%
where the time goes in v6:
time: 504 us; the launch traced here: 494 us
  waiting for transfers between devices  225 us (45%)
  matrix products  76.4 us (15%)
  starting transfers between devices  65.6 us (13%)
  local copies, waits for them, and re-layouts  47.4 us (9%)
  Pallas kernels  33.4 us (7%)
  other arithmetic  30.7 us (6%)
  between operations  15.7 us (3%)
    ppermute x52, waiting for transfers between devices, swap(): lax.ppermute(value, axis, [(index, index ^ bit) for index in range(count)])  217 us
    ppermute x52, starting transfers between devices, swap(): lax.ppermute(value, axis, [(index, index ^ bit) for index in range(count)])  61.2 us
    dot_general x9, matrix products, contract(): lax.dot_general(first_operand, second_operand, (((first_dim,), (second_di...  52.4 us
    dot_general x6, matrix products, product(): return jnp.dot(first_operand, second_operand, preferred_element_type=f32)  24 us
    unnamed x196, local copies, waits for them, and re-layouts  23.6 us
    pallas_call x4, Pallas kernels, on_own_rows(): pl.pallas_call(kernel, grid=(1,), in_specs=[SCALARS, wide] + [WHOLE] * (2...  17.1 us
  transfers between devices with their start and end apart: 58, of which 39 were waited for; matrix products, arithmetic and copies ran while one was open for 27% of the time, Pallas kernels for 7%

profile of v6, /device:TPU:0, one launch (start us, length us, event | category | flops | bytes accessed | tf_op | source)
XLA Modules:
  0.0 494.3 jit_solution(8168403889074103036)
XLA Ops:
  7.2 3.4 pad_maximum_fusion
  11.9 3.0 collective-permute-start.1
  19.3 27.3 %collective-permute-done.1 = bf16[304,1536]{1,0:T(8,128)(2,1)S(1)} collective-permute-done((bf16[304,1536]{1,0:T(8,128)(2,1)S(1)}, bf16[304,1536]{1,0:T(8,128)(2,1)S(1)}, u32[]{:S(2)}, u32[]{:S(2)}) %collective-permute-start.1) | collective-permute-done | bytes 933920 | tf_op jit(solution)/shard_map/ppermute | solution.py:62
  47.9 3.3 collective-permute-done
  53.3 15.4 %collective-permute-done.4 = bf16[144,1536]{1,0:T(8,128)(2,1)S(1)} collective-permute-done((bf16[144,1536]{1,0:T(8,128)(2,1)S(1)}, bf16[144,1536]{1,0:T(8,128)(2,1)S(1)}, u32[]{:S(2)}, u32[]{:S(2)}) %collective-permute-start.4) | collective-permute-done | bytes 442400 | tf_op jit(solution)/shard_map/ppermute | solution.py:62
  69.5 2.0 collective-permute-done.5
  76.0 2.5 collective-permute-start.2
  82.0 2.6 concatenate.109
  86.6 3.0 fusion.12
  89.6 2.6 fusion.18
  97.4 11.5 %collective-permute-done.7 = bf16[256,512]{1,0:T(8,128)(2,1)S(1)} collective-permute-done((bf16[256,512]{1,0:T(8,128)(2,1)}, bf16[256,512]{1,0:T(8,128)(2,1)S(1)}, u32[]{:S(2)}, u32[]{:S(2)}) %collective-permute-start.7) | collective-permute-done | bytes 262176 | tf_op jit(solution)/shard_map/ppermute | solution.py:62
  108.8 3.9 collective-permute-done.8
  112.8 7.0 %collective-permute-done.9 = bf16[256,512]{1,0:T(8,128)(2,1)} collective-permute-done((bf16[256,512]{1,0:T(8,128)(2,1)}, bf16[256,512]{1,0:T(8,128)(2,1)}, u32[]{:S(2)}, u32[]{:S(2)}) %collective-permute-start.9) | collective-permute-done | bytes 262176 | tf_op jit(solution)/shard_map/ppermute | solution.py:62
  127.7 2.7 attend.1
  130.5 2.2 convolution_convert_fusion.5
  141.7 4.0 collective-permute-done.12
  146.8 2.5 collective-permute-start.13
  150.5 4.9 collective-permute-done.11.one_ref
  155.4 6.9 %collective-permute-done.13.two_ref = bf16[64,2304]{1,0:T(8,128)(2,1)S(1)} collective-permute-done((bf16[64,2304]{1,0:T(8,128)(2,1)S(1)}, bf16[64,2304]{1,0:T(8,128)(2,1)S(1)}, u32[]{:S(2)}, u32[]{:S(2)}) %collective-permute-start.13) | collective-permute-done | bytes 294944 | tf_op jit(solution)/shard_map/ppermute | solution.py:62
  162.2 13.5 %residual.1 = (f32[64,2304]{1,0:T(8,128)S(1)}, f32[64,2304]{1,0:T(8,128)S(1)}, bf16[64,2304]{1,0:T(8,128)(2,1)S(1)}) custom-call(s32[1]{0:T(128)} %bitcast.me_ref, bf16[256,2304]{1,0:T(8,128)(2,1)S(1)} %pad_maximum_fusion.3.part_ref, bf16[64,2304]{1,0:T(8,128)(2,1)S(1)} %collective-permute-done.11.one_ref, ...), custom_call_target="tpu_custom_call" | custom-call | tf_op jit(solution)/shard_map/residual/pallas_call | solution.py:349
  177.4 4.1 collective-permute-start.14
  181.5 10.4 %collective-permute-done.15 = bf16[64,2304]{1,0:T(8,128)(2,1)S(1)} collective-permute-done((bf16[64,2304]{1,0:T(8,128)(2,1)S(1)}, bf16[64,2304]{1,0:T(8,128)(2,1)S(1)}, u32[]{:S(2)}, u32[]{:S(2)}) %collective-permute-start.15) | collective-permute-done | bytes 294944 | tf_op jit(solution)/shard_map/ppermute | solution.py:62
  192.7 6.7 %collective-permute-done.16 = bf16[64,2304]{1,0:T(8,128)(2,1)} collective-permute-done((bf16[64,2304]{1,0:T(8,128)(2,1)S(1)}, bf16[64,2304]{1,0:T(8,128)(2,1)}, u32[]{:S(2)}, u32[]{:S(2)}) %collective-permute-start.16) | collective-permute-done | bytes 294944 | tf_op jit(solution)/shard_map/ppermute | solution.py:62
  199.4 10.4 %fusion.22 = f32[256,4608]{1,0:T(8,128)S(1)} fusion(bf16[2304,4608]{1,0:T(8,128)(2,1)} %all-gather.5.cloned.1.call-done, bf16[64,2304]{1,0:T(8,128)(2,1)} %collective-permute-done.16, bf16[64,2304]{1,0:T(8,128)(2,1)S(1)} %collective-permute-done.15, bf16[64,2304]{1,0:T(8,128)(2,1)} %copy-done.84, bf16[64,2304]{1,0:T(8,128)(2,1)S(1)} %get-tuple-element.64.first_ref), kind=kOutput, calls=%fused_computation.55 | convolution fusion | flops 5440536576 | bytes 27131904 | tf_op jit(solution)/shard_map/dot_general | solution.py:44
  209.8 2.2 copy-done.37
  213.9 5.8 %all-gather.7.cloned.1.call-done = bf16[2304,2304]{1,0:T(8,128)(2,1)} async-done(((bf16[288,2304]{1,0:T(8,128)(2,1)}), bf16[2304,2304]{1,0:T(8,128)(2,1)}) %all-gather.7.cloned.1.call-update) | async-done | bytes 10616848 | tf_op jit(solution)/shard_map/all_gather | solution.py:326
  219.7 7.5 %convolution_convert_fusion.1.part_ref = bf16[256,2304]{1,0:T(8,128)(2,1)S(1)} fusion(bf16[256,2304]{1,0:T(8,128)(2,1)} %multiply_convert_fusion.1, bf16[2304,2304]{1,0:T(8,128)(2,1)} %all-gather.7.cloned.1.call-done), kind=kOutput, calls=%fused_computation.5 | convolution fusion | flops 2718498816 | bytes 12976128 | tf_op jit(solution)/shard_map/dot_general | solution.py:48
  229.3 7.8 %collective-permute-done.18 = bf16[64,2304]{1,0:T(8,128)(2,1)S(1)} collective-permute-done((bf16[64,2304]{1,0:T(8,128)(2,1)S(1)}, bf16[64,2304]{1,0:T(8,128)(2,1)S(1)}, u32[]{:S(2)}, u32[]{:S(2)}) %collective-permute-start.18) | collective-permute-done | bytes 294944 | tf_op jit(solution)/shard_map/ppermute | solution.py:62
  237.2 2.5 collective-permute-start.19
  240.7 7.1 %collective-permute-done.17.one_ref = bf16[64,2304]{1,0:T(8,128)(2,1)S(1)} collective-permute-done((bf16[64,2304]{1,0:T(8,128)(2,1)S(1)}, bf16[64,2304]{1,0:T(8,128)(2,1)S(1)}, u32[]{:S(2)}, u32[]{:S(2)}) %collective-permute-start.17) | collective-permute-done | bytes 294944 | tf_op jit(solution)/shard_map/ppermute | solution.py:62
  247.8 4.5 collective-permute-done.19.two_ref
  253.6 3.4 collective-permute-start.21
  257.0 10.8 %collective-permute-done.21 = bf16[64,2304]{1,0:T(8,128)(2,1)S(1)} collective-permute-done((bf16[64,2304]{1,0:T(8,128)(2,1)S(1)}, bf16[64,2304]{1,0:T(8,128)(2,1)S(1)}, u32[]{:S(2)}, u32[]{:S(2)}) %collective-permute-start.21) | collective-permute-done | bytes 294944 | tf_op jit(solution)/shard_map/ppermute | solution.py:62
  269.3 5.2 %collective-permute-done.22 = bf16[64,2304]{1,0:T(8,128)(2,1)S(1)} collective-permute-done((bf16[64,2304]{1,0:T(8,128)(2,1)S(1)}, bf16[64,2304]{1,0:T(8,128)(2,1)S(1)}, u32[]{:S(2)}, u32[]{:S(2)}) %collective-permute-start.22) | collective-permute-done | bytes 294944 | tf_op jit(solution)/shard_map/ppermute | solution.py:62
  274.5 4.1 fusion.10
  283.2 2.1 collective-permute-start.24
  285.3 12.7 %convolution_convert_fusion.part_ref = bf16[256,2304]{1,0:T(8,128)(2,1)S(1)} fusion(bf16[2304,4608]{1,0:T(8,128)(2,1)} %all-gather.5.cloned.1.call-done, bf16[256,2304]{1,0:T(8,128)(2,1)} %copy-done.54, bf16[256,2304]{1,0:T(8,128)(2,1)} %copy-done.53), kind=kOutput, calls=%fused_computation.4 | convolution fusion | flops 5441126400 | bytes 24772608 | tf_op jit(solution)/shard_map/dot_general | solution.py:48
  301.8 11.1 %collective-permute-done.26 = bf16[64,2304]{1,0:T(8,128)(2,1)S(1)} collective-permute-done((bf16[64,2304]{1,0:T(8,128)(2,1)S(1)}, bf16[64,2304]{1,0:T(8,128)(2,1)S(1)}, u32[]{:S(2)}, u32[]{:S(2)}) %collective-permute-start.26) | collective-permute-done | bytes 294944 | tf_op jit(solution)/shard_map/ppermute | solution.py:62
  314.8 4.2 all-to-all-start
  319.1 5.3 %collective-permute-done.27.two_ref = bf16[64,2304]{1,0:T(8,128)(2,1)} collective-permute-done((bf16[64,2304]{1,0:T(8,128)(2,1)}, bf16[64,2304]{1,0:T(8,128)(2,1)}, u32[]{:S(2)}, u32[]{:S(2)}) %collective-permute-start.27) | collective-permute-done | bytes 294944 | tf_op jit(solution)/shard_map/ppermute | solution.py:62
  328.6 2.0 residual_back.1
  332.8 11.4 %collective-permute-done.29 = bf16[64,2304]{1,0:T(8,128)(2,1)S(1)} collective-permute-done((bf16[64,2304]{1,0:T(8,128)(2,1)S(1)}, bf16[64,2304]{1,0:T(8,128)(2,1)S(1)}, u32[]{:S(2)}, u32[]{:S(2)}) %collective-permute-start.29) | collective-permute-done | bytes 294944 | tf_op jit(solution)/shard_map/ppermute | solution.py:62
  344.2 6.7 %collective-permute-done.30 = bf16[64,2304]{1,0:T(8,128)(2,1)S(1)} collective-permute-done((bf16[64,2304]{1,0:T(8,128)(2,1)S(1)}, bf16[64,2304]{1,0:T(8,128)(2,1)S(1)}, u32[]{:S(2)}, u32[]{:S(2)}) %collective-permute-start.30) | collective-permute-done | bytes 294944 | tf_op jit(solution)/shard_map/ppermute | solution.py:62
  350.9 2.2 fusion.30
  355.1 5.8 %attend_back.1 = (f32[512,256]{1,0:T(8,128)S(1)}, bf16[1024,512]{1,0:T(8,128)(2,1)S(1)}, bf16[1024,512]{1,0:T(8,128)(2,1)S(1)}) custom-call(bf16[512,256]{1,0:T(8,128)(2,1)S(1)} %bitcast.55, bf16[512,256]{1,0:T(8,128)(2,1)S(1)} %bitcast.56, f32[512,256]{1,0:T(8,128)S(1)} %copy-done.20, f32[512,1]{1,0:T(8,128)S(1)} %copy-done.26, ...), custom_call_target="tpu_custom_call" | custom-call | tf_op jit(solution)/shard_map/attend_back/pallas_call | solution.py:176
  363.4 3.4 collective-permute-start.38
  368.5 3.3 collective-permute-start.35
  373.0 5.1 %collective-permute-done.32 = bf16[64,2304]{1,0:T(8,128)(2,1)S(1)} collective-permute-done((bf16[64,2304]{1,0:T(8,128)(2,1)}, bf16[64,2304]{1,0:T(8,128)(2,1)S(1)}, u32[]{:S(2)}, u32[]{:S(2)}) %collective-permute-start.32) | collective-permute-done | bytes 294944 | tf_op jit(solution)/shard_map/ppermute | solution.py:62
  378.1 6.3 %collective-permute-done.35 = bf16[256,512]{1,0:T(8,128)(2,1)S(1)} collective-permute-done((bf16[256,512]{1,0:T(8,128)(2,1)S(1)}, bf16[256,512]{1,0:T(8,128)(2,1)S(1)}, u32[]{:S(2)}, u32[]{:S(2)}) %collective-permute-start.35) | collective-permute-done | bytes 262176 | tf_op jit(solution)/shard_map/ppermute | solution.py:62
  384.5 6.2 %collective-permute-done.34 = bf16[256,512]{1,0:T(8,128)(2,1)S(1)} collective-permute-done((bf16[256,512]{1,0:T(8,128)(2,1)S(1)}, bf16[256,512]{1,0:T(8,128)(2,1)S(1)}, u32[]{:S(2)}, u32[]{:S(2)}) %collective-permute-start.34) | collective-permute-done | bytes 262176 | tf_op jit(solution)/shard_map/ppermute | solution.py:62
  390.6 5.3 %collective-permute-done.33 = bf16[256,512]{1,0:T(8,128)(2,1)S(1)} collective-permute-done((bf16[256,512]{1,0:T(8,128)(2,1)S(1)}, bf16[256,512]{1,0:T(8,128)(2,1)S(1)}, u32[]{:S(2)}, u32[]{:S(2)}) %collective-permute-start.33) | collective-permute-done | bytes 262176 | tf_op jit(solution)/shard_map/ppermute | solution.py:62
  400.0 7.5 %attn_products.1 = bf16[2304,1536]{1,0:T(8,128)(2,1)} custom-call(s32[1]{0:T(128)} %bitcast.me_ref, bf16[256,2304]{1,0:T(8,128)(2,1)} %copy-done.36, bf16[256,1024]{1,0:T(8,128)(2,1)} %pad_maximum_fusion.7.lin_ref, bf16[256,2304]{1,0:T(8,128)(2,1)} %copy-done.43, bf16[256,512]{1,0:T(8,128)(2,1)} %copy-done.27), custom_call_target="tpu_custom_call" | custom-call | tf_op jit(solution)/shard_map/attn_products/pallas_call | solution.py:442
  408.5 2.5 convolution_convert_fusion.3
  411.0 2.5 convolution_convert_fusion.2
  415.3 2.8 collective-permute-done.39
  418.1 2.6 pad_maximum_fusion.1
  423.1 6.9 %collective-permute-done.40 = bf16[64,2304]{1,0:T(8,128)(2,1)S(1)} collective-permute-done((bf16[64,2304]{1,0:T(8,128)(2,1)S(1)}, bf16[64,2304]{1,0:T(8,128)(2,1)S(1)}, u32[]{:S(2)}, u32[]{:S(2)}) %collective-permute-start.40) | collective-permute-done | bytes 294944 | tf_op jit(solution)/shard_map/ppermute | solution.py:62
  431.7 8.7 %fusion.2 = f32[288,2304]{1,0:T(8,128)} fusion(bf16[2048,288]{1,0:T(8,128)(2,1)S(1)} %get-tuple-element.95, bf16[2048,4608]{1,0:T(8,128)(2,1)} %all-gather.11.cloned.1.call-done), kind=kOutput, calls=%fused_computation.2 | convolution fusion | flops 2717908992 | bytes 13271040 | tf_op jit(solution)/shard_map/dot_general | solution.py:48
  440.4 4.8 collective-permute-done.41.two_ref
  446.5 3.4 collective-permute-start.43
  453.0 9.8 %add_reduce_fusion = (f32[288]{0:T(512)S(1)}, f32[288,2304]{1,0:T(8,128)}) fusion(bf16[288,2304]{1,0:T(8,128)(2,1)S(1)} %copy-done.47, f32[288,2304]{1,0:T(8,128)} %fusion.2, bf16[288,2304]{1,0:T(8,128)(2,1)S(1)} %copy-done.48, bf16[2048,288]{1,0:T(8,128)(2,1)S(1)} %copy-done.46, bf16[2048,4608]{1,0:T(8,128)(2,1)} %all-gather.11.cloned.1.call-done), kind=kOutput, calls=%fused_computation.9 | convolution fusion | flops 2721890048 | bytes 18580608 | tf_op jit(solution)/shard_map/dot_general | solution.py:48
  472.4 2.5 collective-permute-start.49
  477.7 4.5 fusion.80
  484.4 2.3 fusion.77
  (383 shorter events, 108.1 us)
Async XLA Ops:
  7.2 192.2 %all-gather.5.cloned.1.call-start = ((), (), s32[]{:S(2)}) async-start(), calls=%async_computation.2 | async-start | bytes 23887872 | tf_op jit(solution)/shard_map/all_gather | solution.py:326
  10.7 209.0 %all-gather.7.cloned.1.call-start = ((), (), s32[]{:S(2)}) async-start(), calls=%async_computation.3 | async-start | bytes 11943936 | tf_op jit(solution)/shard_map/all_gather | solution.py:326
  11.5 270.1 %all-gather.9.cloned.1.call-start = ((), (), s32[]{:S(2)}) async-start(), calls=%async_computation.4 | async-start | bytes 10616832 | tf_op jit(solution)/shard_map/all_gather | solution.py:326
  11.9 34.6 %collective-permute-start.1 = (bf16[304,1536]{1,0:T(8,128)(2,1)S(1)}, bf16[304,1536]{1,0:T(8,128)(2,1)S(1)}, u32[]{:S(2)}, u32[]{:S(2)}) collective-permute-start(bf16[304,1536]{1,0:T(8,128)(2,1)S(1)} %fusion.35), channel_id=1, source_target_pairs={{0,16},{4,20},{8,24},{12,28},{16,0},{20,4},{24,8},{28,12},{1,17},{... | collective-permute-start | bytes 2801672 | tf_op jit(solution)/shard_map/ppermute | solution.py:62
  14.9 36.3 %collective-permute-start = (bf16[304,1536]{1,0:T(8,128)(2,1)S(1)}, bf16[304,1536]{1,0:T(8,128)(2,1)S(1)}, u32[]{:S(2)}, u32[]{:S(2)}) collective-permute-start(bf16[304,1536]{1,0:T(8,128)(2,1)S(1)} %fusion.35), channel_id=1, source_target_pairs={{0,8},{4,12},{8,0},{12,4},{16,24},{20,28},{24,16},{28,20},{1,9},{5... | collective-permute-start | bytes 2801672 | tf_op jit(solution)/shard_map/ppermute | solution.py:62
  46.5 22.2 %collective-permute-start.4 = (bf16[144,1536]{1,0:T(8,128)(2,1)S(1)}, bf16[144,1536]{1,0:T(8,128)(2,1)S(1)}, u32[]{:S(2)}, u32[]{:S(2)}) collective-permute-start(bf16[144,1536]{1,0:T(8,128)(2,1)S(1)} %slice.292), channel_id=1, source_target_pairs={{0,8},{4,12},{8,0},{12,4},{16,24},{20,28},{24,16},{28,20},{1,9},{5... | collective-permute-start | bytes 1327112 | tf_op jit(solution)/shard_map/ppermute | solution.py:62
  51.2 20.3 %collective-permute-start.5 = (bf16[144,1536]{1,0:T(8,128)(2,1)S(1)}, bf16[144,1536]{1,0:T(8,128)(2,1)S(1)}, u32[]{:S(2)}, u32[]{:S(2)}) collective-permute-start(bf16[144,1536]{1,0:T(8,128)(2,1)S(1)} %slice.293), channel_id=1, source_target_pairs={{0,16},{4,20},{8,24},{12,28},{16,0},{20,4},{24,8},{28,12},{1,17},{... | collective-permute-start | bytes 1327112 | tf_op jit(solution)/shard_map/ppermute | solution.py:62
  72.3 14.2 %collective-permute-start.6 = (bf16[1152,1536]{1,0:T(8,128)(2,1)}, bf16[1152,1536]{1,0:T(8,128)(2,1)}, u32[]{:S(2)}, u32[]{:S(2)}) collective-permute-start(bf16[1152,1536]{1,0:T(8,128)(2,1)} %constant_dynamic-update-slice_fusion), channel_id=1, source_target_pairs={{0,4},{4,0},{8,12},{12,8},{16,20},{20,16},{24,28},{28,24},{1,5},{5... | collective-permute-start | bytes 10616840 | tf_op jit(solution)/shard_map/ppermute | solution.py:62
  76.0 4.1 collective-permute-start.2
  80.8 3.8 collective-permute-start.3
  93.1 30.1 %slice-start = ((f32[256,1024]{1,0:T(8,128)}), f32[256,512]{1,0:T(8,128)S(1)}, s32[]{:S(2)}) async-start(f32[256,1024]{1,0:T(8,128)} %copy-done.41), calls=%async_computation.7 | async-start | bytes 1048576 | tf_op jit(solution)/shard_map/slice | solution.py:493
  93.9 15.0 %collective-permute-start.7 = (bf16[256,512]{1,0:T(8,128)(2,1)}, bf16[256,512]{1,0:T(8,128)(2,1)S(1)}, u32[]{:S(2)}, u32[]{:S(2)}) collective-permute-start(bf16[256,512]{1,0:T(8,128)(2,1)} %get-tuple-element.150), channel_id=1, source_target_pairs={{0,8},{4,12},{8,0},{12,4},{16,24},{20,28},{24,16},{28,20},{1,9},{5... | collective-permute-start | bytes 786440 | tf_op jit(solution)/shard_map/ppermute | solution.py:62
  95.9 16.9 %collective-permute-start.8 = (bf16[256,512]{1,0:T(8,128)(2,1)}, bf16[256,512]{1,0:T(8,128)(2,1)S(1)}, u32[]{:S(2)}, u32[]{:S(2)}) collective-permute-start(bf16[256,512]{1,0:T(8,128)(2,1)} %get-tuple-element.150), channel_id=1, source_target_pairs={{0,16},{4,20},{8,24},{12,28},{16,0},{20,4},{24,8},{28,12},{1,17},{... | collective-permute-start | bytes 786440 | tf_op jit(solution)/shard_map/ppermute | solution.py:62
  96.0 23.8 %collective-permute-start.9 = (bf16[256,512]{1,0:T(8,128)(2,1)}, bf16[256,512]{1,0:T(8,128)(2,1)}, u32[]{:S(2)}, u32[]{:S(2)}) collective-permute-start(bf16[256,512]{1,0:T(8,128)(2,1)} %get-tuple-element.150), channel_id=1, source_target_pairs={{0,24},{4,28},{8,16},{12,20},{16,8},{20,12},{24,0},{28,4},{1,25},{... | collective-permute-start | bytes 786440 | tf_op jit(solution)/shard_map/ppermute | solution.py:62
  121.8 4.7 collective-permute-start.10
  135.6 10.1 %collective-permute-start.12 = (bf16[64,2304]{1,0:T(8,128)(2,1)}, bf16[64,2304]{1,0:T(8,128)(2,1)}, u32[]{:S(2)}, u32[]{:S(2)}) collective-permute-start(bf16[64,2304]{1,0:T(8,128)(2,1)} %get-tuple-element.120), channel_id=1, source_target_pairs={{0,1},{1,0},{2,3},{3,2},{4,5},{5,4},{6,7},{7,6},{8,9},{9,8},{10,11... | collective-permute-start | bytes 884744 | tf_op jit(solution)/shard_map/ppermute | solution.py:62
  141.0 34.7 %copy-start.11 = (f32[4,2304]{1,0:T(4,128)}, f32[4,2304]{1,0:T(4,128)S(1)}, u32[]{:S(2)}) copy-start(f32[4,2304]{1,0:T(4,128)S(1)} %convert_element_type.132.refs_1_.refs_2_.refs_3_) | copy-start | bytes 110596
  141.0 14.3 %collective-permute-start.11 = (bf16[64,2304]{1,0:T(8,128)(2,1)}, bf16[64,2304]{1,0:T(8,128)(2,1)S(1)}, u32[]{:S(2)}, u32[]{:S(2)}) collective-permute-start(bf16[64,2304]{1,0:T(8,128)(2,1)} %get-tuple-element.121), channel_id=1, source_target_pairs={{0,1},{1,0},{2,3},{3,2},{4,5},{5,4},{6,7},{7,6},{8,9},{9,8},{10,11... | collective-permute-start | bytes 884744 | tf_op jit(solution)/shard_map/ppermute | solution.py:62
  146.8 15.4 %collective-permute-start.13 = (bf16[64,2304]{1,0:T(8,128)(2,1)S(1)}, bf16[64,2304]{1,0:T(8,128)(2,1)S(1)}, u32[]{:S(2)}, u32[]{:S(2)}) collective-permute-start(bf16[64,2304]{1,0:T(8,128)(2,1)S(1)} %add_convert_fusion.4), channel_id=1, source_target_pairs={{0,2},{1,3},{2,0},{3,1},{4,6},{5,7},{6,4},{7,5},{8,10},{9,11},{10,... | collective-permute-start | bytes 884744 | tf_op jit(solution)/shard_map/ppermute | solution.py:62
  177.4 32.4 %copy-start.21 = (bf16[64,2304]{1,0:T(8,128)(2,1)}, bf16[64,2304]{1,0:T(8,128)(2,1)S(1)}, u32[]{:S(2)}) copy-start(bf16[64,2304]{1,0:T(8,128)(2,1)S(1)} %get-tuple-element.64.first_ref) | copy-start | bytes 884740
  177.4 14.5 %collective-permute-start.15 = (bf16[64,2304]{1,0:T(8,128)(2,1)S(1)}, bf16[64,2304]{1,0:T(8,128)(2,1)S(1)}, u32[]{:S(2)}, u32[]{:S(2)}) collective-permute-start(bf16[64,2304]{1,0:T(8,128)(2,1)S(1)} %get-tuple-element.64.first_ref), channel_id=1, source_target_pairs={{0,2},{1,3},{2,0},{3,1},{4,6},{5,7},{6,4},{7,5},{8,10},{9,11},{10,... | collective-permute-start | bytes 884744 | tf_op jit(solution)/shard_map/ppermute | solution.py:62
  177.4 14.6 %collective-permute-start.14 = (bf16[64,2304]{1,0:T(8,128)(2,1)S(1)}, bf16[64,2304]{1,0:T(8,128)(2,1)S(1)}, u32[]{:S(2)}, u32[]{:S(2)}) collective-permute-start(bf16[64,2304]{1,0:T(8,128)(2,1)S(1)} %get-tuple-element.64.first_ref), channel_id=1, source_target_pairs={{0,1},{1,0},{2,3},{3,2},{4,5},{5,4},{6,7},{7,6},{8,9},{9,8},{10,11... | collective-permute-start | bytes 884744 | tf_op jit(solution)/shard_map/ppermute | solution.py:62
  191.9 7.5 %collective-permute-start.16 = (bf16[64,2304]{1,0:T(8,128)(2,1)S(1)}, bf16[64,2304]{1,0:T(8,128)(2,1)}, u32[]{:S(2)}, u32[]{:S(2)}) collective-permute-start(bf16[64,2304]{1,0:T(8,128)(2,1)S(1)} %collective-permute-done.15), channel_id=1, source_target_pairs={{0,1},{1,0},{2,3},{3,2},{4,5},{5,4},{6,7},{7,6},{8,9},{9,8},{10,11... | collective-permute-start | bytes 884744 | tf_op jit(solution)/shard_map/ppermute | solution.py:62
  213.8 186.1 %all-gather.11.cloned.1.call-start = ((), (), s32[]{:S(2)}) async-start(), calls=%async_computation.5 | async-start | bytes 21233664 | tf_op jit(solution)/shard_map/all_gather | solution.py:326
  219.7 54.8 %copy-start.83 = (bf16[2304,2304]{1,0:T(8,128)(2,1)S(1)}, bf16[2304,2304]{1,0:T(8,128)(2,1)}, u32[]{:S(2)}) copy-start(bf16[2304,2304]{1,0:T(8,128)(2,1)} %all-gather.7.cloned.1.call-done) | copy-start | bytes 31850500
  227.2 9.9 %collective-permute-start.18 = (bf16[64,2304]{1,0:T(8,128)(2,1)S(1)}, bf16[64,2304]{1,0:T(8,128)(2,1)S(1)}, u32[]{:S(2)}, u32[]{:S(2)}) collective-permute-start(bf16[64,2304]{1,0:T(8,128)(2,1)S(1)} %get-tuple-element.118), channel_id=1, source_target_pairs={{0,1},{1,0},{2,3},{3,2},{4,5},{5,4},{6,7},{7,6},{8,9},{9,8},{10,11... | collective-permute-start | bytes 884744 | tf_op jit(solution)/shard_map/ppermute | solution.py:62
  228.8 19.0 %collective-permute-start.17 = (bf16[64,2304]{1,0:T(8,128)(2,1)S(1)}, bf16[64,2304]{1,0:T(8,128)(2,1)S(1)}, u32[]{:S(2)}, u32[]{:S(2)}) collective-permute-start(bf16[64,2304]{1,0:T(8,128)(2,1)S(1)} %get-tuple-element.119), channel_id=1, source_target_pairs={{0,1},{1,0},{2,3},{3,2},{4,5},{5,4},{6,7},{7,6},{8,9},{9,8},{10,11... | collective-permute-start | bytes 884744 | tf_op jit(solution)/shard_map/ppermute | solution.py:62
  237.2 15.1 %collective-permute-start.19 = (bf16[64,2304]{1,0:T(8,128)(2,1)S(1)}, bf16[64,2304]{1,0:T(8,128)(2,1)S(1)}, u32[]{:S(2)}, u32[]{:S(2)}) collective-permute-start(bf16[64,2304]{1,0:T(8,128)(2,1)S(1)} %add_convert_fusion.3), channel_id=1, source_target_pairs={{0,2},{1,3},{2,0},{3,1},{4,6},{5,7},{6,4},{7,5},{8,10},{9,11},{10,... | collective-permute-start | bytes 884744 | tf_op jit(solution)/shard_map/ppermute | solution.py:62
  253.0 16.3 %collective-permute-start.20 = (bf16[64,2304]{1,0:T(8,128)(2,1)S(1)}, bf16[64,2304]{1,0:T(8,128)(2,1)S(1)}, u32[]{:S(2)}, u32[]{:S(2)}) collective-permute-start(bf16[64,2304]{1,0:T(8,128)(2,1)S(1)} %get-tuple-element.67.second_ref), channel_id=1, source_target_pairs={{0,1},{1,0},{2,3},{3,2},{4,5},{5,4},{6,7},{7,6},{8,9},{9,8},{10,11... | collective-permute-start | bytes 884744 | tf_op jit(solution)/shard_map/ppermute | solution.py:62
  253.6 14.2 %collective-permute-start.21 = (bf16[64,2304]{1,0:T(8,128)(2,1)S(1)}, bf16[64,2304]{1,0:T(8,128)(2,1)S(1)}, u32[]{:S(2)}, u32[]{:S(2)}) collective-permute-start(bf16[64,2304]{1,0:T(8,128)(2,1)S(1)} %get-tuple-element.67.second_ref), channel_id=1, source_target_pairs={{0,2},{1,3},{2,0},{3,1},{4,6},{5,7},{6,4},{7,5},{8,10},{9,11},{10,... | collective-permute-start | bytes 884744 | tf_op jit(solution)/shard_map/ppermute | solution.py:62
  267.8 6.7 %collective-permute-start.22 = (bf16[64,2304]{1,0:T(8,128)(2,1)S(1)}, bf16[64,2304]{1,0:T(8,128)(2,1)S(1)}, u32[]{:S(2)}, u32[]{:S(2)}) collective-permute-start(bf16[64,2304]{1,0:T(8,128)(2,1)S(1)} %collective-permute-done.21), channel_id=1, source_target_pairs={{0,1},{1,0},{2,3},{3,2},{4,5},{5,4},{6,7},{7,6},{8,9},{9,8},{10,11... | collective-permute-start | bytes 884744 | tf_op jit(solution)/shard_map/ppermute | solution.py:62
  281.6 32.1 %copy-start.9 = (bf16[64,2304]{1,0:T(8,128)(2,1)S(1)}, bf16[64,2304]{1,0:T(8,128)(2,1)}, u32[]{:S(2)}) copy-start(bf16[64,2304]{1,0:T(8,128)(2,1)} %copy-done.8) | copy-start | bytes 884740
  281.6 32.1 %copy-start.22 = (bf16[64,2304]{1,0:T(8,128)(2,1)S(1)}, bf16[64,2304]{1,0:T(8,128)(2,1)}, u32[]{:S(2)}) copy-start(bf16[64,2304]{1,0:T(8,128)(2,1)} %copy-done.21) | copy-start | bytes 884740
  281.6 16.3 %collective-permute-start.23 = (bf16[64,2304]{1,0:T(8,128)(2,1)}, bf16[64,2304]{1,0:T(8,128)(2,1)S(1)}, u32[]{:S(2)}, u32[]{:S(2)}) collective-permute-start(bf16[64,2304]{1,0:T(8,128)(2,1)} %copy-done.23), channel_id=1, source_target_pairs={{0,1},{1,0},{2,3},{3,2},{4,5},{5,4},{6,7},{7,6},{8,9},{9,8},{10,11... | collective-permute-start | bytes 884744 | tf_op jit(solution)/shard_map/ppermute | solution.py:62
  283.2 15.8 %collective-permute-start.24 = (bf16[64,2304]{1,0:T(8,128)(2,1)}, bf16[64,2304]{1,0:T(8,128)(2,1)S(1)}, u32[]{:S(2)}, u32[]{:S(2)}) collective-permute-start(bf16[64,2304]{1,0:T(8,128)(2,1)} %copy-done.23), channel_id=1, source_target_pairs={{0,2},{1,3},{2,0},{3,1},{4,6},{5,7},{6,4},{7,5},{8,10},{9,11},{10,... | collective-permute-start | bytes 884744 | tf_op jit(solution)/shard_map/ppermute | solution.py:62
  299.8 13.1 %collective-permute-start.26 = (bf16[64,2304]{1,0:T(8,128)(2,1)S(1)}, bf16[64,2304]{1,0:T(8,128)(2,1)S(1)}, u32[]{:S(2)}, u32[]{:S(2)}) collective-permute-start(bf16[64,2304]{1,0:T(8,128)(2,1)S(1)} %get-tuple-element.116), channel_id=1, source_target_pairs={{0,1},{1,0},{2,3},{3,2},{4,5},{5,4},{6,7},{7,6},{8,9},{9,8},{10,11... | collective-permute-start | bytes 884744 | tf_op jit(solution)/shard_map/ppermute | solution.py:62
  300.2 18.9 %collective-permute-start.25 = (bf16[64,2304]{1,0:T(8,128)(2,1)}, bf16[64,2304]{1,0:T(8,128)(2,1)}, u32[]{:S(2)}, u32[]{:S(2)}) collective-permute-start(bf16[64,2304]{1,0:T(8,128)(2,1)} %get-tuple-element.117), channel_id=1, source_target_pairs={{0,1},{1,0},{2,3},{3,2},{4,5},{5,4},{6,7},{7,6},{8,9},{9,8},{10,11... | collective-permute-start | bytes 884744 | tf_op jit(solution)/shard_map/ppermute | solution.py:62
  313.7 10.7 %collective-permute-start.27 = (bf16[64,2304]{1,0:T(8,128)(2,1)}, bf16[64,2304]{1,0:T(8,128)(2,1)}, u32[]{:S(2)}, u32[]{:S(2)}) collective-permute-start(bf16[64,2304]{1,0:T(8,128)(2,1)} %add_convert_fusion.2), channel_id=1, source_target_pairs={{0,2},{1,3},{2,0},{3,1},{4,6},{5,7},{6,4},{7,5},{8,10},{9,11},{10,... | collective-permute-start | bytes 884744 | tf_op jit(solution)/shard_map/ppermute | solution.py:62
  314.8 48.1 %all-to-all-start = ((bf16[8,64,576]{2,1,0:T(8,128)(2,1)}), bf16[8,64,576]{2,1,0:T(8,128)(2,1)}, u32[]{:S(2)}, u32[]{:S(2)}) async-start(bf16[8,64,576]{2,1,0:T(8,128)(2,1)} %copy-done.2), calls=%async_computation | async-start | bytes 1310720 | tf_op jit(solution)/shard_map/all_to_all | solution.py:560
  319.0 165.4 %reduce-scatter.2.cloned.1.call-start = ((), (), s32[]{:S(2)}) async-start(), calls=%async_computation.6 | async-start | bytes 7962624 | tf_op jit(solution)/shard_map/reduce_scatter | solution.py:422
  330.7 13.5 %collective-permute-start.28 = (bf16[64,2304]{1,0:T(8,128)(2,1)S(1)}, bf16[64,2304]{1,0:T(8,128)(2,1)S(1)}, u32[]{:S(2)}, u32[]{:S(2)}) collective-permute-start(bf16[64,2304]{1,0:T(8,128)(2,1)S(1)} %get-tuple-element.71), channel_id=1, source_target_pairs={{0,1},{1,0},{2,3},{3,2},{4,5},{5,4},{6,7},{7,6},{8,9},{9,8},{10,11... | collective-permute-start | bytes 884744 | tf_op jit(solution)/shard_map/ppermute | solution.py:62
  330.7 13.4 %collective-permute-start.29 = (bf16[64,2304]{1,0:T(8,128)(2,1)S(1)}, bf16[64,2304]{1,0:T(8,128)(2,1)S(1)}, u32[]{:S(2)}, u32[]{:S(2)}) collective-permute-start(bf16[64,2304]{1,0:T(8,128)(2,1)S(1)} %get-tuple-element.71), channel_id=1, source_target_pairs={{0,2},{1,3},{2,0},{3,1},{4,6},{5,7},{6,4},{7,5},{8,10},{9,11},{10,... | collective-permute-start | bytes 884744 | tf_op jit(solution)/shard_map/ppermute | solution.py:62
  344.2 6.7 %collective-permute-start.30 = (bf16[64,2304]{1,0:T(8,128)(2,1)S(1)}, bf16[64,2304]{1,0:T(8,128)(2,1)S(1)}, u32[]{:S(2)}, u32[]{:S(2)}) collective-permute-start(bf16[64,2304]{1,0:T(8,128)(2,1)S(1)} %collective-permute-done.29), channel_id=1, source_target_pairs={{0,1},{1,0},{2,3},{3,2},{4,5},{5,4},{6,7},{7,6},{8,9},{9,8},{10,11... | collective-permute-start | bytes 884744 | tf_op jit(solution)/shard_map/ppermute | solution.py:62
  362.9 4.0 collective-permute-start.31
  362.9 15.2 %collective-permute-start.32 = (bf16[64,2304]{1,0:T(8,128)(2,1)}, bf16[64,2304]{1,0:T(8,128)(2,1)S(1)}, u32[]{:S(2)}, u32[]{:S(2)}) collective-permute-start(bf16[64,2304]{1,0:T(8,128)(2,1)} %copy-done.64), channel_id=1, source_target_pairs={{0,1},{1,0},{2,3},{3,2},{4,5},{5,4},{6,7},{7,6},{8,9},{9,8},{10,11... | collective-permute-start | bytes 884744 | tf_op jit(solution)/shard_map/ppermute | solution.py:62
  363.4 33.1 %collective-permute-start.38 = (bf16[8,64,576]{2,1,0:T(8,128)(2,1)}, bf16[8,64,576]{2,1,0:T(8,128)(2,1)}, u32[]{:S(2)}, u32[]{:S(2)}) collective-permute-start(bf16[8,64,576]{2,1,0:T(8,128)(2,1)} %all-to-all-done), channel_id=1, source_target_pairs={{0,2},{1,3},{2,0},{3,1},{4,6},{5,7},{6,4},{7,5},{8,10},{9,11},{10,... | collective-permute-start | bytes 1769480 | tf_op jit(solution)/shard_map/ppermute | solution.py:62
  368.5 16.0 %collective-permute-start.35 = (bf16[256,512]{1,0:T(8,128)(2,1)S(1)}, bf16[256,512]{1,0:T(8,128)(2,1)S(1)}, u32[]{:S(2)}, u32[]{:S(2)}) collective-permute-start(bf16[256,512]{1,0:T(8,128)(2,1)S(1)} %get-tuple-element.135), channel_id=1, source_target_pairs={{0,24},{4,28},{8,16},{12,20},{16,8},{20,12},{24,0},{28,4},{1,25},{... | collective-permute-start | bytes 786440 | tf_op jit(solution)/shard_map/ppermute | solution.py:62
  371.7 18.9 %collective-permute-start.34 = (bf16[256,512]{1,0:T(8,128)(2,1)S(1)}, bf16[256,512]{1,0:T(8,128)(2,1)S(1)}, u32[]{:S(2)}, u32[]{:S(2)}) collective-permute-start(bf16[256,512]{1,0:T(8,128)(2,1)S(1)} %get-tuple-element.136), channel_id=1, source_target_pairs={{0,16},{4,20},{8,24},{12,28},{16,0},{20,4},{24,8},{28,12},{1,17},{... | collective-permute-start | bytes 786440 | tf_op jit(solution)/shard_map/ppermute | solution.py:62
  371.9 24.0 %collective-permute-start.33 = (bf16[256,512]{1,0:T(8,128)(2,1)S(1)}, bf16[256,512]{1,0:T(8,128)(2,1)S(1)}, u32[]{:S(2)}, u32[]{:S(2)}) collective-permute-start(bf16[256,512]{1,0:T(8,128)(2,1)S(1)} %get-tuple-element.137), channel_id=1, source_target_pairs={{0,8},{4,12},{8,0},{12,4},{16,24},{20,28},{24,16},{28,20},{1,9},{5... | collective-permute-start | bytes 786440 | tf_op jit(solution)/shard_map/ppermute | solution.py:62
  378.1 40.0 %collective-permute-start.37 = (bf16[8,64,576]{2,1,0:T(8,128)(2,1)}, bf16[8,64,576]{2,1,0:T(8,128)(2,1)}, u32[]{:S(2)}, u32[]{:S(2)}) collective-permute-start(bf16[8,64,576]{2,1,0:T(8,128)(2,1)} %all-to-all-done), channel_id=1, source_target_pairs={{0,1},{1,0},{2,3},{3,2},{4,5},{5,4},{6,7},{7,6},{8,9},{9,8},{10,11... | collective-permute-start | bytes 1769480 | tf_op jit(solution)/shard_map/ppermute | solution.py:62
  396.5 21.6 %collective-permute-start.39 = (bf16[8,64,576]{2,1,0:T(8,128)(2,1)}, bf16[8,64,576]{2,1,0:T(8,128)(2,1)}, u32[]{:S(2)}, u32[]{:S(2)}) collective-permute-start(bf16[8,64,576]{2,1,0:T(8,128)(2,1)} %collective-permute-done.38), channel_id=1, source_target_pairs={{0,1},{1,0},{2,3},{3,2},{4,5},{5,4},{6,7},{7,6},{8,9},{9,8},{10,11... | collective-permute-start | bytes 1769480 | tf_op jit(solution)/shard_map/ppermute | solution.py:62
  413.6 26.8 %collective-permute-start.36 = (bf16[64,2304]{1,0:T(8,128)(2,1)S(1)}, bf16[64,2304]{1,0:T(8,128)(2,1)S(1)}, u32[]{:S(2)}, u32[]{:S(2)}) collective-permute-start(bf16[64,2304]{1,0:T(8,128)(2,1)S(1)} %get-tuple-element.115), channel_id=1, source_target_pairs={{0,1},{1,0},{2,3},{3,2},{4,5},{5,4},{6,7},{7,6},{8,9},{9,8},{10,11... | collective-permute-start | bytes 884744 | tf_op jit(solution)/shard_map/ppermute | solution.py:62
  421.0 8.9 %collective-permute-start.40 = (bf16[64,2304]{1,0:T(8,128)(2,1)S(1)}, bf16[64,2304]{1,0:T(8,128)(2,1)S(1)}, u32[]{:S(2)}, u32[]{:S(2)}) collective-permute-start(bf16[64,2304]{1,0:T(8,128)(2,1)S(1)} %get-tuple-element.114), channel_id=1, source_target_pairs={{0,1},{1,0},{2,3},{3,2},{4,5},{5,4},{6,7},{7,6},{8,9},{9,8},{10,11... | collective-permute-start | bytes 884744 | tf_op jit(solution)/shard_map/ppermute | solution.py:62
  430.0 15.2 %collective-permute-start.41 = (bf16[64,2304]{1,0:T(8,128)(2,1)S(1)}, bf16[64,2304]{1,0:T(8,128)(2,1)S(1)}, u32[]{:S(2)}, u32[]{:S(2)}) collective-permute-start(bf16[64,2304]{1,0:T(8,128)(2,1)S(1)} %add_convert_fusion.1), channel_id=1, source_target_pairs={{0,2},{1,3},{2,0},{3,1},{4,6},{5,7},{6,4},{7,5},{8,10},{9,11},{10,... | collective-permute-start | bytes 884744 | tf_op jit(solution)/shard_map/ppermute | solution.py:62
  446.2 16.6 %collective-permute-start.42 = (bf16[64,2304]{1,0:T(8,128)(2,1)S(1)}, bf16[64,2304]{1,0:T(8,128)(2,1)}, u32[]{:S(2)}, u32[]{:S(2)}) collective-permute-start(bf16[64,2304]{1,0:T(8,128)(2,1)S(1)} %get-tuple-element.93), channel_id=1, source_target_pairs={{0,1},{1,0},{2,3},{3,2},{4,5},{5,4},{6,7},{7,6},{8,9},{9,8},{10,11... | collective-permute-start | bytes 884744 | tf_op jit(solution)/shard_map/ppermute | solution.py:62
  446.5 22.2 %collective-permute-start.43 = (bf16[64,2304]{1,0:T(8,128)(2,1)S(1)}, bf16[64,2304]{1,0:T(8,128)(2,1)}, u32[]{:S(2)}, u32[]{:S(2)}) collective-permute-start(bf16[64,2304]{1,0:T(8,128)(2,1)S(1)} %get-tuple-element.93), channel_id=1, source_target_pairs={{0,2},{1,3},{2,0},{3,1},{4,6},{5,7},{6,4},{7,5},{8,10},{9,11},{10,... | collective-permute-start | bytes 884744 | tf_op jit(solution)/shard_map/ppermute | solution.py:62
  462.9 1.3 collective-permute-start.45
  464.2 4.8 collective-permute-start.48
  465.9 3.7 collective-permute-start.47
  466.7 3.7 collective-permute-start.46
  468.7 14.1 %collective-permute-start.44 = (bf16[64,2304]{1,0:T(8,128)(2,1)}, bf16[64,2304]{1,0:T(8,128)(2,1)S(1)}, u32[]{:S(2)}, u32[]{:S(2)}) collective-permute-start(bf16[64,2304]{1,0:T(8,128)(2,1)} %collective-permute-done.43), channel_id=1, source_target_pairs={{0,1},{1,0},{2,3},{3,2},{4,5},{5,4},{6,7},{7,6},{8,9},{9,8},{10,11... | collective-permute-start | bytes 884744 | tf_op jit(solution)/shard_map/ppermute | solution.py:62
  470.4 6.7 %collective-permute-start.51 = (f32[4,288]{1,0:T(4,128)S(1)}, f32[4,288]{1,0:T(4,128)S(1)}, u32[]{:S(2)}, u32[]{:S(2)}) collective-permute-start(f32[4,288]{1,0:T(4,128)S(1)} %pad_maximum_fusion.10), channel_id=1, source_target_pairs={{0,3},{1,2},{2,1},{3,0},{4,7},{5,6},{6,5},{7,4},{8,11},{9,10},{10,... | collective-permute-start | bytes 13832 | tf_op jit(solution)/shard_map/ppermute | solution.py:62
  472.0 5.1 %collective-permute-start.50 = (f32[4,288]{1,0:T(4,128)S(1)}, f32[4,288]{1,0:T(4,128)S(1)}, u32[]{:S(2)}, u32[]{:S(2)}) collective-permute-start(f32[4,288]{1,0:T(4,128)S(1)} %pad_maximum_fusion.10), channel_id=1, source_target_pairs={{0,2},{1,3},{2,0},{3,1},{4,6},{5,7},{6,4},{7,5},{8,10},{9,11},{10,... | collective-permute-start | bytes 13832 | tf_op jit(solution)/shard_map/ppermute | solution.py:62
  472.4 5.2 %collective-permute-start.49 = (f32[4,288]{1,0:T(4,128)S(1)}, f32[4,288]{1,0:T(4,128)S(1)}, u32[]{:S(2)}, u32[]{:S(2)}) collective-permute-start(f32[4,288]{1,0:T(4,128)S(1)} %pad_maximum_fusion.10), channel_id=1, source_target_pairs={{0,1},{1,0},{2,3},{3,2},{4,5},{5,4},{6,7},{7,6},{8,9},{9,8},{10,11... | collective-permute-start | bytes 13832 | tf_op jit(solution)/shard_map/ppermute | solution.py:62
  (83 other events, 646.3 us)
Sparse Core Ops, SparseCore 0:
  10.8 143.0 all-gather.4
  155.8 63.8 all-gather.6
  222.2 58.8 all-gather.8
  283.3 116.5 all-gather.10
  407.6 65.7 reduce-scatter.1
